TPU v7x, 32 devices: a whole 2x2x4 slice. The times are simulated.
32 devices in a mesh: dp: 2 (over x), section: 16 (over z, y, core).
Axes of the slice: x: 2, y: 2, z: 4, core: 2. Of those that a mesh axis runs over, the one named last changes fastest.
Arguments:
- edge_rows: bfloat16 [16, 6144, 256], P('dp', 'section'), may hold values from -6 to 6
- lengths: int32 [16], P('dp'), may hold values from 512 to 3072, as said below
- norm_gain: float32 [2, 2, 256], replicated, may hold values from 0.5 to 1.5
- norm_bias: float32 [2, 2, 256], replicated, may hold values from -3 to 3
- w_qkv: bfloat16 [2, 256, 512], replicated, may hold values from -0.375 to 0.375
- w_out: bfloat16 [2, 256, 256], replicated, may hold values from -1 to 1
- w_up: bfloat16 [2, 256, 512], replicated, may hold values from -0.375 to 0.375
- w_down: bfloat16 [2, 512, 256], replicated, may hold values from -0.25 to 0.25
Outputs:
- forward_rows: float32 [16, 6144, 256], P('dp', 'section')
- backward_rows: float32 [16, 6144, 256], P('dp', 'section')
- rms_values: float32 [6, 16], P(None, 'dp')
- grad_gain: float32 [2, 2, 256], replicated
- grad_bias: float32 [2, 2, 256], replicated
- grad_qkv: float32 [2, 256, 512], replicated
- grad_out: float32 [2, 256, 256], replicated
- grad_up: float32 [2, 256, 512], replicated
- grad_down: float32 [2, 512, 256], replicated
Inputs may be any that keep to these rules, and one draw needn't show every extreme that they name: `lengths`: in every group of 2 consecutive images one image has length 3072.
All inputs are finite; a program needn't handle non-finite values.
Results may differ from a plain program's by a relative error of at most 0.01.
Values may be sent and summed in bfloat16 or wider, within the bound.
No kernel may reach another device: no remote copies, remote signals or barrier semaphores. Data moves between devices by JAX's collectives and lax.ppermute only.
A program may use at most 384 MiB of HBM per device.

v0:
```python
import math

import jax
import jax.numpy as jnp
from jax import lax
from jax.sharding import PartitionSpec as P

HEADS = 2
WIN = 128
STRIDE = 128
MB = 4


def from_behind(block, axis, distance):
    devices = range(lax.axis_size(axis))
    route = [(i - distance, i) for i in devices if i - distance in devices]
    return lax.ppermute(block, axis, route)


def normalize(stream, gain_row, offset):
    centre = stream - jnp.mean(stream, axis=-1, keepdims=True)
    spread = jnp.mean(centre * centre, axis=-1, keepdims=True)
    return centre * lax.rsqrt(spread + 1e-05) * gain_row + offset


def gelu_tanh(hidden):
    return jax.nn.gelu(hidden, approximate=True)


def log_normalizer(score_list, mask_list):
    largest = None
    for scores, allowed in zip(score_list, mask_list):
        block_max = jnp.max(jnp.where(allowed, scores, -1e30), axis=-1)
        largest = block_max if largest is None else jnp.maximum(largest, block_max)
    exp_total = None
    for scores, allowed in zip(score_list, mask_list):
        addend = jnp.sum(jnp.exp(jnp.where(allowed, scores - largest[..., None], -1e30)), axis=-1)
        exp_total = addend if exp_total is None else exp_total + addend
    return largest + jnp.log(jnp.maximum(exp_total, 1.0))


def soft_weights(scores, allowed, log_total):
    return jnp.exp(jnp.where(allowed, scores - log_total[..., None], -1e30))


def body(edge_rows, lengths, norm_gain, norm_bias, w_qkv, w_out, w_up, w_down):
    section_count = lax.axis_size("section")
    half_size = section_count // 2
    section_index = lax.axis_index("section")
    section_half = section_index // half_size
    slot_index = section_index % half_size
    lower_half = section_half == 0
    upper_half = section_half == 1
    images_dev, row_count, model_width = edge_rows.shape
    per_batch = images_dev // MB
    seq_len = row_count * half_size
    grid_count = seq_len // STRIDE
    mixed_width = w_qkv.shape[2]
    query_width = (mixed_width - model_width) // 2
    key_size = query_width // HEADS
    value_size = model_width // HEADS
    score_scale = 1.0 / math.sqrt(key_size)
    extent = WIN + row_count

    def own_layer(stacked):
        return lax.dynamic_index_in_dim(stacked, section_half, 0, keepdims=False)

    gain_rows = own_layer(norm_gain)
    offsets = own_layer(norm_bias)
    w_mix = own_layer(w_qkv)
    w_proj = own_layer(w_out)
    w_in = own_layer(w_up)
    w_back = own_layer(w_down)
    positions = slot_index * row_count + jnp.arange(row_count, dtype=jnp.int32)
    residue = positions % STRIDE
    ext_pos = slot_index * row_count - WIN + jnp.arange(extent, dtype=jnp.int32)
    grid_pos = jnp.arange(grid_count, dtype=jnp.int32)[:, None] * STRIDE + residue[None, :]
    residue_table = (residue[:, None] == jnp.arange(STRIDE, dtype=jnp.int32)[None, :]).astype(
        jnp.float32
    )

    def batch_lengths(batch_number):
        return lengths[batch_number * per_batch : (batch_number + 1) * per_batch]

    def batch_rows(batch_number):
        return edge_rows[batch_number * per_batch : (batch_number + 1) * per_batch].astype(
            jnp.float32
        )

    def whole_of(window):
        doubled = jnp.concatenate([window, window], axis=1)
        return lax.dynamic_slice_in_dim(
            doubled, (half_size - 1 - slot_index) * row_count, seq_len, 1
        )

    def near_mask_of(limits):
        limit_col = limits[:, None, None]
        query_pos = positions[None, :, None]
        window = ext_pos[None, None, :]
        near_mask = (
            (window <= query_pos)
            & (window > query_pos - WIN)
            & (window >= 0)
            & ((window < limit_col) | (window == query_pos))
        )
        return near_mask[:, None]

    def far_mask_of(limits):
        limit_col = limits[:, None, None]
        query_pos = positions[None, :, None]
        column = jnp.transpose(grid_pos)[None, :, :]
        far_mask = (column < query_pos) & (column < limit_col) & upper_half
        return far_mask[:, None]

    def split_near(extended):
        near_keys = extended[..., :query_width].reshape(per_batch, extent, HEADS, key_size)
        near_values = extended[..., query_width:].reshape(per_batch, extent, HEADS, value_size)
        return (near_keys, near_values)

    def split_far(whole_seq):
        grid_cols = whole_seq.reshape(per_batch, grid_count, STRIDE, whole_seq.shape[2])
        picked = jnp.take(grid_cols, residue, axis=2)
        far_keys = picked[..., :query_width].reshape(
            per_batch, grid_count, row_count, HEADS, key_size
        )
        far_values = picked[..., query_width:].reshape(
            per_batch, grid_count, row_count, HEADS, value_size
        )
        return (far_keys, far_values)

    def square_sums(limits, stream, branch, feed_out):
        inside = (positions[None, :] < limits[:, None])[..., None]
        return jnp.stack(
            [
                jnp.sum(jnp.where(inside, member * member, 0.0), axis=(1, 2))
                for member in (stream, branch, feed_out)
            ]
        )

    zero_rows = jnp.zeros((per_batch, row_count, model_width), jnp.bfloat16)
    arrived = zero_rows
    returned = zero_rows
    forward_list = []
    stat_list = []
    kept_list = []
    backward_list = {}
    running = None
    for moment in range(MB + 2):
        if moment <= MB:
            local_batch = min(moment, MB - 1)
            earlier_batch = max(moment - 1, 0)
            stream = jnp.where(lower_half, batch_rows(local_batch), arrived.astype(jnp.float32))
            limits = jnp.where(lower_half, batch_lengths(local_batch), batch_lengths(earlier_batch))
            forward_normed_low = normalize(stream, gain_rows[0], offsets[0]).astype(jnp.bfloat16)
            mixed_rows = jnp.einsum(
                "brd,de->bre", forward_normed_low, w_mix, preferred_element_type=jnp.float32
            )
            queries_low = (mixed_rows[..., :query_width] * score_scale).astype(jnp.bfloat16)
            forward_key_value = mixed_rows[..., query_width:].astype(jnp.bfloat16)
            forward_queries = queries_low.reshape(per_batch, row_count, HEADS, key_size)
            collect_window = forward_key_value
            step = 1
            while step < half_size:
                collect_received = from_behind(collect_window, "section", step)
                slot_of = (
                    slot_index
                    - 2 * step
                    + 1
                    + jnp.arange(step * row_count, dtype=jnp.int32) // row_count
                )
                collect_received = jnp.where(
                    (slot_of >= 0)[None, :, None],
                    collect_received,
                    jnp.zeros_like(collect_received),
                )
                collect_window = jnp.concatenate([collect_received, collect_window], axis=1)
                step = step * 2
            forward_extended = jnp.concatenate(
                [
                    collect_window[
                        :, (half_size - 1) * row_count - WIN : (half_size - 1) * row_count
                    ],
                    forward_key_value,
                ],
                axis=1,
            )
            forward_near_keys, forward_near_values = split_near(forward_extended)
            forward_near_scores = jnp.einsum(
                "brhd,behd->bhre",
                forward_queries,
                forward_near_keys,
                preferred_element_type=jnp.float32,
            )
            forward_near_mask = near_mask_of(limits)
            forward_far_keys, forward_far_values = split_far(whole_of(collect_window))
            forward_far_scores = jnp.einsum(
                "brhd,bgrhd->bhrg",
                forward_queries,
                forward_far_keys,
                preferred_element_type=jnp.float32,
            )
            forward_far_mask = far_mask_of(limits)
            forward_joint_log = log_normalizer(
                [forward_near_scores, forward_far_scores], [forward_near_mask, forward_far_mask]
            )
            forward_near_weights = soft_weights(
                forward_near_scores, forward_near_mask, forward_joint_log
            )
            forward_far_weights = soft_weights(
                forward_far_scores, forward_far_mask, forward_joint_log
            )
            attended = jnp.einsum(
                "bhre,behd->brhd",
                forward_near_weights.astype(jnp.bfloat16),
                forward_near_values,
                preferred_element_type=jnp.float32,
            )
            attended = attended + jnp.einsum(
                "bhrg,bgrhd->brhd",
                forward_far_weights.astype(jnp.bfloat16),
                forward_far_values,
                preferred_element_type=jnp.float32,
            )
            forward_attended_low = attended.reshape(per_batch, row_count, model_width).astype(
                jnp.bfloat16
            )
            forward_route_state = (forward_joint_log, collect_window)
            forward_branch = jnp.einsum(
                "brd,de->bre", forward_attended_low, w_proj, preferred_element_type=jnp.float32
            )
            forward_middle = stream + forward_branch
            forward_normed_two_low = normalize(forward_middle, gain_rows[1], offsets[1]).astype(
                jnp.bfloat16
            )
            forward_hidden = jnp.einsum(
                "brd,df->brf", forward_normed_two_low, w_in, preferred_element_type=jnp.float32
            )
            forward_active_low = gelu_tanh(forward_hidden).astype(jnp.bfloat16)
            forward_feed_out = jnp.einsum(
                "brf,fd->brd", forward_active_low, w_back, preferred_element_type=jnp.float32
            )
            forward_kept_state = (
                stream,
                forward_normed_low,
                forward_queries,
                forward_extended,
                forward_route_state,
                forward_attended_low,
                forward_middle,
                forward_normed_two_low,
                forward_hidden,
                forward_active_low,
                limits,
            )
            result = forward_middle + forward_feed_out
            branch = forward_branch
            feed_out = forward_feed_out
            forward_list.append(result)
            stat_list.append(square_sums(limits, stream, branch, feed_out))
            kept_list.append(forward_kept_state)
            if moment < MB:
                arrived = from_behind(result.astype(jnp.bfloat16), "section", half_size)
        if moment >= 1:
            late_state = kept_list[max(moment - 2, 0)]
            now_state = kept_list[min(moment, MB)]
            chosen = jax.tree.map(
                lambda upper_item, lower_item: jnp.where(upper_half, upper_item, lower_item),
                now_state,
                late_state,
            )
            cotangent = batch_rows(min(moment - 1, MB - 1))
            in_length = (positions[None, :] < chosen[-1][:, None]).astype(jnp.float32)[..., None]
            upstream = jnp.where(upper_half, cotangent * in_length, returned.astype(jnp.float32))
            (
                backward_stream,
                normed_low,
                queries,
                backward_extended,
                route_state,
                attended_low,
                middle,
                normed_two_low,
                hidden,
                active_low,
                backward_limits,
            ) = chosen
            upstream_low = upstream.astype(jnp.bfloat16)
            grad_back = jnp.einsum(
                "brf,brd->fd", active_low, upstream_low, preferred_element_type=jnp.float32
            )
            grad_active = jnp.einsum(
                "brd,fd->brf", upstream_low, w_back, preferred_element_type=jnp.float32
            )
            unused_value, gelu_pull = jax.vjp(gelu_tanh, hidden)
            grad_hidden = gelu_pull(grad_active)[0].astype(jnp.bfloat16)
            grad_in = jnp.einsum(
                "brd,brf->df", normed_two_low, grad_hidden, preferred_element_type=jnp.float32
            )
            grad_normed_two = jnp.einsum(
                "brf,df->brd", grad_hidden, w_in, preferred_element_type=jnp.float32
            )
            unused_norm, second_pull = jax.vjp(normalize, middle, gain_rows[1], offsets[1])
            middle_part, gain_two, offset_two = second_pull(grad_normed_two)
            grad_middle = upstream + middle_part
            branch_low = grad_middle.astype(jnp.bfloat16)
            grad_proj = jnp.einsum(
                "brd,bre->de", attended_low, branch_low, preferred_element_type=jnp.float32
            )
            grad_attended_low = jnp.einsum(
                "bre,de->brd", branch_low, w_proj, preferred_element_type=jnp.float32
            ).astype(jnp.bfloat16)
            grad_attended = grad_attended_low.reshape(per_batch, row_count, HEADS, value_size)
            joint_log = route_state[0]
            backward_window = route_state[1]
            backward_near_keys, backward_near_values = split_near(backward_extended)
            near_scores = jnp.einsum(
                "brhd,behd->bhre", queries, backward_near_keys, preferred_element_type=jnp.float32
            )
            backward_near_mask = near_mask_of(backward_limits)
            near_pull = jnp.einsum(
                "brhd,behd->bhre",
                grad_attended,
                backward_near_values,
                preferred_element_type=jnp.float32,
            )
            backward_far_keys, backward_far_values = split_far(whole_of(backward_window))
            far_scores = jnp.einsum(
                "brhd,bgrhd->bhrg", queries, backward_far_keys, preferred_element_type=jnp.float32
            )
            backward_far_mask = far_mask_of(backward_limits)
            near_weights = soft_weights(near_scores, backward_near_mask, joint_log)
            far_weights = soft_weights(far_scores, backward_far_mask, joint_log)
            far_pull = jnp.einsum(
                "brhd,bgrhd->bhrg",
                grad_attended,
                backward_far_values,
                preferred_element_type=jnp.float32,
            )
            centred = jnp.sum(near_weights * near_pull, axis=-1) + jnp.sum(
                far_weights * far_pull, axis=-1
            )
            far_grad = (far_weights * (far_pull - centred[..., None])).astype(jnp.bfloat16)
            far_query_grad = jnp.einsum(
                "bhrg,bgrhd->brhd", far_grad, backward_far_keys, preferred_element_type=jnp.float32
            )
            far_key_grad = jnp.einsum(
                "bhrg,brhd->bgrhd", far_grad, queries, preferred_element_type=jnp.float32
            )
            far_value_grad = jnp.einsum(
                "bhrg,brhd->bgrhd",
                far_weights.astype(jnp.bfloat16),
                grad_attended,
                preferred_element_type=jnp.float32,
            )
            far_both = jnp.concatenate(
                [
                    far_key_grad.reshape(per_batch, grid_count, row_count, query_width),
                    far_value_grad.reshape(per_batch, grid_count, row_count, model_width),
                ],
                axis=-1,
            )
            folded = jnp.einsum(
                "bgrf,rs->bgsf", far_both, residue_table, precision=lax.Precision.HIGHEST
            )
            folded = folded.reshape(per_batch, seq_len, far_both.shape[3])
            near_grad = (near_weights * (near_pull - centred[..., None])).astype(jnp.bfloat16)
            grad_queries = (
                jnp.einsum(
                    "bhre,behd->brhd",
                    near_grad,
                    backward_near_keys,
                    preferred_element_type=jnp.float32,
                )
                + far_query_grad
            )
            near_key_grad = jnp.einsum(
                "bhre,brhd->behd", near_grad, queries, preferred_element_type=jnp.float32
            )
            near_value_grad = jnp.einsum(
                "bhre,brhd->behd",
                near_weights.astype(jnp.bfloat16),
                grad_attended,
                preferred_element_type=jnp.float32,
            )
            near_both = jnp.concatenate(
                [
                    near_key_grad.reshape(per_batch, extent, query_width),
                    near_value_grad.reshape(per_batch, extent, model_width),
                ],
                axis=-1,
            )
            padded = jnp.concatenate(
                [jnp.zeros((per_batch, WIN, near_both.shape[2]), jnp.float32), folded], axis=1
            )
            region = lax.dynamic_slice_in_dim(padded, slot_index * row_count, extent, 1) + near_both
            padded = lax.dynamic_update_slice_in_dim(padded, region, slot_index * row_count, 1)
            absolute = padded[:, WIN:]
            backward_doubled = jnp.concatenate([absolute, absolute], axis=1)
            relative = lax.dynamic_slice_in_dim(
                backward_doubled, (slot_index + 1) * row_count % seq_len, seq_len, 1
            )
            width_now = half_size
            while width_now > 1:
                part = width_now // 2
                sent = relative[:, : part * row_count]
                relative = relative[:, part * row_count :]
                received = from_behind(sent.astype(jnp.bfloat16), "section", -part).astype(
                    sent.dtype
                )
                relative = relative + jnp.where(slot_index + part < half_size, received, 0.0)
                width_now = part
            grad_mixed = jnp.concatenate(
                [grad_queries.reshape(per_batch, row_count, query_width) * score_scale, relative],
                axis=-1,
            ).astype(jnp.bfloat16)
            grad_mix = jnp.einsum(
                "brd,bre->de", normed_low, grad_mixed, preferred_element_type=jnp.float32
            )
            grad_normed = jnp.einsum(
                "bre,de->brd", grad_mixed, w_mix, preferred_element_type=jnp.float32
            )
            unused_first, first_pull = jax.vjp(normalize, backward_stream, gain_rows[0], offsets[0])
            stream_part, gain_one, offset_one = first_pull(grad_normed)
            weight_grads = (
                jnp.stack([gain_one, gain_two]),
                jnp.stack([offset_one, offset_two]),
                grad_mix,
                grad_proj,
                grad_in,
                grad_back,
            )
            grad_stream, weight_grads = (grad_middle + stream_part, weight_grads)
            useful = jnp.where(upper_half, moment - 1 < MB, moment >= 2).astype(jnp.float32)
            if running is None:
                running = tuple((member * useful for member in weight_grads))
            else:
                running = tuple(
                    (before + addition * useful for before, addition in zip(running, weight_grads))
                )
            backward_list[moment] = grad_stream
            if moment <= MB:
                returned = from_behind(grad_stream.astype(jnp.bfloat16), "section", -half_size)
    forward_rows = jnp.concatenate(
        [
            jnp.where(lower_half, forward_list[batch_number], forward_list[batch_number + 1])
            for batch_number in range(MB)
        ],
        axis=0,
    )
    backward_rows = jnp.concatenate(
        [
            jnp.where(lower_half, backward_list[batch_number + 2], backward_list[batch_number + 1])
            for batch_number in range(MB)
        ],
        axis=0,
    )
    own_stats = jnp.concatenate(
        [
            jnp.where(lower_half, stat_list[batch_number], stat_list[batch_number + 1])
            for batch_number in range(MB)
        ],
        axis=1,
    )
    layered = jnp.concatenate(
        [jnp.where(lower_half, own_stats, 0.0), jnp.where(upper_half, own_stats, 0.0)], axis=0
    )
    summed_stats = lax.psum(layered, "section")
    rms_values = jnp.sqrt(summed_stats / (lengths.astype(jnp.float32)[None, :] * model_width))
    stacked = tuple(
        (
            jnp.stack([jnp.where(lower_half, member, 0.0), jnp.where(upper_half, member, 0.0)])
            for member in running
        )
    )
    gain_sum, bias_sum, mix_sum, proj_sum, up_sum, down_sum = stacked
    results = lax.psum((gain_sum, bias_sum, mix_sum, proj_sum, up_sum, down_sum), ("dp", "section"))
    return (forward_rows, backward_rows, rms_values) + tuple(results)


def solution(mesh):
    placed = (P("dp", "section", None), P("dp"), P(), P(), P(), P(), P(), P())
    return jax.shard_map(
        body,
        mesh=mesh,
        in_specs=placed,
        out_specs=(
            P("dp", "section", None),
            P("dp", "section", None),
            P(None, "dp"),
            P(),
            P(),
            P(),
            P(),
            P(),
            P(),
        ),
        check_vma=False,
    )
```

profile of v0, /device:TPU:0, one launch (start us, length us, event | category | flops | bytes accessed | tf_op | source)
XLA Modules:
  0.0 3281.0 jit_solution(13513899106183057106)
XLA Ops:
  75.9 37.2 %collective-permute-done.2 = bf16[2,1536,384]{2,1,0:T(8,128)(2,1)} collective-permute-done((bf16[2,1536,384]{2,1,0:T(8,128)(2,1)}, bf16[2,1536,384]{2,1,0:T(8,128)(2,1)}, u32[]{:S(2)}, u32[]{:S(2)}) %collective-permute-start.2) | collective-permute-done | bytes 2359328 | tf_op jit(solution)/shard_map/ppermute | solution.py:17
  196.0 25.7 multiply_reduce_fusion.9
  314.7 34.2 %collective-permute-done.6 = bf16[2,1536,384]{2,1,0:T(8,128)(2,1)} collective-permute-done((bf16[2,1536,384]{2,1,0:T(8,128)(2,1)}, bf16[2,1536,384]{2,1,0:T(8,128)(2,1)}, u32[]{:S(2)}, u32[]{:S(2)}) %collective-permute-start.6) | collective-permute-done | bytes 2359328 | tf_op jit(solution)/shard_map/ppermute | solution.py:17
  431.1 25.7 multiply_reduce_fusion.8
  667.0 26.5 multiply_reduce_fusion.7
  790.5 35.2 %collective-permute-done.14 = bf16[2,1536,384]{2,1,0:T(8,128)(2,1)} collective-permute-done((bf16[2,1536,384]{2,1,0:T(8,128)(2,1)}, bf16[2,1536,384]{2,1,0:T(8,128)(2,1)}, u32[]{:S(2)}, u32[]{:S(2)}) %collective-permute-start.14) | collective-permute-done | bytes 2359328 | tf_op jit(solution)/shard_map/ppermute | solution.py:17
  908.3 26.5 multiply_reduce_fusion.6
  1244.0 57.0 %select_bitcast_fusion = (bf16[2,24,384,384]{3,1,0,2:T(8,128)(2,1)}, bf16[2,24,384,384]{3,1,0,2:T(8,128)(2,1)}, bf16[2,24,384,384]{3,1,0,2:T(8,128)(2,1)}, bf16[...) fusion(bf16[384,2,24,384]{3,2,1,0:T(8,128)(2,1)} %gather_fusion.9, ...), kind=kLoop, calls=%fused_computation.55 | loop fusion | flops 42467328 | bytes 169869696 | tf_op jit(solution)/shard_map/jit(_take)/select_n | solution.py:122
  1360.1 25.8 multiply_reduce_fusion.5
  1421.1 26.8 multiply_reduce_fusion.4
  1594.7 55.0 %collective-permute-done.19 = bf16[2,1536,384]{2,1,0:T(8,128)(2,1)} collective-permute-done((bf16[2,1536,384]{2,1,0:T(8,128)(2,1)}, bf16[2,1536,384]{2,1,0:T(8,128)(2,1)}, u32[]{:S(2)}, u32[]{:S(2)}) %collective-permute-start.19) | collective-permute-done | bytes 2359328 | tf_op jit(solution)/shard_map/ppermute | solution.py:17
  1780.3 26.4 multiply_reduce_fusion.3
  1944.1 52.1 %collective-permute-done.23 = bf16[2,1536,384]{2,1,0:T(8,128)(2,1)} collective-permute-done((bf16[2,1536,384]{2,1,0:T(8,128)(2,1)}, bf16[2,1536,384]{2,1,0:T(8,128)(2,1)}, u32[]{:S(2)}, u32[]{:S(2)}) %collective-permute-start.23) | collective-permute-done | bytes 2359328 | tf_op jit(solution)/shard_map/ppermute | solution.py:17
  2115.4 26.7 multiply_reduce_fusion.2
  2154.8 25.2 multiply_bitcast_fusion.2
  2298.1 36.8 %collective-permute-done.27 = bf16[2,1536,384]{2,1,0:T(8,128)(2,1)} collective-permute-done((bf16[2,1536,384]{2,1,0:T(8,128)(2,1)}, bf16[2,1536,384]{2,1,0:T(8,128)(2,1)}, u32[]{:S(2)}, u32[]{:S(2)}) %collective-permute-start.27) | collective-permute-done | bytes 2359328 | tf_op jit(solution)/shard_map/ppermute | solution.py:17
  2442.6 27.3 collective-permute-done.30
  2491.0 26.9 multiply_reduce_fusion.1
  2674.9 36.4 %collective-permute-done.31 = bf16[2,1536,384]{2,1,0:T(8,128)(2,1)} collective-permute-done((bf16[2,1536,384]{2,1,0:T(8,128)(2,1)}, bf16[2,1536,384]{2,1,0:T(8,128)(2,1)}, u32[]{:S(2)}, u32[]{:S(2)}) %collective-permute-start.31) | collective-permute-done | bytes 2359328 | tf_op jit(solution)/shard_map/ppermute | solution.py:17
  2720.1 54.0 %psum.49 = f32[6,8]{1,0:T(8,128)} all-reduce(f32[6,8]{1,0:T(8,128)} %pad_maximum_fusion.41), channel_id=1, replica_groups=mesh['dp'=2,'section'=16] {'section'}, use_global_device_ids=true, to_apply=%region_105.107 | all-reduce | flops 48 | bytes 384 | tf_op jit(solution)/shard_map/psum | solution.py:467
  2853.5 26.8 multiply_reduce_fusion
  3035.9 41.3 %collective-permute-done.35 = bf16[2,1536,384]{2,1,0:T(8,128)(2,1)S(1)} collective-permute-done((bf16[2,1536,384]{2,1,0:T(8,128)(2,1)S(1)}, bf16[2,1536,384]{2,1,0:T(8,128)(2,1)S(1)}, u32[]{:S(2)}, u32[]{:S(2)}) %collective-permute-start.35) | collective-permute-done | bytes 2359328 | tf_op jit(solution)/shard_map/ppermute | solution.py:17
  3130.0 45.4 %all-reduce.5 = (f32[2,2,256]{2,1,0:T(2,128)}, f32[2,2,256]{2,1,0:T(2,128)}) all-reduce(f32[2,2,256]{2,1,0:T(2,128)S(1)} %pad_maximum_fusion.42, f32[2,2,256]{2,1,0:T(2,128)S(1)} %pad_maximum_fusion.43), channel_id=1, replica_groups=mesh['dp'=2,'section'=16] {'dp','section'}, use_global_device_ids=true, to_apply=%region_116.118 | all-reduce | flops 2048 | bytes 16384 | tf_op jit(solution)/shard_map/psum | solution.py:476
  3175.4 92.2 %all-reduce.9.cloned.1.call-done = (f32[2,256,512]{2,1,0:T(8,128)}, f32[2,256,256]{2,1,0:T(8,128)}, f32[2,256,512]{2,1,0:T(8,128)}, f32[2,512,256]{2,1,0:T(8,128)}) async-done(((f32[2,256,512]{2,1,0:T(8,128)}, f32[2,256,256]{2,1,0:T(8,128)}, f32[2,256,512]{2,1,0:T(8,128)}, f32[2,512,256]{2,1,0:T(8,128)}), (f32[2,256,512]{2,1,0:T(8,128)}, f32[2,256,256]{2,1,0:T(8,128)}, f32[2,256,512]{2,1,0:T(8,128)}, ...) | async-done | bytes 3670032 | tf_op jit(solution)/shard_map/psum | solution.py:476
  (1865 shorter events, 2365.7 us)
Async XLA Ops:
  7.2 3260.4 %all-reduce.9.cloned.1.call-start = ((), (), s32[]{:S(2)}) async-start(), calls=%async_computation | async-start | bytes 7340032 | tf_op jit(solution)/shard_map/psum | solution.py:476
  20.0 36.5 %collective-permute-start.1 = (bf16[2,768,384]{2,1,0:T(8,128)(2,1)S(1)}, bf16[2,768,384]{2,1,0:T(8,128)(2,1)S(1)}, u32[]{:S(2)}, u32[]{:S(2)}) collective-permute-start(bf16[2,768,384]{2,1,0:T(8,128)(2,1)S(1)} %pad_maximum_fusion.17), channel_id=1, source_target_pairs={{0,2},{1,3},{2,4},{3,5},{4,6},{5,7},{6,8},{7,9},{8,10},{9,11},{10,... | collective-permute-start | bytes 3538952 | tf_op jit(solution)/shard_map/ppermute | solution.py:17
  59.5 53.5 %collective-permute-start.2 = (bf16[2,1536,384]{2,1,0:T(8,128)(2,1)}, bf16[2,1536,384]{2,1,0:T(8,128)(2,1)}, u32[]{:S(2)}, u32[]{:S(2)}) collective-permute-start(bf16[2,1536,384]{2,1,0:T(8,128)(2,1)} %pad_maximum_fusion.7), channel_id=1, source_target_pairs={{0,4},{1,5},{2,6},{3,7},{4,8},{5,9},{6,10},{7,11},{8,12},{9,13},{1... | collective-permute-start | bytes 7077896 | tf_op jit(solution)/shard_map/ppermute | solution.py:17
  247.9 32.9 %collective-permute-start.5 = (bf16[2,768,384]{2,1,0:T(8,128)(2,1)S(1)}, bf16[2,768,384]{2,1,0:T(8,128)(2,1)S(1)}, u32[]{:S(2)}, u32[]{:S(2)}) collective-permute-start(bf16[2,768,384]{2,1,0:T(8,128)(2,1)S(1)} %pad_maximum_fusion.18), channel_id=1, source_target_pairs={{0,2},{1,3},{2,4},{3,5},{4,6},{5,7},{6,8},{7,9},{8,10},{9,11},{10,... | collective-permute-start | bytes 3538952 | tf_op jit(solution)/shard_map/ppermute | solution.py:17
  284.8 64.2 %collective-permute-start.6 = (bf16[2,1536,384]{2,1,0:T(8,128)(2,1)}, bf16[2,1536,384]{2,1,0:T(8,128)(2,1)}, u32[]{:S(2)}, u32[]{:S(2)}) collective-permute-start(bf16[2,1536,384]{2,1,0:T(8,128)(2,1)} %pad_maximum_fusion.8), channel_id=1, source_target_pairs={{0,4},{1,5},{2,6},{3,7},{4,8},{5,9},{6,10},{7,11},{8,12},{9,13},{1... | collective-permute-start | bytes 7077896 | tf_op jit(solution)/shard_map/ppermute | solution.py:17
  485.9 33.7 %collective-permute-start.9 = (bf16[2,768,384]{2,1,0:T(8,128)(2,1)S(1)}, bf16[2,768,384]{2,1,0:T(8,128)(2,1)S(1)}, u32[]{:S(2)}, u32[]{:S(2)}) collective-permute-start(bf16[2,768,384]{2,1,0:T(8,128)(2,1)S(1)} %pad_maximum_fusion.19), channel_id=1, source_target_pairs={{0,2},{1,3},{2,4},{3,5},{4,6},{5,7},{6,8},{7,9},{8,10},{9,11},{10,... | collective-permute-start | bytes 3538952 | tf_op jit(solution)/shard_map/ppermute | solution.py:17
  522.6 62.3 %collective-permute-start.10 = (bf16[2,1536,384]{2,1,0:T(8,128)(2,1)}, bf16[2,1536,384]{2,1,0:T(8,128)(2,1)}, u32[]{:S(2)}, u32[]{:S(2)}) collective-permute-start(bf16[2,1536,384]{2,1,0:T(8,128)(2,1)} %pad_maximum_fusion.9), channel_id=1, source_target_pairs={{0,4},{1,5},{2,6},{3,7},{4,8},{5,9},{6,10},{7,11},{8,12},{9,13},{1... | collective-permute-start | bytes 7077896 | tf_op jit(solution)/shard_map/ppermute | solution.py:17
  726.8 33.0 %collective-permute-start.13 = (bf16[2,768,384]{2,1,0:T(8,128)(2,1)S(1)}, bf16[2,768,384]{2,1,0:T(8,128)(2,1)S(1)}, u32[]{:S(2)}, u32[]{:S(2)}) collective-permute-start(bf16[2,768,384]{2,1,0:T(8,128)(2,1)S(1)} %pad_maximum_fusion.20), channel_id=1, source_target_pairs={{0,2},{1,3},{2,4},{3,5},{4,6},{5,7},{6,8},{7,9},{8,10},{9,11},{10,... | collective-permute-start | bytes 3538952 | tf_op jit(solution)/shard_map/ppermute | solution.py:17
  763.8 62.0 %collective-permute-start.14 = (bf16[2,1536,384]{2,1,0:T(8,128)(2,1)}, bf16[2,1536,384]{2,1,0:T(8,128)(2,1)}, u32[]{:S(2)}, u32[]{:S(2)}) collective-permute-start(bf16[2,1536,384]{2,1,0:T(8,128)(2,1)} %pad_maximum_fusion.10), channel_id=1, source_target_pairs={{0,4},{1,5},{2,6},{3,7},{4,8},{5,9},{6,10},{7,11},{8,12},{9,13},{1... | collective-permute-start | bytes 7077896 | tf_op jit(solution)/shard_map/ppermute | solution.py:17
  966.7 41.5 %collective-permute-start.17 = (bf16[2,768,384]{2,1,0:T(8,128)(2,1)}, bf16[2,768,384]{2,1,0:T(8,128)(2,1)}, u32[]{:S(2)}, u32[]{:S(2)}) collective-permute-start(bf16[2,768,384]{2,1,0:T(8,128)(2,1)} %pad_maximum_fusion.21), channel_id=1, source_target_pairs={{0,2},{1,3},{2,4},{3,5},{4,6},{5,7},{6,8},{7,9},{8,10},{9,11},{10,... | collective-permute-start | bytes 3538952 | tf_op jit(solution)/shard_map/ppermute | solution.py:17
  1012.5 58.5 %collective-permute-start.18 = (bf16[2,1536,384]{2,1,0:T(8,128)(2,1)}, bf16[2,1536,384]{2,1,0:T(8,128)(2,1)}, u32[]{:S(2)}, u32[]{:S(2)}) collective-permute-start(bf16[2,1536,384]{2,1,0:T(8,128)(2,1)} %pad_maximum_fusion.11), channel_id=1, source_target_pairs={{0,4},{1,5},{2,6},{3,7},{4,8},{5,9},{6,10},{7,11},{8,12},{9,13},{1... | collective-permute-start | bytes 7077896 | tf_op jit(solution)/shard_map/ppermute | solution.py:17
  1593.4 56.3 %collective-permute-start.19 = (bf16[2,1536,384]{2,1,0:T(8,128)(2,1)}, bf16[2,1536,384]{2,1,0:T(8,128)(2,1)}, u32[]{:S(2)}, u32[]{:S(2)}) collective-permute-start(bf16[2,1536,384]{2,1,0:T(8,128)(2,1)} %slice.729), channel_id=1, source_target_pairs={{4,0},{5,1},{6,2},{7,3},{8,4},{9,5},{10,6},{11,7},{12,8},{13,9},{1... | collective-permute-start | bytes 7077896 | tf_op jit(solution)/shard_map/ppermute | solution.py:17
  1656.5 29.6 collective-permute-start.20
  1690.6 38.4 %collective-permute-start.21 = (bf16[2,384,384]{2,1,0:T(8,128)(2,1)}, bf16[2,384,384]{2,1,0:T(8,128)(2,1)}, u32[]{:S(2)}, u32[]{:S(2)}) collective-permute-start(bf16[2,384,384]{2,1,0:T(8,128)(2,1)} %slice.739), channel_id=1, source_target_pairs={{1,0},{2,1},{3,2},{4,3},{5,4},{6,5},{7,6},{8,7},{9,8},{10,9},{11,1... | collective-permute-start | bytes 1769480 | tf_op jit(solution)/shard_map/ppermute | solution.py:17
  1738.7 24.2 collective-permute-start.22
  1940.9 55.2 %collective-permute-start.23 = (bf16[2,1536,384]{2,1,0:T(8,128)(2,1)}, bf16[2,1536,384]{2,1,0:T(8,128)(2,1)}, u32[]{:S(2)}, u32[]{:S(2)}) collective-permute-start(bf16[2,1536,384]{2,1,0:T(8,128)(2,1)} %slice.728), channel_id=1, source_target_pairs={{4,0},{5,1},{6,2},{7,3},{8,4},{9,5},{10,6},{11,7},{12,8},{13,9},{1... | collective-permute-start | bytes 7077896 | tf_op jit(solution)/shard_map/ppermute | solution.py:17
  2003.0 44.3 %collective-permute-start.24 = (bf16[2,768,384]{2,1,0:T(8,128)(2,1)}, bf16[2,768,384]{2,1,0:T(8,128)(2,1)}, u32[]{:S(2)}, u32[]{:S(2)}) collective-permute-start(bf16[2,768,384]{2,1,0:T(8,128)(2,1)} %slice.733), channel_id=1, source_target_pairs={{2,0},{3,1},{4,2},{5,3},{6,4},{7,5},{8,6},{9,7},{10,8},{11,9},{12,... | collective-permute-start | bytes 3538952 | tf_op jit(solution)/shard_map/ppermute | solution.py:17
  2280.1 54.7 %collective-permute-start.27 = (bf16[2,1536,384]{2,1,0:T(8,128)(2,1)}, bf16[2,1536,384]{2,1,0:T(8,128)(2,1)}, u32[]{:S(2)}, u32[]{:S(2)}) collective-permute-start(bf16[2,1536,384]{2,1,0:T(8,128)(2,1)} %slice.727), channel_id=1, source_target_pairs={{4,0},{5,1},{6,2},{7,3},{8,4},{9,5},{10,6},{11,7},{12,8},{13,9},{1... | collective-permute-start | bytes 7077896 | tf_op jit(solution)/shard_map/ppermute | solution.py:17
  2341.7 81.7 %collective-permute-start.28 = (bf16[2,768,384]{2,1,0:T(8,128)(2,1)}, bf16[2,768,384]{2,1,0:T(8,128)(2,1)}, u32[]{:S(2)}, u32[]{:S(2)}) collective-permute-start(bf16[2,768,384]{2,1,0:T(8,128)(2,1)} %slice.732), channel_id=1, source_target_pairs={{2,0},{3,1},{4,2},{5,3},{6,4},{7,5},{8,6},{9,7},{10,8},{11,9},{12,... | collective-permute-start | bytes 3538952 | tf_op jit(solution)/shard_map/ppermute | solution.py:17
  2440.6 29.3 collective-permute-start.30
  2656.2 55.1 %collective-permute-start.31 = (bf16[2,1536,384]{2,1,0:T(8,128)(2,1)}, bf16[2,1536,384]{2,1,0:T(8,128)(2,1)}, u32[]{:S(2)}, u32[]{:S(2)}) collective-permute-start(bf16[2,1536,384]{2,1,0:T(8,128)(2,1)} %slice.726), channel_id=1, source_target_pairs={{4,0},{5,1},{6,2},{7,3},{8,4},{9,5},{10,6},{11,7},{12,8},{13,9},{1... | collective-permute-start | bytes 7077896 | tf_op jit(solution)/shard_map/ppermute | solution.py:17
  2718.2 64.3 %collective-permute-start.32 = (bf16[2,768,384]{2,1,0:T(8,128)(2,1)}, bf16[2,768,384]{2,1,0:T(8,128)(2,1)}, u32[]{:S(2)}, u32[]{:S(2)}) collective-permute-start(bf16[2,768,384]{2,1,0:T(8,128)(2,1)} %slice.731), channel_id=1, source_target_pairs={{2,0},{3,1},{4,2},{5,3},{6,4},{7,5},{8,6},{9,7},{10,8},{11,9},{12,... | collective-permute-start | bytes 3538952 | tf_op jit(solution)/shard_map/ppermute | solution.py:17
  3021.9 55.3 %collective-permute-start.35 = (bf16[2,1536,384]{2,1,0:T(8,128)(2,1)S(1)}, bf16[2,1536,384]{2,1,0:T(8,128)(2,1)S(1)}, u32[]{:S(2)}, u32[]{:S(2)}) collective-permute-start(bf16[2,1536,384]{2,1,0:T(8,128)(2,1)S(1)} %slice.725), channel_id=1, source_target_pairs={{4,0},{5,1},{6,2},{7,3},{8,4},{9,5},{10,6},{11,7},{12,8},{13,9},{1... | collective-permute-start | bytes 7077896 | tf_op jit(solution)/shard_map/ppermute | solution.py:17
  3079.0 29.7 collective-permute-start.36
  (580 other events, 8491.5 us)
Sparse Core Ops, SparseCore 0:
  3121.3 146.3 all-reduce.8
where the time goes:
time: 3300 us; the launch traced here: 3280 us
  local copies, waits for them, and re-layouts  1080 us (33%)
  other arithmetic  913 us (28%)
  waiting for transfers between devices  694 us (21%)
  matrix products  288 us (9%)
  starting transfers between devices  187 us (6%)
  blocking collectives  99.4 us (3%)
    ppermute x38, waiting for transfers between devices, from_behind(): return lax.ppermute(block, axis, route)  601 us
    unnamed x61, other arithmetic  310 us
    unnamed x1170, local copies, waits for them, and re-layouts  194 us
    ppermute x38, starting transfers between devices, from_behind(): return lax.ppermute(block, axis, route)  187 us
    reshape x10, local copies, waits for them, and re-layouts, split_far(): picked[..., query_width:]  139 us
    gather x10, local copies, waits for them, and re-layouts, split_far(): picked = jnp.take(grid_cols, residue, axis=2)  137 us
    transpose x5, other arithmetic, body(): jnp.einsum('bhrg,brhd->bgrhd', far_weights.astype(jnp.bfloat16), grad_att...  124 us
    reshape x5, local copies, waits for them, and re-layouts, body(): far_value_grad.reshape(per_batch, grid_count, row_count, model_width)  121 us
  transfers between devices with their start and end apart: 39, of which 30 were waited for; matrix products, arithmetic and copies ran while one was open for 11% of the time, Pallas kernels for 0%

commit v1 on v0

v1 whole, which is shorter than its diff:
```python
import functools
import math

import jax
import jax.numpy as jnp
from jax import lax
from jax.experimental import pallas as pl
from jax.experimental.pallas import tpu as pltpu
from jax.sharding import PartitionSpec as P

HEADS = 2
WIN = 128
STRIDE = 128
NEG = -1e30
F32 = jnp.float32
BF16 = jnp.bfloat16
TB = 256
RES = 4
UNROLL = 2
VMEM_LIMIT = 56 * 1024 * 1024


def dot(left, right):
    return lax.dot_general(left, right, (((1,), (0,)), ((), ())), preferred_element_type=F32)


def dot_t(left, right):
    return lax.dot_general(left, right, (((1,), (1,)), ((), ())), preferred_element_type=F32)


def t_dot(left, right):
    return lax.dot_general(left, right, (((0,), (0,)), ((), ())), preferred_element_type=F32)


def score_scale(query_width):
    return 1.0 / math.sqrt(query_width // HEADS)


def norm_parts(rows):
    centre = rows - jnp.mean(rows, axis=-1, keepdims=True)
    scale = lax.rsqrt(jnp.mean(centre * centre, axis=-1, keepdims=True) + 1e-05)
    return centre * scale, scale


def norm_back(grad, unit, scale, gain):
    scaled = grad * gain
    first = jnp.mean(scaled, axis=-1, keepdims=True)
    second = jnp.mean(scaled * unit, axis=-1, keepdims=True)
    return scale * (scaled - first - unit * second)


def col_sum(rows):
    return jnp.sum(rows.reshape(rows.shape[0] // 8, 8, rows.shape[1]), axis=0)


def gelu_pair(hidden):
    c0 = math.sqrt(2.0 / math.pi)
    square = hidden * hidden
    share = 0.5 + 0.5 * jnp.tanh(hidden * (c0 + (c0 * 0.044715) * square))
    active = hidden * share
    slope = share + active * (1.0 - share) * (2.0 * c0 + (6.0 * c0 * 0.044715) * square)
    return active, slope


def head_split(rows):
    lane = lax.broadcasted_iota(jnp.int32, rows.shape, 1)
    zero = jnp.zeros_like(rows)
    low = lane < rows.shape[1] // HEADS
    return jnp.concatenate([jnp.where(low, rows, zero), jnp.where(low, zero, rows)], axis=0)


def head_join(stacked):
    half = stacked.shape[0] // 2
    lane = lax.broadcasted_iota(jnp.int32, (half, stacked.shape[1]), 1)
    return jnp.where(lane < stacked.shape[1] // HEADS, stacked[:half], stacked[half:])


def near_masks(base, limit):
    row = lax.broadcasted_iota(jnp.int32, (2 * WIN, WIN), 0)
    row = jnp.where(row >= WIN, row - WIN, row)
    col = lax.broadcasted_iota(jnp.int32, (2 * WIN, WIN), 1)
    own = col <= row
    key = base + col - jnp.where(own, 0, WIN)
    allowed = (key >= 0) & ((key < limit) | (col == row))
    return own, allowed


def near_scores(split_q, keys, own, allowed):
    scores = dot_t(split_q, keys)
    folded = jnp.where(own, scores[:, WIN:], scores[:, :WIN])
    return jnp.where(allowed, folded, NEG)


def unfold(folded, own):
    return jnp.concatenate([jnp.where(own, 0.0, folded), jnp.where(own, folded, 0.0)], axis=1).astype(BF16)


def near_forward(queries, keys, values, base, limit):
    own, allowed = near_masks(base, limit)
    scores = near_scores(head_split(queries), keys, own, allowed)
    largest = jnp.max(scores, axis=-1, keepdims=True)
    powers = jnp.exp(scores - largest)
    total = jnp.sum(powers, axis=-1, keepdims=True)
    weights = unfold(powers, own)
    hd = values.shape[1] // HEADS
    out = [dot(weights[h * WIN : (h + 1) * WIN], values[:, h * hd : (h + 1) * hd]) for h in range(HEADS)]
    return out, largest, total


def near_backward(queries, keys, values, grad_out, log_total, delta, base, limit):
    own, allowed = near_masks(base, limit)
    split_q = head_split(queries)
    weights = jnp.exp(near_scores(split_q, keys, own, allowed) - log_total)
    hd = values.shape[1] // HEADS
    pull = jnp.concatenate(
        [dot_t(grad_out[:, h * hd : (h + 1) * hd], values[:, h * hd : (h + 1) * hd]) for h in range(HEADS)], axis=0
    )
    pull = jnp.where(own, pull[:, WIN:], pull[:, :WIN])
    slope = unfold(weights * (pull - delta), own)
    weights = unfold(weights, own)
    grad_q = head_join(dot(slope, keys))
    grad_k = t_dot(slope, split_q)
    grad_v = jnp.concatenate(
        [t_dot(weights[h * WIN : (h + 1) * WIN], grad_out[:, h * hd : (h + 1) * hd]) for h in range(HEADS)], axis=1
    )
    return grad_q, grad_k, grad_v


def stack_stat(stat, width=128):
    return jnp.concatenate([stat[:, 0:1], stat[:, width // 2 : width // 2 + 1]], axis=0)


def spread_stat(stacked, width=128):
    half = stacked.shape[0] // 2
    lane = lax.broadcasted_iota(jnp.int32, (half, width), 1)
    return jnp.where(lane < width // 2, stacked[:half], stacked[half:])


def masked_squares(rows, base, limit):
    pos = base + lax.broadcasted_iota(jnp.int32, (rows.shape[0], 1), 0)
    return col_sum(jnp.where(pos < limit, rows * rows, 0.0))


def gather_pieces(info, pieces, target, sems, want_low):
    quarter = len(pieces) // 2
    rows = pieces[0].shape[0]

    def each(act):
        for t in range(quarter):
            place = target.at[pl.ds((t ^ info[2]) * rows, rows)]
            low, high = (t, t + quarter) if want_low else (t + quarter, t)

            @pl.when(info[3] == 0)
            def _():
                act(pltpu.make_async_copy(pieces[low], place, sems.at[t]))

            @pl.when(info[3] != 0)
            def _():
                act(pltpu.make_async_copy(pieces[high], place, sems.at[t]))

    each(lambda c: c.start())
    each(lambda c: c.wait())


def first_kernel(info, *refs):
    pieces = refs[:8]
    gain, bias, w_mix, x_out, q_out, kv_out, sems = refs[8:]
    gather_pieces(info, pieces, x_out, sems, True)
    qw = q_out.shape[1]

    def block(i, _):
        at = pl.ds(pl.multiple_of(i * TB, TB), TB)
        unit, _ = norm_parts(x_out[at].astype(F32))
        normed = (unit * gain[0:1] + bias[0:1]).astype(BF16)
        mixed = dot(normed, w_mix[...])
        q_out[at] = (mixed[:, :qw] * score_scale(qw)).astype(BF16)
        kv_out[at] = mixed[:, qw:].astype(BF16)
        return 0

    lax.fori_loop(0, x_out.shape[0] // TB, block, 0)


def load_extended(halo, kv, ext):
    ext[: halo.shape[0]] = halo[...]
    ext[halo.shape[0] :] = kv[...]


def second_kernel(
    info, x, q, kv, halo, gain, bias, w_proj, w_in, w_back, gain_next, bias_next, w_mix_next,
    z_out, q_next, kv_next, o_out, lse_out, active_out, slope_out, mid_out, squares, ext,
):
    step = pl.program_id(0)
    qw = q.shape[1]
    n = kv.shape[0]

    @pl.when(step == 0)
    def _():
        load_extended(halo, kv, ext)
        squares[...] = jnp.zeros_like(squares)

    limit = info[1]
    start = step * TB
    base = info[0] * n + start
    outs = []
    for sub in range(TB // WIN):
        near = pl.ds(pl.multiple_of(start + sub * WIN, WIN), 2 * WIN)
        keys = ext[near, :qw]
        values = ext[near, qw:]
        queries = q[sub * WIN : (sub + 1) * WIN]
        out, largest, total = near_forward(queries, keys, values, base + sub * WIN, limit)
        inverse = 1.0 / total
        lse_out[sub * WIN : (sub + 1) * WIN] = spread_stat(largest + jnp.log(total))
        outs.append(jnp.concatenate([out[0] * inverse[:WIN], out[1] * inverse[WIN:]], axis=1))
    attended = jnp.concatenate(outs, axis=0).astype(BF16)
    o_out[...] = attended
    stream = x[...].astype(F32)
    branch = dot(attended, w_proj[...])
    middle = stream + branch
    mid_out[...] = middle
    unit, _ = norm_parts(middle)
    normed = (unit * gain[1:2] + bias[1:2]).astype(BF16)
    active, slope = gelu_pair(dot(normed, w_in[...]))
    active = active.astype(BF16)
    active_out[...] = active
    slope_out[...] = slope.astype(BF16)
    feed = dot(active, w_back[...])
    z = (middle + feed).astype(BF16)
    z_out[...] = z
    squares[0] += masked_squares(stream, base, limit)
    squares[1] += masked_squares(branch, base, limit)
    squares[2] += masked_squares(feed, base, limit)
    unit, _ = norm_parts(z.astype(F32))
    normed = (unit * gain_next[0:1] + bias_next[0:1]).astype(BF16)
    mixed = dot(normed, w_mix_next[...])
    q_next[...] = (mixed[:, :qw] * score_scale(qw)).astype(BF16)
    kv_next[...] = mixed[:, qw:].astype(BF16)


def far_mask(grid_q, grid_k, part_grid):
    shape = (HEADS * RES * grid_q, RES * grid_k)
    row = lax.broadcasted_iota(jnp.int32, shape, 0)
    col = lax.broadcasted_iota(jnp.int32, shape, 1)
    row = jnp.where(row >= RES * grid_q, row - RES * grid_q, row)
    row_res = jnp.zeros(shape, jnp.int32)
    col_res = jnp.zeros(shape, jnp.int32)
    for r in range(1, RES):
        row_res += (row >= r * grid_q).astype(jnp.int32)
        col_res += (col >= r * grid_k).astype(jnp.int32)
    row_grid = row - row_res * grid_q + part_grid
    col_grid = col - col_res * grid_k
    allowed = (row_res == col_res) & (col_grid < row_grid)
    return allowed, col_grid * STRIDE + col_res


def far_forward_kernel(info, q, kv, other, qr, kr, vr, o_far, lse_far, q_s, k_s, v_s, o_s, lse_s):
    n, qw = q.shape
    grid_q = n // STRIDE
    grid_k = 2 * grid_q
    part = info[0]
    limit = info[1]

    def place(g, _):
        at = pl.ds(pl.multiple_of(g * STRIDE, STRIDE), STRIDE)
        own = kv[at].astype(F32)
        early = jnp.where(part == 0, own, other[at].astype(F32))
        q_s[pl.ds(g, STRIDE, stride=grid_q), :] = q[at].astype(F32)
        k_s[pl.ds(g, STRIDE, stride=grid_k), :] = early[:, :qw]
        k_s[pl.ds(g + grid_q, STRIDE, stride=grid_k), :] = own[:, :qw]
        hd = v_s.shape[1]
        for h in range(HEADS):
            v_s[h, pl.ds(g, STRIDE, stride=grid_k), :] = early[:, qw + h * 128 : qw + (h + 1) * 128]
            v_s[h, pl.ds(g + grid_q, STRIDE, stride=grid_k), :] = own[:, qw + h * 128 : qw + (h + 1) * 128]
        return 0

    lax.fori_loop(0, grid_q, place, 0)
    base_mask, key_pos = far_mask(grid_q, grid_k, part * grid_q)
    rows_q = RES * grid_q
    rows_k = RES * grid_k

    def one(i):
        at_q = pl.ds(pl.multiple_of(i * rows_q, rows_q), rows_q)
        at_k = pl.ds(pl.multiple_of(i * rows_k, rows_k), rows_k)
        queries = q_s[at_q].astype(BF16)
        keys = k_s[at_k].astype(BF16)
        values = [v_s[h, at_k].astype(BF16) for h in range(HEADS)]
        qr[at_q] = queries
        kr[at_k] = keys
        for h in range(HEADS):
            vr[at_k, h * 128 : (h + 1) * 128] = values[h]
        allowed = base_mask & (key_pos + i * RES < limit)
        scores = jnp.where(allowed, dot_t(head_split(queries), keys), NEG)
        largest = jnp.max(scores, axis=-1, keepdims=True)
        powers = jnp.where(allowed, jnp.exp(scores - largest), 0.0)
        total = jnp.sum(powers, axis=-1, keepdims=True)
        safe = jnp.maximum(total, 1e-30)
        weights = (powers * (1.0 / safe)).astype(BF16)
        lse = jnp.where(total > 0.0, largest + jnp.log(safe), NEG)
        lse_s[at_q] = spread_stat(lse)
        for h in range(HEADS):
            o_s[h, at_q] = dot(weights[h * rows_q : (h + 1) * rows_q], values[h])

    def group(i, _):
        for u in range(UNROLL):
            one(i * UNROLL + u)
        return 0

    lax.fori_loop(0, STRIDE // RES // UNROLL, group, 0)

    def back(g, _):
        at = pl.ds(pl.multiple_of(g * STRIDE, STRIDE), STRIDE)
        pick = pl.ds(g, STRIDE, stride=grid_q)
        lse_far[at] = lse_s[pick, :]
        for h in range(HEADS):
            o_far[at, h * 128 : (h + 1) * 128] = o_s[h, pick, :]
        return 0

    lax.fori_loop(0, grid_q, back, 0)


def third_kernel(
    info, *refs,
):
    pieces = refs[:8]
    (q, kv, halo, o_far, lse_far, z, gain, bias, w_proj, w_in, w_back,
     y_out, go_out, stat_out, gq_out, gk_out, gv_out, gmid_out, d_proj, d_in, d_back, d_gain, d_bias, squares,
     ext, cot, sems) = refs[8:]
    step = pl.program_id(0)
    qw = q.shape[1]
    n = kv.shape[0]

    @pl.when(step == 0)
    def _():
        gather_pieces(info, pieces, cot, sems, False)
        load_extended(halo, kv, ext)
        for ref in (squares, gk_out, gv_out, d_proj, d_in, d_back, d_gain, d_bias):
            ref[...] = jnp.zeros_like(ref)

    limit = info[1]
    start = pl.multiple_of(step * TB, TB)
    base = info[0] * n + start
    outs = []
    logs = []
    for sub in range(TB // WIN):
        rows = slice(sub * WIN, (sub + 1) * WIN)
        near = pl.ds(pl.multiple_of(start + sub * WIN, WIN), 2 * WIN)
        out, largest, total = near_forward(q[rows], ext[near, :qw], ext[near, qw:], base + sub * WIN, limit)
        far_log = stack_stat(lse_far[rows])
        top = jnp.maximum(largest, far_log)
        near_share = jnp.exp(largest - top)
        far_share = jnp.exp(far_log - top)
        whole = total * near_share + far_share
        inverse = 1.0 / whole
        near_share = near_share * inverse
        far_share = far_share * inverse
        logs.append(top + jnp.log(whole))
        far = o_far[rows]
        outs.append(
            jnp.concatenate(
                [
                    out[h] * near_share[h * WIN : (h + 1) * WIN]
                    + far[:, h * 128 : (h + 1) * 128] * far_share[h * WIN : (h + 1) * WIN]
                    for h in range(HEADS)
                ],
                axis=1,
            )
        )
    attended_wide = jnp.concatenate(outs, axis=0)
    attended = attended_wide.astype(BF16)
    stream = z[...].astype(F32)
    branch = dot(attended, w_proj[...])
    middle = stream + branch
    unit, scale = norm_parts(middle)
    normed = (unit * gain[1:2] + bias[1:2]).astype(BF16)
    active, slope = gelu_pair(dot(normed, w_in[...]))
    active = active.astype(BF16)
    feed = dot(active, w_back[...])
    y_out[...] = (middle + feed).astype(BF16)
    squares[0] += masked_squares(stream, base, limit)
    squares[1] += masked_squares(branch, base, limit)
    squares[2] += masked_squares(feed, base, limit)

    pos = base + lax.broadcasted_iota(jnp.int32, (TB, 1), 0)
    upstream = jnp.where(pos < limit, cot[pl.ds(start, TB)].astype(F32), 0.0)
    grad_out, grad_mid = feed_backward(
        upstream, active, slope, normed, unit, scale, attended, gain, w_proj, w_in, w_back,
        d_proj, d_in, d_back, d_gain, d_bias,
    )
    gmid_out[...] = grad_mid
    go_out[...] = grad_out
    weighted = grad_out.astype(F32) * attended_wide
    for sub in range(TB // WIN):
        rows = slice(sub * WIN, (sub + 1) * WIN)
        near = pl.ds(pl.multiple_of(start + sub * WIN, WIN), 2 * WIN)
        delta = jnp.concatenate(
            [jnp.sum(weighted[rows, h * 128 : (h + 1) * 128], axis=-1, keepdims=True) for h in range(HEADS)], axis=0
        )
        stat_out[rows] = pack_stats(logs[sub], delta)
        gq, gk, gv = near_backward(
            q[rows], ext[near, :qw], ext[near, qw:], grad_out[rows], logs[sub], delta, base + sub * WIN, limit
        )
        gq_out[rows] = gq
        gk_out[near] += gk
        gv_out[near] += gv


def pack_stats(lse, delta):
    half = lse.shape[0] // 2
    lane = lax.broadcasted_iota(jnp.int32, (half, 128), 1)
    low = jnp.where(lane < 32, lse[:half], lse[half:])
    high = jnp.where(lane < 96, delta[:half], delta[half:])
    return jnp.where(lane < 64, low, high)


def feed_backward(
    upstream, active, slope, normed, unit, scale, attended, gain, w_proj, w_in, w_back,
    d_proj, d_in, d_back, d_gain, d_bias,
):
    low = upstream.astype(BF16)
    d_back[...] += t_dot(active, low)
    grad_hidden = (dot_t(low, w_back[...]) * slope).astype(BF16)
    d_in[...] += t_dot(normed, grad_hidden)
    grad_normed = dot_t(grad_hidden, w_in[...])
    d_gain[...] += col_sum(grad_normed * unit)
    d_bias[...] += col_sum(grad_normed)
    grad_mid = upstream + norm_back(grad_normed, unit, scale, gain[1:2])
    branch_low = grad_mid.astype(BF16)
    d_proj[...] += t_dot(attended, branch_low)
    grad_out = dot_t(branch_low, w_proj[...]).astype(BF16)
    return grad_out, grad_mid


def far_backward_kernel(
    info, qr, kr, vr, go, stat, gq_near, gk_near, gv_near, gq_out, gkv_own, gkv_send,
    go_s, stat_s, gq_s, gk_s, gv_s,
):
    n, qw = gq_near.shape
    grid_q = n // STRIDE
    grid_k = 2 * grid_q
    part = info[0]
    limit = info[1]

    def place(g, _):
        at = pl.ds(pl.multiple_of(g * STRIDE, STRIDE), STRIDE)
        pick = pl.ds(g, STRIDE, stride=grid_q)
        rows = go[at].astype(F32)
        for h in range(HEADS):
            go_s[h, pick, :] = rows[:, h * 128 : (h + 1) * 128]
        stat_s[pick, :] = stat[at]
        return 0

    lax.fori_loop(0, grid_q, place, 0)
    base_mask, key_pos = far_mask(grid_q, grid_k, part * grid_q)
    rows_q = RES * grid_q
    rows_k = RES * grid_k

    def one(i):
        at_q = pl.ds(pl.multiple_of(i * rows_q, rows_q), rows_q)
        at_k = pl.ds(pl.multiple_of(i * rows_k, rows_k), rows_k)
        keys = kr[at_k]
        split_q = head_split(qr[at_q])
        grads = [go_s[h, at_q].astype(BF16) for h in range(HEADS)]
        stats = stat_s[at_q]
        lse = jnp.concatenate([stats[:, 0:1], stats[:, 32:33]], axis=0)
        delta = jnp.concatenate([stats[:, 64:65], stats[:, 96:97]], axis=0)
        allowed = base_mask & (key_pos + i * RES < limit)
        weights = jnp.exp(jnp.where(allowed, dot_t(split_q, keys), NEG) - lse)
        pull = jnp.concatenate([dot_t(grads[h], vr[at_k, h * 128 : (h + 1) * 128]) for h in range(HEADS)], axis=0)
        slope = (weights * (pull - delta)).astype(BF16)
        weights = weights.astype(BF16)
        gq_s[at_q] = head_join(dot(slope, keys))
        gk_s[at_k] = t_dot(slope, split_q)
        for h in range(HEADS):
            gv_s[h, at_k] = t_dot(weights[h * rows_q : (h + 1) * rows_q], grads[h])

    def group(i, _):
        for u in range(UNROLL):
            one(i * UNROLL + u)
        return 0

    lax.fori_loop(0, STRIDE // RES // UNROLL, group, 0)

    def back(g, _):
        at = pl.ds(pl.multiple_of(g * STRIDE, STRIDE), STRIDE)
        shifted = pl.ds(pl.multiple_of(g * STRIDE + WIN, STRIDE), STRIDE)
        gq_out[at] = gq_near[at] + gq_s[pl.ds(g, STRIDE, stride=grid_q), :]
        mine = pl.ds(g + part * grid_q, STRIDE, stride=grid_k)
        sent = pl.ds(g, STRIDE, stride=grid_k)
        last = jnp.where(g == grid_q - 1, 1.0, 0.0)
        gkv_own[at, :qw] = gk_near[shifted] + gk_s[mine, :]
        gkv_send[at, :qw] = (gk_s[sent, :] + last * gk_near[:WIN]).astype(BF16)
        for h in range(HEADS):
            cols = slice(h * 128, (h + 1) * 128)
            wide = slice(qw + h * 128, qw + (h + 1) * 128)
            gkv_own[at, wide] = gv_near[shifted, cols] + gv_s[h, mine, :]
            gkv_send[at, wide] = (gv_s[h, sent, :] + last * gv_near[:WIN, cols]).astype(BF16)
        return 0

    lax.fori_loop(0, grid_q, back, 0)


def mix_backward(grad_q, grad_kv, rows, gain, bias, w_mix, d_mix, d_gain, d_bias, carried):
    grad_mixed = jnp.concatenate([grad_q * score_scale(grad_q.shape[1]), grad_kv], axis=1).astype(BF16)
    unit, scale = norm_parts(rows)
    normed = (unit * gain[0:1] + bias[0:1]).astype(BF16)
    d_mix[...] += t_dot(normed, grad_mixed)
    grad_normed = dot_t(grad_mixed, w_mix[...])
    d_gain[...] += col_sum(grad_normed * unit)
    d_bias[...] += col_sum(grad_normed)
    return carried + norm_back(grad_normed, unit, scale, gain[0:1])


def fourth_kernel(
    info, gq, gkv, got, z, gmid, gain_next, bias_next, w_mix_next,
    q, kv, halo, o, lse, active, slope, mid, gain, bias, w_proj, w_in, w_back,
    gz_out, gq_out, gk_out, gv_out, gmid_out, d_mix, dn_gain, dn_bias, d_proj, d_in, d_back, d_gain, d_bias,
    ext,
):
    step = pl.program_id(0)
    qw = q.shape[1]
    n = kv.shape[0]

    @pl.when(step == 0)
    def _():
        load_extended(halo, kv, ext)
        for ref in (gk_out, gv_out, d_mix, dn_gain, dn_bias, d_proj, d_in, d_back, d_gain, d_bias):
            ref[...] = jnp.zeros_like(ref)

    limit = info[1]
    start = pl.multiple_of(step * TB, TB)
    base = info[0] * n + start
    grad_kv = gkv[...] + got[...].astype(F32)
    grad_z = mix_backward(
        gq[...], grad_kv, z[...].astype(F32), gain_next, bias_next, w_mix_next, d_mix, dn_gain, dn_bias, gmid[...]
    )
    grad_low = grad_z.astype(BF16)
    gz_out[...] = grad_low
    unit, scale = norm_parts(mid[...])
    normed = (unit * gain[1:2] + bias[1:2]).astype(BF16)
    attended = o[...]
    grad_out, grad_mid = feed_backward(
        grad_low.astype(F32), active[...], slope[...].astype(F32), normed, unit, scale, attended, gain,
        w_proj, w_in, w_back, d_proj, d_in, d_back, d_gain, d_bias,
    )
    gmid_out[...] = grad_mid
    weighted = grad_out.astype(F32) * attended.astype(F32)
    for sub in range(TB // WIN):
        rows = slice(sub * WIN, (sub + 1) * WIN)
        near = pl.ds(pl.multiple_of(start + sub * WIN, WIN), 2 * WIN)
        delta = jnp.concatenate(
            [jnp.sum(weighted[rows, h * 128 : (h + 1) * 128], axis=-1, keepdims=True) for h in range(HEADS)], axis=0
        )
        g_q, g_k, g_v = near_backward(
            q[rows], ext[near, :qw], ext[near, qw:], grad_out[rows], stack_stat(lse[rows]), delta,
            base + sub * WIN, limit,
        )
        gq_out[rows] = g_q
        gk_out[near] += g_k
        gv_out[near] += g_v


def fifth_kernel(info, gq, gk, gv, got, x, gmid, gain, bias, w_mix, gx_out, d_mix, d_gain, d_bias):
    step = pl.program_id(0)

    @pl.when(step == 0)
    def _():
        for ref in (d_mix, d_gain, d_bias):
            ref[...] = jnp.zeros_like(ref)

    at = pl.ds(pl.multiple_of(step * TB + WIN, WIN), TB)
    last = jnp.where(step == pl.num_programs(0) - 1, 1.0, 0.0)
    tail = got[...].astype(F32) * last
    extra = jnp.concatenate([jnp.zeros((TB - WIN, got.shape[1]), F32), tail], axis=0)
    grad_kv = jnp.concatenate([gk[at], gv[at]], axis=1) + extra
    grad_x = mix_backward(
        gq[...], grad_kv, x[...].astype(F32), gain, bias, w_mix, d_mix, d_gain, d_bias, gmid[...]
    )
    gx_out[...] = grad_x.astype(BF16)


def assemble_kernel(info, *refs):
    count = 8
    low, high, out, narrow, wide, sem_in, sem_out = refs[:count], refs[count : 2 * count], *refs[2 * count :]

    def each(t, act):
        @pl.when(info[5] == 0)
        def _():
            act(pltpu.make_async_copy(low[t], narrow.at[t], sem_in.at[t]))

        @pl.when(info[5] != 0)
        def _():
            act(pltpu.make_async_copy(high[t], narrow.at[t], sem_in.at[t]))

    def leave(t):
        return pltpu.make_async_copy(wide.at[t], out.at[t ^ info[4]], sem_out.at[t])

    for t in range(count):
        each(t, lambda c: c.start())
    for t in range(count):
        each(t, lambda c: c.wait())
        wide[t] = narrow[t].astype(F32)
        leave(t).start()
    for t in range(count):
        leave(t).wait()


def call(kernel, info, operands, specs, outs, out_specs, scratch=(), grid=()):
    return pl.pallas_call(
        kernel,
        grid_spec=pltpu.PrefetchScalarGridSpec(
            num_scalar_prefetch=1, grid=grid, in_specs=specs, out_specs=out_specs, scratch_shapes=list(scratch)
        ),
        out_shape=outs,
        compiler_params=pltpu.CompilerParams(vmem_limit_bytes=VMEM_LIMIT),
    )(info, *operands)


def whole(array):
    zeros = (0,) * len(array.shape)
    return pl.BlockSpec(array.shape, lambda *_: zeros)


def tiled(array):
    return pl.BlockSpec((TB, array.shape[1]), lambda i, *_: (i, 0))


ANY = pl.BlockSpec(memory_space=pl.ANY)


def shape(dims, kind):
    return jax.ShapeDtypeStruct(dims, kind)


def body(edge_rows, lengths, norm_gain, norm_bias, w_qkv, w_out, w_up, w_down):
    sections = lax.axis_size("section")
    index = lax.axis_index("section")
    images, rows_dev, width = edge_rows.shape
    seats = 2 * images
    rep = sections // seats
    seat = index // rep
    twin = index % rep
    rows_piece = rows_dev * rep
    qw = (w_qkv.shape[2] - width) // 2
    kvw = w_qkv.shape[2] - qw
    hidden = w_up.shape[2]
    n = rows_piece * images // 2
    quarter = images // 2
    steps = (n // TB,)

    def route(pairs):
        return [(s * rep + e, d * rep + e) for s, d in pairs for e in range(rep)]

    if rep > 1:
        groups = [[s * rep + e for e in range(rep)] for s in range(seats)]
        edge_rows = lax.all_gather(edge_rows, "section", axis_index_groups=groups, axis=1, tiled=True)

    def source_key(s):
        return (s // images) * quarter + s % quarter, (s % images) // quarter

    def source_seat(key, core):
        return (key // quarter) * images + core * quarter + key % quarter

    half = seat // images
    my_key = half * quarter + seat % quarter
    chip = seat // 2
    part = seat % 2
    limit = lengths[chip]
    info = jnp.stack([part, limit, chip % quarter, chip // quarter, my_key, half]).astype(jnp.int32)

    def scatter_route(t):
        return route([(s, 2 * (source_key(s)[0] ^ t) + source_key(s)[1]) for s in range(seats)])

    def return_route(t, to_half):
        pairs = []
        for s in range(seats):
            key = (s // 2) ^ t
            if key // quarter == to_half:
                pairs.append((s, source_seat(key, s % 2)))
        return route(pairs)

    received = [None] * images
    for t in list(range(quarter, images)) + list(range(quarter)):
        piece = lax.dynamic_index_in_dim(edge_rows, my_key ^ t, 0, keepdims=False)
        received[t] = lax.ppermute(piece, "section", scatter_route(t))

    def send_back(rows, to_half):
        blocks = rows.reshape(quarter, rows_piece, width)
        out = []
        for t in range(images):
            piece = lax.dynamic_index_in_dim(blocks, (chip ^ t) % quarter, 0, keepdims=False)
            out.append(lax.ppermute(piece, "section", return_route(t, to_half)))
        return out

    first_to_second = route([(2 * c, 2 * c + 1) for c in range(images)])
    second_to_first = route([(2 * c + 1, 2 * c) for c in range(images)])

    dma = pltpu.SemaphoreType.DMA
    rows_q = shape((n, qw), BF16)
    rows_kv = shape((n, kvw), BF16)
    rows_low = shape((n, width), BF16)
    rows_wide = shape((n, width), F32)
    rows_stat = shape((n, 128), F32)
    rows_hidden = shape((n, hidden), BF16)
    grad_k_shape = shape((n + WIN, qw), F32)
    grad_v_shape = shape((n + WIN, width), F32)
    d_mix_shape = shape(w_qkv.shape[1:], F32)
    d_proj_shape = shape(w_out.shape[1:], F32)
    d_in_shape = shape(w_up.shape[1:], F32)
    d_back_shape = shape(w_down.shape[1:], F32)
    vec_shape = shape((8, width), F32)
    squares_shape = shape((3, 8, width), F32)
    ext = pltpu.VMEM((n + WIN, kvw), BF16)

    g0, g1, b0, b1 = norm_gain[0], norm_gain[1], norm_bias[0], norm_bias[1]

    outs = [rows_low, rows_q, rows_kv]
    x, q0, kv0 = call(
        first_kernel, info, received + [g0, b0, w_qkv[0]],
        [ANY] * images + [whole(g0), whole(b0), whole(w_qkv[0])],
        outs, [whole(o) for o in outs], [dma((quarter,))],
    )
    halo0 = lax.ppermute(kv0[n - WIN :], "section", first_to_second)

    outs = [rows_low, rows_q, rows_kv, rows_low, rows_stat, rows_hidden, rows_hidden, rows_wide, squares_shape]
    z, q1, kv1, o0, lse0, active0, slope0, mid0, squares0 = call(
        second_kernel, info, [x, q0, kv0, halo0, g0, b0, w_out[0], w_up[0], w_down[0], g1, b1, w_qkv[1]],
        [tiled(x), tiled(q0)] + [whole(a) for a in (kv0, halo0, g0, b0, w_out[0], w_up[0], w_down[0], g1, b1, w_qkv[1])],
        outs, [tiled(o) for o in outs[:-1]] + [whole(outs[-1])], [ext], steps,
    )
    kv_other = lax.ppermute(kv1, "section", first_to_second)
    y0_back = send_back(z, 0)

    rows_k_all = shape((2 * n, qw), BF16)
    rows_v_all = shape((2 * n, width), BF16)
    outs = [rows_q, rows_k_all, rows_v_all, rows_wide, rows_stat]
    qr, kr, vr, o_far, lse_far = call(
        far_forward_kernel, info, [q1, kv1, kv_other], [whole(a) for a in (q1, kv1, kv_other)],
        outs, [whole(o) for o in outs],
        [pltpu.VMEM((n, qw), F32), pltpu.VMEM((2 * n, qw), F32), pltpu.VMEM((HEADS, 2 * n, 128), F32),
         pltpu.VMEM((HEADS, n, 128), F32), pltpu.VMEM((n, 128), F32)],
    )

    halo1 = kv_other[n - WIN :]
    outs = [rows_low, rows_low, rows_stat, shape((n, qw), F32), grad_k_shape, grad_v_shape, rows_wide,
            d_proj_shape, d_in_shape, d_back_shape, vec_shape, vec_shape, squares_shape]
    (y1, go1, stat1, gq_near, gk_near, gv_near, gmid1, d_proj1, d_in1, d_back1, d_gain11, d_bias11, squares1) = call(
        third_kernel, info,
        received + [q1, kv1, halo1, o_far, lse_far, z, g1, b1, w_out[1], w_up[1], w_down[1]],
        [ANY] * images + [tiled(q1), whole(kv1), whole(halo1), tiled(o_far), tiled(lse_far), tiled(z)]
        + [whole(a) for a in (g1, b1, w_out[1], w_up[1], w_down[1])],
        outs,
        [tiled(o) for o in outs[:4]] + [whole(outs[4]), whole(outs[5]), tiled(outs[6])] + [whole(o) for o in outs[7:]],
        [ext, pltpu.VMEM((n, width), BF16), dma((quarter,))], steps,
    )
    y1_back = send_back(y1, 1)

    outs = [shape((n, qw), F32), shape((n, kvw), F32), rows_kv]
    operands = [qr, kr, vr, go1, stat1, gq_near, gk_near, gv_near]
    gq1, gkv1, gkv_send = call(
        far_backward_kernel, info, operands, [whole(a) for a in operands], outs, [whole(o) for o in outs],
        [pltpu.VMEM((HEADS, n, 128), F32), pltpu.VMEM((n, 128), F32), pltpu.VMEM((n, qw), F32),
         pltpu.VMEM((2 * n, qw), F32), pltpu.VMEM((HEADS, 2 * n, 128), F32)],
    )
    gkv_got = lax.ppermute(gkv_send, "section", second_to_first)

    outs = [rows_low, shape((n, qw), F32), grad_k_shape, grad_v_shape, rows_wide,
            d_mix_shape, vec_shape, vec_shape, d_proj_shape, d_in_shape, d_back_shape, vec_shape, vec_shape]
    (gz, gq0, gk0, gv0, gmid0, d_mix1, d_gain10, d_bias10, d_proj0, d_in0, d_back0, d_gain01, d_bias01) = call(
        fourth_kernel, info,
        [gq1, gkv1, gkv_got, z, gmid1, g1, b1, w_qkv[1], q0, kv0, halo0, o0, lse0, active0, slope0, mid0, g0, b0,
         w_out[0], w_up[0], w_down[0]],
        [tiled(a) for a in (gq1, gkv1, gkv_got, z, gmid1)] + [whole(a) for a in (g1, b1, w_qkv[1])]
        + [tiled(q0), whole(kv0), whole(halo0)] + [tiled(a) for a in (o0, lse0, active0, slope0, mid0)]
        + [whole(a) for a in (g0, b0, w_out[0], w_up[0], w_down[0])],
        outs,
        [tiled(outs[0]), tiled(outs[1]), whole(outs[2]), whole(outs[3]), tiled(outs[4])] + [whole(o) for o in outs[5:]],
        [ext], steps,
    )
    halo_send = jnp.concatenate([gk0[:WIN], gv0[:WIN]], axis=1).astype(BF16)
    halo_got = lax.ppermute(halo_send, "section", second_to_first)
    gz_back = send_back(gz, 1)

    outs = [rows_low, d_mix_shape, vec_shape, vec_shape]
    gx, d_mix0, d_gain00, d_bias00 = call(
        fifth_kernel, info, [gq0, gk0, gv0, halo_got, x, gmid0, g0, b0, w_qkv[0]],
        [tiled(gq0), whole(gk0), whole(gv0), whole(halo_got), tiled(x), tiled(gmid0), whole(g0), whole(b0), whole(w_qkv[0])],
        outs, [tiled(outs[0])] + [whole(o) for o in outs[1:]], (), steps,
    )
    gx_back = send_back(gx, 0)

    def assemble(low, high):
        out = call(
            assemble_kernel, info, low + high, [ANY] * (2 * images),
            shape((images, rows_piece, width), F32), ANY,
            [pltpu.VMEM((images, rows_piece, width), BF16), pltpu.VMEM((images, rows_piece, width), F32),
             dma((images,)), dma((images,))],
        )
        if rep > 1:
            out = lax.dynamic_slice_in_dim(out, twin * rows_dev, rows_dev, 1)
        return out

    forward_rows = assemble(y0_back, y1_back)
    backward_rows = assemble(gx_back, gz_back)

    once = (twin == 0).astype(F32)
    squares = jnp.concatenate([squares0, squares1]).sum(axis=(1, 2))
    spread = squares[:, None] * (jnp.arange(images) == chip).astype(F32)[None, :] * once
    summed = lax.psum(spread, "section")
    rms_values = jnp.sqrt(summed / (lengths.astype(F32)[None, :] * width))

    d_gain = jnp.stack([jnp.stack([d_gain00, d_gain01]), jnp.stack([d_gain10, d_gain11])]).sum(axis=2)
    d_bias = jnp.stack([jnp.stack([d_bias00, d_bias01]), jnp.stack([d_bias10, d_bias11])]).sum(axis=2)
    grads = (
        d_gain, d_bias, jnp.stack([d_mix0, d_mix1]), jnp.stack([d_proj0, d_proj1]),
        jnp.stack([d_in0, d_in1]), jnp.stack([d_back0, d_back1]),
    )
    grads = lax.psum(tuple(g * once for g in grads), ("dp", "section"))
    return (forward_rows, backward_rows, rms_values) + tuple(grads)


def solution(mesh):
    placed = (P("dp", "section", None), P("dp"), P(), P(), P(), P(), P(), P())
    return jax.shard_map(
        body,
        mesh=mesh,
        in_specs=placed,
        out_specs=(P("dp", "section", None), P("dp", "section", None), P(None, "dp"), P(), P(), P(), P(), P(), P()),
        check_vma=False,
    )
```

time: 3300 us -> 451 us (0.14)
  local copies, waits for them, and re-layouts: 1080 us -> 24.6 us
  other arithmetic: 913 us -> 6.93 us
  waiting for transfers between devices: 694 us -> 47.9 us
  matrix products: 288 us -> 0 us
  Pallas kernels: 0 us -> 112 us
  starting transfers between devices: 187 us -> 128 us
    ppermute x38 -> x44, waiting for transfers between devices: 601 us -> 47.9 us  [the longest x32 33.4 us: send_back(): out.append(lax.ppermute(piece, 'section', return_route(t, to_half)))]
    reshape x45 -> x0, local copies, waits for them, and re-layouts: 384 us -> none  [the longest x10 139 us: split_far(): picked[..., query_width:]]
    unnamed x61 -> x0, other arithmetic: 310 us -> none
    dot_general x100 -> x0, matrix products: 288 us -> none  [the longest x5 92.4 us: body(): jnp.einsum('bgrf,rs->bgsf', far_both, residue_table, precision=lax.Precis...]
    slice x67 -> x4, local copies, waits for them, and re-layouts: 211 us -> 3.43 us  [the longest x2 1.84 us: body(): halo_send = jnp.concatenate([gk0[:WIN], gv0[:WIN]], axis=1).astype(BF16)]
    unnamed x1170 -> x152, local copies, waits for them, and re-layouts: 194 us -> 10.2 us
    select_n x41 -> x0, other arithmetic: 154 us -> none  [the longest x6 89.6 us: split_far(): picked = jnp.take(grid_cols, residue, axis=2)]
    gather x10 -> x0, local copies, waits for them, and re-layouts: 137 us -> none  [split_far(): picked = jnp.take(grid_cols, residue, axis=2)]
  transfers between devices with their start and end apart: 39 -> 45, of which waited for: 30 -> 7; matrix products, arithmetic and copies ran while one was open for 11% -> 4% of each run, Pallas kernels for 0% -> 8%
where the time goes in v1:
time: 451 us; the launch traced here: 449 us
  starting transfers between devices  128 us (28%)
  blocking collectives  114 us (25%)
  Pallas kernels  112 us (25%)
  waiting for transfers between devices  47.9 us (11%)
  local copies, waits for them, and re-layouts  24.6 us (5%)
  between operations  15.6 us (3%)
  other arithmetic  6.93 us (2%)
    pallas_call x9, Pallas kernels, call(): pl.pallas_call(kernel, grid_spec=pltpu.PrefetchScalarGridSpec(num_scalar_...  112 us
    ppermute x32, starting transfers between devices, send_back(): out.append(lax.ppermute(piece, 'section', return_route(t, to_half)))  89.4 us
    psum x1, blocking collectives, body(): grads = lax.psum(tuple((g * once for g in grads)), ('dp', 'section'))  71.1 us
    psum x1, blocking collectives, body(): summed = lax.psum(spread, 'section')  43.2 us
    ppermute x32, waiting for transfers between devices, send_back(): out.append(lax.ppermute(piece, 'section', return_route(t, to_half)))  33.4 us
    ppermute x8, starting transfers between devices, body(): received[t] = lax.ppermute(piece, 'section', scatter_route(t))  32.2 us
    ppermute x8, waiting for transfers between devices, body(): received[t] = lax.ppermute(piece, 'section', scatter_route(t))  11.7 us
    unnamed x152, local copies, waits for them, and re-layouts  10.2 us
  transfers between devices with their start and end apart: 45, of which 7 were waited for; matrix products, arithmetic and copies ran while one was open for 4% of the time, Pallas kernels for 8%

profile of v1, /device:TPU:0, one launch (start us, length us, event | category | flops | bytes accessed | tf_op | source)
XLA Modules:
  0.0 449.2 jit_solution(10441140383634611630)
XLA Ops:
  11.4 4.9 %collective-permute-start.1 = (bf16[384,256]{1,0:T(8,128)(2,1)}, bf16[384,256]{1,0:T(8,128)(2,1)S(1)}, u32[]{:S(2)}, u32[]{:S(2)}) collective-permute-start(bf16[384,256]{1,0:T(8,128)(2,1)} %get-tuple-element.120), channel_id=1, source_target_pairs={{0,2},{1,0},{2,6},{3,4},{4,3},{5,1},{6,7},{7,5},{8,10},{9,8},{10,1... | collective-permute-start | bytes 589832 | tf_op jit(solution)/shard_map/ppermute | solution.py:683
  26.5 8.6 %collective-permute-start.5 = (bf16[384,256]{1,0:T(8,128)(2,1)S(1)}, bf16[384,256]{1,0:T(8,128)(2,1)S(1)}, u32[]{:S(2)}, u32[]{:S(2)}) collective-permute-start(bf16[384,256]{1,0:T(8,128)(2,1)S(1)} %get-tuple-element.116), channel_id=1, source_target_pairs={{0,10},{1,8},{2,14},{3,12},{4,11},{5,9},{6,15},{7,13},{8,2},{9,0},... | collective-permute-start | bytes 589832 | tf_op jit(solution)/shard_map/ppermute | solution.py:683
  35.1 10.7 %collective-permute-start.6 = (bf16[384,256]{1,0:T(8,128)(2,1)S(1)}, bf16[384,256]{1,0:T(8,128)(2,1)S(1)}, u32[]{:S(2)}, u32[]{:S(2)}) collective-permute-start(bf16[384,256]{1,0:T(8,128)(2,1)S(1)} %get-tuple-element.122), channel_id=1, source_target_pairs={{0,12},{1,14},{2,8},{3,10},{4,13},{5,15},{6,9},{7,11},{8,4},{9,6},... | collective-permute-start | bytes 589832 | tf_op jit(solution)/shard_map/ppermute | solution.py:683
  46.9 9.5 %collective-permute-done.6.refs_6_ = bf16[384,256]{1,0:T(8,128)(2,1)S(1)} collective-permute-done((bf16[384,256]{1,0:T(8,128)(2,1)S(1)}, bf16[384,256]{1,0:T(8,128)(2,1)S(1)}, u32[]{:S(2)}, u32[]{:S(2)}) %collective-permute-start.6) | collective-permute-done | bytes 196640 | tf_op jit(solution)/shard_map/ppermute | solution.py:683
  59.3 6.5 %shard_map.151 = (bf16[1536,256]{1,0:T(8,128)(2,1)}, bf16[1536,128]{1,0:T(8,128)(2,1)}, bf16[1536,384]{1,0:T(8,128)(2,1)}) custom-call(s32[6]{0:T(128)} %stack.113.info, bf16[384,256]{1,0:T(8,128)(2,1)} %copy-done.8, bf16[384,256]{1,0:T(8,128)(2,1)} %copy-done.9, bf16[384,256]{1,0:T(8,128)(2,1)} %copy-done.10, bf16[384,256]{1,0:T(8,128)(2,1)} %copy-done.11, ...), custom_call_target="tpu_custom_call" | custom-call | tf_op jit(solution)/shard_map/pallas_call | solution.py:607
  69.6 14.8 %shard_map.152 = (bf16[1536,256]{1,0:T(8,128)(2,1)}, bf16[1536,128]{1,0:T(8,128)(2,1)}, bf16[1536,384]{1,0:T(8,128)(2,1)}, bf16[1536,256]{1,0:T(8,128)(2,1)}, f3...) custom-call(s32[6]{0:T(128)} %stack.113.info, ...), custom_call_target="tpu_custom_call" | custom-call | tf_op jit(solution)/shard_map/pallas_call | solution.py:607
  90.4 13.6 %shard_map.153 = (bf16[1536,128]{1,0:T(8,128)(2,1)}, bf16[3072,128]{1,0:T(8,128)(2,1)}, bf16[3072,256]{1,0:T(8,128)(2,1)}, f32[1536,256]{1,0:T(8,128)}, f32[1536,128]{1,0:T(8,128)}) custom-call(s32[6]{0:T(128)} %stack.113.info, bf16[1536,128]{1,0:T(8,128)(2,1)} %get-tuple-element.63.q.refs_8_, bf16[1536,384]{1,0:T(8,128)(2,1)} %get-tuple-element.64.kv.refs_9_, ...), custom_call_target="tpu_custom_call" | custom-call | tf_op jit(solution)/shard_map/pallas_call | solution.py:607
  104.0 23.8 %shard_map.154 = (bf16[1536,256]{1,0:T(8,128)(2,1)}, bf16[1536,256]{1,0:T(8,128)(2,1)}, f32[1536,128]{1,0:T(8,128)}, f32[1536,128]{1,0:T(8,128)}, f32[1664,128]{...) custom-call(s32[6]{0:T(128)} %stack.113.info, ...), custom_call_target="tpu_custom_call" | custom-call | tf_op jit(solution)/shard_map/pallas_call | solution.py:607
  127.8 17.7 %shard_map.156 = (f32[1536,128]{1,0:T(8,128)}, f32[1536,384]{1,0:T(8,128)}, bf16[1536,384]{1,0:T(8,128)(2,1)}) custom-call(s32[6]{0:T(128)} %stack.113.info, bf16[1536,128]{1,0:T(8,128)(2,1)} %get-tuple-element.68.qr, bf16[3072,128]{1,0:T(8,128)(2,1)} %get-tuple-element.69.kr, bf16[3072,256]{1,0:T(8,128)(2,1)} %get-tuple-element.70.vr, ...), custom_call_target="tpu_custom_call" | custom-call | tf_op jit(solution)/shard_map/pallas_call | solution.py:607
  147.1 3.1 collective-permute-start.10
  154.0 20.1 %shard_map.157 = (bf16[1536,256]{1,0:T(8,128)(2,1)}, f32[1536,128]{1,0:T(8,128)}, f32[1664,128]{1,0:T(8,128)}, f32[1664,256]{1,0:T(8,128)}, f32[1536,256]{1,0:T(...) custom-call(s32[6]{0:T(128)} %stack.113.info, ...), custom_call_target="tpu_custom_call" | custom-call | tf_op jit(solution)/shard_map/pallas_call | solution.py:607
  182.2 8.3 %shard_map.158 = (bf16[1536,256]{1,0:T(8,128)(2,1)}, f32[256,512]{1,0:T(8,128)}, f32[8,256]{1,0:T(8,128)}, f32[8,256]{1,0:T(8,128)}) custom-call(s32[6]{0:T(128)} %stack.113.info, f32[1536,128]{1,0:T(8,128)} %get-tuple-element.85.gq, f32[1664,128]{1,0:T(8,128)} %get-tuple-element.86.gk, f32[1664,256]{1,0:T(8,128)} %get-tuple-element.87.gv, ...), custom_call_target="tpu_custom_call" | custom-call | tf_op jit(solution)/shard_map/pallas_call | solution.py:607
  192.6 3.6 collective-permute-start.12
  204.5 18.7 %collective-permute-done.13.refs_4_ = bf16[384,256]{1,0:T(8,128)(2,1)S(1)} collective-permute-done((bf16[384,256]{1,0:T(8,128)(2,1)S(1)}, bf16[384,256]{1,0:T(8,128)(2,1)S(1)}, u32[]{:S(2)}, u32[]{:S(2)}) %collective-permute-start.13) | collective-permute-done | bytes 196640 | tf_op jit(solution)/shard_map/ppermute | solution.py:690
  223.8 13.3 %collective-permute-done.14.refs_5_ = bf16[384,256]{1,0:T(8,128)(2,1)S(1)} collective-permute-done((bf16[384,256]{1,0:T(8,128)(2,1)S(1)}, bf16[384,256]{1,0:T(8,128)(2,1)S(1)}, u32[]{:S(2)}, u32[]{:S(2)}) %collective-permute-start.14) | collective-permute-done | bytes 196640 | tf_op jit(solution)/shard_map/ppermute | solution.py:690
  240.4 15.9 %collective-permute-start.22 = (bf16[384,256]{1,0:T(8,128)(2,1)}, bf16[384,256]{1,0:T(8,128)(2,1)S(1)}, u32[]{:S(2)}, u32[]{:S(2)}) collective-permute-start(bf16[384,256]{1,0:T(8,128)(2,1)} %get-tuple-element.142), channel_id=1, source_target_pairs={{0,8},{1,12},{2,9},{3,13},{4,10},{5,14},{6,11},{7,15},{16,24},{17,... | collective-permute-start | bytes 589832 | tf_op jit(solution)/shard_map/ppermute | solution.py:690
  261.0 43.2 %psum.49 = f32[6,8]{1,0:T(8,128)S(1)} all-reduce(f32[6,8]{1,0:T(8,128)S(1)} %broadcast_multiply_fusion), channel_id=1, replica_groups=mesh['dp'=2,'section'=16] {'section'}, use_global_device_ids=true, to_apply=%region_1.2 | all-reduce | flops 48 | bytes 384 | tf_op jit(solution)/shard_map/psum | solution.py:807
  306.3 16.0 %collective-permute-start.40 = (bf16[384,256]{1,0:T(8,128)(2,1)}, bf16[384,256]{1,0:T(8,128)(2,1)S(1)}, u32[]{:S(2)}, u32[]{:S(2)}) collective-permute-start(bf16[384,256]{1,0:T(8,128)(2,1)} %get-tuple-element.126), channel_id=1, source_target_pairs={{0,8},{1,12},{2,9},{3,13},{4,10},{5,14},{6,11},{7,15},{16,24},{17,... | collective-permute-start | bytes 589832 | tf_op jit(solution)/shard_map/ppermute | solution.py:690
  324.4 3.6 shard_map.155
  332.8 5.1 %collective-permute-start.29 = (bf16[384,256]{1,0:T(8,128)(2,1)S(1)}, bf16[384,256]{1,0:T(8,128)(2,1)S(1)}, u32[]{:S(2)}, u32[]{:S(2)}) collective-permute-start(bf16[384,256]{1,0:T(8,128)(2,1)S(1)} %get-tuple-element.137), channel_id=1, source_target_pairs={{0,1},{1,5},{2,0},{3,4},{4,3},{5,7},{6,2},{7,6},{16,17},{17,21},{1... | collective-permute-start | bytes 589832 | tf_op jit(solution)/shard_map/ppermute | solution.py:690
  337.9 3.5 collective-permute-start.30
  341.5 14.1 %collective-permute-start.31 = (bf16[384,256]{1,0:T(8,128)(2,1)}, bf16[384,256]{1,0:T(8,128)(2,1)S(1)}, u32[]{:S(2)}, u32[]{:S(2)}) collective-permute-start(bf16[384,256]{1,0:T(8,128)(2,1)} %get-tuple-element.135), channel_id=1, source_target_pairs={{0,3},{1,7},{2,2},{3,6},{4,1},{5,5},{6,0},{7,4},{16,19},{17,23},{1... | collective-permute-start | bytes 589832 | tf_op jit(solution)/shard_map/ppermute | solution.py:690
  361.1 71.1 %all-reduce = (f32[2,2,256]{2,1,0:T(2,128)}, f32[2,2,256]{2,1,0:T(2,128)}) all-reduce(f32[2,2,256]{2,1,0:T(2,128)S(1)} %maximum_reduce_fusion.1, f32[2,2,256]{2,1,0:T(2,128)S(1)} %maximum_reduce_fusion.2), channel_id=1, replica_groups=mesh['dp'=2,'section'=16] {'dp','section'}, use_global_device_ids=true, to_apply=%region_3.4 | all-reduce | flops 2048 | bytes 16384 | tf_op jit(solution)/shard_map/psum | solution.py:816
  433.7 3.4 shard_map.159
  (262 shorter events, 80.6 us)
Async XLA Ops:
  7.2 430.0 %all-reduce.4.cloned.1.call-start = ((), (), s32[]{:S(2)}) async-start(), calls=%async_computation | async-start | bytes 7340032 | tf_op jit(solution)/shard_map/psum | solution.py:816
  16.3 29.5 %collective-permute-start.2 = (bf16[384,256]{1,0:T(8,128)(2,1)}, bf16[384,256]{1,0:T(8,128)(2,1)S(1)}, u32[]{:S(2)}, u32[]{:S(2)}) collective-permute-start(bf16[384,256]{1,0:T(8,128)(2,1)} %get-tuple-element.119), channel_id=1, source_target_pairs={{0,4},{1,6},{2,0},{3,2},{4,5},{5,7},{6,1},{7,3},{8,12},{9,14},{10,... | collective-permute-start | bytes 589832 | tf_op jit(solution)/shard_map/ppermute | solution.py:683
  17.5 29.4 %collective-permute-start.3 = (bf16[384,256]{1,0:T(8,128)(2,1)S(1)}, bf16[384,256]{1,0:T(8,128)(2,1)S(1)}, u32[]{:S(2)}, u32[]{:S(2)}) collective-permute-start(bf16[384,256]{1,0:T(8,128)(2,1)S(1)} %get-tuple-element.118), channel_id=1, source_target_pairs={{0,6},{1,4},{2,2},{3,0},{4,7},{5,5},{6,3},{7,1},{8,14},{9,12},{10,... | collective-permute-start | bytes 589832 | tf_op jit(solution)/shard_map/ppermute | solution.py:683
  19.4 27.4 %collective-permute-start.4 = (bf16[384,256]{1,0:T(8,128)(2,1)S(1)}, bf16[384,256]{1,0:T(8,128)(2,1)S(1)}, u32[]{:S(2)}, u32[]{:S(2)}) collective-permute-start(bf16[384,256]{1,0:T(8,128)(2,1)S(1)} %get-tuple-element.117), channel_id=1, source_target_pairs={{0,8},{1,10},{2,12},{3,14},{4,9},{5,11},{6,13},{7,15},{8,0},{9,2},... | collective-permute-start | bytes 589832 | tf_op jit(solution)/shard_map/ppermute | solution.py:683
  147.1 51.7 %collective-permute-start.10 = (bf16[384,256]{1,0:T(8,128)(2,1)S(1)}, bf16[384,256]{1,0:T(8,128)(2,1)S(1)}, u32[]{:S(2)}, u32[]{:S(2)}) collective-permute-start(bf16[384,256]{1,0:T(8,128)(2,1)S(1)} %get-tuple-element.153), channel_id=1, source_target_pairs={{0,1},{1,5},{2,0},{3,4},{4,3},{5,7},{6,2},{7,6},{16,17},{17,21},{1... | collective-permute-start | bytes 589832 | tf_op jit(solution)/shard_map/ppermute | solution.py:690
  150.2 49.9 %collective-permute-start.11 = (bf16[384,256]{1,0:T(8,128)(2,1)S(1)}, bf16[384,256]{1,0:T(8,128)(2,1)S(1)}, u32[]{:S(2)}, u32[]{:S(2)}) collective-permute-start(bf16[384,256]{1,0:T(8,128)(2,1)S(1)} %get-tuple-element.152), channel_id=1, source_target_pairs={{0,2},{1,6},{2,3},{3,7},{4,0},{5,4},{6,1},{7,5},{16,18},{17,22},{1... | collective-permute-start | bytes 589832 | tf_op jit(solution)/shard_map/ppermute | solution.py:690
  196.2 27.0 %collective-permute-start.13 = (bf16[384,256]{1,0:T(8,128)(2,1)S(1)}, bf16[384,256]{1,0:T(8,128)(2,1)S(1)}, u32[]{:S(2)}, u32[]{:S(2)}) collective-permute-start(bf16[384,256]{1,0:T(8,128)(2,1)S(1)} %get-tuple-element.150), channel_id=1, source_target_pairs={{8,0},{9,4},{10,1},{11,5},{12,2},{13,6},{14,3},{15,7},{24,16},{25,... | collective-permute-start | bytes 589832 | tf_op jit(solution)/shard_map/ppermute | solution.py:690
  197.5 39.6 %collective-permute-start.14 = (bf16[384,256]{1,0:T(8,128)(2,1)S(1)}, bf16[384,256]{1,0:T(8,128)(2,1)S(1)}, u32[]{:S(2)}, u32[]{:S(2)}) collective-permute-start(bf16[384,256]{1,0:T(8,128)(2,1)S(1)} %get-tuple-element.149), channel_id=1, source_target_pairs={{8,1},{9,5},{10,0},{11,4},{12,3},{13,7},{14,2},{15,6},{24,17},{25,... | collective-permute-start | bytes 589832 | tf_op jit(solution)/shard_map/ppermute | solution.py:690
  198.8 38.9 %collective-permute-start.15 = (bf16[384,256]{1,0:T(8,128)(2,1)S(1)}, bf16[384,256]{1,0:T(8,128)(2,1)S(1)}, u32[]{:S(2)}, u32[]{:S(2)}) collective-permute-start(bf16[384,256]{1,0:T(8,128)(2,1)S(1)} %get-tuple-element.148), channel_id=1, source_target_pairs={{8,2},{9,6},{10,3},{11,7},{12,0},{13,4},{14,1},{15,5},{24,18},{25,... | collective-permute-start | bytes 589832 | tf_op jit(solution)/shard_map/ppermute | solution.py:690
  200.1 38.3 %collective-permute-start.16 = (bf16[384,256]{1,0:T(8,128)(2,1)S(1)}, bf16[384,256]{1,0:T(8,128)(2,1)S(1)}, u32[]{:S(2)}, u32[]{:S(2)}) collective-permute-start(bf16[384,256]{1,0:T(8,128)(2,1)S(1)} %get-tuple-element.147), channel_id=1, source_target_pairs={{8,3},{9,7},{10,2},{11,6},{12,1},{13,5},{14,0},{15,4},{24,19},{25,... | collective-permute-start | bytes 589832 | tf_op jit(solution)/shard_map/ppermute | solution.py:690
  203.8 36.5 %collective-permute-start.9 = (bf16[384,256]{1,0:T(8,128)(2,1)S(1)}, bf16[384,256]{1,0:T(8,128)(2,1)S(1)}, u32[]{:S(2)}, u32[]{:S(2)}) collective-permute-start(bf16[384,256]{1,0:T(8,128)(2,1)S(1)} %get-tuple-element.154), channel_id=1, source_target_pairs={{0,0},{1,4},{2,1},{3,5},{4,2},{5,6},{6,3},{7,7},{16,16},{17,20},{1... | collective-permute-start | bytes 589832 | tf_op jit(solution)/shard_map/ppermute | solution.py:690
  223.2 33.1 %collective-permute-start.18 = (bf16[384,256]{1,0:T(8,128)(2,1)S(1)}, bf16[384,256]{1,0:T(8,128)(2,1)S(1)}, u32[]{:S(2)}, u32[]{:S(2)}) collective-permute-start(bf16[384,256]{1,0:T(8,128)(2,1)S(1)} %get-tuple-element.146), channel_id=1, source_target_pairs={{8,8},{9,12},{10,9},{11,13},{12,10},{13,14},{14,11},{15,15},{24,24... | collective-permute-start | bytes 589832 | tf_op jit(solution)/shard_map/ppermute | solution.py:690
  240.4 63.8 %collective-permute-start.22 = (bf16[384,256]{1,0:T(8,128)(2,1)}, bf16[384,256]{1,0:T(8,128)(2,1)S(1)}, u32[]{:S(2)}, u32[]{:S(2)}) collective-permute-start(bf16[384,256]{1,0:T(8,128)(2,1)} %get-tuple-element.142), channel_id=1, source_target_pairs={{0,8},{1,12},{2,9},{3,13},{4,10},{5,14},{6,11},{7,15},{16,24},{17,... | collective-permute-start | bytes 589832 | tf_op jit(solution)/shard_map/ppermute | solution.py:690
  256.3 48.6 %collective-permute-start.23 = (bf16[384,256]{1,0:T(8,128)(2,1)}, bf16[384,256]{1,0:T(8,128)(2,1)S(1)}, u32[]{:S(2)}, u32[]{:S(2)}) collective-permute-start(bf16[384,256]{1,0:T(8,128)(2,1)} %get-tuple-element.141), channel_id=1, source_target_pairs={{0,9},{1,13},{2,8},{3,12},{4,11},{5,15},{6,10},{7,14},{16,25},{17,... | collective-permute-start | bytes 589832 | tf_op jit(solution)/shard_map/ppermute | solution.py:690
  257.6 48.0 %collective-permute-start.24 = (bf16[384,256]{1,0:T(8,128)(2,1)}, bf16[384,256]{1,0:T(8,128)(2,1)S(1)}, u32[]{:S(2)}, u32[]{:S(2)}) collective-permute-start(bf16[384,256]{1,0:T(8,128)(2,1)} %get-tuple-element.140), channel_id=1, source_target_pairs={{0,10},{1,14},{2,11},{3,15},{4,8},{5,12},{6,9},{7,13},{16,26},{17,... | collective-permute-start | bytes 589832 | tf_op jit(solution)/shard_map/ppermute | solution.py:690
  258.9 47.4 %collective-permute-start.25 = (bf16[384,256]{1,0:T(8,128)(2,1)}, bf16[384,256]{1,0:T(8,128)(2,1)S(1)}, u32[]{:S(2)}, u32[]{:S(2)}) collective-permute-start(bf16[384,256]{1,0:T(8,128)(2,1)} %get-tuple-element.139), channel_id=1, source_target_pairs={{0,11},{1,15},{2,10},{3,14},{4,9},{5,13},{6,8},{7,12},{16,27},{17,... | collective-permute-start | bytes 589832 | tf_op jit(solution)/shard_map/ppermute | solution.py:690
  260.3 62.1 %collective-permute-start.36 = (bf16[384,256]{1,0:T(8,128)(2,1)}, bf16[384,256]{1,0:T(8,128)(2,1)S(1)}, u32[]{:S(2)}, u32[]{:S(2)}) collective-permute-start(bf16[384,256]{1,0:T(8,128)(2,1)} %get-tuple-element.130), channel_id=1, source_target_pairs={{8,8},{9,12},{10,9},{11,13},{12,10},{13,14},{14,11},{15,15},{24,24... | collective-permute-start | bytes 589832 | tf_op jit(solution)/shard_map/ppermute | solution.py:690
  305.6 26.5 %collective-permute-start.39 = (bf16[384,256]{1,0:T(8,128)(2,1)}, bf16[384,256]{1,0:T(8,128)(2,1)S(1)}, u32[]{:S(2)}, u32[]{:S(2)}) collective-permute-start(bf16[384,256]{1,0:T(8,128)(2,1)} %get-tuple-element.127), channel_id=1, source_target_pairs={{8,11},{9,15},{10,10},{11,14},{12,9},{13,13},{14,8},{15,12},{24,27... | collective-permute-start | bytes 589832 | tf_op jit(solution)/shard_map/ppermute | solution.py:690
  306.3 26.5 %collective-permute-start.40 = (bf16[384,256]{1,0:T(8,128)(2,1)}, bf16[384,256]{1,0:T(8,128)(2,1)S(1)}, u32[]{:S(2)}, u32[]{:S(2)}) collective-permute-start(bf16[384,256]{1,0:T(8,128)(2,1)} %get-tuple-element.126), channel_id=1, source_target_pairs={{0,8},{1,12},{2,9},{3,13},{4,10},{5,14},{6,11},{7,15},{16,24},{17,... | collective-permute-start | bytes 589832 | tf_op jit(solution)/shard_map/ppermute | solution.py:690
  341.5 90.6 %collective-permute-start.31 = (bf16[384,256]{1,0:T(8,128)(2,1)}, bf16[384,256]{1,0:T(8,128)(2,1)S(1)}, u32[]{:S(2)}, u32[]{:S(2)}) collective-permute-start(bf16[384,256]{1,0:T(8,128)(2,1)} %get-tuple-element.135), channel_id=1, source_target_pairs={{0,3},{1,7},{2,2},{3,6},{4,1},{5,5},{6,0},{7,4},{16,19},{17,23},{1... | collective-permute-start | bytes 589832 | tf_op jit(solution)/shard_map/ppermute | solution.py:690
  355.7 76.5 %collective-permute-start.32 = (bf16[384,256]{1,0:T(8,128)(2,1)}, bf16[384,256]{1,0:T(8,128)(2,1)S(1)}, u32[]{:S(2)}, u32[]{:S(2)}) collective-permute-start(bf16[384,256]{1,0:T(8,128)(2,1)} %get-tuple-element.134), channel_id=1, source_target_pairs={{8,0},{9,4},{10,1},{11,5},{12,2},{13,6},{14,3},{15,7},{24,16},{25,... | collective-permute-start | bytes 589832 | tf_op jit(solution)/shard_map/ppermute | solution.py:690
  357.0 75.2 %collective-permute-start.33 = (bf16[384,256]{1,0:T(8,128)(2,1)S(1)}, bf16[384,256]{1,0:T(8,128)(2,1)S(1)}, u32[]{:S(2)}, u32[]{:S(2)}) collective-permute-start(bf16[384,256]{1,0:T(8,128)(2,1)S(1)} %get-tuple-element.133), channel_id=1, source_target_pairs={{8,1},{9,5},{10,0},{11,4},{12,3},{13,7},{14,2},{15,6},{24,17},{25,... | collective-permute-start | bytes 589832 | tf_op jit(solution)/shard_map/ppermute | solution.py:690
  358.3 73.9 %collective-permute-start.34 = (bf16[384,256]{1,0:T(8,128)(2,1)S(1)}, bf16[384,256]{1,0:T(8,128)(2,1)S(1)}, u32[]{:S(2)}, u32[]{:S(2)}) collective-permute-start(bf16[384,256]{1,0:T(8,128)(2,1)S(1)} %get-tuple-element.132), channel_id=1, source_target_pairs={{8,2},{9,6},{10,3},{11,7},{12,0},{13,4},{14,1},{15,5},{24,18},{25,... | collective-permute-start | bytes 589832 | tf_op jit(solution)/shard_map/ppermute | solution.py:690
  359.6 72.6 %collective-permute-start.35 = (bf16[384,256]{1,0:T(8,128)(2,1)S(1)}, bf16[384,256]{1,0:T(8,128)(2,1)S(1)}, u32[]{:S(2)}, u32[]{:S(2)}) collective-permute-start(bf16[384,256]{1,0:T(8,128)(2,1)S(1)} %get-tuple-element.131), channel_id=1, source_target_pairs={{8,3},{9,7},{10,2},{11,6},{12,1},{13,5},{14,0},{15,4},{24,19},{25,... | collective-permute-start | bytes 589832 | tf_op jit(solution)/shard_map/ppermute | solution.py:690
  (95 other events, 2401.4 us)
Sparse Core Ops, SparseCore 0:
  192.7 215.0 all-reduce.3

commit v2 on v1

--- a/solution.py
+++ b/solution.py
@@ -14,9 +14,9 @@
 NEG = -1e30
 F32 = jnp.float32
 BF16 = jnp.bfloat16
-TB = 256
-RES = 4
-UNROLL = 2
+TB = 512
+RES = 8
+UNROLL = 16
 VMEM_LIMIT = 56 * 1024 * 1024
 
 
@@ -322,7 +322,7 @@
 ):
     pieces = refs[:8]
     (q, kv, halo, o_far, lse_far, z, gain, bias, w_proj, w_in, w_back,
-     y_out, go_out, stat_out, gq_out, gk_out, gv_out, gmid_out, d_proj, d_in, d_back, d_gain, d_bias, squares,
+     y_out, go_out, stat_out, gq_out, gk_out, gv_out, gmid_out, slab, d_gain, d_bias, squares,
      ext, cot, sems) = refs[8:]
     step = pl.program_id(0)
     qw = q.shape[1]
@@ -332,7 +332,7 @@
     def _():
         gather_pieces(info, pieces, cot, sems, False)
         load_extended(halo, kv, ext)
-        for ref in (squares, gk_out, gv_out, d_proj, d_in, d_back, d_gain, d_bias):
+        for ref in (squares, gk_out, gv_out, slab, d_gain, d_bias):
             ref[...] = jnp.zeros_like(ref)
 
     limit = info[1]
@@ -382,8 +382,7 @@
     pos = base + lax.broadcasted_iota(jnp.int32, (TB, 1), 0)
     upstream = jnp.where(pos < limit, cot[pl.ds(start, TB)].astype(F32), 0.0)
     grad_out, grad_mid = feed_backward(
-        upstream, active, slope, normed, unit, scale, attended, gain, w_proj, w_in, w_back,
-        d_proj, d_in, d_back, d_gain, d_bias,
+        upstream, active, slope, normed, unit, scale, attended, gain, w_proj, w_in, w_back, slab, 0, d_gain, d_bias
     )
     gmid_out[...] = grad_mid
     go_out[...] = grad_out
@@ -411,20 +410,28 @@
     return jnp.where(lane < 64, low, high)
 
 
+def add_columns(slab, at, grad):
+    rows, cols = grad.shape
+    width = slab.shape[1]
+    for i in range(cols // width):
+        slab[at + i * rows : at + (i + 1) * rows] += grad[:, i * width : (i + 1) * width]
+
+
 def feed_backward(
-    upstream, active, slope, normed, unit, scale, attended, gain, w_proj, w_in, w_back,
-    d_proj, d_in, d_back, d_gain, d_bias,
+    upstream, active, slope, normed, unit, scale, attended, gain, w_proj, w_in, w_back, slab, at, d_gain, d_bias,
 ):
     low = upstream.astype(BF16)
-    d_back[...] += t_dot(active, low)
+    width = low.shape[1]
+    hidden = active.shape[1]
+    slab[at + width + hidden : at + width + 2 * hidden] += t_dot(active, low)
     grad_hidden = (dot_t(low, w_back[...]) * slope).astype(BF16)
-    d_in[...] += t_dot(normed, grad_hidden)
+    add_columns(slab, at + width, t_dot(normed, grad_hidden))
     grad_normed = dot_t(grad_hidden, w_in[...])
     d_gain[...] += col_sum(grad_normed * unit)
     d_bias[...] += col_sum(grad_normed)
     grad_mid = upstream + norm_back(grad_normed, unit, scale, gain[1:2])
     branch_low = grad_mid.astype(BF16)
-    d_proj[...] += t_dot(attended, branch_low)
+    slab[at : at + width] += t_dot(attended, branch_low)
     grad_out = dot_t(branch_low, w_proj[...]).astype(BF16)
     return grad_out, grad_mid
 
@@ -498,11 +505,11 @@
     lax.fori_loop(0, grid_q, back, 0)
 
 
-def mix_backward(grad_q, grad_kv, rows, gain, bias, w_mix, d_mix, d_gain, d_bias, carried):
+def mix_backward(grad_q, grad_kv, rows, gain, bias, w_mix, slab, d_gain, d_bias, carried):
     grad_mixed = jnp.concatenate([grad_q * score_scale(grad_q.shape[1]), grad_kv], axis=1).astype(BF16)
     unit, scale = norm_parts(rows)
     normed = (unit * gain[0:1] + bias[0:1]).astype(BF16)
-    d_mix[...] += t_dot(normed, grad_mixed)
+    add_columns(slab, 0, t_dot(normed, grad_mixed))
     grad_normed = dot_t(grad_mixed, w_mix[...])
     d_gain[...] += col_sum(grad_normed * unit)
     d_bias[...] += col_sum(grad_normed)
@@ -512,7 +519,7 @@
 def fourth_kernel(
     info, gq, gkv, got, z, gmid, gain_next, bias_next, w_mix_next,
     q, kv, halo, o, lse, active, slope, mid, gain, bias, w_proj, w_in, w_back,
-    gz_out, gq_out, gk_out, gv_out, gmid_out, d_mix, dn_gain, dn_bias, d_proj, d_in, d_back, d_gain, d_bias,
+    gz_out, gq_out, gk_out, gv_out, gmid_out, slab, dn_gain, dn_bias, d_gain, d_bias,
     ext,
 ):
     step = pl.program_id(0)
@@ -522,7 +529,7 @@
     @pl.when(step == 0)
     def _():
         load_extended(halo, kv, ext)
-        for ref in (gk_out, gv_out, d_mix, dn_gain, dn_bias, d_proj, d_in, d_back, d_gain, d_bias):
+        for ref in (gk_out, gv_out, slab, dn_gain, dn_bias, d_gain, d_bias):
             ref[...] = jnp.zeros_like(ref)
 
     limit = info[1]
@@ -530,7 +537,7 @@
     base = info[0] * n + start
     grad_kv = gkv[...] + got[...].astype(F32)
     grad_z = mix_backward(
-        gq[...], grad_kv, z[...].astype(F32), gain_next, bias_next, w_mix_next, d_mix, dn_gain, dn_bias, gmid[...]
+        gq[...], grad_kv, z[...].astype(F32), gain_next, bias_next, w_mix_next, slab, dn_gain, dn_bias, gmid[...]
     )
     grad_low = grad_z.astype(BF16)
     gz_out[...] = grad_low
@@ -539,7 +546,7 @@
     attended = o[...]
     grad_out, grad_mid = feed_backward(
         grad_low.astype(F32), active[...], slope[...].astype(F32), normed, unit, scale, attended, gain,
-        w_proj, w_in, w_back, d_proj, d_in, d_back, d_gain, d_bias,
+        w_proj, w_in, w_back, slab, w_mix_next.size // w_proj.shape[1], d_gain, d_bias,
     )
     gmid_out[...] = grad_mid
     weighted = grad_out.astype(F32) * attended.astype(F32)
@@ -558,12 +565,13 @@
         gv_out[near] += g_v
 
 
-def fifth_kernel(info, gq, gk, gv, got, x, gmid, gain, bias, w_mix, gx_out, d_mix, d_gain, d_bias):
+def fifth_kernel(info, gq, gk, gv, got, x, gmid, gain, bias, w_mix, *rest):
+    gx_out, slab, d_gain, d_bias = rest[-4:]
     step = pl.program_id(0)
 
     @pl.when(step == 0)
     def _():
-        for ref in (d_mix, d_gain, d_bias):
+        for ref in (slab, d_gain, d_bias):
             ref[...] = jnp.zeros_like(ref)
 
     at = pl.ds(pl.multiple_of(step * TB + WIN, WIN), TB)
@@ -572,38 +580,94 @@
     extra = jnp.concatenate([jnp.zeros((TB - WIN, got.shape[1]), F32), tail], axis=0)
     grad_kv = jnp.concatenate([gk[at], gv[at]], axis=1) + extra
     grad_x = mix_backward(
-        gq[...], grad_kv, x[...].astype(F32), gain, bias, w_mix, d_mix, d_gain, d_bias, gmid[...]
+        gq[...], grad_kv, x[...].astype(F32), gain, bias, w_mix, slab, d_gain, d_bias, gmid[...]
     )
     gx_out[...] = grad_x.astype(BF16)
 
 
 def assemble_kernel(info, *refs):
-    count = 8
-    low, high, out, narrow, wide, sem_in, sem_out = refs[:count], refs[count : 2 * count], *refs[2 * count :]
-
-    def each(t, act):
-        @pl.when(info[5] == 0)
-        def _():
-            act(pltpu.make_async_copy(low[t], narrow.at[t], sem_in.at[t]))
-
-        @pl.when(info[5] != 0)
-        def _():
-            act(pltpu.make_async_copy(high[t], narrow.at[t], sem_in.at[t]))
+    half = info[5]
+    core = info[0]
+    own, other, out, narrow, wide, sem_in, sem_out = refs[:4], *refs[4:]
+    rows = out.shape[1]
+    place = info[4]
+
+    def enter(t):
+        if t < 4:
+            return pltpu.make_async_copy(own[t].at[pl.ds(core * rows, rows)], narrow.at[t], sem_in.at[t])
+        return pltpu.make_async_copy(other.at[t - 4], narrow.at[t], sem_in.at[t])
 
     def leave(t):
-        return pltpu.make_async_copy(wide.at[t], out.at[t ^ info[4]], sem_out.at[t])
-
-    for t in range(count):
-        each(t, lambda c: c.start())
-    for t in range(count):
-        each(t, lambda c: c.wait())
+        tz, ty = (t % 4) // 2, t % 2
+        column = core if t < 4 else 1 - core
+        image = (half ^ tz) * 4 + column * 2 + (place ^ ty)
+        return pltpu.make_async_copy(wide.at[t], out.at[image], sem_out.at[t])
+
+    for t in range(8):
+        enter(t).start()
+    for t in range(8):
+        enter(t).wait()
         wide[t] = narrow[t].astype(F32)
         leave(t).start()
-    for t in range(count):
+    for t in range(8):
         leave(t).wait()
 
 
-def call(kernel, info, operands, specs, outs, out_specs, scratch=(), grid=()):
+def small_kernel(info, *refs):
+    vectors, (first, second, out) = refs[:8], refs[8:]
+    width = out.shape[1]
+    once = jnp.where(info[7] == 0, 1.0, 0.0)
+    lane = lax.broadcasted_iota(jnp.int32, (1, width), 1)
+    out[...] = jnp.zeros_like(out)
+    for i, vector in enumerate(vectors):
+        out[i : i + 1] = jnp.sum(vector[...], axis=0, keepdims=True) * once
+    for i in range(6):
+        rows = (first if i < 3 else second)[i % 3]
+        total = jnp.sum(jnp.sum(rows, axis=0, keepdims=True), axis=1, keepdims=True)
+        out[8 + i : 9 + i] = jnp.where(lane == info[6], total * once, 0.0)
+
+
+def unpack_kernel(info, mine, theirs, small, mix, proj, up, down, gain, bias, wide, *, sizes):
+    core = info[0]
+    wide[core] = mine[...].astype(F32)
+    wide[1 - core] = theirs[...].astype(F32)
+    rows_a, rows_b, rows_c, ways = sizes
+    early = (rows_a + rows_b) // 2 // ways
+    late = rows_c // 2 // ways
+    rows_mix = rows_c
+
+    def pieces(slab, start, stop):
+        total = {"a": rows_a, "b": rows_b, "c": rows_c}[slab] // 2
+        size, shift, skip = (late, early, 0) if slab == "c" else (early, 0, rows_a // 2 if slab == "b" else 0)
+        at = start
+        while at < stop:
+            half, row = at // total, at % total
+            along = row + skip
+            count = min(stop - at, total - row, size - along % size)
+            yield at - start, half, along // size * (early + late) + shift + along % size, count
+            at += count
+
+    width = wide.shape[2]
+    places = {0: (("c", 0), ("b", rows_mix)), 1: (("b", 0), ("a", 0))}
+    for layer in range(2):
+        (slab, at), (feed, feed_at) = places[layer]
+        for out, name in ((mix, slab), (proj, feed), (up, feed), (down, feed)):
+            if name == feed and out is not mix:
+                at = feed_at
+            rows, cols = out.shape[1:]
+            for i in range(cols // width):
+                for offset, half, row, count in pieces(name, at + i * rows, at + (i + 1) * rows):
+                    out[layer, offset : offset + count, i * width : (i + 1) * width] = wide[half, row : row + count]
+            if out is not mix:
+                feed_at = at + rows * cols // width
+    for layer in range(2):
+        for norm in range(2):
+            gain[layer, norm : norm + 1] = small[2 * layer + norm : 2 * layer + norm + 1]
+            bias[layer, norm : norm + 1] = small[4 + 2 * layer + norm : 5 + 2 * layer + norm]
+
+
+def call(kernel, info, operands, specs, outs, out_specs, scratch=(), grid=(), work=0):
+    moved = sum(math.prod(a.shape) * a.dtype.itemsize for a in list(operands) + jax.tree.leaves(outs))
     return pl.pallas_call(
         kernel,
         grid_spec=pltpu.PrefetchScalarGridSpec(
@@ -611,6 +675,7 @@
         ),
         out_shape=outs,
         compiler_params=pltpu.CompilerParams(vmem_limit_bytes=VMEM_LIMIT),
+        cost_estimate=pl.CostEstimate(flops=int(work * 1.15e9), bytes_accessed=moved, transcendentals=0),
     )(info, *operands)
 
 
@@ -628,6 +693,10 @@
 
 def shape(dims, kind):
     return jax.ShapeDtypeStruct(dims, kind)
+
+
+def after(value, *others):
+    return lax.optimization_barrier((value, others))[0]
 
 
 def body(edge_rows, lengths, norm_gain, norm_bias, w_qkv, w_out, w_up, w_down):
@@ -664,31 +733,44 @@
     chip = seat // 2
     part = seat % 2
     limit = lengths[chip]
-    info = jnp.stack([part, limit, chip % quarter, chip // quarter, my_key, half]).astype(jnp.int32)
+    spot = lax.axis_index("dp") * images + chip
+    info = jnp.stack([part, limit, chip % quarter, chip // quarter, chip % 2, half, spot, twin]).astype(jnp.int32)
 
     def scatter_route(t):
         return route([(s, 2 * (source_key(s)[0] ^ t) + source_key(s)[1]) for s in range(seats)])
-
-    def return_route(t, to_half):
-        pairs = []
-        for s in range(seats):
-            key = (s // 2) ^ t
-            if key // quarter == to_half:
-                pairs.append((s, source_seat(key, s % 2)))
-        return route(pairs)
 
     received = [None] * images
     for t in list(range(quarter, images)) + list(range(quarter)):
         piece = lax.dynamic_index_in_dim(edge_rows, my_key ^ t, 0, keepdims=False)
         received[t] = lax.ppermute(piece, "section", scatter_route(t))
 
-    def send_back(rows, to_half):
-        blocks = rows.reshape(quarter, rows_piece, width)
+    fz, fl, fy = chip // 4, (chip // 2) % 2, chip % 2
+    swap = route([(s, s ^ 1) for s in range(seats)])
+
+    def return_route(tz, ty):
+        pairs = []
+        for s in range(seats):
+            z, l, y, p = s // 8, (s // 4) % 2, (s // 2) % 2, s % 2
+            pairs.append((s, ((z ^ tz) * 4 + p * 2 + (y ^ ty)) * 2 + l))
+        return route(pairs)
+
+    def send_back(low, high, which=(2, 3, 0, 1)):
+        low = low.reshape(2, 2 * rows_piece, width)
+        high = high.reshape(2, 2 * rows_piece, width)
         out = []
-        for t in range(images):
-            piece = lax.dynamic_index_in_dim(blocks, (chip ^ t) % quarter, 0, keepdims=False)
-            out.append(lax.ppermute(piece, "section", return_route(t, to_half)))
-        return out
+        for t in which:
+            tz, ty = t // 2, t % 2
+            piece = jnp.where(
+                (fz ^ tz) == 0,
+                lax.dynamic_index_in_dim(low, fy ^ ty, 0, keepdims=False),
+                lax.dynamic_index_in_dim(high, fy ^ ty, 0, keepdims=False),
+            )
+            out.append((t, lax.ppermute(piece, "section", return_route(tz, ty))))
+        return [piece for _, piece in sorted(out, key=lambda p: p[0])]
+
+    def trade(got):
+        send = jnp.stack([lax.dynamic_slice_in_dim(g, (1 - part) * rows_piece, rows_piece, 0) for g in got])
+        return lax.ppermute(send, "section", swap)
 
     first_to_second = route([(2 * c, 2 * c + 1) for c in range(images)])
     second_to_first = route([(2 * c + 1, 2 * c) for c in range(images)])
@@ -702,10 +784,11 @@
     rows_hidden = shape((n, hidden), BF16)
     grad_k_shape = shape((n + WIN, qw), F32)
     grad_v_shape = shape((n + WIN, width), F32)
-    d_mix_shape = shape(w_qkv.shape[1:], F32)
-    d_proj_shape = shape(w_out.shape[1:], F32)
-    d_in_shape = shape(w_up.shape[1:], F32)
-    d_back_shape = shape(w_down.shape[1:], F32)
+    mix_rows = w_qkv.shape[1] * w_qkv.shape[2] // width
+    feed_rows = (w_out[0].size + w_up[0].size + w_down[0].size) // width
+    feed_slab = shape((feed_rows, width), F32)
+    both_slab = shape((mix_rows + feed_rows, width), F32)
+    mix_slab = shape((mix_rows, width), F32)
     vec_shape = shape((8, width), F32)
     squares_shape = shape((3, 8, width), F32)
     ext = pltpu.VMEM((n + WIN, kvw), BF16)
@@ -716,7 +799,7 @@
     x, q0, kv0 = call(
         first_kernel, info, received + [g0, b0, w_qkv[0]],
         [ANY] * images + [whole(g0), whole(b0), whole(w_qkv[0])],
-        outs, [whole(o) for o in outs], [dma((quarter,))],
+        outs, [whole(o) for o in outs], [dma((quarter,))], work=6,
     )
     halo0 = lax.ppermute(kv0[n - WIN :], "section", first_to_second)
 
@@ -724,10 +807,9 @@
     z, q1, kv1, o0, lse0, active0, slope0, mid0, squares0 = call(
         second_kernel, info, [x, q0, kv0, halo0, g0, b0, w_out[0], w_up[0], w_down[0], g1, b1, w_qkv[1]],
         [tiled(x), tiled(q0)] + [whole(a) for a in (kv0, halo0, g0, b0, w_out[0], w_up[0], w_down[0], g1, b1, w_qkv[1])],
-        outs, [tiled(o) for o in outs[:-1]] + [whole(outs[-1])], [ext], steps,
+        outs, [tiled(o) for o in outs[:-1]] + [whole(outs[-1])], [ext], steps, work=15,
     )
     kv_other = lax.ppermute(kv1, "section", first_to_second)
-    y0_back = send_back(z, 0)
 
     rows_k_all = shape((2 * n, qw), BF16)
     rows_v_all = shape((2 * n, width), BF16)
@@ -736,35 +818,37 @@
         far_forward_kernel, info, [q1, kv1, kv_other], [whole(a) for a in (q1, kv1, kv_other)],
         outs, [whole(o) for o in outs],
         [pltpu.VMEM((n, qw), F32), pltpu.VMEM((2 * n, qw), F32), pltpu.VMEM((HEADS, 2 * n, 128), F32),
-         pltpu.VMEM((HEADS, n, 128), F32), pltpu.VMEM((n, 128), F32)],
+         pltpu.VMEM((HEADS, n, 128), F32), pltpu.VMEM((n, 128), F32)], work=14,
     )
 
     halo1 = kv_other[n - WIN :]
     outs = [rows_low, rows_low, rows_stat, shape((n, qw), F32), grad_k_shape, grad_v_shape, rows_wide,
-            d_proj_shape, d_in_shape, d_back_shape, vec_shape, vec_shape, squares_shape]
-    (y1, go1, stat1, gq_near, gk_near, gv_near, gmid1, d_proj1, d_in1, d_back1, d_gain11, d_bias11, squares1) = call(
+            feed_slab, vec_shape, vec_shape, squares_shape]
+    (y1, go1, stat1, gq_near, gk_near, gv_near, gmid1, slab_a, d_gain11, d_bias11, squares1) = call(
         third_kernel, info,
         received + [q1, kv1, halo1, o_far, lse_far, z, g1, b1, w_out[1], w_up[1], w_down[1]],
         [ANY] * images + [tiled(q1), whole(kv1), whole(halo1), tiled(o_far), tiled(lse_far), tiled(z)]
         + [whole(a) for a in (g1, b1, w_out[1], w_up[1], w_down[1])],
         outs,
         [tiled(o) for o in outs[:4]] + [whole(outs[4]), whole(outs[5]), tiled(outs[6])] + [whole(o) for o in outs[7:]],
-        [ext, pltpu.VMEM((n, width), BF16), dma((quarter,))], steps,
-    )
-    y1_back = send_back(y1, 1)
+        [ext, pltpu.VMEM((n, width), BF16), dma((quarter,))], steps, work=24,
+    )
+    second_way = send_back(z, y1, (2,))
 
     outs = [shape((n, qw), F32), shape((n, kvw), F32), rows_kv]
     operands = [qr, kr, vr, go1, stat1, gq_near, gk_near, gv_near]
     gq1, gkv1, gkv_send = call(
         far_backward_kernel, info, operands, [whole(a) for a in operands], outs, [whole(o) for o in outs],
         [pltpu.VMEM((HEADS, n, 128), F32), pltpu.VMEM((n, 128), F32), pltpu.VMEM((n, qw), F32),
-         pltpu.VMEM((2 * n, qw), F32), pltpu.VMEM((HEADS, 2 * n, 128), F32)],
-    )
-    gkv_got = lax.ppermute(gkv_send, "section", second_to_first)
+         pltpu.VMEM((2 * n, qw), F32), pltpu.VMEM((HEADS, 2 * n, 128), F32)], work=18,
+    )
+    gkv_got = lax.ppermute(after(gkv_send, *second_way), "section", second_to_first)
+    first_way, other_way, third_way = send_back(after(z, *second_way), y1, (3, 0, 1))
+    forward_back = [first_way, other_way, *second_way, third_way]
 
     outs = [rows_low, shape((n, qw), F32), grad_k_shape, grad_v_shape, rows_wide,
-            d_mix_shape, vec_shape, vec_shape, d_proj_shape, d_in_shape, d_back_shape, vec_shape, vec_shape]
-    (gz, gq0, gk0, gv0, gmid0, d_mix1, d_gain10, d_bias10, d_proj0, d_in0, d_back0, d_gain01, d_bias01) = call(
+            both_slab, vec_shape, vec_shape, vec_shape, vec_shape]
+    (gz, gq0, gk0, gv0, gmid0, slab_b, d_gain10, d_bias10, d_gain01, d_bias01) = call(
         fourth_kernel, info,
         [gq1, gkv1, gkv_got, z, gmid1, g1, b1, w_qkv[1], q0, kv0, halo0, o0, lse0, active0, slope0, mid0, g0, b0,
          w_out[0], w_up[0], w_down[0]],
@@ -773,24 +857,83 @@
         + [whole(a) for a in (g0, b0, w_out[0], w_up[0], w_down[0])],
         outs,
         [tiled(outs[0]), tiled(outs[1]), whole(outs[2]), whole(outs[3]), tiled(outs[4])] + [whole(o) for o in outs[5:]],
-        [ext], steps,
-    )
+        [ext], steps, work=20,
+    )
+    gk0, gv0, slab_b = after((gk0, gv0, slab_b), *forward_back)
     halo_send = jnp.concatenate([gk0[:WIN], gv0[:WIN]], axis=1).astype(BF16)
     halo_got = lax.ppermute(halo_send, "section", second_to_first)
-    gz_back = send_back(gz, 1)
-
-    outs = [rows_low, d_mix_shape, vec_shape, vec_shape]
-    gx, d_mix0, d_gain00, d_bias00 = call(
+
+    once = (twin == 0).astype(F32)
+    dp_count = lax.axis_size("dp")
+    dp_index = lax.axis_index("dp")
+
+    def partners(masks):
+        total = dp_count * sections
+        spot = dp_index * sections + index
+        digit = sum(((spot // m) % 2) << i for i, m in enumerate(masks))
+        routes = []
+        for c in range(1, 1 << len(masks)):
+            flips = sum(m for i, m in enumerate(masks) if (c >> i) & 1)
+            routes.append((c, [(s, s ^ flips) for s in range(total)]))
+        return digit, routes
+
+    def chunk(slabs, which, ways):
+        return jnp.concatenate(
+            [lax.dynamic_slice_in_dim(s, which * (s.shape[0] // ways), s.shape[0] // ways, 0) for s in slabs]
+        )
+
+    def scatter(slabs, masks, vectors=None):
+        digit, routes = partners(masks)
+        ways = 1 << len(masks)
+        kept = chunk(slabs, digit, ways)
+        count = kept.shape[0]
+        riders = []
+        if vectors is not None:
+            coarse = vectors.astype(BF16)
+            riders = [coarse, (vectors - coarse.astype(F32)).astype(BF16)]
+        got = [
+            lax.ppermute(jnp.concatenate([chunk(slabs, digit ^ c, ways).astype(BF16)] + riders), ("dp", "section"), way)
+            for c, way in routes
+        ]
+        for g in got:
+            kept = kept + g[:count].astype(F32)
+            if vectors is not None:
+                rest = g[count:].astype(F32)
+                vectors = vectors + (rest[: vectors.shape[0]] + rest[vectors.shape[0] :])
+        return kept if vectors is None else (kept, vectors)
+
+    def gather(piece, masks):
+        digit, routes = partners(masks)
+        pieces = [piece] + [lax.ppermute(piece, ("dp", "section"), way) for _, way in routes]
+        stacked = jnp.stack(pieces)
+        return jnp.concatenate(
+            [lax.dynamic_index_in_dim(stacked, digit ^ j, 0, keepdims=False) for j in range(len(pieces))]
+        )
+
+    dp_masks = [sections << b for b in range(dp_count.bit_length() - 1)]
+    section_masks = [1 << b for b in range(1, sections.bit_length() - 1)]
+    plane = [dp_masks[0], section_masks[0]]
+    rest = section_masks[1:] + dp_masks[1:]
+    rest = [rest[i : i + 2] for i in range(0, len(rest), 2)]
+    early = scatter([slab_a * once, slab_b * once] if rep > 1 else [slab_a, slab_b], [1])
+    gq0 = after(gq0, early)
+    early = scatter([early], plane)
+
+    outs = [rows_low, mix_slab, vec_shape, vec_shape]
+    gx, slab_c, d_gain00, d_bias00 = call(
         fifth_kernel, info, [gq0, gk0, gv0, halo_got, x, gmid0, g0, b0, w_qkv[0]],
         [tiled(gq0), whole(gk0), whole(gv0), whole(halo_got), tiled(x), tiled(gmid0), whole(g0), whole(b0), whole(w_qkv[0])],
-        outs, [tiled(outs[0])] + [whole(o) for o in outs[1:]], (), steps,
-    )
-    gx_back = send_back(gx, 0)
-
-    def assemble(low, high):
+        outs, [tiled(outs[0])] + [whole(o) for o in outs[1:]], (), steps, work=8,
+    )
+    forward_trade = trade(after(forward_back, gx))
+
+    operands = [d_gain00, d_gain01, d_gain10, d_gain11, d_bias00, d_bias01, d_bias10, d_bias11, squares0, squares1]
+    small_shape = shape((16, width), F32)
+    small = call(small_kernel, info, operands, [whole(a) for a in operands], small_shape, whole(small_shape))
+
+    def assemble(own, other):
         out = call(
-            assemble_kernel, info, low + high, [ANY] * (2 * images),
-            shape((images, rows_piece, width), F32), ANY,
+            assemble_kernel, info, own + [other], [ANY] * 5, shape((images, rows_piece, width), F32), ANY,
             [pltpu.VMEM((images, rows_piece, width), BF16), pltpu.VMEM((images, rows_piece, width), F32),
              dma((images,)), dma((images,))],
         )
@@ -798,23 +941,34 @@
             out = lax.dynamic_slice_in_dim(out, twin * rows_dev, rows_dev, 1)
         return out
 
-    forward_rows = assemble(y0_back, y1_back)
-    backward_rows = assemble(gx_back, gz_back)
-
-    once = (twin == 0).astype(F32)
-    squares = jnp.concatenate([squares0, squares1]).sum(axis=(1, 2))
-    spread = squares[:, None] * (jnp.arange(images) == chip).astype(F32)[None, :] * once
-    summed = lax.psum(spread, "section")
-    rms_values = jnp.sqrt(summed / (lengths.astype(F32)[None, :] * width))
-
-    d_gain = jnp.stack([jnp.stack([d_gain00, d_gain01]), jnp.stack([d_gain10, d_gain11])]).sum(axis=2)
-    d_bias = jnp.stack([jnp.stack([d_bias00, d_bias01]), jnp.stack([d_bias10, d_bias11])]).sum(axis=2)
-    grads = (
-        d_gain, d_bias, jnp.stack([d_mix0, d_mix1]), jnp.stack([d_proj0, d_proj1]),
-        jnp.stack([d_in0, d_in1]), jnp.stack([d_back0, d_back1]),
-    )
-    grads = lax.psum(tuple(g * once for g in grads), ("dp", "section"))
-    return (forward_rows, backward_rows, rms_values) + tuple(grads)
+    crossing = send_back(gx, gz, (2, 3))
+    late, small = scatter([after(slab_c * once if rep > 1 else slab_c, early)], [1], small)
+    late, small = scatter([late], plane, small)
+    early_rows = early.shape[0]
+    forward_rows = assemble(forward_back, forward_trade)
+    both, _ = after((jnp.concatenate([early, late]), forward_rows), *crossing)
+    staying = send_back(after(gx, *crossing), gz, (0, 1))
+    for masks in rest:
+        both, small = scatter([both], masks, small)
+    both = both.astype(BF16)
+    for masks in rest[::-1]:
+        both = gather(both, masks)
+    backward_back = staying + crossing
+    backward_trade = trade(backward_back)
+    both = gather(both, plane)
+    backward_rows = assemble(backward_back, backward_trade)
+    both = after(both, backward_rows)
+    (theirs,) = (lax.ppermute(both, ("dp", "section"), way) for _, way in partners([1])[1])
+    sums = lax.dynamic_slice_in_dim(small[8:14], dp_index * images, images, 1)
+    rms_values = jnp.sqrt(sums / (lengths.astype(F32)[None, :] * width))
+    outs = [shape(w.shape, F32) for w in (w_qkv, w_out, w_up, w_down, norm_gain, norm_bias)]
+    sizes = (slab_a.shape[0], slab_b.shape[0], slab_c.shape[0], 1 << len(plane))
+    grads = call(
+        functools.partial(unpack_kernel, sizes=sizes), jnp.stack([index % 2]).astype(jnp.int32), [both, theirs, small],
+        [whole(both), whole(theirs), whole(small)], outs, [whole(o) for o in outs],
+        [pltpu.VMEM((2,) + both.shape, F32)],
+    )
+    return (forward_rows, backward_rows, rms_values, grads[4], grads[5]) + tuple(grads[:4])
 
 
 def solution(mesh):

time: 451 us -> 265 us (0.59)
  blocking collectives: 114 us -> 0 us
  starting transfers between devices: 128 us -> 70.9 us
  waiting for transfers between devices: 47.9 us -> 65.4 us
  Pallas kernels: 112 us -> 97.6 us
  between operations: 15.6 us -> 1.56 us
    psum x2 -> x0, blocking collectives: 114 us -> none  [the longest x1 71.1 us: body(): grads = lax.psum(tuple((g * once for g in grads)), ('dp', 'section'))]
    ppermute x33 -> x29, starting transfers between devices: 90.7 us -> 34 us  [the longest x11 14.8 us: scatter(): lax.ppermute(jnp.concatenate([chunk(slabs, digit ^ c, ways).astype(BF16)]...]
    ppermute x33 -> x29, waiting for transfers between devices: 33.4 us -> 51.1 us  [the longest x8 22.2 us: send_back(): out.append((t, lax.ppermute(piece, 'section', return_route(tz, ty))))]
    pallas_call x9 -> x11, Pallas kernels: 112 us -> 97.6 us  [call(): pl.pallas_call(kernel, grid_spec=pltpu.PrefetchScalarGridSpec(num_scalar_...]
    another operation x8 -> x5, other arithmetic: 6.06 us -> 0.38 us  [the longest x2 0.2 us: trade(): jnp.stack([lax.dynamic_slice_in_dim(g, (1 - part) * rows_piece, rows_piec...]
    unnamed x152 -> x72, local copies, waits for them, and re-layouts: 10.2 us -> 6.15 us
  transfers between devices with their start and end apart: 45 -> 40, of which waited for: 7 -> 18; matrix products, arithmetic and copies ran while one was open for 4% -> 6% of each run, Pallas kernels for 8% -> 16%
where the time goes in v2:
time: 265 us; the launch traced here: 263 us
  Pallas kernels  97.6 us (37%)
  starting transfers between devices  70.9 us (27%)
  waiting for transfers between devices  65.4 us (25%)
  local copies, waits for them, and re-layouts  21.1 us (8%)
  other arithmetic  6.93 us (3%)
    pallas_call x11, Pallas kernels, call(): pl.pallas_call(kernel, grid_spec=pltpu.PrefetchScalarGridSpec(num_scalar_...  97.6 us
    ppermute x8, starting transfers between devices, body(): received[t] = lax.ppermute(piece, 'section', scatter_route(t))  32 us
    ppermute x8, waiting for transfers between devices, send_back(): out.append((t, lax.ppermute(piece, 'section', return_route(tz, ty))))  22.2 us
    ppermute x11, starting transfers between devices, scatter(): lax.ppermute(jnp.concatenate([chunk(slabs, digit ^ c, ways).astype(BF16)]...  14.8 us
    ppermute x11, waiting for transfers between devices, scatter(): lax.ppermute(jnp.concatenate([chunk(slabs, digit ^ c, ways).astype(BF16)]...  14.2 us
    ppermute x6, waiting for transfers between devices, gather(): lax.ppermute(piece, ('dp', 'section'), way)  12.4 us
    ppermute x8, waiting for transfers between devices, body(): received[t] = lax.ppermute(piece, 'section', scatter_route(t))  11.5 us
    ppermute x8, starting transfers between devices, send_back(): out.append((t, lax.ppermute(piece, 'section', return_route(tz, ty))))  9.4 us
  transfers between devices with their start and end apart: 40, of which 18 were waited for; matrix products, arithmetic and copies ran while one was open for 6% of the time, Pallas kernels for 16%

profile of v2, /device:TPU:0, one launch (start us, length us, event | category | flops | bytes accessed | tf_op | source)
XLA Modules:
  0.0 263.5 jit_solution(3698604780762445080)
XLA Ops:
  3.2 5.8 %collective-permute-start.1 = (bf16[384,256]{1,0:T(8,128)(2,1)S(1)}, bf16[384,256]{1,0:T(8,128)(2,1)S(1)}, u32[]{:S(2)}, u32[]{:S(2)}) collective-permute-start(bf16[384,256]{1,0:T(8,128)(2,1)S(1)} %get-tuple-element.162), channel_id=1, source_target_pairs={{0,2},{1,0},{2,6},{3,4},{4,3},{5,1},{6,7},{7,5},{8,10},{9,8},{10,1... | collective-permute-start | bytes 589832 | tf_op jit(solution)/shard_map/ppermute | solution.py:745
  19.2 19.0 %collective-permute-start.6 = (bf16[384,256]{1,0:T(8,128)(2,1)S(1)}, bf16[384,256]{1,0:T(8,128)(2,1)S(1)}, u32[]{:S(2)}, u32[]{:S(2)}) collective-permute-start(bf16[384,256]{1,0:T(8,128)(2,1)S(1)} %get-tuple-element.164), channel_id=1, source_target_pairs={{0,12},{1,14},{2,8},{3,10},{4,13},{5,15},{6,9},{7,11},{8,4},{9,6},... | collective-permute-start | bytes 589832 | tf_op jit(solution)/shard_map/ppermute | solution.py:745
  39.4 9.2 %collective-permute-done.6.refs_6_ = bf16[384,256]{1,0:T(8,128)(2,1)S(1)} collective-permute-done((bf16[384,256]{1,0:T(8,128)(2,1)S(1)}, bf16[384,256]{1,0:T(8,128)(2,1)S(1)}, u32[]{:S(2)}, u32[]{:S(2)}) %collective-permute-start.6) | collective-permute-done | bytes 196640 | tf_op jit(solution)/shard_map/ppermute | solution.py:745
  51.6 5.8 %shard_map.151 = (bf16[1536,256]{1,0:T(8,128)(2,1)}, bf16[1536,128]{1,0:T(8,128)(2,1)}, bf16[1536,384]{1,0:T(8,128)(2,1)}) custom-call(s32[8]{0:T(128)} %stack.89.info, bf16[384,256]{1,0:T(8,128)(2,1)} %copy-done.28, bf16[384,256]{1,0:T(8,128)(2,1)} %copy-done.29, bf16[384,256]{1,0:T(8,128)(2,1)} %collective-permute-done.2.refs_2_, ...), custom_call_target="tpu_custom_call" | custom-call | flops 6899999744 | bytes 4198400 | tf_op jit(solution)/shard_map/pallas_call | solution.py:671
  61.2 11.6 %shard_map.152 = (bf16[1536,256]{1,0:T(8,128)(2,1)}, bf16[1536,128]{1,0:T(8,128)(2,1)}, bf16[1536,384]{1,0:T(8,128)(2,1)}, bf16[1536,256]{1,0:T(8,128)(2,1)}, f3...) custom-call(s32[8]{0:T(128)} %stack.89.info, ...), custom_call_target="tpu_custom_call" | custom-call | flops 17250000896 | bytes 12058624 | tf_op jit(solution)/shard_map/pallas_call | solution.py:671
  78.8 8.3 %shard_map.153 = (bf16[1536,128]{1,0:T(8,128)(2,1)}, bf16[3072,128]{1,0:T(8,128)(2,1)}, bf16[3072,256]{1,0:T(8,128)(2,1)}, f32[1536,256]{1,0:T(8,128)}, f32[1536,128]{1,0:T(8,128)}) custom-call(s32[8]{0:T(128)} %stack.89.info, bf16[1536,128]{1,0:T(8,128)(2,1)} %get-tuple-element.78.q.refs_8_, bf16[1536,384]{1,0:T(8,128)(2,1)} %get-tuple-element.79.kv.refs_9_, ...), custom_call_target="tpu_custom_call" | custom-call | flops 16099999744 | bytes 7864320 | tf_op jit(solution)/shard_map/pallas_call | solution.py:671
  87.1 21.5 %shard_map.154 = (bf16[1536,256]{1,0:T(8,128)(2,1)}, bf16[1536,256]{1,0:T(8,128)(2,1)}, f32[1536,128]{1,0:T(8,128)}, f32[1536,128]{1,0:T(8,128)}, f32[1664,128]{...) custom-call(s32[8]{0:T(128)} %stack.89.info, ...), custom_call_target="tpu_custom_call" | custom-call | flops 27599998976 | bytes 15675392 | tf_op jit(solution)/shard_map/pallas_call | solution.py:671
  110.8 13.3 %shard_map.155 = (f32[1536,128]{1,0:T(8,128)}, f32[1536,384]{1,0:T(8,128)}, bf16[1536,384]{1,0:T(8,128)(2,1)}) custom-call(s32[8]{0:T(128)} %stack.89.info, bf16[1536,128]{1,0:T(8,128)(2,1)} %get-tuple-element.84.qr, bf16[3072,128]{1,0:T(8,128)(2,1)} %get-tuple-element.85.kr, bf16[3072,256]{1,0:T(8,128)(2,1)} %get-tuple-element.86.vr, ...), custom_call_target="tpu_custom_call" | custom-call | flops 20700000256 | bytes 11993088 | tf_op jit(solution)/shard_map/pallas_call | solution.py:671
  124.0 4.8 %collective-permute-done.10.refs_2_ = bf16[768,256]{1,0:T(8,128)(2,1)S(1)} collective-permute-done((bf16[768,256]{1,0:T(8,128)(2,1)S(1)}, bf16[768,256]{1,0:T(8,128)(2,1)S(1)}, u32[]{:S(2)}, u32[]{:S(2)}) %collective-permute-start.10) | collective-permute-done | bytes 393248 | tf_op jit(solution)/shard_map/ppermute | solution.py:768
  135.0 17.8 %shard_map.156 = (bf16[1536,256]{1,0:T(8,128)(2,1)}, f32[1536,128]{1,0:T(8,128)}, f32[1664,128]{1,0:T(8,128)}, f32[1664,256]{1,0:T(8,128)}, f32[1536,256]{1,0:T(...) custom-call(s32[8]{0:T(128)} %stack.89.info, ...), custom_call_target="tpu_custom_call" | custom-call | flops 23000000512 | bytes 23142400 | tf_op jit(solution)/shard_map/pallas_call | solution.py:671
  155.4 3.4 %collective-permute-start.15 = (bf16[1536,256]{1,0:T(8,128)(2,1)}, bf16[1536,256]{1,0:T(8,128)(2,1)}, u32[]{:S(2)}, u32[]{:S(2)}) collective-permute-start(bf16[1536,256]{1,0:T(8,128)(2,1)} %pad_maximum_fusion.2), channel_id=1, source_target_pairs={{0,1},{1,0},{2,3},{3,2},{4,5},{5,4},{6,7},{7,6},{8,9},{9,8},{10,11... | collective-permute-start | bytes 2359304 | tf_op jit(solution)/shard_map/ppermute | solution.py:895
  168.7 6.8 %shard_map.157 = (bf16[1536,256]{1,0:T(8,128)(2,1)}, f32[512,256]{1,0:T(8,128)}, f32[8,256]{1,0:T(8,128)}, f32[8,256]{1,0:T(8,128)}) custom-call(s32[8]{0:T(128)} %stack.89.info, f32[1536,128]{1,0:T(8,128)} %get-tuple-element.108.gq, f32[1664,128]{1,0:T(8,128)} %get-tuple-element.109.gk, f32[1664,256]{1,0:T(8,128)} %get-tuple-element.110.gv, ...), custom_call_target="tpu_custom_call" | custom-call | flops 9200000000 | bytes 7393280 | tf_op jit(solution)/shard_map/pallas_call | solution.py:671
  188.4 2.9 %collective-permute-done.29 = bf16[96,256]{1,0:T(8,128)(2,1)S(1)} collective-permute-done((bf16[96,256]{1,0:T(8,128)(2,1)S(1)}, bf16[96,256]{1,0:T(8,128)(2,1)S(1)}, u32[]{:S(2)}, u32[]{:S(2)}) %collective-permute-start.29) | collective-permute-done | bytes 49184 | tf_op jit(solution)/shard_map/ppermute | solution.py:895
  191.6 4.2 %collective-permute-done.28 = bf16[96,256]{1,0:T(8,128)(2,1)S(1)} collective-permute-done((bf16[96,256]{1,0:T(8,128)(2,1)S(1)}, bf16[96,256]{1,0:T(8,128)(2,1)S(1)}, u32[]{:S(2)}, u32[]{:S(2)}) %collective-permute-start.28) | collective-permute-done | bytes 49184 | tf_op jit(solution)/shard_map/ppermute | solution.py:895
  195.9 10.6 %collective-permute-done.18.refs_2_ = bf16[768,256]{1,0:T(8,128)(2,1)S(1)} collective-permute-done((bf16[768,256]{1,0:T(8,128)(2,1)S(1)}, bf16[768,256]{1,0:T(8,128)(2,1)S(1)}, u32[]{:S(2)}, u32[]{:S(2)}) %collective-permute-start.18) | collective-permute-done | bytes 393248 | tf_op jit(solution)/shard_map/ppermute | solution.py:768
  206.5 6.8 %collective-permute-done.19.refs_3_ = bf16[768,256]{1,0:T(8,128)(2,1)S(1)} collective-permute-done((bf16[768,256]{1,0:T(8,128)(2,1)S(1)}, bf16[768,256]{1,0:T(8,128)(2,1)S(1)}, u32[]{:S(2)}, u32[]{:S(2)}) %collective-permute-start.19) | collective-permute-done | bytes 393248 | tf_op jit(solution)/shard_map/ppermute | solution.py:768
  216.9 3.4 %shard_map.158 = f32[8,384,256]{2,1,0:T(8,128)} custom-call(s32[8]{0:T(128)} %stack.89.info, bf16[768,256]{1,0:T(8,128)(2,1)} %copy-done.8, bf16[768,256]{1,0:T(8,128)(2,1)} %copy-done.9, bf16[768,256]{1,0:T(8,128)(2,1)} %copy-done.7, bf16[768,256]{1,0:T(8,128)(2,1)} %copy-done.10, bf16[4,384,256]{2,1,0:T(8,128)(2,1)} %copy-done.16), custom_call_target="tpu_custom_call" | custom-call | bytes 5505024 | tf_op jit(solution)/shard_map/pallas_call | solution.py:671
  225.6 2.9 %collective-permute-done.31 = bf16[144,256]{1,0:T(8,128)(2,1)S(1)} collective-permute-done((bf16[144,256]{1,0:T(8,128)(2,1)S(1)}, bf16[144,256]{1,0:T(8,128)(2,1)S(1)}, u32[]{:S(2)}, u32[]{:S(2)}) %collective-permute-start.31) | collective-permute-done | bytes 73760 | tf_op jit(solution)/shard_map/ppermute | solution.py:895
  232.8 2.8 %collective-permute-start.35 = (bf16[112,256]{1,0:T(8,128)(2,1)S(1)}, bf16[112,256]{1,0:T(8,128)(2,1)S(1)}, u32[]{:S(2)}, u32[]{:S(2)}) collective-permute-start(bf16[112,256]{1,0:T(8,128)(2,1)S(1)} %add_convert_fusion), channel_id=1, source_target_pairs={{0,12},{1,13},{2,14},{3,15},{4,8},{5,9},{6,10},{7,11},{8,4},{9,5},... | collective-permute-start | bytes 172040 | tf_op jit(solution)/shard_map/ppermute | solution.py:907
  235.8 4.0 %collective-permute-done.34 = bf16[112,256]{1,0:T(8,128)(2,1)S(1)} collective-permute-done((bf16[112,256]{1,0:T(8,128)(2,1)S(1)}, bf16[112,256]{1,0:T(8,128)(2,1)S(1)}, u32[]{:S(2)}, u32[]{:S(2)}) %collective-permute-start.34) | collective-permute-done | bytes 57376 | tf_op jit(solution)/shard_map/ppermute | solution.py:907
  243.4 4.7 %collective-permute-done.36 = bf16[448,256]{1,0:T(8,128)(2,1)S(1)} collective-permute-done((bf16[448,256]{1,0:T(8,128)(2,1)S(1)}, bf16[448,256]{1,0:T(8,128)(2,1)S(1)}, u32[]{:S(2)}, u32[]{:S(2)}) %collective-permute-start.36) | collective-permute-done | bytes 229408 | tf_op jit(solution)/shard_map/ppermute | solution.py:907
  248.1 3.7 %collective-permute-done.37 = bf16[448,256]{1,0:T(8,128)(2,1)S(1)} collective-permute-done((bf16[448,256]{1,0:T(8,128)(2,1)S(1)}, bf16[448,256]{1,0:T(8,128)(2,1)S(1)}, u32[]{:S(2)}, u32[]{:S(2)}) %collective-permute-start.37) | collective-permute-done | bytes 229408 | tf_op jit(solution)/shard_map/ppermute | solution.py:907
  253.0 3.4 %shard_map.159 = f32[8,384,256]{2,1,0:T(8,128)} custom-call(s32[8]{0:T(128)} %stack.89.info, bf16[768,256]{1,0:T(8,128)(2,1)} %copy-done.14, bf16[768,256]{1,0:T(8,128)(2,1)} %copy-done.13, bf16[768,256]{1,0:T(8,128)(2,1)} %copy-done.11, bf16[768,256]{1,0:T(8,128)(2,1)} %copy-done.12, bf16[4,384,256]{2,1,0:T(8,128)(2,1)} %copy-done.15), custom_call_target="tpu_custom_call" | custom-call | bytes 5505024 | tf_op jit(solution)/shard_map/pallas_call | solution.py:671
  259.9 3.6 %shard_map.161 = (f32[2,256,512]{2,1,0:T(8,128)}, f32[2,256,256]{2,1,0:T(8,128)}, f32[2,256,512]{2,1,0:T(8,128)}, f32[2,512,256]{2,1,0:T(8,128)}, f32[2,2,256]{2,1,0:T(2,128)}, /*index=5*/f32[2,2,256]{2,1,0:T(2,128)}) custom-call(s32[1]{0:T(128)} %bitcast.info, bf16[1792,256]{1,0:T(8,128)(2,1)} %copy-done, bf16[1792,256]{1,0:T(8,128)(2,1)} %copy-done.6, ...), custom_call_target="tpu_custom_call" | custom-call | bytes 5529600 | tf_op jit(solution)/shard_map/pallas_call | solution.py:671
  (204 shorter events, 81.9 us)
Async XLA Ops:
  2.4 16.7 %collective-permute-start = (bf16[384,256]{1,0:T(8,128)(2,1)S(1)}, bf16[384,256]{1,0:T(8,128)(2,1)S(1)}, u32[]{:S(2)}, u32[]{:S(2)}) collective-permute-start(bf16[384,256]{1,0:T(8,128)(2,1)S(1)} %get-tuple-element.163), channel_id=1, source_target_pairs={{0,0},{1,2},{2,4},{3,6},{4,1},{5,3},{6,5},{7,7},{8,8},{9,10},{10,1... | collective-permute-start | bytes 589832 | tf_op jit(solution)/shard_map/ppermute | solution.py:745
  3.2 16.0 %collective-permute-start.1 = (bf16[384,256]{1,0:T(8,128)(2,1)S(1)}, bf16[384,256]{1,0:T(8,128)(2,1)S(1)}, u32[]{:S(2)}, u32[]{:S(2)}) collective-permute-start(bf16[384,256]{1,0:T(8,128)(2,1)S(1)} %get-tuple-element.162), channel_id=1, source_target_pairs={{0,2},{1,0},{2,6},{3,4},{4,3},{5,1},{6,7},{7,5},{8,10},{9,8},{10,1... | collective-permute-start | bytes 589832 | tf_op jit(solution)/shard_map/ppermute | solution.py:745
  9.0 29.3 %collective-permute-start.2 = (bf16[384,256]{1,0:T(8,128)(2,1)S(1)}, bf16[384,256]{1,0:T(8,128)(2,1)}, u32[]{:S(2)}, u32[]{:S(2)}) collective-permute-start(bf16[384,256]{1,0:T(8,128)(2,1)S(1)} %get-tuple-element.161), channel_id=1, source_target_pairs={{0,4},{1,6},{2,0},{3,2},{4,5},{5,7},{6,1},{7,3},{8,12},{9,14},{10,... | collective-permute-start | bytes 589832 | tf_op jit(solution)/shard_map/ppermute | solution.py:745
  10.2 29.2 %collective-permute-start.3 = (bf16[384,256]{1,0:T(8,128)(2,1)S(1)}, bf16[384,256]{1,0:T(8,128)(2,1)}, u32[]{:S(2)}, u32[]{:S(2)}) collective-permute-start(bf16[384,256]{1,0:T(8,128)(2,1)S(1)} %get-tuple-element.160), channel_id=1, source_target_pairs={{0,6},{1,4},{2,2},{3,0},{4,7},{5,5},{6,3},{7,1},{8,14},{9,12},{10,... | collective-permute-start | bytes 589832 | tf_op jit(solution)/shard_map/ppermute | solution.py:745
  12.2 27.2 %collective-permute-start.4 = (bf16[384,256]{1,0:T(8,128)(2,1)S(1)}, bf16[384,256]{1,0:T(8,128)(2,1)}, u32[]{:S(2)}, u32[]{:S(2)}) collective-permute-start(bf16[384,256]{1,0:T(8,128)(2,1)S(1)} %get-tuple-element.159), channel_id=1, source_target_pairs={{0,8},{1,10},{2,12},{3,14},{4,9},{5,11},{6,13},{7,15},{8,0},{9,2},... | collective-permute-start | bytes 589832 | tf_op jit(solution)/shard_map/ppermute | solution.py:745
  19.1 20.3 %collective-permute-start.5 = (bf16[384,256]{1,0:T(8,128)(2,1)S(1)}, bf16[384,256]{1,0:T(8,128)(2,1)S(1)}, u32[]{:S(2)}, u32[]{:S(2)}) collective-permute-start(bf16[384,256]{1,0:T(8,128)(2,1)S(1)} %get-tuple-element.158), channel_id=1, source_target_pairs={{0,10},{1,8},{2,14},{3,12},{4,11},{5,9},{6,15},{7,13},{8,2},{9,0},... | collective-permute-start | bytes 589832 | tf_op jit(solution)/shard_map/ppermute | solution.py:745
  19.2 29.4 %collective-permute-start.6 = (bf16[384,256]{1,0:T(8,128)(2,1)S(1)}, bf16[384,256]{1,0:T(8,128)(2,1)S(1)}, u32[]{:S(2)}, u32[]{:S(2)}) collective-permute-start(bf16[384,256]{1,0:T(8,128)(2,1)S(1)} %get-tuple-element.164), channel_id=1, source_target_pairs={{0,12},{1,14},{2,8},{3,10},{4,13},{5,15},{6,9},{7,11},{8,4},{9,6},... | collective-permute-start | bytes 589832 | tf_op jit(solution)/shard_map/ppermute | solution.py:745
  38.3 12.7 %collective-permute-start.7 = (bf16[384,256]{1,0:T(8,128)(2,1)S(1)}, bf16[384,256]{1,0:T(8,128)(2,1)S(1)}, u32[]{:S(2)}, u32[]{:S(2)}) collective-permute-start(bf16[384,256]{1,0:T(8,128)(2,1)S(1)} %get-tuple-element.157), channel_id=1, source_target_pairs={{0,14},{1,12},{2,10},{3,8},{4,15},{5,13},{6,11},{7,9},{8,6},{9,4},... | collective-permute-start | bytes 589832 | tf_op jit(solution)/shard_map/ppermute | solution.py:745
  109.6 19.2 %collective-permute-start.10 = (bf16[768,256]{1,0:T(8,128)(2,1)S(1)}, bf16[768,256]{1,0:T(8,128)(2,1)S(1)}, u32[]{:S(2)}, u32[]{:S(2)}) collective-permute-start(bf16[768,256]{1,0:T(8,128)(2,1)S(1)} %select_bitcast_fusion.7), channel_id=1, source_target_pairs={{0,8},{1,12},{2,10},{3,14},{4,9},{5,13},{6,11},{7,15},{8,0},{9,4},... | collective-permute-start | bytes 1179656 | tf_op jit(solution)/shard_map/ppermute | solution.py:768
  131.6 21.2 %collective-permute-start.11 = (bf16[768,256]{1,0:T(8,128)(2,1)S(1)}, bf16[768,256]{1,0:T(8,128)(2,1)S(1)}, u32[]{:S(2)}, u32[]{:S(2)}) collective-permute-start(bf16[768,256]{1,0:T(8,128)(2,1)S(1)} %get-tuple-element.155), channel_id=1, source_target_pairs={{0,0},{1,4},{2,2},{3,6},{4,1},{5,5},{6,3},{7,7},{8,8},{9,12},{10,1... | collective-permute-start | bytes 1179656 | tf_op jit(solution)/shard_map/ppermute | solution.py:768
  132.3 20.5 %collective-permute-start.12 = (bf16[768,256]{1,0:T(8,128)(2,1)S(1)}, bf16[768,256]{1,0:T(8,128)(2,1)S(1)}, u32[]{:S(2)}, u32[]{:S(2)}) collective-permute-start(bf16[768,256]{1,0:T(8,128)(2,1)S(1)} %get-tuple-element.156), channel_id=1, source_target_pairs={{0,2},{1,6},{2,0},{3,4},{4,3},{5,7},{6,1},{7,5},{8,10},{9,14},{10,... | collective-permute-start | bytes 1179656 | tf_op jit(solution)/shard_map/ppermute | solution.py:768
  133.1 19.7 %collective-permute-start.13 = (bf16[768,256]{1,0:T(8,128)(2,1)S(1)}, bf16[768,256]{1,0:T(8,128)(2,1)S(1)}, u32[]{:S(2)}, u32[]{:S(2)}) collective-permute-start(bf16[768,256]{1,0:T(8,128)(2,1)S(1)} %get-tuple-element.154), channel_id=1, source_target_pairs={{0,10},{1,14},{2,8},{3,12},{4,11},{5,15},{6,9},{7,13},{8,2},{9,6},... | collective-permute-start | bytes 1179656 | tf_op jit(solution)/shard_map/ppermute | solution.py:768
  164.5 19.4 %collective-permute-start.23 = (bf16[384,256]{1,0:T(8,128)(2,1)S(1)}, bf16[384,256]{1,0:T(8,128)(2,1)S(1)}, u32[]{:S(2)}, u32[]{:S(2)}) collective-permute-start(bf16[384,256]{1,0:T(8,128)(2,1)S(1)} %get-tuple-element.147), channel_id=1, source_target_pairs={{0,16},{1,17},{2,18},{3,19},{4,20},{5,21},{6,22},{7,23},{8,24},{9,... | collective-permute-start | bytes 589832 | tf_op jit(solution)/shard_map/ppermute | solution.py:895
  166.1 17.8 %collective-permute-start.24 = (bf16[384,256]{1,0:T(8,128)(2,1)S(1)}, bf16[384,256]{1,0:T(8,128)(2,1)S(1)}, u32[]{:S(2)}, u32[]{:S(2)}) collective-permute-start(bf16[384,256]{1,0:T(8,128)(2,1)S(1)} %get-tuple-element.149), channel_id=1, source_target_pairs={{0,2},{1,3},{2,0},{3,1},{4,6},{5,7},{6,4},{7,5},{8,10},{9,11},{10,... | collective-permute-start | bytes 589832 | tf_op jit(solution)/shard_map/ppermute | solution.py:895
  167.7 16.2 %collective-permute-start.25 = (bf16[384,256]{1,0:T(8,128)(2,1)S(1)}, bf16[384,256]{1,0:T(8,128)(2,1)S(1)}, u32[]{:S(2)}, u32[]{:S(2)}) collective-permute-start(bf16[384,256]{1,0:T(8,128)(2,1)S(1)} %get-tuple-element.148), channel_id=1, source_target_pairs={{0,18},{1,19},{2,16},{3,17},{4,22},{5,23},{6,20},{7,21},{8,26},{9,... | collective-permute-start | bytes 589832 | tf_op jit(solution)/shard_map/ppermute | solution.py:895
  176.7 29.8 %collective-permute-start.18 = (bf16[768,256]{1,0:T(8,128)(2,1)S(1)}, bf16[768,256]{1,0:T(8,128)(2,1)S(1)}, u32[]{:S(2)}, u32[]{:S(2)}) collective-permute-start(bf16[768,256]{1,0:T(8,128)(2,1)S(1)} %get-tuple-element.153), channel_id=1, source_target_pairs={{0,8},{1,12},{2,10},{3,14},{4,9},{5,13},{6,11},{7,15},{8,0},{9,4},... | collective-permute-start | bytes 1179656 | tf_op jit(solution)/shard_map/ppermute | solution.py:768
  178.3 35.0 %collective-permute-start.19 = (bf16[768,256]{1,0:T(8,128)(2,1)S(1)}, bf16[768,256]{1,0:T(8,128)(2,1)S(1)}, u32[]{:S(2)}, u32[]{:S(2)}) collective-permute-start(bf16[768,256]{1,0:T(8,128)(2,1)S(1)} %get-tuple-element.152), channel_id=1, source_target_pairs={{0,10},{1,14},{2,8},{3,12},{4,11},{5,15},{6,9},{7,13},{8,2},{9,6},... | collective-permute-start | bytes 1179656 | tf_op jit(solution)/shard_map/ppermute | solution.py:768
  187.7 28.3 %collective-permute-start.17 = (bf16[4,384,256]{2,1,0:T(8,128)(2,1)S(1)}, bf16[4,384,256]{2,1,0:T(8,128)(2,1)S(1)}, u32[]{:S(2)}, u32[]{:S(2)}) collective-permute-start(bf16[4,384,256]{2,1,0:T(8,128)(2,1)S(1)} %pad_maximum_fusion.3), channel_id=1, source_target_pairs={{0,1},{1,0},{2,3},{3,2},{4,5},{5,4},{6,7},{7,6},{8,9},{9,8},{10,11... | collective-permute-start | bytes 2359304 | tf_op jit(solution)/shard_map/ppermute | solution.py:773
  213.4 11.4 %collective-permute-start.21 = (bf16[768,256]{1,0:T(8,128)(2,1)S(1)}, bf16[768,256]{1,0:T(8,128)(2,1)S(1)}, u32[]{:S(2)}, u32[]{:S(2)}) collective-permute-start(bf16[768,256]{1,0:T(8,128)(2,1)S(1)} %get-tuple-element.150), channel_id=1, source_target_pairs={{0,2},{1,6},{2,0},{3,4},{4,3},{5,7},{6,1},{7,5},{8,10},{9,14},{10,... | collective-permute-start | bytes 1179656 | tf_op jit(solution)/shard_map/ppermute | solution.py:768
  215.2 9.6 %collective-permute-start.20 = (bf16[768,256]{1,0:T(8,128)(2,1)S(1)}, bf16[768,256]{1,0:T(8,128)(2,1)S(1)}, u32[]{:S(2)}, u32[]{:S(2)}) collective-permute-start(bf16[768,256]{1,0:T(8,128)(2,1)S(1)} %get-tuple-element.151), channel_id=1, source_target_pairs={{0,0},{1,4},{2,2},{3,6},{4,1},{5,5},{6,3},{7,7},{8,8},{9,12},{10,1... | collective-permute-start | bytes 1179656 | tf_op jit(solution)/shard_map/ppermute | solution.py:768
  235.7 16.4 %collective-permute-start.22 = (bf16[4,384,256]{2,1,0:T(8,128)(2,1)S(1)}, bf16[4,384,256]{2,1,0:T(8,128)(2,1)S(1)}, u32[]{:S(2)}, u32[]{:S(2)}) collective-permute-start(bf16[4,384,256]{2,1,0:T(8,128)(2,1)S(1)} %pad_maximum_fusion.4), channel_id=1, source_target_pairs={{0,1},{1,0},{2,3},{3,2},{4,5},{5,4},{6,7},{7,6},{8,9},{9,8},{10,11... | collective-permute-start | bytes 2359304 | tf_op jit(solution)/shard_map/ppermute | solution.py:773
  239.9 8.3 %collective-permute-start.36 = (bf16[448,256]{1,0:T(8,128)(2,1)S(1)}, bf16[448,256]{1,0:T(8,128)(2,1)S(1)}, u32[]{:S(2)}, u32[]{:S(2)}) collective-permute-start(bf16[448,256]{1,0:T(8,128)(2,1)S(1)} %get-tuple-element.184), channel_id=1, source_target_pairs={{0,16},{1,17},{2,18},{3,19},{4,20},{5,21},{6,22},{7,23},{8,24},{9,... | collective-permute-start | bytes 688136 | tf_op jit(solution)/shard_map/ppermute | solution.py:907
  241.4 10.4 %collective-permute-start.37 = (bf16[448,256]{1,0:T(8,128)(2,1)S(1)}, bf16[448,256]{1,0:T(8,128)(2,1)S(1)}, u32[]{:S(2)}, u32[]{:S(2)}) collective-permute-start(bf16[448,256]{1,0:T(8,128)(2,1)S(1)} %get-tuple-element.184), channel_id=1, source_target_pairs={{0,2},{1,3},{2,0},{3,1},{4,6},{5,7},{6,4},{7,5},{8,10},{9,11},{10,... | collective-permute-start | bytes 688136 | tf_op jit(solution)/shard_map/ppermute | solution.py:907
  241.9 9.9 %collective-permute-start.38 = (bf16[448,256]{1,0:T(8,128)(2,1)S(1)}, bf16[448,256]{1,0:T(8,128)(2,1)S(1)}, u32[]{:S(2)}, u32[]{:S(2)}) collective-permute-start(bf16[448,256]{1,0:T(8,128)(2,1)S(1)} %get-tuple-element.184), channel_id=1, source_target_pairs={{0,18},{1,19},{2,16},{3,17},{4,22},{5,23},{6,20},{7,21},{8,26},{9,... | collective-permute-start | bytes 688136 | tf_op jit(solution)/shard_map/ppermute | solution.py:907
  (52 other events, 574.1 us)

commit v3 on v2

--- a/solution.py
+++ b/solution.py
@@ -17,7 +17,7 @@
 TB = 512
 RES = 8
 UNROLL = 16
-VMEM_LIMIT = 56 * 1024 * 1024
+VMEM_LIMIT = 16 * 1024 * 1024
 
 
 def dot(left, right):
@@ -141,30 +141,54 @@
     return col_sum(jnp.where(pos < limit, rows * rows, 0.0))
 
 
-def gather_pieces(info, pieces, target, sems, want_low):
-    quarter = len(pieces) // 2
+def gather_pieces(info, pieces, target, sems, low):
     rows = pieces[0].shape[0]
 
     def each(act):
-        for t in range(quarter):
-            place = target.at[pl.ds((t ^ info[2]) * rows, rows)]
-            low, high = (t, t + quarter) if want_low else (t + quarter, t)
-
-            @pl.when(info[3] == 0)
+        for ty in range(2):
+            place = target.at[pl.ds((ty ^ info[4]) * rows, rows)]
+
+            @pl.when(info[5] == (0 if low else 1))
             def _():
-                act(pltpu.make_async_copy(pieces[low], place, sems.at[t]))
-
-            @pl.when(info[3] != 0)
+                act(pltpu.make_async_copy(pieces[ty], place, sems.at[ty]))
+
+            @pl.when(info[5] == (1 if low else 0))
             def _():
-                act(pltpu.make_async_copy(pieces[high], place, sems.at[t]))
+                act(pltpu.make_async_copy(pieces[2 + ty], place, sems.at[ty]))
 
     each(lambda c: c.start())
     each(lambda c: c.wait())
 
 
+def emit_messages(info, step, cross, local, low, high):
+    half = cross[0].shape[0]
+    lower = info[5] == 0
+    for sub in range(TB // 256):
+        rows = slice(sub * 256, (sub + 1) * 256)
+        number = step * (TB // 256) + sub
+        block = number // (half // 256)
+        at = pl.ds(pl.multiple_of((number - block * (half // 256)) * 256, 256), 256)
+        leaving = jnp.where(lower, high[rows], low[rows])
+        staying = jnp.where(lower, low[rows], high[rows])
+        for ty in range(2):
+
+            @pl.when((block ^ info[4]) == ty)
+            def _():
+                cross[ty][at] = leaving
+                local[ty][at] = staying
+
+
+def split_slab(info, slab, keep, send):
+    once = jnp.where(info[7] == 0, 1.0, 0.0)
+    half = keep.shape[0]
+    mine = info[8]
+    keep[...] = slab[pl.ds(pl.multiple_of(mine * half, 8), half)] * once
+    send[:half] = (slab[pl.ds(pl.multiple_of((1 - mine) * half, 8), half)] * once).astype(BF16)
+
+
 def first_kernel(info, *refs):
-    pieces = refs[:8]
-    gain, bias, w_mix, x_out, q_out, kv_out, sems = refs[8:]
+    pieces = refs[:4]
+    gain, bias, w_mix, x_out, q_out, kv_out, halo_out, sems = refs[4:]
     gather_pieces(info, pieces, x_out, sems, True)
     qw = q_out.shape[1]
 
@@ -178,6 +202,7 @@
         return 0
 
     lax.fori_loop(0, x_out.shape[0] // TB, block, 0)
+    halo_out[...] = kv_out[kv_out.shape[0] - WIN :]
 
 
 def load_extended(halo, kv, ext):
@@ -320,10 +345,10 @@
 def third_kernel(
     info, *refs,
 ):
-    pieces = refs[:8]
+    pieces = refs[:4]
     (q, kv, halo, o_far, lse_far, z, gain, bias, w_proj, w_in, w_back,
-     y_out, go_out, stat_out, gq_out, gk_out, gv_out, gmid_out, slab, d_gain, d_bias, squares,
-     ext, cot, sems) = refs[8:]
+     cross0, cross1, local0, local1, go_out, stat_out, gq_out, gk_out, gv_out, gmid_out, keep, send,
+     d_gain, d_bias, squares, ext, cot, slab, sems) = refs[4:]
     step = pl.program_id(0)
     qw = q.shape[1]
     n = kv.shape[0]
@@ -374,7 +399,7 @@
     active, slope = gelu_pair(dot(normed, w_in[...]))
     active = active.astype(BF16)
     feed = dot(active, w_back[...])
-    y_out[...] = (middle + feed).astype(BF16)
+    emit_messages(info, step, (cross0, cross1), (local0, local1), z[...], (middle + feed).astype(BF16))
     squares[0] += masked_squares(stream, base, limit)
     squares[1] += masked_squares(branch, base, limit)
     squares[2] += masked_squares(feed, base, limit)
@@ -400,6 +425,10 @@
         gq_out[rows] = gq
         gk_out[near] += gk
         gv_out[near] += gv
+
+    @pl.when(step == pl.num_programs(0) - 1)
+    def _():
+        split_slab(info, slab, keep, send)
 
 
 def pack_stats(lse, delta):
@@ -519,8 +548,8 @@
 def fourth_kernel(
     info, gq, gkv, got, z, gmid, gain_next, bias_next, w_mix_next,
     q, kv, halo, o, lse, active, slope, mid, gain, bias, w_proj, w_in, w_back,
-    gz_out, gq_out, gk_out, gv_out, gmid_out, slab, dn_gain, dn_bias, d_gain, d_bias,
-    ext,
+    gz_out, gq_out, gk_out, gv_out, gmid_out, halo_out, keep, send, dn_gain, dn_bias, d_gain, d_bias,
+    ext, slab,
 ):
     step = pl.program_id(0)
     qw = q.shape[1]
@@ -564,9 +593,17 @@
         gk_out[near] += g_k
         gv_out[near] += g_v
 
-
-def fifth_kernel(info, gq, gk, gv, got, x, gmid, gain, bias, w_mix, *rest):
-    gx_out, slab, d_gain, d_bias = rest[-4:]
+    @pl.when(step == pl.num_programs(0) - 1)
+    def _():
+        halo_out[...] = jnp.concatenate([gk_out[:WIN], gv_out[:WIN]], axis=1).astype(BF16)
+        split_slab(info, slab, keep, send)
+
+
+def fifth_kernel(
+    info, gq, gk, gv, got, x, gmid, gz, gain, bias, w_mix, *refs,
+):
+    vectors, squares = refs[:6], refs[6:8]
+    cross0, cross1, local0, local1, keep, send, small, slab, d_gain, d_bias = refs[8:]
     step = pl.program_id(0)
 
     @pl.when(step == 0)
@@ -582,39 +619,41 @@
     grad_x = mix_backward(
         gq[...], grad_kv, x[...].astype(F32), gain, bias, w_mix, slab, d_gain, d_bias, gmid[...]
     )
-    gx_out[...] = grad_x.astype(BF16)
+    emit_messages(info, step, (cross0, cross1), (local0, local1), grad_x.astype(BF16), gz[...])
+
+    @pl.when(step == pl.num_programs(0) - 1)
+    def _():
+        split_slab(info, slab, keep, send)
+        small_rows(info, (d_gain,) + vectors[:3] + (d_bias,) + vectors[3:], squares, small)
+        half = keep.shape[0]
+        count = small.shape[0]
+        coarse = small[...].astype(BF16)
+        send[half : half + count] = coarse
+        send[half + count :] = (small[...] - coarse.astype(F32)).astype(BF16)
 
 
 def assemble_kernel(info, *refs):
-    half = info[5]
+    own, other, out, wide, sems = refs[:4], *refs[4:]
     core = info[0]
-    own, other, out, narrow, wide, sem_in, sem_out = refs[:4], *refs[4:]
     rows = out.shape[1]
-    place = info[4]
-
-    def enter(t):
+
+    def leave(t):
+        column = core if t < 4 else 1 - core
+        image = (info[5] ^ (t % 4 // 2)) * 4 + column * 2 + (info[4] ^ (t % 2))
+        return pltpu.make_async_copy(wide.at[t], out.at[image], sems.at[t])
+
+    for t in range(8):
         if t < 4:
-            return pltpu.make_async_copy(own[t].at[pl.ds(core * rows, rows)], narrow.at[t], sem_in.at[t])
-        return pltpu.make_async_copy(other.at[t - 4], narrow.at[t], sem_in.at[t])
-
-    def leave(t):
-        tz, ty = (t % 4) // 2, t % 2
-        column = core if t < 4 else 1 - core
-        image = (half ^ tz) * 4 + column * 2 + (place ^ ty)
-        return pltpu.make_async_copy(wide.at[t], out.at[image], sem_out.at[t])
-
-    for t in range(8):
-        enter(t).start()
-    for t in range(8):
-        enter(t).wait()
-        wide[t] = narrow[t].astype(F32)
+            block = own[t][pl.ds(pl.multiple_of(core * rows, rows), rows)]
+        else:
+            block = other[t - 4]
+        wide[t] = block.astype(F32)
         leave(t).start()
     for t in range(8):
         leave(t).wait()
 
 
-def small_kernel(info, *refs):
-    vectors, (first, second, out) = refs[:8], refs[8:]
+def small_rows(info, vectors, squares, out):
     width = out.shape[1]
     once = jnp.where(info[7] == 0, 1.0, 0.0)
     lane = lax.broadcasted_iota(jnp.int32, (1, width), 1)
@@ -622,9 +661,15 @@
     for i, vector in enumerate(vectors):
         out[i : i + 1] = jnp.sum(vector[...], axis=0, keepdims=True) * once
     for i in range(6):
-        rows = (first if i < 3 else second)[i % 3]
-        total = jnp.sum(jnp.sum(rows, axis=0, keepdims=True), axis=1, keepdims=True)
+        total = jnp.sum(jnp.sum(squares[i // 3][i % 3], axis=0, keepdims=True), axis=1, keepdims=True)
         out[8 + i : 9 + i] = jnp.where(lane == info[6], total * once, 0.0)
+
+
+def trade_kernel(info, *refs):
+    pieces, out = refs[:4], refs[4]
+    rows = out.shape[1]
+    for t in range(4):
+        out[t] = pieces[t][pl.ds(pl.multiple_of((1 - info[0]) * rows, rows), rows)]
 
 
 def unpack_kernel(info, mine, theirs, small, mix, proj, up, down, gain, bias, wide, *, sizes):
@@ -666,12 +711,29 @@
             bias[layer, norm : norm + 1] = small[4 + 2 * layer + norm : 5 + 2 * layer + norm]
 
 
+VMEM = pl.BlockSpec(memory_space=pltpu.VMEM)
+
+
 def call(kernel, info, operands, specs, outs, out_specs, scratch=(), grid=(), work=0):
     moved = sum(math.prod(a.shape) * a.dtype.itemsize for a in list(operands) + jax.tree.leaves(outs))
+    single = not isinstance(outs, list)
+    views = list(specs) + ([out_specs] if single else list(out_specs))
+
+    def body_of(info, *refs):
+        seen = [view(ref) if callable(view) else ref for view, ref in zip(views, refs)]
+        kernel(info, *seen, *refs[len(views) :])
+
+    def plain(view):
+        return VMEM if callable(view) else view
+
     return pl.pallas_call(
-        kernel,
+        body_of,
         grid_spec=pltpu.PrefetchScalarGridSpec(
-            num_scalar_prefetch=1, grid=grid, in_specs=specs, out_specs=out_specs, scratch_shapes=list(scratch)
+            num_scalar_prefetch=1,
+            grid=grid,
+            in_specs=[plain(v) for v in specs],
+            out_specs=plain(out_specs) if single else [plain(v) for v in out_specs],
+            scratch_shapes=list(scratch),
         ),
         out_shape=outs,
         compiler_params=pltpu.CompilerParams(vmem_limit_bytes=VMEM_LIMIT),
@@ -680,12 +742,15 @@
 
 
 def whole(array):
-    zeros = (0,) * len(array.shape)
-    return pl.BlockSpec(array.shape, lambda *_: zeros)
+    return VMEM
 
 
 def tiled(array):
-    return pl.BlockSpec((TB, array.shape[1]), lambda i, *_: (i, 0))
+    return lambda ref: ref.at[pl.ds(pl.multiple_of(pl.program_id(0) * TB, TB), TB)]
+
+
+def last_rows(ref):
+    return ref.at[pl.ds(ref.shape[0] - WIN, WIN)]
 
 
 ANY = pl.BlockSpec(memory_space=pl.ANY)
@@ -722,54 +787,44 @@
         groups = [[s * rep + e for e in range(rep)] for s in range(seats)]
         edge_rows = lax.all_gather(edge_rows, "section", axis_index_groups=groups, axis=1, tiled=True)
 
-    def source_key(s):
-        return (s // images) * quarter + s % quarter, (s % images) // quarter
-
-    def source_seat(key, core):
-        return (key // quarter) * images + core * quarter + key % quarter
-
-    half = seat // images
-    my_key = half * quarter + seat % quarter
     chip = seat // 2
     part = seat % 2
+    fz, fl, fy = chip // 4, (chip // 2) % 2, chip % 2
     limit = lengths[chip]
     spot = lax.axis_index("dp") * images + chip
-    info = jnp.stack([part, limit, chip % quarter, chip // quarter, chip % 2, half, spot, twin]).astype(jnp.int32)
-
-    def scatter_route(t):
-        return route([(s, 2 * (source_key(s)[0] ^ t) + source_key(s)[1]) for s in range(seats)])
-
-    received = [None] * images
-    for t in list(range(quarter, images)) + list(range(quarter)):
-        piece = lax.dynamic_index_in_dim(edge_rows, my_key ^ t, 0, keepdims=False)
-        received[t] = lax.ppermute(piece, "section", scatter_route(t))
-
-    fz, fl, fy = chip // 4, (chip // 2) % 2, chip % 2
+    info = jnp.stack([part, limit, chip % quarter, fz, fy, fz, spot, twin, index % 2]).astype(jnp.int32)
     swap = route([(s, s ^ 1) for s in range(seats)])
 
-    def return_route(tz, ty):
+    def bits(s):
+        return s // 8, (s // 4) % 2, (s // 2) % 2, s % 2
+
+    by_column = edge_rows.reshape(2, 2, 2, rows_piece, width)
+    traded = lax.dynamic_index_in_dim(by_column, 1 - part, 1, keepdims=False).reshape(4, rows_piece, width)
+    traded = lax.ppermute(traded, "section", swap)
+    column = lax.dynamic_index_in_dim(by_column, part, 1, keepdims=False).reshape(4, rows_piece, width)
+    received = [None] * 4
+    for t in (2, 3, 0, 1):
+        tz, ty = t // 2, t % 2
+        image = (fz ^ tz) * 2 + (fy ^ ty)
+        own = lax.dynamic_index_in_dim(column, image, 0, keepdims=False)
+        got = lax.dynamic_index_in_dim(traded, image, 0, keepdims=False)
+        message = jnp.where(part == 0, jnp.concatenate([own, got]), jnp.concatenate([got, own]))
         pairs = []
         for s in range(seats):
-            z, l, y, p = s // 8, (s // 4) % 2, (s // 2) % 2, s % 2
+            z, l, y, k = bits(s)
+            pairs.append((s, ((z ^ tz) * 4 + k * 2 + (y ^ ty)) * 2 + l))
+        received[t] = lax.ppermute(message, "section", route(pairs))
+
+    def send_back(message, tz, ty):
+        pairs = []
+        for s in range(seats):
+            z, l, y, p = bits(s)
             pairs.append((s, ((z ^ tz) * 4 + p * 2 + (y ^ ty)) * 2 + l))
-        return route(pairs)
-
-    def send_back(low, high, which=(2, 3, 0, 1)):
-        low = low.reshape(2, 2 * rows_piece, width)
-        high = high.reshape(2, 2 * rows_piece, width)
-        out = []
-        for t in which:
-            tz, ty = t // 2, t % 2
-            piece = jnp.where(
-                (fz ^ tz) == 0,
-                lax.dynamic_index_in_dim(low, fy ^ ty, 0, keepdims=False),
-                lax.dynamic_index_in_dim(high, fy ^ ty, 0, keepdims=False),
-            )
-            out.append((t, lax.ppermute(piece, "section", return_route(tz, ty))))
-        return [piece for _, piece in sorted(out, key=lambda p: p[0])]
+        return lax.ppermute(message, "section", route(pairs))
 
     def trade(got):
-        send = jnp.stack([lax.dynamic_slice_in_dim(g, (1 - part) * rows_piece, rows_piece, 0) for g in got])
+        out = shape((4, rows_piece, width), BF16)
+        send = call(trade_kernel, info, got, [VMEM] * 4, out, whole(out))
         return lax.ppermute(send, "section", swap)
 
     first_to_second = route([(2 * c, 2 * c + 1) for c in range(images)])
@@ -786,22 +841,19 @@
     grad_v_shape = shape((n + WIN, width), F32)
     mix_rows = w_qkv.shape[1] * w_qkv.shape[2] // width
     feed_rows = (w_out[0].size + w_up[0].size + w_down[0].size) // width
-    feed_slab = shape((feed_rows, width), F32)
-    both_slab = shape((mix_rows + feed_rows, width), F32)
-    mix_slab = shape((mix_rows, width), F32)
     vec_shape = shape((8, width), F32)
     squares_shape = shape((3, 8, width), F32)
     ext = pltpu.VMEM((n + WIN, kvw), BF16)
 
     g0, g1, b0, b1 = norm_gain[0], norm_gain[1], norm_bias[0], norm_bias[1]
 
-    outs = [rows_low, rows_q, rows_kv]
-    x, q0, kv0 = call(
-        first_kernel, info, received + [g0, b0, w_qkv[0]],
-        [ANY] * images + [whole(g0), whole(b0), whole(w_qkv[0])],
-        outs, [whole(o) for o in outs], [dma((quarter,))], work=6,
-    )
-    halo0 = lax.ppermute(kv0[n - WIN :], "section", first_to_second)
+    halo_shape = shape((WIN, kvw), BF16)
+    outs = [rows_low, rows_q, rows_kv, halo_shape]
+    x, q0, kv0, halo0 = call(
+        first_kernel, info, received + [g0, b0, w_qkv[0]], [ANY] * 4 + [whole(g0), whole(b0), whole(w_qkv[0])],
+        outs, [whole(o) for o in outs], [dma((2,))], work=6,
+    )
+    halo0 = lax.ppermute(halo0, "section", first_to_second)
 
     outs = [rows_low, rows_q, rows_kv, rows_low, rows_stat, rows_hidden, rows_hidden, rows_wide, squares_shape]
     z, q1, kv1, o0, lse0, active0, slope0, mid0, squares0 = call(
@@ -821,19 +873,24 @@
          pltpu.VMEM((HEADS, n, 128), F32), pltpu.VMEM((n, 128), F32)], work=14,
     )
 
-    halo1 = kv_other[n - WIN :]
-    outs = [rows_low, rows_low, rows_stat, shape((n, qw), F32), grad_k_shape, grad_v_shape, rows_wide,
-            feed_slab, vec_shape, vec_shape, squares_shape]
-    (y1, go1, stat1, gq_near, gk_near, gv_near, gmid1, slab_a, d_gain11, d_bias11, squares1) = call(
+    message = shape((2 * rows_piece, width), BF16)
+    outs = [message] * 4 + [rows_low, rows_stat, shape((n, qw), F32), grad_k_shape, grad_v_shape, rows_wide,
+            shape((feed_rows // 2, width), F32), shape((feed_rows // 2, width), BF16),
+            vec_shape, vec_shape, squares_shape]
+    (cross0, cross1, local0, local1, go1, stat1, gq_near, gk_near, gv_near, gmid1, keep_a, send_a,
+     d_gain11, d_bias11, squares1) = call(
         third_kernel, info,
-        received + [q1, kv1, halo1, o_far, lse_far, z, g1, b1, w_out[1], w_up[1], w_down[1]],
-        [ANY] * images + [tiled(q1), whole(kv1), whole(halo1), tiled(o_far), tiled(lse_far), tiled(z)]
+        received + [q1, kv1, kv_other, o_far, lse_far, z, g1, b1, w_out[1], w_up[1], w_down[1]],
+        [ANY] * 4
+        + [tiled(q1), whole(kv1), last_rows]
+        + [tiled(o_far), tiled(lse_far), tiled(z)]
         + [whole(a) for a in (g1, b1, w_out[1], w_up[1], w_down[1])],
         outs,
-        [tiled(o) for o in outs[:4]] + [whole(outs[4]), whole(outs[5]), tiled(outs[6])] + [whole(o) for o in outs[7:]],
-        [ext, pltpu.VMEM((n, width), BF16), dma((quarter,))], steps, work=24,
-    )
-    second_way = send_back(z, y1, (2,))
+        [whole(message)] * 4 + [tiled(o) for o in outs[4:7]] + [whole(outs[7]), whole(outs[8]), tiled(outs[9])]
+        + [whole(o) for o in outs[10:]],
+        [ext, pltpu.VMEM((n, width), BF16), pltpu.VMEM((feed_rows, width), F32), dma((2,))], steps, work=24,
+    )
+    forward_back = [None, None, send_back(cross0, 1, 0), None]
 
     outs = [shape((n, qw), F32), shape((n, kvw), F32), rows_kv]
     operands = [qr, kr, vr, go1, stat1, gq_near, gk_near, gv_near]
@@ -842,13 +899,16 @@
         [pltpu.VMEM((HEADS, n, 128), F32), pltpu.VMEM((n, 128), F32), pltpu.VMEM((n, qw), F32),
          pltpu.VMEM((2 * n, qw), F32), pltpu.VMEM((HEADS, 2 * n, 128), F32)], work=18,
     )
-    gkv_got = lax.ppermute(after(gkv_send, *second_way), "section", second_to_first)
-    first_way, other_way, third_way = send_back(after(z, *second_way), y1, (3, 0, 1))
-    forward_back = [first_way, other_way, *second_way, third_way]
-
-    outs = [rows_low, shape((n, qw), F32), grad_k_shape, grad_v_shape, rows_wide,
-            both_slab, vec_shape, vec_shape, vec_shape, vec_shape]
-    (gz, gq0, gk0, gv0, gmid0, slab_b, d_gain10, d_bias10, d_gain01, d_bias01) = call(
+    gkv_got = lax.ppermute(after(gkv_send, forward_back[2]), "section", second_to_first)
+    forward_back[3] = send_back(after(cross1, forward_back[2]), 1, 1)
+    forward_back[0] = send_back(after(local0, forward_back[2]), 0, 0)
+    forward_back[1] = send_back(after(local1, forward_back[2]), 0, 1)
+
+    slab_rows = mix_rows + feed_rows
+    outs = [rows_low, shape((n, qw), F32), grad_k_shape, grad_v_shape, rows_wide, halo_shape,
+            shape((slab_rows // 2, width), F32), shape((slab_rows // 2, width), BF16),
+            vec_shape, vec_shape, vec_shape, vec_shape]
+    (gz, gq0, gk0, gv0, gmid0, halo_send, keep_b, send_b, d_gain10, d_bias10, d_gain01, d_bias01) = call(
         fourth_kernel, info,
         [gq1, gkv1, gkv_got, z, gmid1, g1, b1, w_qkv[1], q0, kv0, halo0, o0, lse0, active0, slope0, mid0, g0, b0,
          w_out[0], w_up[0], w_down[0]],
@@ -857,13 +917,11 @@
         + [whole(a) for a in (g0, b0, w_out[0], w_up[0], w_down[0])],
         outs,
         [tiled(outs[0]), tiled(outs[1]), whole(outs[2]), whole(outs[3]), tiled(outs[4])] + [whole(o) for o in outs[5:]],
-        [ext], steps, work=20,
-    )
-    gk0, gv0, slab_b = after((gk0, gv0, slab_b), *forward_back)
-    halo_send = jnp.concatenate([gk0[:WIN], gv0[:WIN]], axis=1).astype(BF16)
+        [ext, pltpu.VMEM((slab_rows, width), F32)], steps, work=20,
+    )
+    halo_send, send_b = after((halo_send, send_b), *forward_back)
     halo_got = lax.ppermute(halo_send, "section", second_to_first)
 
-    once = (twin == 0).astype(F32)
     dp_count = lax.axis_size("dp")
     dp_index = lax.axis_index("dp")
 
@@ -910,59 +968,84 @@
             [lax.dynamic_index_in_dim(stacked, digit ^ j, 0, keepdims=False) for j in range(len(pieces))]
         )
 
+    def pair(message):
+        return lax.ppermute(message, ("dp", "section"), partners([1])[1][0][1])
+
+    def riders_of(vectors):
+        coarse = vectors.astype(BF16)
+        return [coarse, (vectors - coarse.astype(F32)).astype(BF16)]
+
+    def ridden(rest):
+        rest = rest.astype(F32)
+        return rest[: rest.shape[0] // 2] + rest[rest.shape[0] // 2 :]
+
+    def exchange(rows, masks, vectors):
+        rows = rows.astype(BF16)
+        count = rows.shape[0]
+        riders = riders_of(vectors)
+        got = lax.ppermute(jnp.concatenate([rows] + riders), ("dp", "section"), partners(masks)[1][0][1])
+        rows = (rows.astype(F32) + got[:count].astype(F32)).astype(BF16)
+        return rows, ridden(jnp.concatenate(riders)) + ridden(got[count:])
+
     dp_masks = [sections << b for b in range(dp_count.bit_length() - 1)]
     section_masks = [1 << b for b in range(1, sections.bit_length() - 1)]
     plane = [dp_masks[0], section_masks[0]]
     rest = section_masks[1:] + dp_masks[1:]
-    rest = [rest[i : i + 2] for i in range(0, len(rest), 2)]
-    early = scatter([slab_a * once, slab_b * once] if rep > 1 else [slab_a, slab_b], [1])
+    got_early = pair(jnp.concatenate([send_a, send_b]))
+    early = jnp.concatenate([keep_a, keep_b]) + got_early.astype(F32)
     gq0 = after(gq0, early)
     early = scatter([early], plane)
 
-    outs = [rows_low, mix_slab, vec_shape, vec_shape]
-    gx, slab_c, d_gain00, d_bias00 = call(
-        fifth_kernel, info, [gq0, gk0, gv0, halo_got, x, gmid0, g0, b0, w_qkv[0]],
-        [tiled(gq0), whole(gk0), whole(gv0), whole(halo_got), tiled(x), tiled(gmid0), whole(g0), whole(b0), whole(w_qkv[0])],
-        outs, [tiled(outs[0])] + [whole(o) for o in outs[1:]], (), steps, work=8,
-    )
-    forward_trade = trade(after(forward_back, gx))
-
-    operands = [d_gain00, d_gain01, d_gain10, d_gain11, d_bias00, d_bias01, d_bias10, d_bias11, squares0, squares1]
     small_shape = shape((16, width), F32)
-    small = call(small_kernel, info, operands, [whole(a) for a in operands], small_shape, whole(small_shape))
+    outs = [message] * 4 + [shape((mix_rows // 2, width), F32),
+            shape((mix_rows // 2 + 2 * small_shape.shape[0], width), BF16), small_shape]
+    operands = [gq0, gk0, gv0, halo_got, x, gmid0, gz, g0, b0, w_qkv[0]]
+    partial = [d_gain01, d_gain10, d_gain11, d_bias01, d_bias10, d_bias11, squares0, squares1]
+    cross0, cross1, local0, local1, late, send_c, small = call(
+        fifth_kernel, info, operands + partial,
+        [tiled(gq0), whole(gk0), whole(gv0), whole(halo_got), tiled(x), tiled(gmid0), tiled(gz)]
+        + [whole(a) for a in operands[7:] + partial],
+        outs, [whole(o) for o in outs],
+        [pltpu.VMEM((mix_rows, width), F32), pltpu.VMEM((8, width), F32), pltpu.VMEM((8, width), F32)], steps, work=8,
+    )
 
     def assemble(own, other):
         out = call(
-            assemble_kernel, info, own + [other], [ANY] * 5, shape((images, rows_piece, width), F32), ANY,
-            [pltpu.VMEM((images, rows_piece, width), BF16), pltpu.VMEM((images, rows_piece, width), F32),
-             dma((images,)), dma((images,))],
+            assemble_kernel, info, own + [other], [VMEM] * 5, shape((images, rows_piece, width), F32), ANY,
+            [pltpu.VMEM((images, rows_piece, width), F32), dma((images,))],
         )
         if rep > 1:
             out = lax.dynamic_slice_in_dim(out, twin * rows_dev, rows_dev, 1)
         return out
 
-    crossing = send_back(gx, gz, (2, 3))
-    late, small = scatter([after(slab_c * once if rep > 1 else slab_c, early)], [1], small)
+    backward_back = [send_back(local0, 0, 0), None, send_back(cross0, 1, 0), None]
+    got_late = pair(after(send_c, early))
+    late_rows = late.shape[0]
+    late = late + got_late[:late_rows].astype(F32)
+    small = small + ridden(got_late[late_rows:])
     late, small = scatter([late], plane, small)
     early_rows = early.shape[0]
+    forward_trade = trade(after(forward_back, late))
     forward_rows = assemble(forward_back, forward_trade)
-    both, _ = after((jnp.concatenate([early, late]), forward_rows), *crossing)
-    staying = send_back(after(gx, *crossing), gz, (0, 1))
-    for masks in rest:
-        both, small = scatter([both], masks, small)
-    both = both.astype(BF16)
-    for masks in rest[::-1]:
-        both = gather(both, masks)
-    backward_back = staying + crossing
+    both = after(jnp.concatenate([early, late]), backward_back[0], backward_back[2])
+    backward_back[3] = send_back(after(cross1, backward_back[2]), 1, 1)
+    backward_back[1] = send_back(after(local1, backward_back[2]), 0, 1)
+    for mask in rest[:-1]:
+        both, small = scatter([both], [mask], small)
+    both = after(both, forward_rows)
+    both, small = exchange(both, rest[-1:], small)
+    for mask in rest[-2::-1]:
+        both = gather(both, [mask])
+    both = after(both, backward_back[1], backward_back[3])
+    both = gather(both, plane)
     backward_trade = trade(backward_back)
-    both = gather(both, plane)
+    both = after(both, backward_trade)
+    theirs = pair(both)
     backward_rows = assemble(backward_back, backward_trade)
-    both = after(both, backward_rows)
-    (theirs,) = (lax.ppermute(both, ("dp", "section"), way) for _, way in partners([1])[1])
     sums = lax.dynamic_slice_in_dim(small[8:14], dp_index * images, images, 1)
     rms_values = jnp.sqrt(sums / (lengths.astype(F32)[None, :] * width))
     outs = [shape(w.shape, F32) for w in (w_qkv, w_out, w_up, w_down, norm_gain, norm_bias)]
-    sizes = (slab_a.shape[0], slab_b.shape[0], slab_c.shape[0], 1 << len(plane))
+    sizes = (feed_rows, slab_rows, mix_rows, 1 << len(plane))
     grads = call(
         functools.partial(unpack_kernel, sizes=sizes), jnp.stack([index % 2]).astype(jnp.int32), [both, theirs, small],
         [whole(both), whole(theirs), whole(small)], outs, [whole(o) for o in outs],

time: 265 us -> 232 us (0.88)
  waiting for transfers between devices: 65.4 us -> 100 us
  Pallas kernels: 97.6 us -> 65.8 us
  starting transfers between devices: 70.9 us -> 39.5 us
  local copies, waits for them, and re-layouts: 21.1 us -> 12.1 us
  other arithmetic: 6.93 us -> 11.8 us
    ppermute x19, waiting for transfers between devices: 36.2 us -> 80.3 us  [the longest x4 33.2 us: body(): received[t] = lax.ppermute(message, 'section', route(pairs))]
    pallas_call x11 -> x12, Pallas kernels: 97.6 us -> 65.8 us  [call(): pl.pallas_call(body_of, grid_spec=pltpu.PrefetchScalarGridSpec(num_scalar...]
    ppermute x19, starting transfers between devices: 44.3 us -> 23.3 us  [the longest x8 12.1 us: send_back(): return lax.ppermute(message, 'section', route(pairs))]
    ppermute x11 -> x7, waiting for transfers between devices: 14.2 us -> 7.43 us  [scatter(): lax.ppermute(jnp.concatenate([chunk(slabs, digit ^ c, ways).astype(BF16)]...]
    ppermute x11 -> x7, starting transfers between devices: 14.8 us -> 8.62 us  [scatter(): lax.ppermute(jnp.concatenate([chunk(slabs, digit ^ c, ways).astype(BF16)]...]
    ppermute x6 -> x4, starting transfers between devices: 8.01 us -> 3.62 us  [gather(): lax.ppermute(piece, ('dp', 'section'), way)]
    another operation x11 -> x1, local copies, waits for them, and re-layouts: 4.12 us -> 0.73 us  [body(): jnp.stack([part, limit, chip % quarter, fz, fy, fz, spot, twin, index % 2])]
    slice x4 -> x0, local copies, waits for them, and re-layouts: 3.34 us -> none  [the longest x2 1.76 us: body(): halo_send = jnp.concatenate([gk0[:WIN], gv0[:WIN]], axis=1).astype(BF16)]
  transfers between devices with their start and end apart: 40 -> 34, of which waited for: 18 -> 17; matrix products, arithmetic and copies ran while one was open for 6% -> 4% of each run, Pallas kernels for 16% -> 12%
where the time goes in v3:
time: 232 us; the launch traced here: 231 us
  waiting for transfers between devices  100 us (43%)
  Pallas kernels  65.8 us (28%)
  starting transfers between devices  39.5 us (17%)
  local copies, waits for them, and re-layouts  12.1 us (5%)
  other arithmetic  11.8 us (5%)
    pallas_call x12, Pallas kernels, call(): pl.pallas_call(body_of, grid_spec=pltpu.PrefetchScalarGridSpec(num_scalar...  65.8 us
    ppermute x4, waiting for transfers between devices, body(): received[t] = lax.ppermute(message, 'section', route(pairs))  33.2 us
    ppermute x8, waiting for transfers between devices, send_back(): return lax.ppermute(message, 'section', route(pairs))  28.9 us
    ppermute x1, waiting for transfers between devices, exchange(): lax.ppermute(jnp.concatenate([rows] + riders), ('dp', 'section'), partner...  12.8 us
    ppermute x8, starting transfers between devices, send_back(): return lax.ppermute(message, 'section', route(pairs))  12.1 us
    ppermute x4, waiting for transfers between devices, gather(): lax.ppermute(piece, ('dp', 'section'), way)  10.5 us
    unnamed x66, local copies, waits for them, and re-layouts  8.89 us
    ppermute x7, starting transfers between devices, scatter(): lax.ppermute(jnp.concatenate([chunk(slabs, digit ^ c, ways).astype(BF16)]...  8.62 us
  transfers between devices with their start and end apart: 34, of which 17 were waited for; matrix products, arithmetic and copies ran while one was open for 4% of the time, Pallas kernels for 12%

profile of v3, /device:TPU:0, one launch (start us, length us, event | category | flops | bytes accessed | tf_op | source)
XLA Modules:
  0.0 231.2 jit_solution(13643554946153239923)
XLA Ops:
  4.9 5.0 %collective-permute-start.4 = (bf16[768,256]{1,0:T(8,128)(2,1)S(1)}, bf16[768,256]{1,0:T(8,128)(2,1)S(1)}, u32[]{:S(2)}, u32[]{:S(2)}) collective-permute-start(bf16[768,256]{1,0:T(8,128)(2,1)S(1)} %maximum_select_fusion.3), channel_id=1, source_target_pairs={{0,10},{1,14},{2,8},{3,12},{4,11},{5,15},{6,9},{7,13},{8,2},{9,6},... | collective-permute-start | bytes 1179656 | tf_op jit(solution)/shard_map/ppermute | solution.py:816
  11.8 24.9 %collective-permute-done.4.refs_3_ = bf16[768,256]{1,0:T(8,128)(2,1)S(1)} collective-permute-done((bf16[768,256]{1,0:T(8,128)(2,1)S(1)}, bf16[768,256]{1,0:T(8,128)(2,1)S(1)}, u32[]{:S(2)}, u32[]{:S(2)}) %collective-permute-start.4) | collective-permute-done | bytes 393248 | tf_op jit(solution)/shard_map/ppermute | solution.py:816
  36.7 8.3 %collective-permute-done.3.refs_2_ = bf16[768,256]{1,0:T(8,128)(2,1)S(1)} collective-permute-done((bf16[768,256]{1,0:T(8,128)(2,1)S(1)}, bf16[768,256]{1,0:T(8,128)(2,1)S(1)}, u32[]{:S(2)}, u32[]{:S(2)}) %collective-permute-start.3) | collective-permute-done | bytes 393248 | tf_op jit(solution)/shard_map/ppermute | solution.py:816
  45.0 2.6 %shard_map.151 = (bf16[1536,256]{1,0:T(8,128)(2,1)S(1)}, bf16[1536,128]{1,0:T(8,128)(2,1)S(1)}, bf16[1536,384]{1,0:T(8,128)(2,1)S(1)}, bf16[128,384]{1,0:T(8,128)(2,1)S(1)}) custom-call(s32[9]{0:T(128)S(1)} %stack.51.info, bf16[768,256]{1,0:T(8,128)(2,1)S(1)} %collective-permute-done.1.refs_0_, bf16[768,256]{1,0:T(8,128)(2,1)S(1)} %collective-permute-done.2.refs_1_, ...), custom_call_target="tpu_custom_call" | custom-call | flops 6899999744 | bytes 4296704 | tf_op jit(solution)/shard_map/pallas_call | solution.py:729
  49.8 8.2 %shard_map.152 = (bf16[1536,256]{1,0:T(8,128)(2,1)S(1)}, bf16[1536,128]{1,0:T(8,128)(2,1)S(1)}, bf16[1536,384]{1,0:T(8,128)(2,1)S(1)}, bf16[1536,256]{1,0:T(8,12...) custom-call(s32[9]{0:T(128)S(1)} %stack.51.info, ...), custom_call_target="tpu_custom_call" | custom-call | flops 17250000896 | bytes 12058624 | tf_op jit(solution)/shard_map/pallas_call | solution.py:729
  58.0 2.5 %collective-permute-start.6 = (bf16[1536,384]{1,0:T(8,128)(2,1)S(1)}, bf16[1536,384]{1,0:T(8,128)(2,1)S(1)}, u32[]{:S(2)}, u32[]{:S(2)}) collective-permute-start(bf16[1536,384]{1,0:T(8,128)(2,1)S(1)} %get-tuple-element.93.refs_1_.refs_5_), channel_id=1, source_target_pairs={{0,1},{2,3},{4,5},{6,7},{8,9},{10,11},{12,13},{14,15},{16,17},{18,... | collective-permute-start | bytes 3538952 | tf_op jit(solution)/shard_map/ppermute | solution.py:864
  60.6 2.2 collective-permute-done.6.refs_2_.refs_6_
  62.8 4.1 %shard_map.153 = (bf16[1536,128]{1,0:T(8,128)(2,1)S(1)}, bf16[3072,128]{1,0:T(8,128)(2,1)S(1)}, bf16[3072,256]{1,0:T(8,128)(2,1)S(1)}, f32[1536,256]{1,0:T(8,128)S(1)}, f32[1536,128]{1,0:T(8,128)S(1)}) custom-call(s32[9]{0:T(128)S(1)} %stack.51.info, bf16[1536,128]{1,0:T(8,128)(2,1)S(1)} %get-tuple-element.92.refs_0_.refs_4_, ...), custom_call_target="tpu_custom_call" | custom-call | flops 16099999744 | bytes 7864320 | tf_op jit(solution)/shard_map/pallas_call | solution.py:729
  66.8 17.3 %shard_map.154 = (bf16[768,256]{1,0:T(8,128)(2,1)S(1)}, bf16[768,256]{1,0:T(8,128)(2,1)S(1)}, bf16[768,256]{1,0:T(8,128)(2,1)S(1)}, bf16[768,256]{1,0:T(8,128)(2...) custom-call(s32[9]{0:T(128)S(1)} %stack.51.info, ...), custom_call_target="tpu_custom_call" | custom-call | flops 27599998976 | bytes 17215488 | tf_op jit(solution)/shard_map/pallas_call | solution.py:729
  86.2 8.0 %shard_map.155 = (f32[1536,128]{1,0:T(8,128)S(1)}, f32[1536,384]{1,0:T(8,128)S(1)}, bf16[1536,384]{1,0:T(8,128)(2,1)S(1)}) custom-call(s32[9]{0:T(128)S(1)} %stack.51.info, bf16[1536,128]{1,0:T(8,128)(2,1)S(1)} %get-tuple-element.104.refs_0_, bf16[3072,128]{1,0:T(8,128)(2,1)S(1)} %get-tuple-element.105.refs_1_, ...), custom_call_target="tpu_custom_call" | custom-call | flops 20700000256 | bytes 11993088 | tf_op jit(solution)/shard_map/pallas_call | solution.py:729
  94.2 10.1 %collective-permute-done.7.refs_2_ = bf16[768,256]{1,0:T(8,128)(2,1)S(1)} collective-permute-done((bf16[768,256]{1,0:T(8,128)(2,1)S(1)}, bf16[768,256]{1,0:T(8,128)(2,1)S(1)}, u32[]{:S(2)}, u32[]{:S(2)}) %collective-permute-start.7) | collective-permute-done | bytes 393248 | tf_op jit(solution)/shard_map/ppermute | solution.py:823
  109.0 12.1 %shard_map.156 = (bf16[1536,256]{1,0:T(8,128)(2,1)S(1)}, f32[1536,128]{1,0:T(8,128)S(1)}, f32[1664,128]{1,0:T(8,128)S(1)}, f32[1664,256]{1,0:T(8,128)S(1)}, f32[...) custom-call(s32[9]{0:T(128)S(1)} %stack.51.info, ...), custom_call_target="tpu_custom_call" | custom-call | flops 23000000512 | bytes 22781952 | tf_op jit(solution)/shard_map/pallas_call | solution.py:729
  140.1 4.5 %shard_map.157 = (bf16[768,256]{1,0:T(8,128)(2,1)S(1)}, bf16[768,256]{1,0:T(8,128)(2,1)}, bf16[768,256]{1,0:T(8,128)(2,1)S(1)}, bf16[768,256]{1,0:T(8,128)(2,1)}...) custom-call(s32[9]{0:T(128)S(1)} %stack.51.info, f32[1536,128]{1,0:T(8,128)S(1)} %copy-done.11, ...), custom_call_target="tpu_custom_call" | custom-call | flops 9200000000 | bytes 8949760 | tf_op jit(solution)/shard_map/pallas_call | solution.py:729
  144.7 2.2 collective-permute-done.15
  154.0 3.0 %collective-permute-start.23 = (bf16[768,256]{1,0:T(8,128)(2,1)S(1)}, bf16[768,256]{1,0:T(8,128)(2,1)S(1)}, u32[]{:S(2)}, u32[]{:S(2)}) collective-permute-start(bf16[768,256]{1,0:T(8,128)(2,1)S(1)} %get-tuple-element.153), channel_id=1, source_target_pairs={{0,8},{1,12},{2,10},{3,14},{4,9},{5,13},{6,11},{7,15},{8,0},{9,4},... | collective-permute-start | bytes 1179656 | tf_op jit(solution)/shard_map/ppermute | solution.py:823
  163.8 10.9 %collective-permute-done.23.refs_2_ = bf16[768,256]{1,0:T(8,128)(2,1)S(1)} collective-permute-done((bf16[768,256]{1,0:T(8,128)(2,1)S(1)}, bf16[768,256]{1,0:T(8,128)(2,1)S(1)}, u32[]{:S(2)}, u32[]{:S(2)}) %collective-permute-start.23) | collective-permute-done | bytes 393248 | tf_op jit(solution)/shard_map/ppermute | solution.py:823
  176.7 3.1 %collective-permute-done.27 = bf16[256,256]{1,0:T(8,128)(2,1)S(1)} collective-permute-done((bf16[256,256]{1,0:T(8,128)(2,1)S(1)}, bf16[256,256]{1,0:T(8,128)(2,1)S(1)}, u32[]{:S(2)}, u32[]{:S(2)}) %collective-permute-start.27) | collective-permute-done | bytes 131104 | tf_op jit(solution)/shard_map/ppermute | solution.py:953
  180.8 3.4 %shard_map.159 = f32[8,384,256]{2,1,0:T(8,128)} custom-call(s32[9]{0:T(128)S(1)} %stack.51.info, bf16[768,256]{1,0:T(8,128)(2,1)S(1)} %collective-permute-done.8.refs_0_, bf16[768,256]{1,0:T(8,128)(2,1)S(1)} %collective-permute-done.9.refs_1_, bf16[768,256]{1,0:T(8,128)(2,1)S(1)} %collective-permute-done.7.refs_2_, ...), custom_call_target="tpu_custom_call" | custom-call | bytes 5505024 | tf_op jit(solution)/shard_map/pallas_call | solution.py:729
  184.4 4.0 %collective-permute-start.25 = (bf16[768,256]{1,0:T(8,128)(2,1)}, bf16[768,256]{1,0:T(8,128)(2,1)S(1)}, u32[]{:S(2)}, u32[]{:S(2)}) collective-permute-start(bf16[768,256]{1,0:T(8,128)(2,1)} %get-tuple-element.156), channel_id=1, source_target_pairs={{0,10},{1,14},{2,8},{3,12},{4,11},{5,15},{6,9},{7,13},{8,2},{9,6},... | collective-permute-start | bytes 1179656 | tf_op jit(solution)/shard_map/ppermute | solution.py:823
  188.8 12.8 %collective-permute-done.28 = bf16[256,256]{1,0:T(8,128)(2,1)S(1)} collective-permute-done((bf16[256,256]{1,0:T(8,128)(2,1)S(1)}, bf16[256,256]{1,0:T(8,128)(2,1)S(1)}, u32[]{:S(2)}, u32[]{:S(2)}) %collective-permute-start.28) | collective-permute-done | bytes 131104 | tf_op jit(solution)/shard_map/ppermute | solution.py:986
  201.7 7.9 %collective-permute-done.25.refs_3_ = bf16[768,256]{1,0:T(8,128)(2,1)S(1)} collective-permute-done((bf16[768,256]{1,0:T(8,128)(2,1)}, bf16[768,256]{1,0:T(8,128)(2,1)S(1)}, u32[]{:S(2)}, u32[]{:S(2)}) %collective-permute-start.25) | collective-permute-done | bytes 393248 | tf_op jit(solution)/shard_map/ppermute | solution.py:823
  214.0 5.0 %collective-permute-done.30 = bf16[448,256]{1,0:T(8,128)(2,1)} collective-permute-done((bf16[448,256]{1,0:T(8,128)(2,1)S(1)}, bf16[448,256]{1,0:T(8,128)(2,1)}, u32[]{:S(2)}, u32[]{:S(2)}) %collective-permute-start.30) | collective-permute-done | bytes 229408 | tf_op jit(solution)/shard_map/ppermute | solution.py:965
  219.0 5.5 %collective-permute-done.31 = bf16[448,256]{1,0:T(8,128)(2,1)} collective-permute-done((bf16[448,256]{1,0:T(8,128)(2,1)S(1)}, bf16[448,256]{1,0:T(8,128)(2,1)}, u32[]{:S(2)}, u32[]{:S(2)}) %collective-permute-start.31) | collective-permute-done | bytes 229408 | tf_op jit(solution)/shard_map/ppermute | solution.py:965
  226.7 2.3 shard_map.161
  (169 shorter events, 59.8 us)
Async XLA Ops:
  4.9 31.8 %collective-permute-start.4 = (bf16[768,256]{1,0:T(8,128)(2,1)S(1)}, bf16[768,256]{1,0:T(8,128)(2,1)S(1)}, u32[]{:S(2)}, u32[]{:S(2)}) collective-permute-start(bf16[768,256]{1,0:T(8,128)(2,1)S(1)} %maximum_select_fusion.3), channel_id=1, source_target_pairs={{0,10},{1,14},{2,8},{3,12},{4,11},{5,15},{6,9},{7,13},{8,2},{9,6},... | collective-permute-start | bytes 1179656 | tf_op jit(solution)/shard_map/ppermute | solution.py:816
  10.0 35.0 %collective-permute-start.3 = (bf16[768,256]{1,0:T(8,128)(2,1)S(1)}, bf16[768,256]{1,0:T(8,128)(2,1)S(1)}, u32[]{:S(2)}, u32[]{:S(2)}) collective-permute-start(bf16[768,256]{1,0:T(8,128)(2,1)S(1)} %maximum_select_fusion.2), channel_id=1, source_target_pairs={{0,8},{1,12},{2,10},{3,14},{4,9},{5,13},{6,11},{7,15},{8,0},{9,4},... | collective-permute-start | bytes 1179656 | tf_op jit(solution)/shard_map/ppermute | solution.py:816
  10.6 34.4 %collective-permute-start.2 = (bf16[768,256]{1,0:T(8,128)(2,1)S(1)}, bf16[768,256]{1,0:T(8,128)(2,1)S(1)}, u32[]{:S(2)}, u32[]{:S(2)}) collective-permute-start(bf16[768,256]{1,0:T(8,128)(2,1)S(1)} %maximum_select_fusion.1), channel_id=1, source_target_pairs={{0,2},{1,6},{2,0},{3,4},{4,3},{5,7},{6,1},{7,5},{8,10},{9,14},{10,... | collective-permute-start | bytes 1179656 | tf_op jit(solution)/shard_map/ppermute | solution.py:816
  11.0 33.9 %collective-permute-start.1 = (bf16[768,256]{1,0:T(8,128)(2,1)S(1)}, bf16[768,256]{1,0:T(8,128)(2,1)S(1)}, u32[]{:S(2)}, u32[]{:S(2)}) collective-permute-start(bf16[768,256]{1,0:T(8,128)(2,1)S(1)} %maximum_select_fusion), channel_id=1, source_target_pairs={{0,0},{1,4},{2,2},{3,6},{4,1},{5,5},{6,3},{7,7},{8,8},{9,12},{10,1... | collective-permute-start | bytes 1179656 | tf_op jit(solution)/shard_map/ppermute | solution.py:816
  84.2 20.1 %collective-permute-start.7 = (bf16[768,256]{1,0:T(8,128)(2,1)S(1)}, bf16[768,256]{1,0:T(8,128)(2,1)S(1)}, u32[]{:S(2)}, u32[]{:S(2)}) collective-permute-start(bf16[768,256]{1,0:T(8,128)(2,1)S(1)} %get-tuple-element.98), channel_id=1, source_target_pairs={{0,8},{1,12},{2,10},{3,14},{4,9},{5,13},{6,11},{7,15},{8,0},{9,4},... | collective-permute-start | bytes 1179656 | tf_op jit(solution)/shard_map/ppermute | solution.py:823
  105.6 21.8 %collective-permute-start.10 = (bf16[768,256]{1,0:T(8,128)(2,1)S(1)}, bf16[768,256]{1,0:T(8,128)(2,1)S(1)}, u32[]{:S(2)}, u32[]{:S(2)}) collective-permute-start(bf16[768,256]{1,0:T(8,128)(2,1)S(1)} %get-tuple-element.103), channel_id=1, source_target_pairs={{0,10},{1,14},{2,8},{3,12},{4,11},{5,15},{6,9},{7,13},{8,2},{9,6},... | collective-permute-start | bytes 1179656 | tf_op jit(solution)/shard_map/ppermute | solution.py:823
  105.7 21.7 %collective-permute-start.9 = (bf16[768,256]{1,0:T(8,128)(2,1)S(1)}, bf16[768,256]{1,0:T(8,128)(2,1)S(1)}, u32[]{:S(2)}, u32[]{:S(2)}) collective-permute-start(bf16[768,256]{1,0:T(8,128)(2,1)S(1)} %get-tuple-element.101), channel_id=1, source_target_pairs={{0,2},{1,6},{2,0},{3,4},{4,3},{5,7},{6,1},{7,5},{8,10},{9,14},{10,... | collective-permute-start | bytes 1179656 | tf_op jit(solution)/shard_map/ppermute | solution.py:823
  106.6 20.7 %collective-permute-start.8 = (bf16[768,256]{1,0:T(8,128)(2,1)S(1)}, bf16[768,256]{1,0:T(8,128)(2,1)S(1)}, u32[]{:S(2)}, u32[]{:S(2)}) collective-permute-start(bf16[768,256]{1,0:T(8,128)(2,1)S(1)} %get-tuple-element.99), channel_id=1, source_target_pairs={{0,0},{1,4},{2,2},{3,6},{4,1},{5,5},{6,3},{7,7},{8,8},{9,12},{10,1... | collective-permute-start | bytes 1179656 | tf_op jit(solution)/shard_map/ppermute | solution.py:823
  130.3 7.5 %collective-permute-start.13 = (bf16[128,384]{1,0:T(8,128)(2,1)S(1)}, bf16[128,384]{1,0:T(8,128)(2,1)S(1)}, u32[]{:S(2)}, u32[]{:S(2)}) collective-permute-start(bf16[128,384]{1,0:T(8,128)(2,1)S(1)} %get-tuple-element.132), channel_id=1, source_target_pairs={{1,0},{3,2},{5,4},{7,6},{9,8},{11,10},{13,12},{15,14},{17,16},{19,... | collective-permute-start | bytes 294920 | tf_op jit(solution)/shard_map/ppermute | solution.py:923
  134.2 10.5 %collective-permute-start.14 = (bf16[384,256]{1,0:T(8,128)(2,1)S(1)}, bf16[384,256]{1,0:T(8,128)(2,1)S(1)}, u32[]{:S(2)}, u32[]{:S(2)}) collective-permute-start(bf16[384,256]{1,0:T(8,128)(2,1)S(1)} %get-tuple-element.175), channel_id=1, source_target_pairs={{0,16},{1,17},{2,18},{3,19},{4,20},{5,21},{6,22},{7,23},{8,24},{9,... | collective-permute-start | bytes 589832 | tf_op jit(solution)/shard_map/ppermute | solution.py:953
  135.8 11.1 %collective-permute-start.15 = (bf16[384,256]{1,0:T(8,128)(2,1)S(1)}, bf16[384,256]{1,0:T(8,128)(2,1)S(1)}, u32[]{:S(2)}, u32[]{:S(2)}) collective-permute-start(bf16[384,256]{1,0:T(8,128)(2,1)S(1)} %get-tuple-element.177), channel_id=1, source_target_pairs={{0,2},{1,3},{2,0},{3,1},{4,6},{5,7},{6,4},{7,5},{8,10},{9,11},{10,... | collective-permute-start | bytes 589832 | tf_op jit(solution)/shard_map/ppermute | solution.py:953
  137.3 9.6 %collective-permute-start.16 = (bf16[384,256]{1,0:T(8,128)(2,1)S(1)}, bf16[384,256]{1,0:T(8,128)(2,1)S(1)}, u32[]{:S(2)}, u32[]{:S(2)}) collective-permute-start(bf16[384,256]{1,0:T(8,128)(2,1)S(1)} %get-tuple-element.176), channel_id=1, source_target_pairs={{0,18},{1,19},{2,16},{3,17},{4,22},{5,23},{6,20},{7,21},{8,26},{9,... | collective-permute-start | bytes 589832 | tf_op jit(solution)/shard_map/ppermute | solution.py:953
  151.6 7.7 %collective-permute-start.20 = (bf16[96,256]{1,0:T(8,128)(2,1)}, bf16[96,256]{1,0:T(8,128)(2,1)}, u32[]{:S(2)}, u32[]{:S(2)}) collective-permute-start(bf16[96,256]{1,0:T(8,128)(2,1)} %get-tuple-element.207), channel_id=1, source_target_pairs={{0,18},{1,19},{2,16},{3,17},{4,22},{5,23},{6,20},{7,21},{8,26},{9,... | collective-permute-start | bytes 147464 | tf_op jit(solution)/shard_map/ppermute | solution.py:953
  153.0 10.8 %collective-permute-start.22 = (bf16[768,256]{1,0:T(8,128)(2,1)S(1)}, bf16[768,256]{1,0:T(8,128)(2,1)S(1)}, u32[]{:S(2)}, u32[]{:S(2)}) collective-permute-start(bf16[768,256]{1,0:T(8,128)(2,1)S(1)} %get-tuple-element.151), channel_id=1, source_target_pairs={{0,0},{1,4},{2,2},{3,6},{4,1},{5,5},{6,3},{7,7},{8,8},{9,12},{10,1... | collective-permute-start | bytes 1179656 | tf_op jit(solution)/shard_map/ppermute | solution.py:823
  154.0 20.8 %collective-permute-start.23 = (bf16[768,256]{1,0:T(8,128)(2,1)S(1)}, bf16[768,256]{1,0:T(8,128)(2,1)S(1)}, u32[]{:S(2)}, u32[]{:S(2)}) collective-permute-start(bf16[768,256]{1,0:T(8,128)(2,1)S(1)} %get-tuple-element.153), channel_id=1, source_target_pairs={{0,8},{1,12},{2,10},{3,14},{4,9},{5,13},{6,11},{7,15},{8,0},{9,4},... | collective-permute-start | bytes 1179656 | tf_op jit(solution)/shard_map/ppermute | solution.py:823
  157.0 5.2 %collective-permute-start.18 = (bf16[96,256]{1,0:T(8,128)(2,1)}, bf16[96,256]{1,0:T(8,128)(2,1)S(1)}, u32[]{:S(2)}, u32[]{:S(2)}) collective-permute-start(bf16[96,256]{1,0:T(8,128)(2,1)} %get-tuple-element.205), channel_id=1, source_target_pairs={{0,16},{1,17},{2,18},{3,19},{4,20},{5,21},{6,22},{7,23},{8,24},{9,... | collective-permute-start | bytes 147464 | tf_op jit(solution)/shard_map/ppermute | solution.py:953
  184.3 17.2 %collective-permute-start.28 = (bf16[256,256]{1,0:T(8,128)(2,1)S(1)}, bf16[256,256]{1,0:T(8,128)(2,1)S(1)}, u32[]{:S(2)}, u32[]{:S(2)}) collective-permute-start(bf16[256,256]{1,0:T(8,128)(2,1)S(1)} %pad_maximum_fusion.6), channel_id=1, source_target_pairs={{0,8},{1,9},{2,10},{3,11},{4,12},{5,13},{6,14},{7,15},{8,0},{9,1},... | collective-permute-start | bytes 393224 | tf_op jit(solution)/shard_map/ppermute | solution.py:986
  184.4 25.2 %collective-permute-start.25 = (bf16[768,256]{1,0:T(8,128)(2,1)}, bf16[768,256]{1,0:T(8,128)(2,1)S(1)}, u32[]{:S(2)}, u32[]{:S(2)}) collective-permute-start(bf16[768,256]{1,0:T(8,128)(2,1)} %get-tuple-element.156), channel_id=1, source_target_pairs={{0,10},{1,14},{2,8},{3,12},{4,11},{5,15},{6,9},{7,13},{8,2},{9,6},... | collective-permute-start | bytes 1179656 | tf_op jit(solution)/shard_map/ppermute | solution.py:823
  188.3 21.2 %collective-permute-start.24 = (bf16[768,256]{1,0:T(8,128)(2,1)}, bf16[768,256]{1,0:T(8,128)(2,1)S(1)}, u32[]{:S(2)}, u32[]{:S(2)}) collective-permute-start(bf16[768,256]{1,0:T(8,128)(2,1)} %get-tuple-element.154), channel_id=1, source_target_pairs={{0,2},{1,6},{2,0},{3,4},{4,3},{5,7},{6,1},{7,5},{8,10},{9,14},{10,... | collective-permute-start | bytes 1179656 | tf_op jit(solution)/shard_map/ppermute | solution.py:823
  201.6 8.7 %collective-permute-start.29 = (bf16[224,256]{1,0:T(8,128)(2,1)S(1)}, bf16[224,256]{1,0:T(8,128)(2,1)S(1)}, u32[]{:S(2)}, u32[]{:S(2)}) collective-permute-start(bf16[224,256]{1,0:T(8,128)(2,1)S(1)} %add_convert_fusion), channel_id=1, source_target_pairs={{0,4},{1,5},{2,6},{3,7},{4,0},{5,1},{6,2},{7,3},{8,12},{9,13},{10,... | collective-permute-start | bytes 344072 | tf_op jit(solution)/shard_map/ppermute | solution.py:965
  210.2 15.7 %collective-permute-start.26 = (bf16[4,384,256]{2,1,0:T(8,128)(2,1)S(1)}, bf16[4,384,256]{2,1,0:T(8,128)(2,1)S(1)}, u32[]{:S(2)}, u32[]{:S(2)}) collective-permute-start(bf16[4,384,256]{2,1,0:T(8,128)(2,1)S(1)} %shard_map.160), channel_id=1, source_target_pairs={{0,1},{1,0},{2,3},{3,2},{4,5},{5,4},{6,7},{7,6},{8,9},{9,8},{10,11... | collective-permute-start | bytes 2359304 | tf_op jit(solution)/shard_map/ppermute | solution.py:828
  210.4 8.6 %collective-permute-start.30 = (bf16[448,256]{1,0:T(8,128)(2,1)S(1)}, bf16[448,256]{1,0:T(8,128)(2,1)}, u32[]{:S(2)}, u32[]{:S(2)}) collective-permute-start(bf16[448,256]{1,0:T(8,128)(2,1)S(1)} %pad_maximum_fusion.4), channel_id=1, source_target_pairs={{0,16},{1,17},{2,18},{3,19},{4,20},{5,21},{6,22},{7,23},{8,24},{9,... | collective-permute-start | bytes 688136 | tf_op jit(solution)/shard_map/ppermute | solution.py:965
  211.7 12.7 %collective-permute-start.31 = (bf16[448,256]{1,0:T(8,128)(2,1)S(1)}, bf16[448,256]{1,0:T(8,128)(2,1)}, u32[]{:S(2)}, u32[]{:S(2)}) collective-permute-start(bf16[448,256]{1,0:T(8,128)(2,1)S(1)} %pad_maximum_fusion.4), channel_id=1, source_target_pairs={{0,2},{1,3},{2,0},{3,1},{4,6},{5,7},{6,4},{7,5},{8,10},{9,11},{10,... | collective-permute-start | bytes 688136 | tf_op jit(solution)/shard_map/ppermute | solution.py:965
  212.5 12.0 %collective-permute-start.32 = (bf16[448,256]{1,0:T(8,128)(2,1)S(1)}, bf16[448,256]{1,0:T(8,128)(2,1)}, u32[]{:S(2)}, u32[]{:S(2)}) collective-permute-start(bf16[448,256]{1,0:T(8,128)(2,1)S(1)} %pad_maximum_fusion.4), channel_id=1, source_target_pairs={{0,18},{1,19},{2,16},{3,17},{4,22},{5,23},{6,20},{7,21},{8,26},{9,... | collective-permute-start | bytes 688136 | tf_op jit(solution)/shard_map/ppermute | solution.py:965
  (43 other events, 173.8 us)

commit v4 on v3

--- a/solution.py
+++ b/solution.py
@@ -160,22 +160,24 @@
     each(lambda c: c.wait())
 
 
-def emit_messages(info, step, cross, local, low, high):
-    half = cross[0].shape[0]
-    lower = info[5] == 0
-    for sub in range(TB // 256):
-        rows = slice(sub * 256, (sub + 1) * 256)
-        number = step * (TB // 256) + sub
-        block = number // (half // 256)
-        at = pl.ds(pl.multiple_of((number - block * (half // 256)) * 256, 256), 256)
-        leaving = jnp.where(lower, high[rows], low[rows])
-        staying = jnp.where(lower, low[rows], high[rows])
+def emit_rows(info, first, rows, to_lower, cross, local):
+    units = cross[0].shape[0] // WIN
+    stays = info[5] == (0 if to_lower else 1)
+    for sub in range(rows.shape[0] // WIN):
+        number = first + sub
+        block = number // units
+        at = pl.ds(pl.multiple_of((number - block * units) * WIN, WIN), WIN)
+        value = rows[sub * WIN : (sub + 1) * WIN]
         for ty in range(2):
-
-            @pl.when((block ^ info[4]) == ty)
+            fits = (number >= 0) & ((block ^ info[4]) == ty)
+
+            @pl.when(fits & stays)
             def _():
-                cross[ty][at] = leaving
-                local[ty][at] = staying
+                local[ty][at] = value
+
+            @pl.when(fits & jnp.logical_not(stays))
+            def _():
+                cross[ty][at] = value
 
 
 def split_slab(info, slab, keep, send):
@@ -189,19 +191,20 @@
 def first_kernel(info, *refs):
     pieces = refs[:4]
     gain, bias, w_mix, x_out, q_out, kv_out, halo_out, sems = refs[4:]
-    gather_pieces(info, pieces, x_out, sems, True)
+    gather_pieces(info, pieces, x_out.at[pl.ds(WIN, x_out.shape[0] - WIN)], sems, True)
+    x_out[:WIN] = jnp.zeros((WIN, x_out.shape[1]), BF16)
     qw = q_out.shape[1]
 
     def block(i, _):
         at = pl.ds(pl.multiple_of(i * TB, TB), TB)
-        unit, _ = norm_parts(x_out[at].astype(F32))
+        unit, _ = norm_parts(x_out[pl.ds(pl.multiple_of(i * TB + WIN, WIN), TB)].astype(F32))
         normed = (unit * gain[0:1] + bias[0:1]).astype(BF16)
         mixed = dot(normed, w_mix[...])
         q_out[at] = (mixed[:, :qw] * score_scale(qw)).astype(BF16)
         kv_out[at] = mixed[:, qw:].astype(BF16)
         return 0
 
-    lax.fori_loop(0, x_out.shape[0] // TB, block, 0)
+    lax.fori_loop(0, q_out.shape[0] // TB, block, 0)
     halo_out[...] = kv_out[kv_out.shape[0] - WIN :]
 
 
@@ -399,7 +402,9 @@
     active, slope = gelu_pair(dot(normed, w_in[...]))
     active = active.astype(BF16)
     feed = dot(active, w_back[...])
-    emit_messages(info, step, (cross0, cross1), (local0, local1), z[...], (middle + feed).astype(BF16))
+    number = step * (TB // WIN)
+    emit_rows(info, number, z[...], True, (cross0, cross1), (local0, local1))
+    emit_rows(info, number, (middle + feed).astype(BF16), False, (cross0, cross1), (local0, local1))
     squares[0] += masked_squares(stream, base, limit)
     squares[1] += masked_squares(branch, base, limit)
     squares[2] += masked_squares(feed, base, limit)
@@ -547,9 +552,10 @@
 
 def fourth_kernel(
     info, gq, gkv, got, z, gmid, gain_next, bias_next, w_mix_next,
-    q, kv, halo, o, lse, active, slope, mid, gain, bias, w_proj, w_in, w_back,
-    gz_out, gq_out, gk_out, gv_out, gmid_out, halo_out, keep, send, dn_gain, dn_bias, d_gain, d_bias,
-    ext, slab,
+    q, kv, halo, o, lse, active, slope, mid, x, gain, bias, w_mix, w_proj, w_in, w_back, keep_a, send_a,
+    cross0, cross1, local0, local1, gq_last, gkv_last, gmid_last, halo_out, keep, send, slab_last,
+    dn_gain, dn_bias, d_gain, d_bias, d_gain_first, d_bias_first,
+    ext, slab, gq_ext, gk_ext, gv_ext, gmid_ext,
 ):
     step = pl.program_id(0)
     qw = q.shape[1]
@@ -558,7 +564,9 @@
     @pl.when(step == 0)
     def _():
         load_extended(halo, kv, ext)
-        for ref in (gk_out, gv_out, slab, dn_gain, dn_bias, d_gain, d_bias):
+        for ref in (
+            slab, slab_last, dn_gain, dn_bias, d_gain, d_bias, d_gain_first, d_bias_first, gq_ext, gk_ext, gv_ext, gmid_ext
+        ):
             ref[...] = jnp.zeros_like(ref)
 
     limit = info[1]
@@ -569,7 +577,7 @@
         gq[...], grad_kv, z[...].astype(F32), gain_next, bias_next, w_mix_next, slab, dn_gain, dn_bias, gmid[...]
     )
     grad_low = grad_z.astype(BF16)
-    gz_out[...] = grad_low
+    emit_rows(info, step * (TB // WIN), grad_low, False, (cross0, cross1), (local0, local1))
     unit, scale = norm_parts(mid[...])
     normed = (unit * gain[1:2] + bias[1:2]).astype(BF16)
     attended = o[...]
@@ -577,7 +585,8 @@
         grad_low.astype(F32), active[...], slope[...].astype(F32), normed, unit, scale, attended, gain,
         w_proj, w_in, w_back, slab, w_mix_next.size // w_proj.shape[1], d_gain, d_bias,
     )
-    gmid_out[...] = grad_mid
+    shifted = pl.ds(pl.multiple_of(start + WIN, WIN), TB)
+    gmid_ext[shifted] = grad_mid
     weighted = grad_out.astype(F32) * attended.astype(F32)
     for sub in range(TB // WIN):
         rows = slice(sub * WIN, (sub + 1) * WIN)
@@ -589,47 +598,113 @@
             q[rows], ext[near, :qw], ext[near, qw:], grad_out[rows], stack_stat(lse[rows]), delta,
             base + sub * WIN, limit,
         )
-        gq_out[rows] = g_q
-        gk_out[near] += g_k
-        gv_out[near] += g_v
+        gq_ext[pl.ds(pl.multiple_of(start + (sub + 1) * WIN, WIN), WIN)] = g_q
+        gk_ext[near] += g_k
+        gv_ext[near] += g_v
+
+    @pl.when(step == 0)
+    def _():
+        halo_out[...] = jnp.concatenate([gk_ext[:WIN], gv_ext[:WIN]], axis=1).astype(BF16)
+        gk_ext[:WIN] = jnp.zeros((WIN, gk_ext.shape[1]), F32)
+        gv_ext[:WIN] = jnp.zeros((WIN, gv_ext.shape[1]), F32)
+
+    whole_rows = pl.ds(start, TB)
+    grad_x = mix_backward(
+        gq_ext[whole_rows], jnp.concatenate([gk_ext[whole_rows], gv_ext[whole_rows]], axis=1),
+        x[whole_rows].astype(F32), gain, bias, w_mix, slab_last, d_gain_first, d_bias_first, gmid_ext[whole_rows],
+    )
+    emit_rows(info, step * (TB // WIN) - 1, grad_x.astype(BF16), True, (cross0, cross1), (local0, local1))
 
     @pl.when(step == pl.num_programs(0) - 1)
     def _():
-        halo_out[...] = jnp.concatenate([gk_out[:WIN], gv_out[:WIN]], axis=1).astype(BF16)
-        split_slab(info, slab, keep, send)
-
-
-def fifth_kernel(
-    info, gq, gk, gv, got, x, gmid, gz, gain, bias, w_mix, *refs,
-):
-    vectors, squares = refs[:6], refs[6:8]
-    cross0, cross1, local0, local1, keep, send, small, slab, d_gain, d_bias = refs[8:]
-    step = pl.program_id(0)
-
-    @pl.when(step == 0)
-    def _():
-        for ref in (slab, d_gain, d_bias):
-            ref[...] = jnp.zeros_like(ref)
-
-    at = pl.ds(pl.multiple_of(step * TB + WIN, WIN), TB)
-    last = jnp.where(step == pl.num_programs(0) - 1, 1.0, 0.0)
-    tail = got[...].astype(F32) * last
-    extra = jnp.concatenate([jnp.zeros((TB - WIN, got.shape[1]), F32), tail], axis=0)
-    grad_kv = jnp.concatenate([gk[at], gv[at]], axis=1) + extra
+        gq_last[...] = gq_ext[n:]
+        gkv_last[...] = jnp.concatenate([gk_ext[n:], gv_ext[n:]], axis=1)
+        gmid_last[...] = gmid_ext[n:]
+        half = keep_a.shape[0]
+        keep[:half] = keep_a[...]
+        send[:half] = send_a[...]
+        split_slab(info, slab, keep.at[pl.ds(half, keep.shape[0] - half)], send.at[pl.ds(half, send.shape[0] - half)])
+
+
+def fifth_kernel(info, gq, gkv, got, x, gmid, gain, bias, w_mix, slab_in, *refs):
+    vectors, squares = refs[:8], refs[8:10]
+    cross, local, (keep, send, small, slab, d_gain, d_bias) = refs[-10:-8], refs[-8:-6], refs[-6:]
+    slab[...] = slab_in[...]
+    d_gain[...] = vectors[0][...]
+    d_bias[...] = vectors[4][...]
+    n = x.shape[0] - WIN
     grad_x = mix_backward(
-        gq[...], grad_kv, x[...].astype(F32), gain, bias, w_mix, slab, d_gain, d_bias, gmid[...]
-    )
-    emit_messages(info, step, (cross0, cross1), (local0, local1), grad_x.astype(BF16), gz[...])
-
-    @pl.when(step == pl.num_programs(0) - 1)
-    def _():
-        split_slab(info, slab, keep, send)
-        small_rows(info, (d_gain,) + vectors[:3] + (d_bias,) + vectors[3:], squares, small)
-        half = keep.shape[0]
-        count = small.shape[0]
-        coarse = small[...].astype(BF16)
-        send[half : half + count] = coarse
-        send[half + count :] = (small[...] - coarse.astype(F32)).astype(BF16)
+        gq[...], gkv[...] + got[...].astype(F32), x[n:].astype(F32), gain, bias, w_mix, slab, d_gain, d_bias, gmid[...]
+    )
+    emit_rows(info, n // WIN - 1, grad_x.astype(BF16), True, cross, local)
+    split_slab(info, slab, keep, send)
+    small_rows(info, (d_gain,) + vectors[1:4] + (d_bias,) + vectors[5:], squares, small)
+    put_riders(small[...], send, keep.shape[0])
+
+
+def put_riders(rows, send, at):
+    count = rows.shape[0]
+    coarse = rows.astype(BF16)
+    send[at : at + count] = coarse
+    send[at + count :] = (rows - coarse.astype(F32)).astype(BF16)
+
+
+def riders_of(got, at):
+    count = (got.shape[0] - at) // 2
+    return got[at : at + count].astype(F32) + got[at + count :].astype(F32)
+
+
+def stage_kernel(digits, *refs, groups, ways, stage, riders):
+    refs = list(refs)
+    parts = [(refs.pop(0), [refs.pop(0) for _ in range(count)]) for count in groups]
+    small = refs.pop(0) if riders else None
+    messages = [refs.pop(0) for _ in range(max(ways - 1, 1))]
+    kept_out = refs.pop(0) if ways > 1 else None
+    small_out = refs.pop(0) if riders else None
+    total = refs.pop(0)
+    vectors = small[...] if riders else None
+    at = 0
+    for kept, got in parts:
+        rows = kept.shape[0]
+        value = kept[...]
+        for g in got:
+            value = value + g[:rows].astype(F32)
+            if g.shape[0] > rows:
+                vectors = vectors + riders_of(g, rows)
+        total[at : at + rows] = value
+        at += rows
+    chunk = at // ways
+
+    def piece(which):
+        return total[pl.ds(pl.multiple_of(which * chunk, 16), chunk)]
+
+    mine = digits[9 + stage] if ways > 1 else 0
+    for i, message in enumerate(messages):
+        message[:chunk] = piece(mine ^ (i + 1) if ways > 1 else 0).astype(BF16)
+        if riders:
+            put_riders(vectors, message, chunk)
+    if ways > 1:
+        kept_out[...] = piece(mine)
+    if riders:
+        small_out[...] = vectors
+
+
+def exchange_kernel(digits, mine, theirs, rows_out, small_out):
+    count = rows_out.shape[0]
+    rows_out[...] = (mine[:count].astype(F32) + theirs[:count].astype(F32)).astype(BF16)
+    small_out[...] = riders_of(mine, count) + riders_of(theirs, count)
+
+
+def again_kernel(digits, rows, small, message):
+    message[: rows.shape[0]] = rows[...]
+    put_riders(small[...], message, rows.shape[0])
+
+
+def order_kernel(digits, *refs, stage):
+    pieces, out = refs[:-1], refs[-1]
+    rows = pieces[0].shape[0]
+    for c, piece in enumerate(pieces):
+        out[pl.ds(pl.multiple_of((digits[9 + stage] ^ c) * rows, 16), rows)] = piece[...]
 
 
 def assemble_kernel(info, *refs):
@@ -651,6 +726,11 @@
         leave(t).start()
     for t in range(8):
         leave(t).wait()
+
+
+def hold_kernel(info, first, second, *refs):
+    refs[-2][...] = first[...]
+    refs[-1][...] = second[...]
 
 
 def small_rows(info, vectors, squares, out):
@@ -672,8 +752,8 @@
         out[t] = pieces[t][pl.ds(pl.multiple_of((1 - info[0]) * rows, rows), rows)]
 
 
-def unpack_kernel(info, mine, theirs, small, mix, proj, up, down, gain, bias, wide, *, sizes):
-    core = info[0]
+def unpack_kernel(info, mine, theirs, small, counted, mix, proj, up, down, gain, bias, rms, wide, *, sizes):
+    core = info[9]
     wide[core] = mine[...].astype(F32)
     wide[1 - core] = theirs[...].astype(F32)
     rows_a, rows_b, rows_c, ways = sizes
@@ -709,12 +789,15 @@
         for norm in range(2):
             gain[layer, norm : norm + 1] = small[2 * layer + norm : 2 * layer + norm + 1]
             bias[layer, norm : norm + 1] = small[4 + 2 * layer + norm : 5 + 2 * layer + norm]
+    images = rms.shape[1]
+    sums = pltpu.roll(small[8:16], small.shape[1] - (info[6] - info[6] % images), 1)
+    rms[...] = jnp.sqrt(sums[: rms.shape[0], :images] / counted[...])
 
 
 VMEM = pl.BlockSpec(memory_space=pltpu.VMEM)
 
 
-def call(kernel, info, operands, specs, outs, out_specs, scratch=(), grid=(), work=0):
+def call(kernel, info, operands, specs, outs, out_specs, scratch=(), grid=(), work=0, aliases={}):
     moved = sum(math.prod(a.shape) * a.dtype.itemsize for a in list(operands) + jax.tree.leaves(outs))
     single = not isinstance(outs, list)
     views = list(specs) + ([out_specs] if single else list(out_specs))
@@ -736,6 +819,7 @@
             scratch_shapes=list(scratch),
         ),
         out_shape=outs,
+        input_output_aliases=aliases,
         compiler_params=pltpu.CompilerParams(vmem_limit_bytes=VMEM_LIMIT),
         cost_estimate=pl.CostEstimate(flops=int(work * 1.15e9), bytes_accessed=moved, transcendentals=0),
     )(info, *operands)
@@ -747,6 +831,10 @@
 
 def tiled(array):
     return lambda ref: ref.at[pl.ds(pl.multiple_of(pl.program_id(0) * TB, TB), TB)]
+
+
+def tiled_after_window(ref):
+    return ref.at[pl.ds(pl.multiple_of(pl.program_id(0) * TB + WIN, WIN), TB)]
 
 
 def last_rows(ref):
@@ -792,7 +880,26 @@
     fz, fl, fy = chip // 4, (chip // 2) % 2, chip % 2
     limit = lengths[chip]
     spot = lax.axis_index("dp") * images + chip
-    info = jnp.stack([part, limit, chip % quarter, fz, fy, fz, spot, twin, index % 2]).astype(jnp.int32)
+    dp_count = lax.axis_size("dp")
+    dp_index = lax.axis_index("dp")
+
+    def partners(masks):
+        total = dp_count * sections
+        spot = dp_index * sections + index
+        digit = sum(((spot // m) % 2) << i for i, m in enumerate(masks))
+        routes = []
+        for c in range(1, 1 << len(masks)):
+            flips = sum(m for i, m in enumerate(masks) if (c >> i) & 1)
+            routes.append((c, [(s, s ^ flips) for s in range(total)]))
+        return digit, routes
+
+    dp_masks = [sections << b for b in range(dp_count.bit_length() - 1)]
+    section_masks = [1 << b for b in range(1, sections.bit_length() - 1)]
+    plane = [dp_masks[0], section_masks[0]]
+    rest = section_masks[1:] + dp_masks[1:]
+    digits = [partners(masks)[0] for masks in [[1], plane] + [[m] for m in rest]]
+    counted = (lengths.astype(F32) * width)[None, :]
+    info = jnp.stack([part, limit, chip % quarter, fz, fy, fz, spot, twin, index % 2] + digits).astype(jnp.int32)
     swap = route([(s, s ^ 1) for s in range(seats)])
 
     def bits(s):
@@ -848,7 +955,7 @@
     g0, g1, b0, b1 = norm_gain[0], norm_gain[1], norm_bias[0], norm_bias[1]
 
     halo_shape = shape((WIN, kvw), BF16)
-    outs = [rows_low, rows_q, rows_kv, halo_shape]
+    outs = [shape((n + WIN, width), BF16), rows_q, rows_kv, halo_shape]
     x, q0, kv0, halo0 = call(
         first_kernel, info, received + [g0, b0, w_qkv[0]], [ANY] * 4 + [whole(g0), whole(b0), whole(w_qkv[0])],
         outs, [whole(o) for o in outs], [dma((2,))], work=6,
@@ -858,7 +965,7 @@
     outs = [rows_low, rows_q, rows_kv, rows_low, rows_stat, rows_hidden, rows_hidden, rows_wide, squares_shape]
     z, q1, kv1, o0, lse0, active0, slope0, mid0, squares0 = call(
         second_kernel, info, [x, q0, kv0, halo0, g0, b0, w_out[0], w_up[0], w_down[0], g1, b1, w_qkv[1]],
-        [tiled(x), tiled(q0)] + [whole(a) for a in (kv0, halo0, g0, b0, w_out[0], w_up[0], w_down[0], g1, b1, w_qkv[1])],
+        [tiled_after_window, tiled(q0)] + [whole(a) for a in (kv0, halo0, g0, b0, w_out[0], w_up[0], w_down[0], g1, b1, w_qkv[1])],
         outs, [tiled(o) for o in outs[:-1]] + [whole(outs[-1])], [ext], steps, work=15,
     )
     kv_other = lax.ppermute(kv1, "section", first_to_second)
@@ -905,108 +1012,70 @@
     forward_back[1] = send_back(after(local1, forward_back[2]), 0, 1)
 
     slab_rows = mix_rows + feed_rows
-    outs = [rows_low, shape((n, qw), F32), grad_k_shape, grad_v_shape, rows_wide, halo_shape,
-            shape((slab_rows // 2, width), F32), shape((slab_rows // 2, width), BF16),
-            vec_shape, vec_shape, vec_shape, vec_shape]
-    (gz, gq0, gk0, gv0, gmid0, halo_send, keep_b, send_b, d_gain10, d_bias10, d_gain01, d_bias01) = call(
-        fourth_kernel, info,
-        [gq1, gkv1, gkv_got, z, gmid1, g1, b1, w_qkv[1], q0, kv0, halo0, o0, lse0, active0, slope0, mid0, g0, b0,
-         w_out[0], w_up[0], w_down[0]],
-        [tiled(a) for a in (gq1, gkv1, gkv_got, z, gmid1)] + [whole(a) for a in (g1, b1, w_qkv[1])]
-        + [tiled(q0), whole(kv0), whole(halo0)] + [tiled(a) for a in (o0, lse0, active0, slope0, mid0)]
-        + [whole(a) for a in (g0, b0, w_out[0], w_up[0], w_down[0])],
-        outs,
-        [tiled(outs[0]), tiled(outs[1]), whole(outs[2]), whole(outs[3]), tiled(outs[4])] + [whole(o) for o in outs[5:]],
-        [ext, pltpu.VMEM((slab_rows, width), F32)], steps, work=20,
-    )
-    halo_send, send_b = after((halo_send, send_b), *forward_back)
+    early_shape = (feed_rows + slab_rows) // 2, width
+    mix_slab = shape((mix_rows, width), F32)
+    outs = [message] * 4 + [shape((WIN, qw), F32), shape((WIN, kvw), F32), shape((WIN, width), F32), halo_shape,
+            shape(early_shape, F32), shape(early_shape, BF16), mix_slab] + [vec_shape] * 6
+    operands = [gq1, gkv1, gkv_got, z, gmid1, g1, b1, w_qkv[1], q0, kv0, halo0, o0, lse0, active0, slope0, mid0, x, g0,
+                b0, w_qkv[0], w_out[0], w_up[0], w_down[0], keep_a, send_a]
+    (cross0, cross1, local0, local1, gq_last, gkv_last, gmid_last, halo_send, keep_early, send_early, slab_last,
+     d_gain10, d_bias10, d_gain01, d_bias01, d_gain00, d_bias00) = call(
+        fourth_kernel, info, operands,
+        [tiled(a) for a in operands[:5]] + [VMEM] * 3 + [tiled(q0), VMEM, VMEM] + [tiled(a) for a in operands[11:16]]
+        + [VMEM] * 9,
+        outs, [VMEM] * len(outs),
+        [ext, pltpu.VMEM((slab_rows, width), F32), pltpu.VMEM((n + WIN, qw), F32), pltpu.VMEM((n + WIN, qw), F32),
+         pltpu.VMEM((n + WIN, width), F32), pltpu.VMEM((n + WIN, width), F32)], steps, work=20,
+    )
+    outs = [halo_shape, shape(early_shape, BF16)]
+    halo_send, send_early = call(
+        hold_kernel, info, [halo_send, send_early] + forward_back, [VMEM] * 2 + [ANY] * 4, outs, [VMEM] * 2
+    )
     halo_got = lax.ppermute(halo_send, "section", second_to_first)
-
-    dp_count = lax.axis_size("dp")
-    dp_index = lax.axis_index("dp")
-
-    def partners(masks):
-        total = dp_count * sections
-        spot = dp_index * sections + index
-        digit = sum(((spot // m) % 2) << i for i, m in enumerate(masks))
-        routes = []
-        for c in range(1, 1 << len(masks)):
-            flips = sum(m for i, m in enumerate(masks) if (c >> i) & 1)
-            routes.append((c, [(s, s ^ flips) for s in range(total)]))
-        return digit, routes
-
-    def chunk(slabs, which, ways):
-        return jnp.concatenate(
-            [lax.dynamic_slice_in_dim(s, which * (s.shape[0] // ways), s.shape[0] // ways, 0) for s in slabs]
-        )
-
-    def scatter(slabs, masks, vectors=None):
-        digit, routes = partners(masks)
-        ways = 1 << len(masks)
-        kept = chunk(slabs, digit, ways)
-        count = kept.shape[0]
-        riders = []
-        if vectors is not None:
-            coarse = vectors.astype(BF16)
-            riders = [coarse, (vectors - coarse.astype(F32)).astype(BF16)]
-        got = [
-            lax.ppermute(jnp.concatenate([chunk(slabs, digit ^ c, ways).astype(BF16)] + riders), ("dp", "section"), way)
-            for c, way in routes
-        ]
-        for g in got:
-            kept = kept + g[:count].astype(F32)
-            if vectors is not None:
-                rest = g[count:].astype(F32)
-                vectors = vectors + (rest[: vectors.shape[0]] + rest[vectors.shape[0] :])
-        return kept if vectors is None else (kept, vectors)
-
-    def gather(piece, masks):
-        digit, routes = partners(masks)
-        pieces = [piece] + [lax.ppermute(piece, ("dp", "section"), way) for _, way in routes]
-        stacked = jnp.stack(pieces)
-        return jnp.concatenate(
-            [lax.dynamic_index_in_dim(stacked, digit ^ j, 0, keepdims=False) for j in range(len(pieces))]
-        )
 
     def pair(message):
         return lax.ppermute(message, ("dp", "section"), partners([1])[1][0][1])
 
-    def riders_of(vectors):
-        coarse = vectors.astype(BF16)
-        return [coarse, (vectors - coarse.astype(F32)).astype(BF16)]
-
-    def ridden(rest):
-        rest = rest.astype(F32)
-        return rest[: rest.shape[0] // 2] + rest[rest.shape[0] // 2 :]
-
-    def exchange(rows, masks, vectors):
-        rows = rows.astype(BF16)
-        count = rows.shape[0]
-        riders = riders_of(vectors)
-        got = lax.ppermute(jnp.concatenate([rows] + riders), ("dp", "section"), partners(masks)[1][0][1])
-        rows = (rows.astype(F32) + got[:count].astype(F32)).astype(BF16)
-        return rows, ridden(jnp.concatenate(riders)) + ridden(got[count:])
-
-    dp_masks = [sections << b for b in range(dp_count.bit_length() - 1)]
-    section_masks = [1 << b for b in range(1, sections.bit_length() - 1)]
-    plane = [dp_masks[0], section_masks[0]]
-    rest = section_masks[1:] + dp_masks[1:]
-    got_early = pair(jnp.concatenate([send_a, send_b]))
-    early = jnp.concatenate([keep_a, keep_b]) + got_early.astype(F32)
-    gq0 = after(gq0, early)
-    early = scatter([early], plane)
+    def send_all(messages, masks):
+        return [lax.ppermute(m, ("dp", "section"), way) for m, (_, way) in zip(messages, partners(masks)[1])]
 
     small_shape = shape((16, width), F32)
-    outs = [message] * 4 + [shape((mix_rows // 2, width), F32),
-            shape((mix_rows // 2 + 2 * small_shape.shape[0], width), BF16), small_shape]
-    operands = [gq0, gk0, gv0, halo_got, x, gmid0, gz, g0, b0, w_qkv[0]]
-    partial = [d_gain01, d_gain10, d_gain11, d_bias01, d_bias10, d_bias11, squares0, squares1]
-    cross0, cross1, local0, local1, late, send_c, small = call(
-        fifth_kernel, info, operands + partial,
-        [tiled(gq0), whole(gk0), whole(gv0), whole(halo_got), tiled(x), tiled(gmid0), tiled(gz)]
-        + [whole(a) for a in operands[7:] + partial],
-        outs, [whole(o) for o in outs],
-        [pltpu.VMEM((mix_rows, width), F32), pltpu.VMEM((8, width), F32), pltpu.VMEM((8, width), F32)], steps, work=8,
+    rider_rows = 2 * small_shape.shape[0]
+
+    def stage(groups, small, ways, number):
+        operands = [a for kept, got in groups for a in [kept] + got] + ([] if small is None else [small])
+        rows = sum(kept.shape[0] for kept, _ in groups)
+        riders = small is not None
+        outs = [shape((rows // ways + rider_rows * riders, width), BF16)] * max(ways - 1, 1)
+        outs += [shape((rows // ways, width), F32)] * (ways > 1) + [small_shape] * riders
+        kernel = functools.partial(
+            stage_kernel, groups=[len(got) for _, got in groups], ways=ways, stage=number, riders=riders
+        )
+        made = call(
+            kernel, info, operands, [VMEM] * len(operands), outs, [VMEM] * len(outs), [pltpu.VMEM((rows, width), F32)]
+        )
+        sent = max(ways - 1, 1)
+        return made[:sent], made[sent] if ways > 1 else None, made[-1] if riders else None
+
+    def gather(piece, masks, number):
+        pieces = [piece] + [lax.ppermute(piece, ("dp", "section"), way) for _, way in partners(masks)[1]]
+        out = shape((len(pieces) * piece.shape[0], width), BF16)
+        return call(functools.partial(order_kernel, stage=number), info, pieces, [VMEM] * len(pieces), out, VMEM)
+
+    early, kept_early, _ = stage([(keep_early, [pair(send_early)])], None, 4, 1)
+    early_sent = early
+    early = send_all(early, plane)
+
+    outs = [message] * 4 + [shape((mix_rows // 2, width), F32), shape((mix_rows // 2 + rider_rows, width), BF16), small_shape]
+    operands = [gq_last, gkv_last, halo_got, x, gmid_last, g0, b0, w_qkv[0], slab_last]
+    operands += [d_gain00, d_gain01, d_gain10, d_gain11, d_bias00, d_bias01, d_bias10, d_bias11, squares0, squares1]
+    aliases = {1 + len(operands) + i: i for i in range(4)}
+    operands += [cross0, cross1, local0, local1]
+    awaited = list(early_sent)
+    cross0, cross1, local0, local1, keep_late, send_late, small = call(
+        fifth_kernel, info, operands + awaited, [VMEM] * len(operands) + [ANY] * len(awaited), outs, [VMEM] * len(outs),
+        [pltpu.VMEM((mix_rows, width), F32), pltpu.VMEM((8, width), F32), pltpu.VMEM((8, width), F32)],
+        aliases=aliases,
     )
 
     def assemble(own, other):
@@ -1019,39 +1088,46 @@
         return out
 
     backward_back = [send_back(local0, 0, 0), None, send_back(cross0, 1, 0), None]
-    got_late = pair(after(send_c, early))
-    late_rows = late.shape[0]
-    late = late + got_late[:late_rows].astype(F32)
-    small = small + ridden(got_late[late_rows:])
-    late, small = scatter([late], plane, small)
-    early_rows = early.shape[0]
-    forward_trade = trade(after(forward_back, late))
+    late, kept_late, small = stage([(keep_late, [pair(after(send_late, *early))])], small, 4, 1)
+    late = send_all(late, plane)
+    forward_trade = trade(forward_back)
     forward_rows = assemble(forward_back, forward_trade)
-    both = after(jnp.concatenate([early, late]), backward_back[0], backward_back[2])
-    backward_back[3] = send_back(after(cross1, backward_back[2]), 1, 1)
-    backward_back[1] = send_back(after(local1, backward_back[2]), 0, 1)
-    for mask in rest[:-1]:
-        both, small = scatter([both], [mask], small)
-    both = after(both, forward_rows)
-    both, small = exchange(both, rest[-1:], small)
-    for mask in rest[-2::-1]:
-        both = gather(both, [mask])
-    both = after(both, backward_back[1], backward_back[3])
-    both = gather(both, plane)
-    backward_trade = trade(backward_back)
+    groups = [(kept_early, early), (kept_late, late)]
+    number = 2
+    scattered = []
+    while number - 1 < len(rest) and sum(kept.shape[0] for kept, _ in groups) % 32 == 0:
+        messages, kept, small = stage(groups, small, 2, number)
+        groups = [(kept, send_all(messages, [rest[number - 2]]))]
+        scattered.append(number)
+        number += 1
+    scattered_rows = groups[-1][1]
+    backward_back[3] = send_back(after(cross1, backward_back[2], *scattered_rows, forward_rows), 1, 1)
+    backward_back[1] = send_back(after(local1, backward_back[2], *scattered_rows, forward_rows), 0, 1)
+    (both,), _, small = stage(groups, small, 1, 0)
+    both = after(both, backward_back[0], backward_back[2])
+    rows_shape = shape((both.shape[0] - rider_rows, width), BF16)
+    while number - 2 < len(rest):
+        (got,) = send_all([both], [rest[number - 2]])
+        rows, small = call(exchange_kernel, info, [both, got], [VMEM] * 2, [rows_shape, small_shape], [VMEM] * 2)
+        number += 1
+        if number - 2 < len(rest):
+            both = call(again_kernel, info, [rows, small], [VMEM] * 2, shape(both.shape, BF16), VMEM)
+    both = after(rows, backward_back[1], backward_back[3])
+    for number in scattered[::-1]:
+        both = gather(both, [rest[number - 2]], number)
+    backward_trade = trade(after(backward_back, rows))
+    both = gather(both, plane, 1)
     both = after(both, backward_trade)
     theirs = pair(both)
     backward_rows = assemble(backward_back, backward_trade)
-    sums = lax.dynamic_slice_in_dim(small[8:14], dp_index * images, images, 1)
-    rms_values = jnp.sqrt(sums / (lengths.astype(F32)[None, :] * width))
-    outs = [shape(w.shape, F32) for w in (w_qkv, w_out, w_up, w_down, norm_gain, norm_bias)]
+    outs = [shape(w.shape, F32) for w in (w_qkv, w_out, w_up, w_down, norm_gain, norm_bias)] + [shape((6, images), F32)]
     sizes = (feed_rows, slab_rows, mix_rows, 1 << len(plane))
     grads = call(
-        functools.partial(unpack_kernel, sizes=sizes), jnp.stack([index % 2]).astype(jnp.int32), [both, theirs, small],
-        [whole(both), whole(theirs), whole(small)], outs, [whole(o) for o in outs],
+        functools.partial(unpack_kernel, sizes=sizes), info, [both, theirs, small, counted],
+        [VMEM] * 4, outs, [whole(o) for o in outs],
         [pltpu.VMEM((2,) + both.shape, F32)],
     )
-    return (forward_rows, backward_rows, rms_values, grads[4], grads[5]) + tuple(grads[:4])
+    return (forward_rows, backward_rows, grads[6], grads[4], grads[5]) + tuple(grads[:4])
 
 
 def solution(mesh):

time: 232 us -> 213 us (0.918)
  other arithmetic: 11.8 us -> 0.62 us
  local copies, waits for them, and re-layouts: 12.1 us -> 3.08 us
  Pallas kernels: 65.8 us -> 72.9 us
  waiting for transfers between devices: 100 us -> 95 us
    ppermute x8, waiting for transfers between devices: 28.9 us -> 13.3 us  [send_back(): return lax.ppermute(message, 'section', route(pairs))]
    unnamed x66 -> x14, local copies, waits for them, and re-layouts: 8.89 us -> 0.04 us
    pallas_call x12 -> x20, Pallas kernels: 65.8 us -> 72.9 us  [call(): pl.pallas_call(body_of, grid_spec=pltpu.PrefetchScalarGridSpec(num_scalar...]
    ppermute x8, waiting for transfers between devices: 20.2 us -> 24.9 us  [send_all(): lax.ppermute(m, ('dp', 'section'), way)]
    add x6 -> x0, other arithmetic: 4.36 us -> none  [the longest x3 1.93 us: scatter(): kept = kept + g[:count].astype(F32)]
    ppermute x4, waiting for transfers between devices: 10.5 us -> 14.2 us  [gather(): lax.ppermute(piece, ('dp', 'section'), way)]
    convert_element_type x11 -> x0, other arithmetic: 2.87 us -> none  [the longest x2 1.36 us: scatter(): riders = [coarse, (vectors - coarse.astype(F32)).astype(BF16)]]
  transfers between devices with their start and end apart: 34 -> 34, of which waited for: 17 -> 22; matrix products, arithmetic and copies ran while one was open for 4% -> 1% of each run, Pallas kernels for 12% -> 17%
where the time goes in v4:
time: 213 us; the launch traced here: 212 us
  waiting for transfers between devices  95 us (45%)
  Pallas kernels  72.9 us (34%)
  starting transfers between devices  39.7 us (19%)
  local copies, waits for them, and re-layouts  3.08 us (1%)
    pallas_call x20, Pallas kernels, call(): pl.pallas_call(body_of, grid_spec=pltpu.PrefetchScalarGridSpec(num_scalar...  72.9 us
    ppermute x4, waiting for transfers between devices, body(): received[t] = lax.ppermute(message, 'section', route(pairs))  33.2 us
    ppermute x8, waiting for transfers between devices, send_all(): lax.ppermute(m, ('dp', 'section'), way)  24.9 us
    ppermute x4, waiting for transfers between devices, gather(): lax.ppermute(piece, ('dp', 'section'), way)  14.2 us
    ppermute x8, waiting for transfers between devices, send_back(): return lax.ppermute(message, 'section', route(pairs))  13.3 us
    ppermute x8, starting transfers between devices, send_back(): return lax.ppermute(message, 'section', route(pairs))  11.8 us
    ppermute x8, starting transfers between devices, send_all(): lax.ppermute(m, ('dp', 'section'), way)  8.68 us
    ppermute x4, starting transfers between devices, body(): received[t] = lax.ppermute(message, 'section', route(pairs))  6.37 us
  transfers between devices with their start and end apart: 34, of which 22 were waited for; matrix products, arithmetic and copies ran while one was open for 1% of the time, Pallas kernels for 17%

profile of v4, /device:TPU:0, one launch (start us, length us, event | category | flops | bytes accessed | tf_op | source)
XLA Modules:
  0.0 212.4 jit_solution(4610963976546015044)
XLA Ops:
  4.9 5.0 %collective-permute-start.4 = (bf16[768,256]{1,0:T(8,128)(2,1)S(1)}, bf16[768,256]{1,0:T(8,128)(2,1)S(1)}, u32[]{:S(2)}, u32[]{:S(2)}) collective-permute-start(bf16[768,256]{1,0:T(8,128)(2,1)S(1)} %maximum_select_fusion.3), channel_id=1, source_target_pairs={{0,10},{1,14},{2,8},{3,12},{4,11},{5,15},{6,9},{7,13},{8,2},{9,6},... | collective-permute-start | bytes 1179656 | tf_op jit(solution)/shard_map/ppermute | solution.py:923
  11.8 24.9 %collective-permute-done.4.refs_3_ = bf16[768,256]{1,0:T(8,128)(2,1)S(1)} collective-permute-done((bf16[768,256]{1,0:T(8,128)(2,1)S(1)}, bf16[768,256]{1,0:T(8,128)(2,1)S(1)}, u32[]{:S(2)}, u32[]{:S(2)}) %collective-permute-start.4) | collective-permute-done | bytes 393248 | tf_op jit(solution)/shard_map/ppermute | solution.py:923
  36.7 8.3 %collective-permute-done.3.refs_2_ = bf16[768,256]{1,0:T(8,128)(2,1)S(1)} collective-permute-done((bf16[768,256]{1,0:T(8,128)(2,1)S(1)}, bf16[768,256]{1,0:T(8,128)(2,1)S(1)}, u32[]{:S(2)}, u32[]{:S(2)}) %collective-permute-start.3) | collective-permute-done | bytes 393248 | tf_op jit(solution)/shard_map/ppermute | solution.py:923
  45.0 2.6 %shard_map.151 = (bf16[1664,256]{1,0:T(8,128)(2,1)S(1)}, bf16[1536,128]{1,0:T(8,128)(2,1)S(1)}, bf16[1536,384]{1,0:T(8,128)(2,1)S(1)}, bf16[128,384]{1,0:T(8,128)(2,1)S(1)}) custom-call(s32[13]{0:T(128)S(1)} %stack.42.info, bf16[768,256]{1,0:T(8,128)(2,1)S(1)} %collective-permute-done.1.refs_0_, bf16[768,256]{1,0:T(8,128)(2,1)S(1)} %collective-permute-done.2.refs_1_, ...), custom_call_target="tpu_custom_call" | custom-call | flops 6899999744 | bytes 4362240 | tf_op jit(solution)/shard_map/pallas_call | solution.py:812
  49.8 8.2 %shard_map.152 = (bf16[1536,256]{1,0:T(8,128)(2,1)S(1)}, bf16[1536,128]{1,0:T(8,128)(2,1)S(1)}, bf16[1536,384]{1,0:T(8,128)(2,1)S(1)}, bf16[1536,256]{1,0:T(8,12...) custom-call(s32[13]{0:T(128)S(1)} %stack.42.info, ...), custom_call_target="tpu_custom_call" | custom-call | flops 17250000896 | bytes 12124160 | tf_op jit(solution)/shard_map/pallas_call | solution.py:812
  58.0 2.5 %collective-permute-start.6 = (bf16[1536,384]{1,0:T(8,128)(2,1)S(1)}, bf16[1536,384]{1,0:T(8,128)(2,1)S(1)}, u32[]{:S(2)}, u32[]{:S(2)}) collective-permute-start(bf16[1536,384]{1,0:T(8,128)(2,1)S(1)} %get-tuple-element.112.refs_1_.refs_5_), channel_id=1, source_target_pairs={{0,1},{2,3},{4,5},{6,7},{8,9},{10,11},{12,13},{14,15},{16,17},{18,... | collective-permute-start | bytes 3538952 | tf_op jit(solution)/shard_map/ppermute | solution.py:971
  60.5 2.2 %collective-permute-done.6.refs_2_.refs_6_ = bf16[1536,384]{1,0:T(8,128)(2,1)S(1)} collective-permute-done((bf16[1536,384]{1,0:T(8,128)(2,1)S(1)}, bf16[1536,384]{1,0:T(8,128)(2,1)S(1)}, u32[]{:S(2)}, u32[]{:S(2)}) %collective-permute-start.6) | collective-permute-done | bytes 1179680 | tf_op jit(solution)/shard_map/ppermute | solution.py:971
  62.7 4.1 %shard_map.153 = (bf16[1536,128]{1,0:T(8,128)(2,1)S(1)}, bf16[3072,128]{1,0:T(8,128)(2,1)S(1)}, bf16[3072,256]{1,0:T(8,128)(2,1)S(1)}, f32[1536,256]{1,0:T(8,128)S(1)}, f32[1536,128]{1,0:T(8,128)S(1)}) custom-call(s32[13]{0:T(128)S(1)} %stack.42.info, bf16[1536,128]{1,0:T(8,128)(2,1)S(1)} %get-tuple-element.111.refs_0_.refs_4_, ...), custom_call_target="tpu_custom_call" | custom-call | flops 16099999744 | bytes 7864320 | tf_op jit(solution)/shard_map/pallas_call | solution.py:812
  66.8 17.9 %shard_map.154 = (bf16[768,256]{1,0:T(8,128)(2,1)S(1)}, bf16[768,256]{1,0:T(8,128)(2,1)S(1)}, bf16[768,256]{1,0:T(8,128)(2,1)S(1)}, bf16[768,256]{1,0:T(8,128)(2...) custom-call(s32[13]{0:T(128)S(1)} %stack.42.info, ...), custom_call_target="tpu_custom_call" | custom-call | flops 27599998976 | bytes 17215488 | tf_op jit(solution)/shard_map/pallas_call | solution.py:812
  84.7 2.0 collective-permute-start.7
  86.7 8.0 %shard_map.157 = (f32[1536,128]{1,0:T(8,128)S(1)}, f32[1536,384]{1,0:T(8,128)S(1)}, bf16[1536,384]{1,0:T(8,128)(2,1)S(1)}) custom-call(s32[13]{0:T(128)S(1)} %stack.42.info, bf16[1536,128]{1,0:T(8,128)(2,1)S(1)} %get-tuple-element.123.refs_0_, bf16[3072,128]{1,0:T(8,128)(2,1)S(1)} %get-tuple-element.124.refs_1_, ...), custom_call_target="tpu_custom_call" | custom-call | flops 20700000256 | bytes 11993088 | tf_op jit(solution)/shard_map/pallas_call | solution.py:812
  94.7 10.1 %collective-permute-done.7.refs_2_.refs_4_ = bf16[768,256]{1,0:T(8,128)(2,1)S(1)} collective-permute-done((bf16[768,256]{1,0:T(8,128)(2,1)S(1)}, bf16[768,256]{1,0:T(8,128)(2,1)S(1)}, u32[]{:S(2)}, u32[]{:S(2)}) %collective-permute-start.7) | collective-permute-done | bytes 393248 | tf_op jit(solution)/shard_map/ppermute | solution.py:930
  109.6 16.7 %shard_map.158 = (bf16[768,256]{1,0:T(8,128)(2,1)S(1)}, bf16[768,256]{1,0:T(8,128)(2,1)S(1)}, bf16[768,256]{1,0:T(8,128)(2,1)S(1)}, bf16[768,256]{1,0:T(8,128)(2...) custom-call(s32[13]{0:T(128)S(1)} %stack.42.info, ...), custom_call_target="tpu_custom_call" | custom-call | flops 23000000512 | bytes 22667264 | tf_op jit(solution)/shard_map/pallas_call | solution.py:812
  139.5 3.3 %collective-permute-start.16 = (bf16[768,256]{1,0:T(8,128)(2,1)S(1)}, bf16[768,256]{1,0:T(8,128)(2,1)S(1)}, u32[]{:S(2)}, u32[]{:S(2)}) collective-permute-start(bf16[768,256]{1,0:T(8,128)(2,1)S(1)} %get-tuple-element.171), channel_id=1, source_target_pairs={{0,8},{1,12},{2,10},{3,14},{4,9},{5,13},{6,11},{7,15},{8,0},{9,4},... | collective-permute-start | bytes 1179656 | tf_op jit(solution)/shard_map/ppermute | solution.py:930
  150.1 2.0 collective-permute-done.22.refs_6_
  155.7 2.3 %shard_map.156 = f32[8,384,256]{2,1,0:T(8,128)} custom-call(s32[13]{0:T(128)S(1)} %stack.42.info, bf16[768,256]{1,0:T(8,128)(2,1)S(1)} %collective-permute-done.8.refs_0_.refs_2_, bf16[768,256]{1,0:T(8,128)(2,1)S(1)} %collective-permute-done.9.refs_1_.refs_3_, bf16[768,256]{1,0:T(8,128)(2,1)S(1)} %collective-permute-done.7.refs_2_.refs_4_, ...), custom_call_target="tpu_custom_call" | custom-call | bytes 5505024 | tf_op jit(solution)/shard_map/pallas_call | solution.py:812
  158.0 2.7 %collective-permute-done.16.refs_2_ = bf16[768,256]{1,0:T(8,128)(2,1)S(1)} collective-permute-done((bf16[768,256]{1,0:T(8,128)(2,1)S(1)}, bf16[768,256]{1,0:T(8,128)(2,1)S(1)}, u32[]{:S(2)}, u32[]{:S(2)}) %collective-permute-start.16) | collective-permute-done | bytes 393248 | tf_op jit(solution)/shard_map/ppermute | solution.py:930
  161.0 2.7 %collective-permute-start.26 = (bf16[768,256]{1,0:T(8,128)(2,1)S(1)}, bf16[768,256]{1,0:T(8,128)(2,1)S(1)}, u32[]{:S(2)}, u32[]{:S(2)}) collective-permute-start(bf16[768,256]{1,0:T(8,128)(2,1)S(1)} %get-tuple-element.185), channel_id=1, source_target_pairs={{0,10},{1,14},{2,8},{3,12},{4,11},{5,15},{6,9},{7,13},{8,2},{9,6},... | collective-permute-start | bytes 1179656 | tf_op jit(solution)/shard_map/ppermute | solution.py:930
  166.6 19.9 %collective-permute-done.27.refs_1_ = bf16[256,256]{1,0:T(8,128)(2,1)S(1)} collective-permute-done((bf16[256,256]{1,0:T(8,128)(2,1)S(1)}, bf16[256,256]{1,0:T(8,128)(2,1)S(1)}, u32[]{:S(2)}, u32[]{:S(2)}) %collective-permute-start.27) | collective-permute-done | bytes 131104 | tf_op jit(solution)/shard_map/ppermute | solution.py:1040
  188.3 5.0 %collective-permute-done.29.refs_1_ = bf16[224,256]{1,0:T(8,128)(2,1)S(1)} collective-permute-done((bf16[224,256]{1,0:T(8,128)(2,1)S(1)}, bf16[224,256]{1,0:T(8,128)(2,1)S(1)}, u32[]{:S(2)}, u32[]{:S(2)}) %collective-permute-start.29) | collective-permute-done | bytes 114720 | tf_op jit(solution)/shard_map/ppermute | solution.py:1061
  197.4 5.0 %collective-permute-done.30.refs_1_ = bf16[448,256]{1,0:T(8,128)(2,1)S(1)} collective-permute-done((bf16[448,256]{1,0:T(8,128)(2,1)S(1)}, bf16[448,256]{1,0:T(8,128)(2,1)S(1)}, u32[]{:S(2)}, u32[]{:S(2)}) %collective-permute-start.30) | collective-permute-done | bytes 229408 | tf_op jit(solution)/shard_map/ppermute | solution.py:1061
  202.4 4.2 %collective-permute-done.31.refs_2_ = bf16[448,256]{1,0:T(8,128)(2,1)S(1)} collective-permute-done((bf16[448,256]{1,0:T(8,128)(2,1)S(1)}, bf16[448,256]{1,0:T(8,128)(2,1)S(1)}, u32[]{:S(2)}, u32[]{:S(2)}) %collective-permute-start.31) | collective-permute-done | bytes 229408 | tf_op jit(solution)/shard_map/ppermute | solution.py:1061
  207.3 2.3 %shard_map.167 = f32[8,384,256]{2,1,0:T(8,128)} custom-call(s32[13]{0:T(128)S(1)} %stack.42.info, bf16[768,256]{1,0:T(8,128)(2,1)S(1)} %collective-permute-done.15.refs_0_, bf16[768,256]{1,0:T(8,128)(2,1)S(1)} %collective-permute-done.25.refs_1_, bf16[768,256]{1,0:T(8,128)(2,1)S(1)} %collective-permute-done.16.refs_2_, ...), custom_call_target="tpu_custom_call" | custom-call | bytes 5505024 | tf_op jit(solution)/shard_map/pallas_call | solution.py:812
  209.8 2.7 %shard_map.170 = (f32[2,256,512]{2,1,0:T(8,128)}, f32[2,256,256]{2,1,0:T(8,128)}, f32[2,256,512]{2,1,0:T(8,128)}, f32[2,512,256]{2,1,0:T(8,128)}, f32[2,2,256]{2...) custom-call(s32[13]{0:T(128)S(1)} %stack.42.info, bf16[1792,256]{1,0:T(8,128)(2,1)S(1)} %shard_map.169.refs_0_, ...), custom_call_target="tpu_custom_call" | custom-call | bytes 5529824 | tf_op jit(solution)/shard_map/pallas_call | solution.py:812
  (93 shorter events, 46.9 us)
Async XLA Ops:
  4.9 31.8 %collective-permute-start.4 = (bf16[768,256]{1,0:T(8,128)(2,1)S(1)}, bf16[768,256]{1,0:T(8,128)(2,1)S(1)}, u32[]{:S(2)}, u32[]{:S(2)}) collective-permute-start(bf16[768,256]{1,0:T(8,128)(2,1)S(1)} %maximum_select_fusion.3), channel_id=1, source_target_pairs={{0,10},{1,14},{2,8},{3,12},{4,11},{5,15},{6,9},{7,13},{8,2},{9,6},... | collective-permute-start | bytes 1179656 | tf_op jit(solution)/shard_map/ppermute | solution.py:923
  10.0 35.0 %collective-permute-start.3 = (bf16[768,256]{1,0:T(8,128)(2,1)S(1)}, bf16[768,256]{1,0:T(8,128)(2,1)S(1)}, u32[]{:S(2)}, u32[]{:S(2)}) collective-permute-start(bf16[768,256]{1,0:T(8,128)(2,1)S(1)} %maximum_select_fusion.2), channel_id=1, source_target_pairs={{0,8},{1,12},{2,10},{3,14},{4,9},{5,13},{6,11},{7,15},{8,0},{9,4},... | collective-permute-start | bytes 1179656 | tf_op jit(solution)/shard_map/ppermute | solution.py:923
  10.6 34.4 %collective-permute-start.2 = (bf16[768,256]{1,0:T(8,128)(2,1)S(1)}, bf16[768,256]{1,0:T(8,128)(2,1)S(1)}, u32[]{:S(2)}, u32[]{:S(2)}) collective-permute-start(bf16[768,256]{1,0:T(8,128)(2,1)S(1)} %maximum_select_fusion.1), channel_id=1, source_target_pairs={{0,2},{1,6},{2,0},{3,4},{4,3},{5,7},{6,1},{7,5},{8,10},{9,14},{10,... | collective-permute-start | bytes 1179656 | tf_op jit(solution)/shard_map/ppermute | solution.py:923
  11.0 33.9 %collective-permute-start.1 = (bf16[768,256]{1,0:T(8,128)(2,1)S(1)}, bf16[768,256]{1,0:T(8,128)(2,1)S(1)}, u32[]{:S(2)}, u32[]{:S(2)}) collective-permute-start(bf16[768,256]{1,0:T(8,128)(2,1)S(1)} %maximum_select_fusion), channel_id=1, source_target_pairs={{0,0},{1,4},{2,2},{3,6},{4,1},{5,5},{6,3},{7,7},{8,8},{9,12},{10,1... | collective-permute-start | bytes 1179656 | tf_op jit(solution)/shard_map/ppermute | solution.py:923
  84.7 20.1 %collective-permute-start.7 = (bf16[768,256]{1,0:T(8,128)(2,1)S(1)}, bf16[768,256]{1,0:T(8,128)(2,1)S(1)}, u32[]{:S(2)}, u32[]{:S(2)}) collective-permute-start(bf16[768,256]{1,0:T(8,128)(2,1)S(1)} %get-tuple-element.117), channel_id=1, source_target_pairs={{0,8},{1,12},{2,10},{3,14},{4,9},{5,13},{6,11},{7,15},{8,0},{9,4},... | collective-permute-start | bytes 1179656 | tf_op jit(solution)/shard_map/ppermute | solution.py:930
  106.1 20.1 %collective-permute-start.10 = (bf16[768,256]{1,0:T(8,128)(2,1)S(1)}, bf16[768,256]{1,0:T(8,128)(2,1)S(1)}, u32[]{:S(2)}, u32[]{:S(2)}) collective-permute-start(bf16[768,256]{1,0:T(8,128)(2,1)S(1)} %get-tuple-element.122), channel_id=1, source_target_pairs={{0,10},{1,14},{2,8},{3,12},{4,11},{5,15},{6,9},{7,13},{8,2},{9,6},... | collective-permute-start | bytes 1179656 | tf_op jit(solution)/shard_map/ppermute | solution.py:930
  106.2 20.5 %collective-permute-start.9 = (bf16[768,256]{1,0:T(8,128)(2,1)S(1)}, bf16[768,256]{1,0:T(8,128)(2,1)S(1)}, u32[]{:S(2)}, u32[]{:S(2)}) collective-permute-start(bf16[768,256]{1,0:T(8,128)(2,1)S(1)} %get-tuple-element.120), channel_id=1, source_target_pairs={{0,2},{1,6},{2,0},{3,4},{4,3},{5,7},{6,1},{7,5},{8,10},{9,14},{10,... | collective-permute-start | bytes 1179656 | tf_op jit(solution)/shard_map/ppermute | solution.py:930
  107.2 19.5 %collective-permute-start.8 = (bf16[768,256]{1,0:T(8,128)(2,1)S(1)}, bf16[768,256]{1,0:T(8,128)(2,1)S(1)}, u32[]{:S(2)}, u32[]{:S(2)}) collective-permute-start(bf16[768,256]{1,0:T(8,128)(2,1)S(1)} %get-tuple-element.118), channel_id=1, source_target_pairs={{0,0},{1,4},{2,2},{3,6},{4,1},{5,5},{6,3},{7,7},{8,8},{9,12},{10,1... | collective-permute-start | bytes 1179656 | tf_op jit(solution)/shard_map/ppermute | solution.py:930
  129.1 26.6 %collective-permute-start.11 = (bf16[4,384,256]{2,1,0:T(8,128)(2,1)S(1)}, bf16[4,384,256]{2,1,0:T(8,128)(2,1)S(1)}, u32[]{:S(2)}, u32[]{:S(2)}) collective-permute-start(bf16[4,384,256]{2,1,0:T(8,128)(2,1)S(1)} %shard_map.155), channel_id=1, source_target_pairs={{0,1},{1,0},{2,3},{3,2},{4,5},{5,4},{6,7},{7,6},{8,9},{9,8},{10,11... | collective-permute-start | bytes 2359304 | tf_op jit(solution)/shard_map/ppermute | solution.py:935
  131.2 11.5 %collective-permute-start.17 = (bf16[384,256]{1,0:T(8,128)(2,1)S(1)}, bf16[384,256]{1,0:T(8,128)(2,1)S(1)}, u32[]{:S(2)}, u32[]{:S(2)}) collective-permute-start(bf16[384,256]{1,0:T(8,128)(2,1)S(1)} %get-tuple-element.166.refs_23_), channel_id=1, source_target_pairs={{0,16},{1,17},{2,18},{3,19},{4,20},{5,21},{6,22},{7,23},{8,24},{9,... | collective-permute-start | bytes 589832 | tf_op jit(solution)/shard_map/ppermute | solution.py:1040
  132.8 11.1 %collective-permute-start.18 = (bf16[384,256]{1,0:T(8,128)(2,1)S(1)}, bf16[384,256]{1,0:T(8,128)(2,1)S(1)}, u32[]{:S(2)}, u32[]{:S(2)}) collective-permute-start(bf16[384,256]{1,0:T(8,128)(2,1)S(1)} %get-tuple-element.167.refs_24_), channel_id=1, source_target_pairs={{0,2},{1,3},{2,0},{3,1},{4,6},{5,7},{6,4},{7,5},{8,10},{9,11},{10,... | collective-permute-start | bytes 589832 | tf_op jit(solution)/shard_map/ppermute | solution.py:1040
  134.3 9.6 %collective-permute-start.19 = (bf16[384,256]{1,0:T(8,128)(2,1)S(1)}, bf16[384,256]{1,0:T(8,128)(2,1)S(1)}, u32[]{:S(2)}, u32[]{:S(2)}) collective-permute-start(bf16[384,256]{1,0:T(8,128)(2,1)S(1)} %get-tuple-element.168.refs_25_), channel_id=1, source_target_pairs={{0,18},{1,19},{2,16},{3,17},{4,22},{5,23},{6,20},{7,21},{8,26},{9,... | collective-permute-start | bytes 589832 | tf_op jit(solution)/shard_map/ppermute | solution.py:1040
  139.5 21.3 %collective-permute-start.16 = (bf16[768,256]{1,0:T(8,128)(2,1)S(1)}, bf16[768,256]{1,0:T(8,128)(2,1)S(1)}, u32[]{:S(2)}, u32[]{:S(2)}) collective-permute-start(bf16[768,256]{1,0:T(8,128)(2,1)S(1)} %get-tuple-element.171), channel_id=1, source_target_pairs={{0,8},{1,12},{2,10},{3,14},{4,9},{5,13},{6,11},{7,15},{8,0},{9,4},... | collective-permute-start | bytes 1179656 | tf_op jit(solution)/shard_map/ppermute | solution.py:930
  148.1 5.0 %collective-permute-start.23 = (bf16[96,256]{1,0:T(8,128)(2,1)S(1)}, bf16[96,256]{1,0:T(8,128)(2,1)S(1)}, u32[]{:S(2)}, u32[]{:S(2)}) collective-permute-start(bf16[96,256]{1,0:T(8,128)(2,1)S(1)} %get-tuple-element.180), channel_id=1, source_target_pairs={{0,18},{1,19},{2,16},{3,17},{4,22},{5,23},{6,20},{7,21},{8,26},{9,... | collective-permute-start | bytes 147464 | tf_op jit(solution)/shard_map/ppermute | solution.py:1040
  153.8 7.3 %collective-permute-start.24 = (bf16[256,256]{1,0:T(8,128)(2,1)S(1)}, bf16[256,256]{1,0:T(8,128)(2,1)S(1)}, u32[]{:S(2)}, u32[]{:S(2)}) collective-permute-start(bf16[256,256]{1,0:T(8,128)(2,1)S(1)} %get-tuple-element.182), channel_id=1, source_target_pairs={{0,4},{1,5},{2,6},{3,7},{4,0},{5,1},{6,2},{7,3},{8,12},{9,13},{10,... | collective-permute-start | bytes 393224 | tf_op jit(solution)/shard_map/ppermute | solution.py:1040
  155.0 11.3 %collective-permute-start.15 = (bf16[768,256]{1,0:T(8,128)(2,1)S(1)}, bf16[768,256]{1,0:T(8,128)(2,1)S(1)}, u32[]{:S(2)}, u32[]{:S(2)}) collective-permute-start(bf16[768,256]{1,0:T(8,128)(2,1)S(1)} %get-tuple-element.169), channel_id=1, source_target_pairs={{0,0},{1,4},{2,2},{3,6},{4,1},{5,5},{6,3},{7,7},{8,8},{9,12},{10,1... | collective-permute-start | bytes 1179656 | tf_op jit(solution)/shard_map/ppermute | solution.py:930
  161.0 26.0 %collective-permute-start.26 = (bf16[768,256]{1,0:T(8,128)(2,1)S(1)}, bf16[768,256]{1,0:T(8,128)(2,1)S(1)}, u32[]{:S(2)}, u32[]{:S(2)}) collective-permute-start(bf16[768,256]{1,0:T(8,128)(2,1)S(1)} %get-tuple-element.185), channel_id=1, source_target_pairs={{0,10},{1,14},{2,8},{3,12},{4,11},{5,15},{6,9},{7,13},{8,2},{9,6},... | collective-permute-start | bytes 1179656 | tf_op jit(solution)/shard_map/ppermute | solution.py:930
  163.8 23.3 %collective-permute-start.25 = (bf16[768,256]{1,0:T(8,128)(2,1)S(1)}, bf16[768,256]{1,0:T(8,128)(2,1)S(1)}, u32[]{:S(2)}, u32[]{:S(2)}) collective-permute-start(bf16[768,256]{1,0:T(8,128)(2,1)S(1)} %get-tuple-element.183), channel_id=1, source_target_pairs={{0,2},{1,6},{2,0},{3,4},{4,3},{5,7},{6,1},{7,5},{8,10},{9,14},{10,... | collective-permute-start | bytes 1179656 | tf_op jit(solution)/shard_map/ppermute | solution.py:930
  166.3 20.2 %collective-permute-start.27 = (bf16[256,256]{1,0:T(8,128)(2,1)S(1)}, bf16[256,256]{1,0:T(8,128)(2,1)S(1)}, u32[]{:S(2)}, u32[]{:S(2)}) collective-permute-start(bf16[256,256]{1,0:T(8,128)(2,1)S(1)} %get-tuple-element.189.refs_0_), channel_id=1, source_target_pairs={{0,8},{1,9},{2,10},{3,11},{4,12},{5,13},{6,14},{7,15},{8,0},{9,1},... | collective-permute-start | bytes 393224 | tf_op jit(solution)/shard_map/ppermute | solution.py:1040
  187.7 19.6 %collective-permute-start.28 = (bf16[4,384,256]{2,1,0:T(8,128)(2,1)S(1)}, bf16[4,384,256]{2,1,0:T(8,128)(2,1)S(1)}, u32[]{:S(2)}, u32[]{:S(2)}) collective-permute-start(bf16[4,384,256]{2,1,0:T(8,128)(2,1)S(1)} %shard_map.166), channel_id=1, source_target_pairs={{0,1},{1,0},{2,3},{3,2},{4,5},{5,4},{6,7},{7,6},{8,9},{9,8},{10,11... | collective-permute-start | bytes 2359304 | tf_op jit(solution)/shard_map/ppermute | solution.py:935
  187.7 5.6 %collective-permute-start.29 = (bf16[224,256]{1,0:T(8,128)(2,1)S(1)}, bf16[224,256]{1,0:T(8,128)(2,1)S(1)}, u32[]{:S(2)}, u32[]{:S(2)}) collective-permute-start(bf16[224,256]{1,0:T(8,128)(2,1)S(1)} %get-tuple-element.195.refs_0_), channel_id=1, source_target_pairs={{0,4},{1,5},{2,6},{3,7},{4,0},{5,1},{6,2},{7,3},{8,12},{9,13},{10,... | collective-permute-start | bytes 344072 | tf_op jit(solution)/shard_map/ppermute | solution.py:1061
  193.9 8.6 %collective-permute-start.30 = (bf16[448,256]{1,0:T(8,128)(2,1)S(1)}, bf16[448,256]{1,0:T(8,128)(2,1)S(1)}, u32[]{:S(2)}, u32[]{:S(2)}) collective-permute-start(bf16[448,256]{1,0:T(8,128)(2,1)S(1)} %shard_map.168.refs_0_), channel_id=1, source_target_pairs={{0,16},{1,17},{2,18},{3,19},{4,20},{5,21},{6,22},{7,23},{8,24},{9,... | collective-permute-start | bytes 688136 | tf_op jit(solution)/shard_map/ppermute | solution.py:1061
  194.8 11.8 %collective-permute-start.31 = (bf16[448,256]{1,0:T(8,128)(2,1)S(1)}, bf16[448,256]{1,0:T(8,128)(2,1)S(1)}, u32[]{:S(2)}, u32[]{:S(2)}) collective-permute-start(bf16[448,256]{1,0:T(8,128)(2,1)S(1)} %shard_map.168.refs_0_), channel_id=1, source_target_pairs={{0,2},{1,3},{2,0},{3,1},{4,6},{5,7},{6,4},{7,5},{8,10},{9,11},{10,... | collective-permute-start | bytes 688136 | tf_op jit(solution)/shard_map/ppermute | solution.py:1061
  196.2 10.4 %collective-permute-start.32 = (bf16[448,256]{1,0:T(8,128)(2,1)S(1)}, bf16[448,256]{1,0:T(8,128)(2,1)S(1)}, u32[]{:S(2)}, u32[]{:S(2)}) collective-permute-start(bf16[448,256]{1,0:T(8,128)(2,1)S(1)} %shard_map.168.refs_0_), channel_id=1, source_target_pairs={{0,18},{1,19},{2,16},{3,17},{4,22},{5,23},{6,20},{7,21},{8,26},{9,... | collective-permute-start | bytes 688136 | tf_op jit(solution)/shard_map/ppermute | solution.py:1061
  (17 other events, 64.2 us)

commit v5 on v4

--- a/solution.py
+++ b/solution.py
@@ -14,9 +14,11 @@
 NEG = -1e30
 F32 = jnp.float32
 BF16 = jnp.bfloat16
-TB = 512
+TB = 768
 RES = 8
 UNROLL = 16
+RES_BACK = 16
+UNROLL_BACK = 8
 VMEM_LIMIT = 16 * 1024 * 1024
 
 
@@ -104,24 +106,34 @@
     weights = unfold(powers, own)
     hd = values.shape[1] // HEADS
     out = [dot(weights[h * WIN : (h + 1) * WIN], values[:, h * hd : (h + 1) * hd]) for h in range(HEADS)]
-    return out, largest, total
-
-
-def near_backward(queries, keys, values, grad_out, log_total, delta, base, limit):
+    return out, largest, total, powers
+
+
+def near_backward(queries, keys, values, grad_out, log_total, delta, base, limit, weights=None):
     own, allowed = near_masks(base, limit)
     split_q = head_split(queries)
-    weights = jnp.exp(near_scores(split_q, keys, own, allowed) - log_total)
+    if weights is None:
+        weights = jnp.exp(near_scores(split_q, keys, own, allowed) - log_total)
     hd = values.shape[1] // HEADS
     pull = jnp.concatenate(
         [dot_t(grad_out[:, h * hd : (h + 1) * hd], values[:, h * hd : (h + 1) * hd]) for h in range(HEADS)], axis=0
     )
     pull = jnp.where(own, pull[:, WIN:], pull[:, :WIN])
-    slope = unfold(weights * (pull - delta), own)
-    weights = unfold(weights, own)
-    grad_q = head_join(dot(slope, keys))
-    grad_k = t_dot(slope, split_q)
+    slope = weights * (pull - delta)
+    grad_q = head_join(dot(unfold(slope, own), keys))
+    row = lax.broadcasted_iota(jnp.int32, (WIN, 2 * WIN), 0)
+    col = lax.broadcasted_iota(jnp.int32, (WIN, 2 * WIN), 1)
+    here = (row <= jnp.where(col >= WIN, col - WIN, col)).astype(F32).astype(BF16)
+
+    def turned(folded):
+        flat = folded.astype(BF16).T
+        current = flat * here
+        return jnp.concatenate([flat - current, current], axis=0)
+
+    grad_k = dot(turned(slope), split_q)
+    weights = turned(weights)
     grad_v = jnp.concatenate(
-        [t_dot(weights[h * WIN : (h + 1) * WIN], grad_out[:, h * hd : (h + 1) * hd]) for h in range(HEADS)], axis=1
+        [dot(weights[:, h * WIN : (h + 1) * WIN], grad_out[:, h * hd : (h + 1) * hd]) for h in range(HEADS)], axis=1
     )
     return grad_q, grad_k, grad_v
 
@@ -235,7 +247,7 @@
         keys = ext[near, :qw]
         values = ext[near, qw:]
         queries = q[sub * WIN : (sub + 1) * WIN]
-        out, largest, total = near_forward(queries, keys, values, base + sub * WIN, limit)
+        out, largest, total, _ = near_forward(queries, keys, values, base + sub * WIN, limit)
         inverse = 1.0 / total
         lse_out[sub * WIN : (sub + 1) * WIN] = spread_stat(largest + jnp.log(total))
         outs.append(jnp.concatenate([out[0] * inverse[:WIN], out[1] * inverse[WIN:]], axis=1))
@@ -264,14 +276,14 @@
     kv_next[...] = mixed[:, qw:].astype(BF16)
 
 
-def far_mask(grid_q, grid_k, part_grid):
-    shape = (HEADS * RES * grid_q, RES * grid_k)
+def far_mask(grid_q, grid_k, part_grid, residues):
+    shape = (HEADS * residues * grid_q, residues * grid_k)
     row = lax.broadcasted_iota(jnp.int32, shape, 0)
     col = lax.broadcasted_iota(jnp.int32, shape, 1)
-    row = jnp.where(row >= RES * grid_q, row - RES * grid_q, row)
+    row = jnp.where(row >= residues * grid_q, row - residues * grid_q, row)
     row_res = jnp.zeros(shape, jnp.int32)
     col_res = jnp.zeros(shape, jnp.int32)
-    for r in range(1, RES):
+    for r in range(1, residues):
         row_res += (row >= r * grid_q).astype(jnp.int32)
         col_res += (col >= r * grid_k).astype(jnp.int32)
     row_grid = row - row_res * grid_q + part_grid
@@ -301,7 +313,7 @@
         return 0
 
     lax.fori_loop(0, grid_q, place, 0)
-    base_mask, key_pos = far_mask(grid_q, grid_k, part * grid_q)
+    base_mask, key_pos = far_mask(grid_q, grid_k, part * grid_q, RES)
     rows_q = RES * grid_q
     rows_k = RES * grid_k
 
@@ -368,10 +380,11 @@
     base = info[0] * n + start
     outs = []
     logs = []
+    weights = []
     for sub in range(TB // WIN):
         rows = slice(sub * WIN, (sub + 1) * WIN)
         near = pl.ds(pl.multiple_of(start + sub * WIN, WIN), 2 * WIN)
-        out, largest, total = near_forward(q[rows], ext[near, :qw], ext[near, qw:], base + sub * WIN, limit)
+        out, largest, total, powers = near_forward(q[rows], ext[near, :qw], ext[near, qw:], base + sub * WIN, limit)
         far_log = stack_stat(lse_far[rows])
         top = jnp.maximum(largest, far_log)
         near_share = jnp.exp(largest - top)
@@ -380,6 +393,7 @@
         inverse = 1.0 / whole
         near_share = near_share * inverse
         far_share = far_share * inverse
+        weights.append(powers * near_share)
         logs.append(top + jnp.log(whole))
         far = o_far[rows]
         outs.append(
@@ -425,7 +439,8 @@
         )
         stat_out[rows] = pack_stats(logs[sub], delta)
         gq, gk, gv = near_backward(
-            q[rows], ext[near, :qw], ext[near, qw:], grad_out[rows], logs[sub], delta, base + sub * WIN, limit
+            q[rows], ext[near, :qw], ext[near, qw:], grad_out[rows], logs[sub], delta, base + sub * WIN, limit,
+            weights[sub],
         )
         gq_out[rows] = gq
         gk_out[near] += gk
@@ -490,9 +505,9 @@
         return 0
 
     lax.fori_loop(0, grid_q, place, 0)
-    base_mask, key_pos = far_mask(grid_q, grid_k, part * grid_q)
-    rows_q = RES * grid_q
-    rows_k = RES * grid_k
+    base_mask, key_pos = far_mask(grid_q, grid_k, part * grid_q, RES_BACK)
+    rows_q = RES_BACK * grid_q
+    rows_k = RES_BACK * grid_k
 
     def one(i):
         at_q = pl.ds(pl.multiple_of(i * rows_q, rows_q), rows_q)
@@ -503,7 +518,7 @@
         stats = stat_s[at_q]
         lse = jnp.concatenate([stats[:, 0:1], stats[:, 32:33]], axis=0)
         delta = jnp.concatenate([stats[:, 64:65], stats[:, 96:97]], axis=0)
-        allowed = base_mask & (key_pos + i * RES < limit)
+        allowed = base_mask & (key_pos + i * RES_BACK < limit)
         weights = jnp.exp(jnp.where(allowed, dot_t(split_q, keys), NEG) - lse)
         pull = jnp.concatenate([dot_t(grads[h], vr[at_k, h * 128 : (h + 1) * 128]) for h in range(HEADS)], axis=0)
         slope = (weights * (pull - delta)).astype(BF16)
@@ -514,11 +529,11 @@
             gv_s[h, at_k] = t_dot(weights[h * rows_q : (h + 1) * rows_q], grads[h])
 
     def group(i, _):
-        for u in range(UNROLL):
-            one(i * UNROLL + u)
+        for u in range(UNROLL_BACK):
+            one(i * UNROLL_BACK + u)
         return 0
 
-    lax.fori_loop(0, STRIDE // RES // UNROLL, group, 0)
+    lax.fori_loop(0, STRIDE // RES_BACK // UNROLL_BACK, group, 0)
 
     def back(g, _):
         at = pl.ds(pl.multiple_of(g * STRIDE, STRIDE), STRIDE)
@@ -552,7 +567,7 @@
 
 def fourth_kernel(
     info, gq, gkv, got, z, gmid, gain_next, bias_next, w_mix_next,
-    q, kv, halo, o, lse, active, slope, mid, x, gain, bias, w_mix, w_proj, w_in, w_back, keep_a, send_a,
+    q, kv, halo, o, lse, active, slope, mid, x, gain, bias, w_mix, w_proj, w_in, w_back,
     cross0, cross1, local0, local1, gq_last, gkv_last, gmid_last, halo_out, keep, send, slab_last,
     dn_gain, dn_bias, d_gain, d_bias, d_gain_first, d_bias_first,
     ext, slab, gq_ext, gk_ext, gv_ext, gmid_ext,
@@ -620,10 +635,7 @@
         gq_last[...] = gq_ext[n:]
         gkv_last[...] = jnp.concatenate([gk_ext[n:], gv_ext[n:]], axis=1)
         gmid_last[...] = gmid_ext[n:]
-        half = keep_a.shape[0]
-        keep[:half] = keep_a[...]
-        send[:half] = send_a[...]
-        split_slab(info, slab, keep.at[pl.ds(half, keep.shape[0] - half)], send.at[pl.ds(half, send.shape[0] - half)])
+        split_slab(info, slab, keep, send)
 
 
 def fifth_kernel(info, gq, gkv, got, x, gmid, gain, bias, w_mix, slab_in, *refs):
@@ -746,7 +758,7 @@
 
 
 def trade_kernel(info, *refs):
-    pieces, out = refs[:4], refs[4]
+    pieces, out = refs[:4], refs[-1]
     rows = out.shape[1]
     for t in range(4):
         out[t] = pieces[t][pl.ds(pl.multiple_of((1 - info[0]) * rows, rows), rows)]
@@ -757,13 +769,13 @@
     wide[core] = mine[...].astype(F32)
     wide[1 - core] = theirs[...].astype(F32)
     rows_a, rows_b, rows_c, ways = sizes
-    early = (rows_a + rows_b) // 2 // ways
-    late = rows_c // 2 // ways
+    early = rows_a // 2 // ways
+    late = (rows_b + rows_c) // 2 // ways
     rows_mix = rows_c
 
     def pieces(slab, start, stop):
         total = {"a": rows_a, "b": rows_b, "c": rows_c}[slab] // 2
-        size, shift, skip = (late, early, 0) if slab == "c" else (early, 0, rows_a // 2 if slab == "b" else 0)
+        size, shift, skip = {"a": (early, 0, 0), "b": (late, early, 0), "c": (late, early, rows_b // 2)}[slab]
         at = start
         while at < stop:
             half, row = at // total, at % total
@@ -929,9 +941,9 @@
             pairs.append((s, ((z ^ tz) * 4 + p * 2 + (y ^ ty)) * 2 + l))
         return lax.ppermute(message, "section", route(pairs))
 
-    def trade(got):
+    def trade(got, *awaited):
         out = shape((4, rows_piece, width), BF16)
-        send = call(trade_kernel, info, got, [VMEM] * 4, out, whole(out))
+        send = call(trade_kernel, info, got + list(awaited), [VMEM] * 4 + [ANY] * len(awaited), out, VMEM)
         return lax.ppermute(send, "section", swap)
 
     first_to_second = route([(2 * c, 2 * c + 1) for c in range(images)])
@@ -1006,33 +1018,6 @@
         [pltpu.VMEM((HEADS, n, 128), F32), pltpu.VMEM((n, 128), F32), pltpu.VMEM((n, qw), F32),
          pltpu.VMEM((2 * n, qw), F32), pltpu.VMEM((HEADS, 2 * n, 128), F32)], work=18,
     )
-    gkv_got = lax.ppermute(after(gkv_send, forward_back[2]), "section", second_to_first)
-    forward_back[3] = send_back(after(cross1, forward_back[2]), 1, 1)
-    forward_back[0] = send_back(after(local0, forward_back[2]), 0, 0)
-    forward_back[1] = send_back(after(local1, forward_back[2]), 0, 1)
-
-    slab_rows = mix_rows + feed_rows
-    early_shape = (feed_rows + slab_rows) // 2, width
-    mix_slab = shape((mix_rows, width), F32)
-    outs = [message] * 4 + [shape((WIN, qw), F32), shape((WIN, kvw), F32), shape((WIN, width), F32), halo_shape,
-            shape(early_shape, F32), shape(early_shape, BF16), mix_slab] + [vec_shape] * 6
-    operands = [gq1, gkv1, gkv_got, z, gmid1, g1, b1, w_qkv[1], q0, kv0, halo0, o0, lse0, active0, slope0, mid0, x, g0,
-                b0, w_qkv[0], w_out[0], w_up[0], w_down[0], keep_a, send_a]
-    (cross0, cross1, local0, local1, gq_last, gkv_last, gmid_last, halo_send, keep_early, send_early, slab_last,
-     d_gain10, d_bias10, d_gain01, d_bias01, d_gain00, d_bias00) = call(
-        fourth_kernel, info, operands,
-        [tiled(a) for a in operands[:5]] + [VMEM] * 3 + [tiled(q0), VMEM, VMEM] + [tiled(a) for a in operands[11:16]]
-        + [VMEM] * 9,
-        outs, [VMEM] * len(outs),
-        [ext, pltpu.VMEM((slab_rows, width), F32), pltpu.VMEM((n + WIN, qw), F32), pltpu.VMEM((n + WIN, qw), F32),
-         pltpu.VMEM((n + WIN, width), F32), pltpu.VMEM((n + WIN, width), F32)], steps, work=20,
-    )
-    outs = [halo_shape, shape(early_shape, BF16)]
-    halo_send, send_early = call(
-        hold_kernel, info, [halo_send, send_early] + forward_back, [VMEM] * 2 + [ANY] * 4, outs, [VMEM] * 2
-    )
-    halo_got = lax.ppermute(halo_send, "section", second_to_first)
-
     def pair(message):
         return lax.ppermute(message, ("dp", "section"), partners([1])[1][0][1])
 
@@ -1062,18 +1047,43 @@
         out = shape((len(pieces) * piece.shape[0], width), BF16)
         return call(functools.partial(order_kernel, stage=number), info, pieces, [VMEM] * len(pieces), out, VMEM)
 
-    early, kept_early, _ = stage([(keep_early, [pair(send_early)])], None, 4, 1)
-    early_sent = early
-    early = send_all(early, plane)
-
+    messages, kept_a, _ = stage([(keep_a, [pair(send_a)])], None, 4, 1)
+    got_a = send_all(messages, plane)
+    gkv_got = lax.ppermute(after(gkv_send, forward_back[2], *got_a), "section", second_to_first)
+    forward_back[3] = send_back(after(cross1, forward_back[2]), 1, 1)
+    forward_back[0] = send_back(after(local0, forward_back[2]), 0, 0)
+    forward_back[1] = send_back(after(local1, forward_back[2]), 0, 1)
+
+    slab_rows = mix_rows + feed_rows
+    early_shape = slab_rows // 2, width
+    mix_slab = shape((mix_rows, width), F32)
+    outs = [message] * 4 + [shape((WIN, qw), F32), shape((WIN, kvw), F32), shape((WIN, width), F32), halo_shape,
+            shape(early_shape, F32), shape(early_shape, BF16), mix_slab] + [vec_shape] * 6
+    operands = [gq1, gkv1, gkv_got, z, gmid1, g1, b1, w_qkv[1], q0, kv0, halo0, o0, lse0, active0, slope0, mid0, x, g0,
+                b0, w_qkv[0], w_out[0], w_up[0], w_down[0]]
+    (cross0, cross1, local0, local1, gq_last, gkv_last, gmid_last, halo_send, keep_early, send_early, slab_last,
+     d_gain10, d_bias10, d_gain01, d_bias01, d_gain00, d_bias00) = call(
+        fourth_kernel, info, operands,
+        [tiled(a) for a in operands[:5]] + [VMEM] * 3 + [tiled(q0), VMEM, VMEM] + [tiled(a) for a in operands[11:16]]
+        + [VMEM] * 7,
+        outs, [VMEM] * len(outs),
+        [ext, pltpu.VMEM((slab_rows, width), F32), pltpu.VMEM((n + WIN, qw), F32), pltpu.VMEM((n + WIN, qw), F32),
+         pltpu.VMEM((n + WIN, width), F32), pltpu.VMEM((n + WIN, width), F32)], steps, work=20,
+    )
+    outs = [halo_shape, shape(early_shape, BF16)]
+    halo_send, send_early = call(
+        hold_kernel, info, [halo_send, send_early] + forward_back, [VMEM] * 2 + [ANY] * 4, outs, [VMEM] * 2
+    )
+    halo_got = lax.ppermute(halo_send, "section", second_to_first)
+
+    got_early = pair(send_early)
     outs = [message] * 4 + [shape((mix_rows // 2, width), F32), shape((mix_rows // 2 + rider_rows, width), BF16), small_shape]
     operands = [gq_last, gkv_last, halo_got, x, gmid_last, g0, b0, w_qkv[0], slab_last]
     operands += [d_gain00, d_gain01, d_gain10, d_gain11, d_bias00, d_bias01, d_bias10, d_bias11, squares0, squares1]
     aliases = {1 + len(operands) + i: i for i in range(4)}
     operands += [cross0, cross1, local0, local1]
-    awaited = list(early_sent)
     cross0, cross1, local0, local1, keep_late, send_late, small = call(
-        fifth_kernel, info, operands + awaited, [VMEM] * len(operands) + [ANY] * len(awaited), outs, [VMEM] * len(outs),
+        fifth_kernel, info, operands, [VMEM] * len(operands), outs, [VMEM] * len(outs),
         [pltpu.VMEM((mix_rows, width), F32), pltpu.VMEM((8, width), F32), pltpu.VMEM((8, width), F32)],
         aliases=aliases,
     )
@@ -1088,11 +1098,11 @@
         return out
 
     backward_back = [send_back(local0, 0, 0), None, send_back(cross0, 1, 0), None]
-    late, kept_late, small = stage([(keep_late, [pair(after(send_late, *early))])], small, 4, 1)
-    late = send_all(late, plane)
-    forward_trade = trade(forward_back)
+    groups = [(keep_early, [got_early]), (keep_late, [pair(send_late)])]
+    messages, kept, small = stage(groups, small, 4, 1)
+    forward_trade = trade(forward_back, send_late)
     forward_rows = assemble(forward_back, forward_trade)
-    groups = [(kept_early, early), (kept_late, late)]
+    groups = [(kept_a, got_a), (kept, send_all(messages, plane))]
     number = 2
     scattered = []
     while number - 1 < len(rest) and sum(kept.shape[0] for kept, _ in groups) % 32 == 0:
@@ -1115,7 +1125,7 @@
     both = after(rows, backward_back[1], backward_back[3])
     for number in scattered[::-1]:
         both = gather(both, [rest[number - 2]], number)
-    backward_trade = trade(after(backward_back, rows))
+    backward_trade = trade(backward_back, rows)
     both = gather(both, plane, 1)
     both = after(both, backward_trade)
     theirs = pair(both)

time: 213 us -> 206 us (0.967)
  Pallas kernels: 72.9 us -> 69.1 us
    ppermute x8, waiting for transfers between devices: 13.3 us -> 8.56 us  [send_back(): return lax.ppermute(message, 'section', route(pairs))]
    ppermute x8, waiting for transfers between devices: 24.9 us -> 29.1 us  [send_all(): lax.ppermute(m, ('dp', 'section'), way)]
    pallas_call x20, Pallas kernels: 72.9 us -> 69.1 us  [call(): pl.pallas_call(body_of, grid_spec=pltpu.PrefetchScalarGridSpec(num_scalar...]
  transfers between devices with their start and end apart: 34 -> 35, of which waited for: 22 -> 20; matrix products, arithmetic and copies ran while one was open for 1% -> 1% of each run, Pallas kernels for 17% -> 16%
where the time goes in v5:
time: 206 us
  waiting for transfers between devices  93.4 us (45%)
  Pallas kernels  69.1 us (34%)
  starting transfers between devices  38.8 us (19%)
  local copies, waits for them, and re-layouts  3.08 us (1%)
    pallas_call x20, Pallas kernels, call(): pl.pallas_call(body_of, grid_spec=pltpu.PrefetchScalarGridSpec(num_scalar...  69.1 us
    ppermute x4, waiting for transfers between devices, body(): received[t] = lax.ppermute(message, 'section', route(pairs))  33.2 us
    ppermute x8, waiting for transfers between devices, send_all(): lax.ppermute(m, ('dp', 'section'), way)  29.1 us
    ppermute x4, waiting for transfers between devices, gather(): lax.ppermute(piece, ('dp', 'section'), way)  15 us
    ppermute x8, starting transfers between devices, send_all(): lax.ppermute(m, ('dp', 'section'), way)  10.5 us
    ppermute x8, starting transfers between devices, send_back(): return lax.ppermute(message, 'section', route(pairs))  9.76 us
    ppermute x8, waiting for transfers between devices, send_back(): return lax.ppermute(message, 'section', route(pairs))  8.56 us
    ppermute x4, starting transfers between devices, body(): received[t] = lax.ppermute(message, 'section', route(pairs))  6.37 us
  transfers between devices with their start and end apart: 35, of which 20 were waited for; matrix products, arithmetic and copies ran while one was open for 1% of the time, Pallas kernels for 16%

profile of v5, /device:TPU:0, one launch (start us, length us, event | category | flops | bytes accessed | tf_op | source)
XLA Modules:
  0.0 206.1 jit_solution(5007744034107919011)
XLA Ops:
  4.9 5.0 %collective-permute-start.4 = (bf16[768,256]{1,0:T(8,128)(2,1)S(1)}, bf16[768,256]{1,0:T(8,128)(2,1)S(1)}, u32[]{:S(2)}, u32[]{:S(2)}) collective-permute-start(bf16[768,256]{1,0:T(8,128)(2,1)S(1)} %maximum_select_fusion.3), channel_id=1, source_target_pairs={{0,10},{1,14},{2,8},{3,12},{4,11},{5,15},{6,9},{7,13},{8,2},{9,6},... | collective-permute-start | bytes 1179656 | tf_op jit(solution)/shard_map/ppermute | solution.py:935
  11.8 24.9 %collective-permute-done.4.refs_3_ = bf16[768,256]{1,0:T(8,128)(2,1)S(1)} collective-permute-done((bf16[768,256]{1,0:T(8,128)(2,1)S(1)}, bf16[768,256]{1,0:T(8,128)(2,1)S(1)}, u32[]{:S(2)}, u32[]{:S(2)}) %collective-permute-start.4) | collective-permute-done | bytes 393248 | tf_op jit(solution)/shard_map/ppermute | solution.py:935
  36.7 8.3 %collective-permute-done.3.refs_2_ = bf16[768,256]{1,0:T(8,128)(2,1)S(1)} collective-permute-done((bf16[768,256]{1,0:T(8,128)(2,1)S(1)}, bf16[768,256]{1,0:T(8,128)(2,1)S(1)}, u32[]{:S(2)}, u32[]{:S(2)}) %collective-permute-start.3) | collective-permute-done | bytes 393248 | tf_op jit(solution)/shard_map/ppermute | solution.py:935
  45.0 2.4 %shard_map.151 = (bf16[1664,256]{1,0:T(8,128)(2,1)S(1)}, bf16[1536,128]{1,0:T(8,128)(2,1)S(1)}, bf16[1536,384]{1,0:T(8,128)(2,1)S(1)}, bf16[128,384]{1,0:T(8,128)(2,1)S(1)}) custom-call(s32[13]{0:T(128)S(1)} %stack.42.info, bf16[768,256]{1,0:T(8,128)(2,1)S(1)} %collective-permute-done.1.refs_0_, bf16[768,256]{1,0:T(8,128)(2,1)S(1)} %collective-permute-done.2.refs_1_, ...), custom_call_target="tpu_custom_call" | custom-call | flops 6899999744 | bytes 4362240 | tf_op jit(solution)/shard_map/pallas_call | solution.py:824
  49.6 7.4 %shard_map.152 = (bf16[1536,256]{1,0:T(8,128)(2,1)S(1)}, bf16[1536,128]{1,0:T(8,128)(2,1)S(1)}, bf16[1536,384]{1,0:T(8,128)(2,1)S(1)}, bf16[1536,256]{1,0:T(8,12...) custom-call(s32[13]{0:T(128)S(1)} %stack.42.info, ...), custom_call_target="tpu_custom_call" | custom-call | flops 17250000896 | bytes 12124160 | tf_op jit(solution)/shard_map/pallas_call | solution.py:824
  57.0 2.5 %collective-permute-start.6 = (bf16[1536,384]{1,0:T(8,128)(2,1)S(1)}, bf16[1536,384]{1,0:T(8,128)(2,1)S(1)}, u32[]{:S(2)}, u32[]{:S(2)}) collective-permute-start(bf16[1536,384]{1,0:T(8,128)(2,1)S(1)} %get-tuple-element.107.refs_1_.refs_5_), channel_id=1, source_target_pairs={{0,1},{2,3},{4,5},{6,7},{8,9},{10,11},{12,13},{14,15},{16,17},{18,... | collective-permute-start | bytes 3538952 | tf_op jit(solution)/shard_map/ppermute | solution.py:983
  59.6 2.2 %collective-permute-done.6.refs_2_.refs_6_ = bf16[1536,384]{1,0:T(8,128)(2,1)S(1)} collective-permute-done((bf16[1536,384]{1,0:T(8,128)(2,1)S(1)}, bf16[1536,384]{1,0:T(8,128)(2,1)S(1)}, u32[]{:S(2)}, u32[]{:S(2)}) %collective-permute-start.6) | collective-permute-done | bytes 1179680 | tf_op jit(solution)/shard_map/ppermute | solution.py:983
  61.8 4.1 %shard_map.153 = (bf16[1536,128]{1,0:T(8,128)(2,1)S(1)}, bf16[3072,128]{1,0:T(8,128)(2,1)S(1)}, bf16[3072,256]{1,0:T(8,128)(2,1)S(1)}, f32[1536,256]{1,0:T(8,128)S(1)}, f32[1536,128]{1,0:T(8,128)S(1)}) custom-call(s32[13]{0:T(128)S(1)} %stack.42.info, bf16[1536,128]{1,0:T(8,128)(2,1)S(1)} %get-tuple-element.106.refs_0_.refs_4_, ...), custom_call_target="tpu_custom_call" | custom-call | flops 16099999744 | bytes 7864320 | tf_op jit(solution)/shard_map/pallas_call | solution.py:824
  65.8 17.1 %shard_map.154 = (bf16[768,256]{1,0:T(8,128)(2,1)S(1)}, bf16[768,256]{1,0:T(8,128)(2,1)S(1)}, bf16[768,256]{1,0:T(8,128)(2,1)S(1)}, bf16[768,256]{1,0:T(8,128)(2...) custom-call(s32[13]{0:T(128)S(1)} %stack.42.info, ...), custom_call_target="tpu_custom_call" | custom-call | flops 27599998976 | bytes 17215488 | tf_op jit(solution)/shard_map/pallas_call | solution.py:824
  89.6 7.2 %shard_map.155 = (f32[1536,128]{1,0:T(8,128)S(1)}, f32[1536,384]{1,0:T(8,128)S(1)}, bf16[1536,384]{1,0:T(8,128)(2,1)S(1)}) custom-call(s32[13]{0:T(128)S(1)} %stack.42.info, bf16[1536,128]{1,0:T(8,128)(2,1)S(1)} %get-tuple-element.118.refs_0_, bf16[3072,128]{1,0:T(8,128)(2,1)S(1)} %get-tuple-element.119.refs_1_, ...), custom_call_target="tpu_custom_call" | custom-call | flops 20700000256 | bytes 11993088 | tf_op jit(solution)/shard_map/pallas_call | solution.py:824
  96.8 6.6 %collective-permute-done.7.refs_4_.refs_2_ = bf16[768,256]{1,0:T(8,128)(2,1)S(1)} collective-permute-done((bf16[768,256]{1,0:T(8,128)(2,1)S(1)}, bf16[768,256]{1,0:T(8,128)(2,1)S(1)}, u32[]{:S(2)}, u32[]{:S(2)}) %collective-permute-start.7) | collective-permute-done | bytes 393248 | tf_op jit(solution)/shard_map/ppermute | solution.py:942
  108.2 15.6 %shard_map.157 = (bf16[768,256]{1,0:T(8,128)(2,1)S(1)}, bf16[768,256]{1,0:T(8,128)(2,1)S(1)}, bf16[768,256]{1,0:T(8,128)(2,1)S(1)}, bf16[768,256]{1,0:T(8,128)(2...) custom-call(s32[13]{0:T(128)S(1)} %stack.42.info, ...), custom_call_target="tpu_custom_call" | custom-call | flops 23000000512 | bytes 20701184 | tf_op jit(solution)/shard_map/pallas_call | solution.py:824
  131.6 2.2 %collective-permute-start.19 = (bf16[768,256]{1,0:T(8,128)(2,1)S(1)}, bf16[768,256]{1,0:T(8,128)(2,1)S(1)}, u32[]{:S(2)}, u32[]{:S(2)}) collective-permute-start(bf16[768,256]{1,0:T(8,128)(2,1)S(1)} %get-tuple-element.165), channel_id=1, source_target_pairs={{0,8},{1,12},{2,10},{3,14},{4,9},{5,13},{6,11},{7,15},{8,0},{9,4},... | collective-permute-start | bytes 1179656 | tf_op jit(solution)/shard_map/ppermute | solution.py:942
  138.4 2.5 %collective-permute-done.22.refs_5_ = bf16[320,256]{1,0:T(8,128)(2,1)S(1)} collective-permute-done((bf16[320,256]{1,0:T(8,128)(2,1)S(1)}, bf16[320,256]{1,0:T(8,128)(2,1)S(1)}, u32[]{:S(2)}, u32[]{:S(2)}) %collective-permute-start.22) | collective-permute-done | bytes 163872 | tf_op jit(solution)/shard_map/ppermute | solution.py:1025
  140.9 5.3 %collective-permute-done.23.refs_6_ = bf16[320,256]{1,0:T(8,128)(2,1)S(1)} collective-permute-done((bf16[320,256]{1,0:T(8,128)(2,1)S(1)}, bf16[320,256]{1,0:T(8,128)(2,1)S(1)}, u32[]{:S(2)}, u32[]{:S(2)}) %collective-permute-start.23) | collective-permute-done | bytes 163872 | tf_op jit(solution)/shard_map/ppermute | solution.py:1025
  146.9 2.1 %collective-permute-start.25 = (bf16[256,256]{1,0:T(8,128)(2,1)S(1)}, bf16[256,256]{1,0:T(8,128)(2,1)S(1)}, u32[]{:S(2)}, u32[]{:S(2)}) collective-permute-start(bf16[256,256]{1,0:T(8,128)(2,1)S(1)} %get-tuple-element.176), channel_id=1, source_target_pairs={{0,4},{1,5},{2,6},{3,7},{4,0},{5,1},{6,2},{7,3},{8,12},{9,13},{10,... | collective-permute-start | bytes 393224 | tf_op jit(solution)/shard_map/ppermute | solution.py:1025
  149.8 2.3 %shard_map.161 = f32[8,384,256]{2,1,0:T(8,128)} custom-call(s32[13]{0:T(128)S(1)} %stack.42.info, bf16[768,256]{1,0:T(8,128)(2,1)S(1)} %collective-permute-done.8.refs_2_.refs_0_, bf16[768,256]{1,0:T(8,128)(2,1)S(1)} %collective-permute-done.9.refs_3_.refs_1_, bf16[768,256]{1,0:T(8,128)(2,1)S(1)} %collective-permute-done.7.refs_4_.refs_2_, ...), custom_call_target="tpu_custom_call" | custom-call | bytes 5505024 | tf_op jit(solution)/shard_map/pallas_call | solution.py:824
  154.5 2.1 %collective-permute-start.27 = (bf16[768,256]{1,0:T(8,128)(2,1)S(1)}, bf16[768,256]{1,0:T(8,128)(2,1)S(1)}, u32[]{:S(2)}, u32[]{:S(2)}) collective-permute-start(bf16[768,256]{1,0:T(8,128)(2,1)S(1)} %get-tuple-element.179), channel_id=1, source_target_pairs={{0,10},{1,14},{2,8},{3,12},{4,11},{5,15},{6,9},{7,13},{8,2},{9,6},... | collective-permute-start | bytes 1179656 | tf_op jit(solution)/shard_map/ppermute | solution.py:942
  160.0 19.4 %collective-permute-done.28.refs_1_ = bf16[256,256]{1,0:T(8,128)(2,1)S(1)} collective-permute-done((bf16[256,256]{1,0:T(8,128)(2,1)S(1)}, bf16[256,256]{1,0:T(8,128)(2,1)S(1)}, u32[]{:S(2)}, u32[]{:S(2)}) %collective-permute-start.28) | collective-permute-done | bytes 131104 | tf_op jit(solution)/shard_map/ppermute | solution.py:1025
  181.1 5.1 %collective-permute-done.30.refs_1_ = bf16[224,256]{1,0:T(8,128)(2,1)S(1)} collective-permute-done((bf16[224,256]{1,0:T(8,128)(2,1)S(1)}, bf16[224,256]{1,0:T(8,128)(2,1)S(1)}, u32[]{:S(2)}, u32[]{:S(2)}) %collective-permute-start.30) | collective-permute-done | bytes 114720 | tf_op jit(solution)/shard_map/ppermute | solution.py:1046
  190.4 5.0 %collective-permute-done.31.refs_1_ = bf16[448,256]{1,0:T(8,128)(2,1)S(1)} collective-permute-done((bf16[448,256]{1,0:T(8,128)(2,1)S(1)}, bf16[448,256]{1,0:T(8,128)(2,1)S(1)}, u32[]{:S(2)}, u32[]{:S(2)}) %collective-permute-start.31) | collective-permute-done | bytes 229408 | tf_op jit(solution)/shard_map/ppermute | solution.py:1046
  195.4 4.9 %collective-permute-done.32.refs_2_ = bf16[448,256]{1,0:T(8,128)(2,1)S(1)} collective-permute-done((bf16[448,256]{1,0:T(8,128)(2,1)S(1)}, bf16[448,256]{1,0:T(8,128)(2,1)S(1)}, u32[]{:S(2)}, u32[]{:S(2)}) %collective-permute-start.32) | collective-permute-done | bytes 229408 | tf_op jit(solution)/shard_map/ppermute | solution.py:1046
  201.0 2.3 %shard_map.167 = f32[8,384,256]{2,1,0:T(8,128)} custom-call(s32[13]{0:T(128)S(1)} %stack.42.info, bf16[768,256]{1,0:T(8,128)(2,1)S(1)} %collective-permute-done.18.refs_0_, bf16[768,256]{1,0:T(8,128)(2,1)S(1)} %collective-permute-done.26.refs_1_, bf16[768,256]{1,0:T(8,128)(2,1)S(1)} %collective-permute-done.19.refs_2_, ...), custom_call_target="tpu_custom_call" | custom-call | bytes 5505024 | tf_op jit(solution)/shard_map/pallas_call | solution.py:824
  203.5 2.7 %shard_map.170 = (f32[2,256,512]{2,1,0:T(8,128)}, f32[2,256,256]{2,1,0:T(8,128)}, f32[2,256,512]{2,1,0:T(8,128)}, f32[2,512,256]{2,1,0:T(8,128)}, f32[2,2,256]{2...) custom-call(s32[13]{0:T(128)S(1)} %stack.42.info, bf16[1792,256]{1,0:T(8,128)(2,1)S(1)} %shard_map.169.refs_0_, ...), custom_call_target="tpu_custom_call" | custom-call | bytes 5529824 | tf_op jit(solution)/shard_map/pallas_call | solution.py:824
  (95 shorter events, 45.8 us)
Async XLA Ops:
  4.9 31.8 %collective-permute-start.4 = (bf16[768,256]{1,0:T(8,128)(2,1)S(1)}, bf16[768,256]{1,0:T(8,128)(2,1)S(1)}, u32[]{:S(2)}, u32[]{:S(2)}) collective-permute-start(bf16[768,256]{1,0:T(8,128)(2,1)S(1)} %maximum_select_fusion.3), channel_id=1, source_target_pairs={{0,10},{1,14},{2,8},{3,12},{4,11},{5,15},{6,9},{7,13},{8,2},{9,6},... | collective-permute-start | bytes 1179656 | tf_op jit(solution)/shard_map/ppermute | solution.py:935
  10.0 35.0 %collective-permute-start.3 = (bf16[768,256]{1,0:T(8,128)(2,1)S(1)}, bf16[768,256]{1,0:T(8,128)(2,1)S(1)}, u32[]{:S(2)}, u32[]{:S(2)}) collective-permute-start(bf16[768,256]{1,0:T(8,128)(2,1)S(1)} %maximum_select_fusion.2), channel_id=1, source_target_pairs={{0,8},{1,12},{2,10},{3,14},{4,9},{5,13},{6,11},{7,15},{8,0},{9,4},... | collective-permute-start | bytes 1179656 | tf_op jit(solution)/shard_map/ppermute | solution.py:935
  10.6 34.4 %collective-permute-start.2 = (bf16[768,256]{1,0:T(8,128)(2,1)S(1)}, bf16[768,256]{1,0:T(8,128)(2,1)S(1)}, u32[]{:S(2)}, u32[]{:S(2)}) collective-permute-start(bf16[768,256]{1,0:T(8,128)(2,1)S(1)} %maximum_select_fusion.1), channel_id=1, source_target_pairs={{0,2},{1,6},{2,0},{3,4},{4,3},{5,7},{6,1},{7,5},{8,10},{9,14},{10,... | collective-permute-start | bytes 1179656 | tf_op jit(solution)/shard_map/ppermute | solution.py:935
  11.0 33.9 %collective-permute-start.1 = (bf16[768,256]{1,0:T(8,128)(2,1)S(1)}, bf16[768,256]{1,0:T(8,128)(2,1)S(1)}, u32[]{:S(2)}, u32[]{:S(2)}) collective-permute-start(bf16[768,256]{1,0:T(8,128)(2,1)S(1)} %maximum_select_fusion), channel_id=1, source_target_pairs={{0,0},{1,4},{2,2},{3,6},{4,1},{5,5},{6,3},{7,7},{8,8},{9,12},{10,1... | collective-permute-start | bytes 1179656 | tf_op jit(solution)/shard_map/ppermute | solution.py:935
  83.4 20.0 %collective-permute-start.7 = (bf16[768,256]{1,0:T(8,128)(2,1)S(1)}, bf16[768,256]{1,0:T(8,128)(2,1)S(1)}, u32[]{:S(2)}, u32[]{:S(2)}) collective-permute-start(bf16[768,256]{1,0:T(8,128)(2,1)S(1)} %get-tuple-element.112), channel_id=1, source_target_pairs={{0,8},{1,12},{2,10},{3,14},{4,9},{5,13},{6,11},{7,15},{8,0},{9,4},... | collective-permute-start | bytes 1179656 | tf_op jit(solution)/shard_map/ppermute | solution.py:942
  86.0 17.4 %collective-permute-start.12 = (bf16[160,256]{1,0:T(8,128)(2,1)S(1)}, bf16[160,256]{1,0:T(8,128)(2,1)S(1)}, u32[]{:S(2)}, u32[]{:S(2)}) collective-permute-start(bf16[160,256]{1,0:T(8,128)(2,1)S(1)} %get-tuple-element.131), channel_id=1, source_target_pairs={{0,16},{1,17},{2,18},{3,19},{4,20},{5,21},{6,22},{7,23},{8,24},{9,... | collective-permute-start | bytes 245768 | tf_op jit(solution)/shard_map/ppermute | solution.py:1025
  87.6 15.8 %collective-permute-start.13 = (bf16[160,256]{1,0:T(8,128)(2,1)S(1)}, bf16[160,256]{1,0:T(8,128)(2,1)S(1)}, u32[]{:S(2)}, u32[]{:S(2)}) collective-permute-start(bf16[160,256]{1,0:T(8,128)(2,1)S(1)} %get-tuple-element.132), channel_id=1, source_target_pairs={{0,2},{1,3},{2,0},{3,1},{4,6},{5,7},{6,4},{7,5},{8,10},{9,11},{10,... | collective-permute-start | bytes 245768 | tf_op jit(solution)/shard_map/ppermute | solution.py:1025
  88.1 15.3 %collective-permute-start.14 = (bf16[160,256]{1,0:T(8,128)(2,1)S(1)}, bf16[160,256]{1,0:T(8,128)(2,1)S(1)}, u32[]{:S(2)}, u32[]{:S(2)}) collective-permute-start(bf16[160,256]{1,0:T(8,128)(2,1)S(1)} %get-tuple-element.133), channel_id=1, source_target_pairs={{0,18},{1,19},{2,16},{3,17},{4,22},{5,23},{6,20},{7,21},{8,26},{9,... | collective-permute-start | bytes 245768 | tf_op jit(solution)/shard_map/ppermute | solution.py:1025
  104.7 20.0 %collective-permute-start.10 = (bf16[768,256]{1,0:T(8,128)(2,1)S(1)}, bf16[768,256]{1,0:T(8,128)(2,1)S(1)}, u32[]{:S(2)}, u32[]{:S(2)}) collective-permute-start(bf16[768,256]{1,0:T(8,128)(2,1)S(1)} %get-tuple-element.117), channel_id=1, source_target_pairs={{0,10},{1,14},{2,8},{3,12},{4,11},{5,15},{6,9},{7,13},{8,2},{9,6},... | collective-permute-start | bytes 1179656 | tf_op jit(solution)/shard_map/ppermute | solution.py:942
  104.8 20.5 %collective-permute-start.9 = (bf16[768,256]{1,0:T(8,128)(2,1)S(1)}, bf16[768,256]{1,0:T(8,128)(2,1)S(1)}, u32[]{:S(2)}, u32[]{:S(2)}) collective-permute-start(bf16[768,256]{1,0:T(8,128)(2,1)S(1)} %get-tuple-element.115), channel_id=1, source_target_pairs={{0,2},{1,6},{2,0},{3,4},{4,3},{5,7},{6,1},{7,5},{8,10},{9,14},{10,... | collective-permute-start | bytes 1179656 | tf_op jit(solution)/shard_map/ppermute | solution.py:942
  105.8 19.5 %collective-permute-start.8 = (bf16[768,256]{1,0:T(8,128)(2,1)S(1)}, bf16[768,256]{1,0:T(8,128)(2,1)S(1)}, u32[]{:S(2)}, u32[]{:S(2)}) collective-permute-start(bf16[768,256]{1,0:T(8,128)(2,1)S(1)} %get-tuple-element.113), channel_id=1, source_target_pairs={{0,0},{1,4},{2,2},{3,6},{4,1},{5,5},{6,3},{7,7},{8,8},{9,12},{10,1... | collective-permute-start | bytes 1179656 | tf_op jit(solution)/shard_map/ppermute | solution.py:942
  130.9 18.9 %collective-permute-start.17 = (bf16[4,384,256]{2,1,0:T(8,128)(2,1)S(1)}, bf16[4,384,256]{2,1,0:T(8,128)(2,1)S(1)}, u32[]{:S(2)}, u32[]{:S(2)}) collective-permute-start(bf16[4,384,256]{2,1,0:T(8,128)(2,1)S(1)} %shard_map.160), channel_id=1, source_target_pairs={{0,1},{1,0},{2,3},{3,2},{4,5},{5,4},{6,7},{7,6},{8,9},{9,8},{10,11... | collective-permute-start | bytes 2359304 | tf_op jit(solution)/shard_map/ppermute | solution.py:947
  131.6 20.9 %collective-permute-start.19 = (bf16[768,256]{1,0:T(8,128)(2,1)S(1)}, bf16[768,256]{1,0:T(8,128)(2,1)S(1)}, u32[]{:S(2)}, u32[]{:S(2)}) collective-permute-start(bf16[768,256]{1,0:T(8,128)(2,1)S(1)} %get-tuple-element.165), channel_id=1, source_target_pairs={{0,8},{1,12},{2,10},{3,14},{4,9},{5,13},{6,11},{7,15},{8,0},{9,4},... | collective-permute-start | bytes 1179656 | tf_op jit(solution)/shard_map/ppermute | solution.py:942
  136.4 9.8 %collective-permute-start.23 = (bf16[320,256]{1,0:T(8,128)(2,1)S(1)}, bf16[320,256]{1,0:T(8,128)(2,1)S(1)}, u32[]{:S(2)}, u32[]{:S(2)}) collective-permute-start(bf16[320,256]{1,0:T(8,128)(2,1)S(1)} %get-tuple-element.173), channel_id=1, source_target_pairs={{0,2},{1,3},{2,0},{3,1},{4,6},{5,7},{6,4},{7,5},{8,10},{9,11},{10,... | collective-permute-start | bytes 491528 | tf_op jit(solution)/shard_map/ppermute | solution.py:1025
  137.4 8.8 %collective-permute-start.24 = (bf16[320,256]{1,0:T(8,128)(2,1)S(1)}, bf16[320,256]{1,0:T(8,128)(2,1)S(1)}, u32[]{:S(2)}, u32[]{:S(2)}) collective-permute-start(bf16[320,256]{1,0:T(8,128)(2,1)S(1)} %get-tuple-element.174), channel_id=1, source_target_pairs={{0,18},{1,19},{2,16},{3,17},{4,22},{5,23},{6,20},{7,21},{8,26},{9,... | collective-permute-start | bytes 491528 | tf_op jit(solution)/shard_map/ppermute | solution.py:1025
  146.9 7.5 %collective-permute-start.25 = (bf16[256,256]{1,0:T(8,128)(2,1)S(1)}, bf16[256,256]{1,0:T(8,128)(2,1)S(1)}, u32[]{:S(2)}, u32[]{:S(2)}) collective-permute-start(bf16[256,256]{1,0:T(8,128)(2,1)S(1)} %get-tuple-element.176), channel_id=1, source_target_pairs={{0,4},{1,5},{2,6},{3,7},{4,0},{5,1},{6,2},{7,3},{8,12},{9,13},{10,... | collective-permute-start | bytes 393224 | tf_op jit(solution)/shard_map/ppermute | solution.py:1025
  149.1 9.7 %collective-permute-start.18 = (bf16[768,256]{1,0:T(8,128)(2,1)S(1)}, bf16[768,256]{1,0:T(8,128)(2,1)S(1)}, u32[]{:S(2)}, u32[]{:S(2)}) collective-permute-start(bf16[768,256]{1,0:T(8,128)(2,1)S(1)} %get-tuple-element.163), channel_id=1, source_target_pairs={{0,0},{1,4},{2,2},{3,6},{4,1},{5,5},{6,3},{7,7},{8,8},{9,12},{10,1... | collective-permute-start | bytes 1179656 | tf_op jit(solution)/shard_map/ppermute | solution.py:942
  154.5 25.5 %collective-permute-start.27 = (bf16[768,256]{1,0:T(8,128)(2,1)S(1)}, bf16[768,256]{1,0:T(8,128)(2,1)S(1)}, u32[]{:S(2)}, u32[]{:S(2)}) collective-permute-start(bf16[768,256]{1,0:T(8,128)(2,1)S(1)} %get-tuple-element.179), channel_id=1, source_target_pairs={{0,10},{1,14},{2,8},{3,12},{4,11},{5,15},{6,9},{7,13},{8,2},{9,6},... | collective-permute-start | bytes 1179656 | tf_op jit(solution)/shard_map/ppermute | solution.py:942
  156.6 23.4 %collective-permute-start.26 = (bf16[768,256]{1,0:T(8,128)(2,1)S(1)}, bf16[768,256]{1,0:T(8,128)(2,1)S(1)}, u32[]{:S(2)}, u32[]{:S(2)}) collective-permute-start(bf16[768,256]{1,0:T(8,128)(2,1)S(1)} %get-tuple-element.177), channel_id=1, source_target_pairs={{0,2},{1,6},{2,0},{3,4},{4,3},{5,7},{6,1},{7,5},{8,10},{9,14},{10,... | collective-permute-start | bytes 1179656 | tf_op jit(solution)/shard_map/ppermute | solution.py:942
  158.8 20.6 %collective-permute-start.28 = (bf16[256,256]{1,0:T(8,128)(2,1)S(1)}, bf16[256,256]{1,0:T(8,128)(2,1)S(1)}, u32[]{:S(2)}, u32[]{:S(2)}) collective-permute-start(bf16[256,256]{1,0:T(8,128)(2,1)S(1)} %get-tuple-element.183.refs_0_), channel_id=1, source_target_pairs={{0,8},{1,9},{2,10},{3,11},{4,12},{5,13},{6,14},{7,15},{8,0},{9,1},... | collective-permute-start | bytes 393224 | tf_op jit(solution)/shard_map/ppermute | solution.py:1025
  180.6 20.3 %collective-permute-start.29 = (bf16[4,384,256]{2,1,0:T(8,128)(2,1)S(1)}, bf16[4,384,256]{2,1,0:T(8,128)(2,1)S(1)}, u32[]{:S(2)}, u32[]{:S(2)}) collective-permute-start(bf16[4,384,256]{2,1,0:T(8,128)(2,1)S(1)} %shard_map.166), channel_id=1, source_target_pairs={{0,1},{1,0},{2,3},{3,2},{4,5},{5,4},{6,7},{7,6},{8,9},{9,8},{10,11... | collective-permute-start | bytes 2359304 | tf_op jit(solution)/shard_map/ppermute | solution.py:947
  186.8 8.6 %collective-permute-start.31 = (bf16[448,256]{1,0:T(8,128)(2,1)S(1)}, bf16[448,256]{1,0:T(8,128)(2,1)S(1)}, u32[]{:S(2)}, u32[]{:S(2)}) collective-permute-start(bf16[448,256]{1,0:T(8,128)(2,1)S(1)} %shard_map.168.refs_0_), channel_id=1, source_target_pairs={{0,16},{1,17},{2,18},{3,19},{4,20},{5,21},{6,22},{7,23},{8,24},{9,... | collective-permute-start | bytes 688136 | tf_op jit(solution)/shard_map/ppermute | solution.py:1046
  188.5 11.8 %collective-permute-start.32 = (bf16[448,256]{1,0:T(8,128)(2,1)S(1)}, bf16[448,256]{1,0:T(8,128)(2,1)S(1)}, u32[]{:S(2)}, u32[]{:S(2)}) collective-permute-start(bf16[448,256]{1,0:T(8,128)(2,1)S(1)} %shard_map.168.refs_0_), channel_id=1, source_target_pairs={{0,2},{1,3},{2,0},{3,1},{4,6},{5,7},{6,4},{7,5},{8,10},{9,11},{10,... | collective-permute-start | bytes 688136 | tf_op jit(solution)/shard_map/ppermute | solution.py:1046
  188.9 11.4 %collective-permute-start.33 = (bf16[448,256]{1,0:T(8,128)(2,1)S(1)}, bf16[448,256]{1,0:T(8,128)(2,1)S(1)}, u32[]{:S(2)}, u32[]{:S(2)}) collective-permute-start(bf16[448,256]{1,0:T(8,128)(2,1)S(1)} %shard_map.168.refs_0_), channel_id=1, source_target_pairs={{0,18},{1,19},{2,16},{3,17},{4,22},{5,23},{6,20},{7,21},{8,26},{9,... | collective-permute-start | bytes 688136 | tf_op jit(solution)/shard_map/ppermute | solution.py:1046
  (18 other events, 70.3 us)

commit v6 on v5

--- a/solution.py
+++ b/solution.py
@@ -153,23 +153,28 @@
     return col_sum(jnp.where(pos < limit, rows * rows, 0.0))
 
 
-def gather_pieces(info, pieces, target, sems, low):
-    rows = pieces[0].shape[0]
-
-    def each(act):
-        for ty in range(2):
-            place = target.at[pl.ds((ty ^ info[4]) * rows, rows)]
-
-            @pl.when(info[5] == (0 if low else 1))
-            def _():
-                act(pltpu.make_async_copy(pieces[ty], place, sems.at[ty]))
-
-            @pl.when(info[5] == (1 if low else 0))
-            def _():
-                act(pltpu.make_async_copy(pieces[2 + ty], place, sems.at[ty]))
-
-    each(lambda c: c.start())
-    each(lambda c: c.wait())
+def pick_piece(info, pieces, low, block, target):
+    for t, piece in enumerate(pieces):
+        tz, ty = t // 2, t % 2
+
+        @pl.when(((block ^ info[4]) == ty) & ((info[5] ^ (0 if low else 1)) == tz))
+        def _():
+            target[...] = piece[...]
+
+
+def emit_block(info, block, rows, to_lower, first, cross, local):
+    stays = info[5] == (0 if to_lower else 1)
+    at = slice(first, first + rows.shape[0])
+    for ty in range(2):
+        fits = (block ^ info[4]) == ty
+
+        @pl.when(fits & stays)
+        def _():
+            local[ty][at] = rows
+
+        @pl.when(fits & jnp.logical_not(stays))
+        def _():
+            cross[ty][at] = rows
 
 
 def emit_rows(info, first, rows, to_lower, cross, local):
@@ -181,7 +186,7 @@
         at = pl.ds(pl.multiple_of((number - block * units) * WIN, WIN), WIN)
         value = rows[sub * WIN : (sub + 1) * WIN]
         for ty in range(2):
-            fits = (number >= 0) & ((block ^ info[4]) == ty)
+            fits = (block ^ info[4]) == ty
 
             @pl.when(fits & stays)
             def _():
@@ -202,8 +207,9 @@
 
 def first_kernel(info, *refs):
     pieces = refs[:4]
-    gain, bias, w_mix, x_out, q_out, kv_out, halo_out, sems = refs[4:]
-    gather_pieces(info, pieces, x_out.at[pl.ds(WIN, x_out.shape[0] - WIN)], sems, True)
+    gain, bias, w_mix, x_out, q_out, kv_out, halo_out = refs[4:]
+    for half in range(2):
+        pick_piece(info, pieces, True, half, x_out.at[pl.ds(WIN + half * pieces[0].shape[0], pieces[0].shape[0])])
     x_out[:WIN] = jnp.zeros((WIN, x_out.shape[1]), BF16)
     qw = q_out.shape[1]
 
@@ -363,14 +369,13 @@
     pieces = refs[:4]
     (q, kv, halo, o_far, lse_far, z, gain, bias, w_proj, w_in, w_back,
      cross0, cross1, local0, local1, go_out, stat_out, gq_out, gk_out, gv_out, gmid_out, keep, send,
-     d_gain, d_bias, squares, ext, cot, slab, sems) = refs[4:]
+     d_gain, d_bias, squares, ext, cot, slab) = refs[4:]
     step = pl.program_id(0)
     qw = q.shape[1]
     n = kv.shape[0]
 
     @pl.when(step == 0)
     def _():
-        gather_pieces(info, pieces, cot, sems, False)
         load_extended(halo, kv, ext)
         for ref in (squares, gk_out, gv_out, slab, d_gain, d_bias):
             ref[...] = jnp.zeros_like(ref)
@@ -416,15 +421,15 @@
     active, slope = gelu_pair(dot(normed, w_in[...]))
     active = active.astype(BF16)
     feed = dot(active, w_back[...])
-    number = step * (TB // WIN)
-    emit_rows(info, number, z[...], True, (cross0, cross1), (local0, local1))
-    emit_rows(info, number, (middle + feed).astype(BF16), False, (cross0, cross1), (local0, local1))
+    emit_block(info, step, z[...], True, 0, (cross0, cross1), (local0, local1))
+    emit_block(info, step, (middle + feed).astype(BF16), False, 0, (cross0, cross1), (local0, local1))
+    pick_piece(info, pieces, False, step, cot)
     squares[0] += masked_squares(stream, base, limit)
     squares[1] += masked_squares(branch, base, limit)
     squares[2] += masked_squares(feed, base, limit)
 
     pos = base + lax.broadcasted_iota(jnp.int32, (TB, 1), 0)
-    upstream = jnp.where(pos < limit, cot[pl.ds(start, TB)].astype(F32), 0.0)
+    upstream = jnp.where(pos < limit, cot[...].astype(F32), 0.0)
     grad_out, grad_mid = feed_backward(
         upstream, active, slope, normed, unit, scale, attended, gain, w_proj, w_in, w_back, slab, 0, d_gain, d_bias
     )
@@ -592,7 +597,7 @@
         gq[...], grad_kv, z[...].astype(F32), gain_next, bias_next, w_mix_next, slab, dn_gain, dn_bias, gmid[...]
     )
     grad_low = grad_z.astype(BF16)
-    emit_rows(info, step * (TB // WIN), grad_low, False, (cross0, cross1), (local0, local1))
+    emit_block(info, step, grad_low, False, 0, (cross0, cross1), (local0, local1))
     unit, scale = norm_parts(mid[...])
     normed = (unit * gain[1:2] + bias[1:2]).astype(BF16)
     attended = o[...]
@@ -628,7 +633,12 @@
         gq_ext[whole_rows], jnp.concatenate([gk_ext[whole_rows], gv_ext[whole_rows]], axis=1),
         x[whole_rows].astype(F32), gain, bias, w_mix, slab_last, d_gain_first, d_bias_first, gmid_ext[whole_rows],
     )
-    emit_rows(info, step * (TB // WIN) - 1, grad_x.astype(BF16), True, (cross0, cross1), (local0, local1))
+    grad_x = grad_x.astype(BF16)
+    emit_block(info, step, grad_x[WIN:], True, 0, (cross0, cross1), (local0, local1))
+
+    @pl.when(step > 0)
+    def _():
+        emit_rows(info, step * (TB // WIN) - 1, grad_x[:WIN], True, (cross0, cross1), (local0, local1))
 
     @pl.when(step == pl.num_programs(0) - 1)
     def _():
@@ -877,6 +887,8 @@
     kvw = w_qkv.shape[2] - qw
     hidden = w_up.shape[2]
     n = rows_piece * images // 2
+    if n != 2 * TB:
+        raise ValueError("block size")
     quarter = images // 2
     steps = (n // TB,)
 
@@ -969,8 +981,8 @@
     halo_shape = shape((WIN, kvw), BF16)
     outs = [shape((n + WIN, width), BF16), rows_q, rows_kv, halo_shape]
     x, q0, kv0, halo0 = call(
-        first_kernel, info, received + [g0, b0, w_qkv[0]], [ANY] * 4 + [whole(g0), whole(b0), whole(w_qkv[0])],
-        outs, [whole(o) for o in outs], [dma((2,))], work=6,
+        first_kernel, info, received + [g0, b0, w_qkv[0]], [VMEM] * 7,
+        outs, [whole(o) for o in outs], work=6,
     )
     halo0 = lax.ppermute(halo0, "section", first_to_second)
 
@@ -1000,14 +1012,14 @@
      d_gain11, d_bias11, squares1) = call(
         third_kernel, info,
         received + [q1, kv1, kv_other, o_far, lse_far, z, g1, b1, w_out[1], w_up[1], w_down[1]],
-        [ANY] * 4
+        [VMEM] * 4
         + [tiled(q1), whole(kv1), last_rows]
         + [tiled(o_far), tiled(lse_far), tiled(z)]
         + [whole(a) for a in (g1, b1, w_out[1], w_up[1], w_down[1])],
         outs,
         [whole(message)] * 4 + [tiled(o) for o in outs[4:7]] + [whole(outs[7]), whole(outs[8]), tiled(outs[9])]
         + [whole(o) for o in outs[10:]],
-        [ext, pltpu.VMEM((n, width), BF16), pltpu.VMEM((feed_rows, width), F32), dma((2,))], steps, work=24,
+        [ext, pltpu.VMEM((TB, width), BF16), pltpu.VMEM((feed_rows, width), F32)], steps, work=24,
     )
     forward_back = [None, None, send_back(cross0, 1, 0), None]
 

time: 206 us -> 204 us (level)
  no operation moved by 1% of the time
where the time goes in v6:
time: 204 us
  waiting for transfers between devices  95.3 us (47%)
  Pallas kernels  67.1 us (33%)
  starting transfers between devices  36.9 us (18%)
  local copies, waits for them, and re-layouts  3.08 us (2%)
    pallas_call x20, Pallas kernels, call(): pl.pallas_call(body_of, grid_spec=pltpu.PrefetchScalarGridSpec(num_scalar...  67.1 us
    ppermute x4, waiting for transfers between devices, body(): received[t] = lax.ppermute(message, 'section', route(pairs))  33.2 us
    ppermute x8, waiting for transfers between devices, send_all(): lax.ppermute(m, ('dp', 'section'), way)  29.4 us
    ppermute x4, waiting for transfers between devices, gather(): lax.ppermute(piece, ('dp', 'section'), way)  15.1 us
    ppermute x8, waiting for transfers between devices, send_back(): return lax.ppermute(message, 'section', route(pairs))  9.87 us
    ppermute x8, starting transfers between devices, send_all(): lax.ppermute(m, ('dp', 'section'), way)  9.4 us
    ppermute x8, starting transfers between devices, send_back(): return lax.ppermute(message, 'section', route(pairs))  9.28 us
    ppermute x4, starting transfers between devices, body(): received[t] = lax.ppermute(message, 'section', route(pairs))  6.37 us
  transfers between devices with their start and end apart: 35, of which 20 were waited for; matrix products, arithmetic and copies ran while one was open for 1% of the time, Pallas kernels for 16%

profile of v6, /device:TPU:0, one launch (start us, length us, event | category | flops | bytes accessed | tf_op | source)
XLA Modules:
  0.0 204.1 jit_solution(326034209711816315)
XLA Ops:
  4.9 5.0 %collective-permute-start.4 = (bf16[768,256]{1,0:T(8,128)(2,1)S(1)}, bf16[768,256]{1,0:T(8,128)(2,1)S(1)}, u32[]{:S(2)}, u32[]{:S(2)}) collective-permute-start(bf16[768,256]{1,0:T(8,128)(2,1)S(1)} %maximum_select_fusion.3), channel_id=1, source_target_pairs={{0,10},{1,14},{2,8},{3,12},{4,11},{5,15},{6,9},{7,13},{8,2},{9,6},... | collective-permute-start | bytes 1179656 | tf_op jit(solution)/shard_map/ppermute | solution.py:947
  11.8 24.9 %collective-permute-done.4.refs_3_ = bf16[768,256]{1,0:T(8,128)(2,1)S(1)} collective-permute-done((bf16[768,256]{1,0:T(8,128)(2,1)S(1)}, bf16[768,256]{1,0:T(8,128)(2,1)S(1)}, u32[]{:S(2)}, u32[]{:S(2)}) %collective-permute-start.4) | collective-permute-done | bytes 393248 | tf_op jit(solution)/shard_map/ppermute | solution.py:947
  36.7 8.3 %collective-permute-done.3.refs_2_ = bf16[768,256]{1,0:T(8,128)(2,1)S(1)} collective-permute-done((bf16[768,256]{1,0:T(8,128)(2,1)S(1)}, bf16[768,256]{1,0:T(8,128)(2,1)S(1)}, u32[]{:S(2)}, u32[]{:S(2)}) %collective-permute-start.3) | collective-permute-done | bytes 393248 | tf_op jit(solution)/shard_map/ppermute | solution.py:947
  45.0 2.1 %shard_map.151 = (bf16[1664,256]{1,0:T(8,128)(2,1)S(1)}, bf16[1536,128]{1,0:T(8,128)(2,1)S(1)}, bf16[1536,384]{1,0:T(8,128)(2,1)S(1)}, bf16[128,384]{1,0:T(8,128)(2,1)S(1)}) custom-call(s32[13]{0:T(128)S(1)} %stack.42.info, bf16[768,256]{1,0:T(8,128)(2,1)S(1)} %collective-permute-done.1.refs_0_, bf16[768,256]{1,0:T(8,128)(2,1)S(1)} %collective-permute-done.2.refs_1_, ...), custom_call_target="tpu_custom_call" | custom-call | flops 6899999744 | bytes 4362240 | tf_op jit(solution)/shard_map/pallas_call | solution.py:834
  49.3 7.4 %shard_map.152 = (bf16[1536,256]{1,0:T(8,128)(2,1)S(1)}, bf16[1536,128]{1,0:T(8,128)(2,1)S(1)}, bf16[1536,384]{1,0:T(8,128)(2,1)S(1)}, bf16[1536,256]{1,0:T(8,12...) custom-call(s32[13]{0:T(128)S(1)} %stack.42.info, ...), custom_call_target="tpu_custom_call" | custom-call | flops 17250000896 | bytes 12124160 | tf_op jit(solution)/shard_map/pallas_call | solution.py:834
  56.7 2.5 %collective-permute-start.6 = (bf16[1536,384]{1,0:T(8,128)(2,1)S(1)}, bf16[1536,384]{1,0:T(8,128)(2,1)S(1)}, u32[]{:S(2)}, u32[]{:S(2)}) collective-permute-start(bf16[1536,384]{1,0:T(8,128)(2,1)S(1)} %get-tuple-element.107.refs_1_.refs_5_), channel_id=1, source_target_pairs={{0,1},{2,3},{4,5},{6,7},{8,9},{10,11},{12,13},{14,15},{16,17},{18,... | collective-permute-start | bytes 3538952 | tf_op jit(solution)/shard_map/ppermute | solution.py:995
  59.2 2.2 %collective-permute-done.6.refs_2_.refs_6_ = bf16[1536,384]{1,0:T(8,128)(2,1)S(1)} collective-permute-done((bf16[1536,384]{1,0:T(8,128)(2,1)S(1)}, bf16[1536,384]{1,0:T(8,128)(2,1)S(1)}, u32[]{:S(2)}, u32[]{:S(2)}) %collective-permute-start.6) | collective-permute-done | bytes 1179680 | tf_op jit(solution)/shard_map/ppermute | solution.py:995
  61.4 4.1 %shard_map.153 = (bf16[1536,128]{1,0:T(8,128)(2,1)S(1)}, bf16[3072,128]{1,0:T(8,128)(2,1)S(1)}, bf16[3072,256]{1,0:T(8,128)(2,1)S(1)}, f32[1536,256]{1,0:T(8,128)S(1)}, f32[1536,128]{1,0:T(8,128)S(1)}) custom-call(s32[13]{0:T(128)S(1)} %stack.42.info, bf16[1536,128]{1,0:T(8,128)(2,1)S(1)} %get-tuple-element.106.refs_0_.refs_4_, ...), custom_call_target="tpu_custom_call" | custom-call | flops 16099999744 | bytes 7864320 | tf_op jit(solution)/shard_map/pallas_call | solution.py:834
  65.5 16.1 %shard_map.154 = (bf16[768,256]{1,0:T(8,128)(2,1)S(1)}, bf16[768,256]{1,0:T(8,128)(2,1)S(1)}, bf16[768,256]{1,0:T(8,128)(2,1)S(1)}, bf16[768,256]{1,0:T(8,128)(2...) custom-call(s32[13]{0:T(128)S(1)} %stack.42.info, ...), custom_call_target="tpu_custom_call" | custom-call | flops 27599998976 | bytes 17215488 | tf_op jit(solution)/shard_map/pallas_call | solution.py:834
  82.1 2.0 collective-permute-start.7
  88.3 7.2 %shard_map.155 = (f32[1536,128]{1,0:T(8,128)S(1)}, f32[1536,384]{1,0:T(8,128)S(1)}, bf16[1536,384]{1,0:T(8,128)(2,1)S(1)}) custom-call(s32[13]{0:T(128)S(1)} %stack.42.info, bf16[1536,128]{1,0:T(8,128)(2,1)S(1)} %get-tuple-element.118.refs_0_, bf16[3072,128]{1,0:T(8,128)(2,1)S(1)} %get-tuple-element.119.refs_1_, ...), custom_call_target="tpu_custom_call" | custom-call | flops 20700000256 | bytes 11993088 | tf_op jit(solution)/shard_map/pallas_call | solution.py:834
  95.5 6.6 %collective-permute-done.7.refs_4_.refs_2_ = bf16[768,256]{1,0:T(8,128)(2,1)S(1)} collective-permute-done((bf16[768,256]{1,0:T(8,128)(2,1)S(1)}, bf16[768,256]{1,0:T(8,128)(2,1)S(1)}, u32[]{:S(2)}, u32[]{:S(2)}) %collective-permute-start.7) | collective-permute-done | bytes 393248 | tf_op jit(solution)/shard_map/ppermute | solution.py:954
  106.8 14.9 %shard_map.157 = (bf16[768,256]{1,0:T(8,128)(2,1)S(1)}, bf16[768,256]{1,0:T(8,128)(2,1)S(1)}, bf16[768,256]{1,0:T(8,128)(2,1)S(1)}, bf16[768,256]{1,0:T(8,128)(2...) custom-call(s32[13]{0:T(128)S(1)} %stack.42.info, ...), custom_call_target="tpu_custom_call" | custom-call | flops 23000000512 | bytes 20701184 | tf_op jit(solution)/shard_map/pallas_call | solution.py:834
  130.2 2.0 collective-permute-start.19
  137.0 3.3 %collective-permute-done.22.refs_5_ = bf16[320,256]{1,0:T(8,128)(2,1)S(1)} collective-permute-done((bf16[320,256]{1,0:T(8,128)(2,1)S(1)}, bf16[320,256]{1,0:T(8,128)(2,1)S(1)}, u32[]{:S(2)}, u32[]{:S(2)}) %collective-permute-start.22) | collective-permute-done | bytes 163872 | tf_op jit(solution)/shard_map/ppermute | solution.py:1037
  140.3 5.2 %collective-permute-done.23.refs_6_ = bf16[320,256]{1,0:T(8,128)(2,1)S(1)} collective-permute-done((bf16[320,256]{1,0:T(8,128)(2,1)S(1)}, bf16[320,256]{1,0:T(8,128)(2,1)S(1)}, u32[]{:S(2)}, u32[]{:S(2)}) %collective-permute-start.23) | collective-permute-done | bytes 163872 | tf_op jit(solution)/shard_map/ppermute | solution.py:1037
  147.7 2.3 %shard_map.161 = f32[8,384,256]{2,1,0:T(8,128)} custom-call(s32[13]{0:T(128)S(1)} %stack.42.info, bf16[768,256]{1,0:T(8,128)(2,1)S(1)} %collective-permute-done.8.refs_2_.refs_0_, bf16[768,256]{1,0:T(8,128)(2,1)S(1)} %collective-permute-done.9.refs_3_.refs_1_, bf16[768,256]{1,0:T(8,128)(2,1)S(1)} %collective-permute-done.7.refs_4_.refs_2_, ...), custom_call_target="tpu_custom_call" | custom-call | bytes 5505024 | tf_op jit(solution)/shard_map/pallas_call | solution.py:834
  151.2 1.9 collective-permute-done.25.refs_1_
  158.7 19.0 %collective-permute-done.28.refs_1_ = bf16[256,256]{1,0:T(8,128)(2,1)S(1)} collective-permute-done((bf16[256,256]{1,0:T(8,128)(2,1)S(1)}, bf16[256,256]{1,0:T(8,128)(2,1)S(1)}, u32[]{:S(2)}, u32[]{:S(2)}) %collective-permute-start.28) | collective-permute-done | bytes 131104 | tf_op jit(solution)/shard_map/ppermute | solution.py:1037
  179.1 5.5 %collective-permute-done.30.refs_1_ = bf16[224,256]{1,0:T(8,128)(2,1)S(1)} collective-permute-done((bf16[224,256]{1,0:T(8,128)(2,1)S(1)}, bf16[224,256]{1,0:T(8,128)(2,1)S(1)}, u32[]{:S(2)}, u32[]{:S(2)}) %collective-permute-start.30) | collective-permute-done | bytes 114720 | tf_op jit(solution)/shard_map/ppermute | solution.py:1058
  188.7 5.0 %collective-permute-done.31.refs_1_ = bf16[448,256]{1,0:T(8,128)(2,1)S(1)} collective-permute-done((bf16[448,256]{1,0:T(8,128)(2,1)S(1)}, bf16[448,256]{1,0:T(8,128)(2,1)S(1)}, u32[]{:S(2)}, u32[]{:S(2)}) %collective-permute-start.31) | collective-permute-done | bytes 229408 | tf_op jit(solution)/shard_map/ppermute | solution.py:1058
  193.7 4.6 %collective-permute-done.32.refs_2_ = bf16[448,256]{1,0:T(8,128)(2,1)S(1)} collective-permute-done((bf16[448,256]{1,0:T(8,128)(2,1)S(1)}, bf16[448,256]{1,0:T(8,128)(2,1)S(1)}, u32[]{:S(2)}, u32[]{:S(2)}) %collective-permute-start.32) | collective-permute-done | bytes 229408 | tf_op jit(solution)/shard_map/ppermute | solution.py:1058
  199.0 2.3 %shard_map.167 = f32[8,384,256]{2,1,0:T(8,128)} custom-call(s32[13]{0:T(128)S(1)} %stack.42.info, bf16[768,256]{1,0:T(8,128)(2,1)S(1)} %collective-permute-done.18.refs_0_, bf16[768,256]{1,0:T(8,128)(2,1)S(1)} %collective-permute-done.26.refs_1_, bf16[768,256]{1,0:T(8,128)(2,1)S(1)} %collective-permute-done.19.refs_2_, ...), custom_call_target="tpu_custom_call" | custom-call | bytes 5505024 | tf_op jit(solution)/shard_map/pallas_call | solution.py:834
  201.5 2.7 %shard_map.170 = (f32[2,256,512]{2,1,0:T(8,128)}, f32[2,256,256]{2,1,0:T(8,128)}, f32[2,256,512]{2,1,0:T(8,128)}, f32[2,512,256]{2,1,0:T(8,128)}, f32[2,2,256]{2...) custom-call(s32[13]{0:T(128)S(1)} %stack.42.info, bf16[1792,256]{1,0:T(8,128)(2,1)S(1)} %shard_map.169.refs_0_, ...), custom_call_target="tpu_custom_call" | custom-call | bytes 5529824 | tf_op jit(solution)/shard_map/pallas_call | solution.py:834
  (95 shorter events, 46.0 us)
Async XLA Ops:
  4.9 31.8 %collective-permute-start.4 = (bf16[768,256]{1,0:T(8,128)(2,1)S(1)}, bf16[768,256]{1,0:T(8,128)(2,1)S(1)}, u32[]{:S(2)}, u32[]{:S(2)}) collective-permute-start(bf16[768,256]{1,0:T(8,128)(2,1)S(1)} %maximum_select_fusion.3), channel_id=1, source_target_pairs={{0,10},{1,14},{2,8},{3,12},{4,11},{5,15},{6,9},{7,13},{8,2},{9,6},... | collective-permute-start | bytes 1179656 | tf_op jit(solution)/shard_map/ppermute | solution.py:947
  10.0 35.0 %collective-permute-start.3 = (bf16[768,256]{1,0:T(8,128)(2,1)S(1)}, bf16[768,256]{1,0:T(8,128)(2,1)S(1)}, u32[]{:S(2)}, u32[]{:S(2)}) collective-permute-start(bf16[768,256]{1,0:T(8,128)(2,1)S(1)} %maximum_select_fusion.2), channel_id=1, source_target_pairs={{0,8},{1,12},{2,10},{3,14},{4,9},{5,13},{6,11},{7,15},{8,0},{9,4},... | collective-permute-start | bytes 1179656 | tf_op jit(solution)/shard_map/ppermute | solution.py:947
  10.6 34.4 %collective-permute-start.2 = (bf16[768,256]{1,0:T(8,128)(2,1)S(1)}, bf16[768,256]{1,0:T(8,128)(2,1)S(1)}, u32[]{:S(2)}, u32[]{:S(2)}) collective-permute-start(bf16[768,256]{1,0:T(8,128)(2,1)S(1)} %maximum_select_fusion.1), channel_id=1, source_target_pairs={{0,2},{1,6},{2,0},{3,4},{4,3},{5,7},{6,1},{7,5},{8,10},{9,14},{10,... | collective-permute-start | bytes 1179656 | tf_op jit(solution)/shard_map/ppermute | solution.py:947
  11.0 33.9 %collective-permute-start.1 = (bf16[768,256]{1,0:T(8,128)(2,1)S(1)}, bf16[768,256]{1,0:T(8,128)(2,1)S(1)}, u32[]{:S(2)}, u32[]{:S(2)}) collective-permute-start(bf16[768,256]{1,0:T(8,128)(2,1)S(1)} %maximum_select_fusion), channel_id=1, source_target_pairs={{0,0},{1,4},{2,2},{3,6},{4,1},{5,5},{6,3},{7,7},{8,8},{9,12},{10,1... | collective-permute-start | bytes 1179656 | tf_op jit(solution)/shard_map/ppermute | solution.py:947
  82.1 20.0 %collective-permute-start.7 = (bf16[768,256]{1,0:T(8,128)(2,1)S(1)}, bf16[768,256]{1,0:T(8,128)(2,1)S(1)}, u32[]{:S(2)}, u32[]{:S(2)}) collective-permute-start(bf16[768,256]{1,0:T(8,128)(2,1)S(1)} %get-tuple-element.112), channel_id=1, source_target_pairs={{0,8},{1,12},{2,10},{3,14},{4,9},{5,13},{6,11},{7,15},{8,0},{9,4},... | collective-permute-start | bytes 1179656 | tf_op jit(solution)/shard_map/ppermute | solution.py:954
  84.7 17.3 %collective-permute-start.12 = (bf16[160,256]{1,0:T(8,128)(2,1)S(1)}, bf16[160,256]{1,0:T(8,128)(2,1)S(1)}, u32[]{:S(2)}, u32[]{:S(2)}) collective-permute-start(bf16[160,256]{1,0:T(8,128)(2,1)S(1)} %get-tuple-element.131), channel_id=1, source_target_pairs={{0,16},{1,17},{2,18},{3,19},{4,20},{5,21},{6,22},{7,23},{8,24},{9,... | collective-permute-start | bytes 245768 | tf_op jit(solution)/shard_map/ppermute | solution.py:1037
  86.3 15.8 %collective-permute-start.13 = (bf16[160,256]{1,0:T(8,128)(2,1)S(1)}, bf16[160,256]{1,0:T(8,128)(2,1)S(1)}, u32[]{:S(2)}, u32[]{:S(2)}) collective-permute-start(bf16[160,256]{1,0:T(8,128)(2,1)S(1)} %get-tuple-element.132), channel_id=1, source_target_pairs={{0,2},{1,3},{2,0},{3,1},{4,6},{5,7},{6,4},{7,5},{8,10},{9,11},{10,... | collective-permute-start | bytes 245768 | tf_op jit(solution)/shard_map/ppermute | solution.py:1037
  86.8 15.3 %collective-permute-start.14 = (bf16[160,256]{1,0:T(8,128)(2,1)S(1)}, bf16[160,256]{1,0:T(8,128)(2,1)S(1)}, u32[]{:S(2)}, u32[]{:S(2)}) collective-permute-start(bf16[160,256]{1,0:T(8,128)(2,1)S(1)} %get-tuple-element.133), channel_id=1, source_target_pairs={{0,18},{1,19},{2,16},{3,17},{4,22},{5,23},{6,20},{7,21},{8,26},{9,... | collective-permute-start | bytes 245768 | tf_op jit(solution)/shard_map/ppermute | solution.py:1037
  103.4 20.0 %collective-permute-start.10 = (bf16[768,256]{1,0:T(8,128)(2,1)S(1)}, bf16[768,256]{1,0:T(8,128)(2,1)S(1)}, u32[]{:S(2)}, u32[]{:S(2)}) collective-permute-start(bf16[768,256]{1,0:T(8,128)(2,1)S(1)} %get-tuple-element.117), channel_id=1, source_target_pairs={{0,10},{1,14},{2,8},{3,12},{4,11},{5,15},{6,9},{7,13},{8,2},{9,6},... | collective-permute-start | bytes 1179656 | tf_op jit(solution)/shard_map/ppermute | solution.py:954
  103.4 20.5 %collective-permute-start.9 = (bf16[768,256]{1,0:T(8,128)(2,1)S(1)}, bf16[768,256]{1,0:T(8,128)(2,1)S(1)}, u32[]{:S(2)}, u32[]{:S(2)}) collective-permute-start(bf16[768,256]{1,0:T(8,128)(2,1)S(1)} %get-tuple-element.115), channel_id=1, source_target_pairs={{0,2},{1,6},{2,0},{3,4},{4,3},{5,7},{6,1},{7,5},{8,10},{9,14},{10,... | collective-permute-start | bytes 1179656 | tf_op jit(solution)/shard_map/ppermute | solution.py:954
  104.4 19.5 %collective-permute-start.8 = (bf16[768,256]{1,0:T(8,128)(2,1)S(1)}, bf16[768,256]{1,0:T(8,128)(2,1)S(1)}, u32[]{:S(2)}, u32[]{:S(2)}) collective-permute-start(bf16[768,256]{1,0:T(8,128)(2,1)S(1)} %get-tuple-element.113), channel_id=1, source_target_pairs={{0,0},{1,4},{2,2},{3,6},{4,1},{5,5},{6,3},{7,7},{8,8},{9,12},{10,1... | collective-permute-start | bytes 1179656 | tf_op jit(solution)/shard_map/ppermute | solution.py:954
  129.5 18.2 %collective-permute-start.17 = (bf16[4,384,256]{2,1,0:T(8,128)(2,1)S(1)}, bf16[4,384,256]{2,1,0:T(8,128)(2,1)S(1)}, u32[]{:S(2)}, u32[]{:S(2)}) collective-permute-start(bf16[4,384,256]{2,1,0:T(8,128)(2,1)S(1)} %shard_map.160), channel_id=1, source_target_pairs={{0,1},{1,0},{2,3},{3,2},{4,5},{5,4},{6,7},{7,6},{8,9},{9,8},{10,11... | collective-permute-start | bytes 2359304 | tf_op jit(solution)/shard_map/ppermute | solution.py:959
  130.2 20.9 %collective-permute-start.19 = (bf16[768,256]{1,0:T(8,128)(2,1)S(1)}, bf16[768,256]{1,0:T(8,128)(2,1)S(1)}, u32[]{:S(2)}, u32[]{:S(2)}) collective-permute-start(bf16[768,256]{1,0:T(8,128)(2,1)S(1)} %get-tuple-element.165), channel_id=1, source_target_pairs={{0,8},{1,12},{2,10},{3,14},{4,9},{5,13},{6,11},{7,15},{8,0},{9,4},... | collective-permute-start | bytes 1179656 | tf_op jit(solution)/shard_map/ppermute | solution.py:954
  135.0 10.5 %collective-permute-start.23 = (bf16[320,256]{1,0:T(8,128)(2,1)S(1)}, bf16[320,256]{1,0:T(8,128)(2,1)S(1)}, u32[]{:S(2)}, u32[]{:S(2)}) collective-permute-start(bf16[320,256]{1,0:T(8,128)(2,1)S(1)} %get-tuple-element.173), channel_id=1, source_target_pairs={{0,2},{1,3},{2,0},{3,1},{4,6},{5,7},{6,4},{7,5},{8,10},{9,11},{10,... | collective-permute-start | bytes 491528 | tf_op jit(solution)/shard_map/ppermute | solution.py:1037
  136.0 9.5 %collective-permute-start.24 = (bf16[320,256]{1,0:T(8,128)(2,1)S(1)}, bf16[320,256]{1,0:T(8,128)(2,1)S(1)}, u32[]{:S(2)}, u32[]{:S(2)}) collective-permute-start(bf16[320,256]{1,0:T(8,128)(2,1)S(1)} %get-tuple-element.174), channel_id=1, source_target_pairs={{0,18},{1,19},{2,16},{3,17},{4,22},{5,23},{6,20},{7,21},{8,26},{9,... | collective-permute-start | bytes 491528 | tf_op jit(solution)/shard_map/ppermute | solution.py:1037
  146.2 6.9 %collective-permute-start.25 = (bf16[256,256]{1,0:T(8,128)(2,1)S(1)}, bf16[256,256]{1,0:T(8,128)(2,1)S(1)}, u32[]{:S(2)}, u32[]{:S(2)}) collective-permute-start(bf16[256,256]{1,0:T(8,128)(2,1)S(1)} %get-tuple-element.176), channel_id=1, source_target_pairs={{0,4},{1,5},{2,6},{3,7},{4,0},{5,1},{6,2},{7,3},{8,12},{9,13},{10,... | collective-permute-start | bytes 393224 | tf_op jit(solution)/shard_map/ppermute | solution.py:1037
  147.0 10.1 %collective-permute-start.18 = (bf16[768,256]{1,0:T(8,128)(2,1)S(1)}, bf16[768,256]{1,0:T(8,128)(2,1)S(1)}, u32[]{:S(2)}, u32[]{:S(2)}) collective-permute-start(bf16[768,256]{1,0:T(8,128)(2,1)S(1)} %get-tuple-element.163), channel_id=1, source_target_pairs={{0,0},{1,4},{2,2},{3,6},{4,1},{5,5},{6,3},{7,7},{8,8},{9,12},{10,1... | collective-permute-start | bytes 1179656 | tf_op jit(solution)/shard_map/ppermute | solution.py:954
  153.1 25.2 %collective-permute-start.27 = (bf16[768,256]{1,0:T(8,128)(2,1)S(1)}, bf16[768,256]{1,0:T(8,128)(2,1)S(1)}, u32[]{:S(2)}, u32[]{:S(2)}) collective-permute-start(bf16[768,256]{1,0:T(8,128)(2,1)S(1)} %get-tuple-element.179), channel_id=1, source_target_pairs={{0,10},{1,14},{2,8},{3,12},{4,11},{5,15},{6,9},{7,13},{8,2},{9,6},... | collective-permute-start | bytes 1179656 | tf_op jit(solution)/shard_map/ppermute | solution.py:954
  154.5 23.8 %collective-permute-start.26 = (bf16[768,256]{1,0:T(8,128)(2,1)S(1)}, bf16[768,256]{1,0:T(8,128)(2,1)S(1)}, u32[]{:S(2)}, u32[]{:S(2)}) collective-permute-start(bf16[768,256]{1,0:T(8,128)(2,1)S(1)} %get-tuple-element.177), channel_id=1, source_target_pairs={{0,2},{1,6},{2,0},{3,4},{4,3},{5,7},{6,1},{7,5},{8,10},{9,14},{10,... | collective-permute-start | bytes 1179656 | tf_op jit(solution)/shard_map/ppermute | solution.py:954
  157.2 20.5 %collective-permute-start.28 = (bf16[256,256]{1,0:T(8,128)(2,1)S(1)}, bf16[256,256]{1,0:T(8,128)(2,1)S(1)}, u32[]{:S(2)}, u32[]{:S(2)}) collective-permute-start(bf16[256,256]{1,0:T(8,128)(2,1)S(1)} %get-tuple-element.183.refs_0_), channel_id=1, source_target_pairs={{0,8},{1,9},{2,10},{3,11},{4,12},{5,13},{6,14},{7,15},{8,0},{9,1},... | collective-permute-start | bytes 393224 | tf_op jit(solution)/shard_map/ppermute | solution.py:1037
  178.9 20.0 %collective-permute-start.29 = (bf16[4,384,256]{2,1,0:T(8,128)(2,1)S(1)}, bf16[4,384,256]{2,1,0:T(8,128)(2,1)S(1)}, u32[]{:S(2)}, u32[]{:S(2)}) collective-permute-start(bf16[4,384,256]{2,1,0:T(8,128)(2,1)S(1)} %shard_map.166), channel_id=1, source_target_pairs={{0,1},{1,0},{2,3},{3,2},{4,5},{5,4},{6,7},{7,6},{8,9},{9,8},{10,11... | collective-permute-start | bytes 2359304 | tf_op jit(solution)/shard_map/ppermute | solution.py:959
  185.1 8.6 %collective-permute-start.31 = (bf16[448,256]{1,0:T(8,128)(2,1)S(1)}, bf16[448,256]{1,0:T(8,128)(2,1)S(1)}, u32[]{:S(2)}, u32[]{:S(2)}) collective-permute-start(bf16[448,256]{1,0:T(8,128)(2,1)S(1)} %shard_map.168.refs_0_), channel_id=1, source_target_pairs={{0,16},{1,17},{2,18},{3,19},{4,20},{5,21},{6,22},{7,23},{8,24},{9,... | collective-permute-start | bytes 688136 | tf_op jit(solution)/shard_map/ppermute | solution.py:1058
  186.5 11.8 %collective-permute-start.32 = (bf16[448,256]{1,0:T(8,128)(2,1)S(1)}, bf16[448,256]{1,0:T(8,128)(2,1)S(1)}, u32[]{:S(2)}, u32[]{:S(2)}) collective-permute-start(bf16[448,256]{1,0:T(8,128)(2,1)S(1)} %shard_map.168.refs_0_), channel_id=1, source_target_pairs={{0,2},{1,3},{2,0},{3,1},{4,6},{5,7},{6,4},{7,5},{8,10},{9,11},{10,... | collective-permute-start | bytes 688136 | tf_op jit(solution)/shard_map/ppermute | solution.py:1058
  187.5 10.8 %collective-permute-start.33 = (bf16[448,256]{1,0:T(8,128)(2,1)S(1)}, bf16[448,256]{1,0:T(8,128)(2,1)S(1)}, u32[]{:S(2)}, u32[]{:S(2)}) collective-permute-start(bf16[448,256]{1,0:T(8,128)(2,1)S(1)} %shard_map.168.refs_0_), channel_id=1, source_target_pairs={{0,18},{1,19},{2,16},{3,17},{4,22},{5,23},{6,20},{7,21},{8,26},{9,... | collective-permute-start | bytes 688136 | tf_op jit(solution)/shard_map/ppermute | solution.py:1058
  (18 other events, 70.8 us)

commit v7 on v6

--- a/solution.py
+++ b/solution.py
@@ -245,10 +245,11 @@
         squares[...] = jnp.zeros_like(squares)
 
     limit = info[1]
-    start = step * TB
+    count = q.shape[0]
+    start = step * count
     base = info[0] * n + start
     outs = []
-    for sub in range(TB // WIN):
+    for sub in range(count // WIN):
         near = pl.ds(pl.multiple_of(start + sub * WIN, WIN), 2 * WIN)
         keys = ext[near, :qw]
         values = ext[near, qw:]
@@ -722,15 +723,16 @@
     put_riders(small[...], message, rows.shape[0])
 
 
-def order_kernel(digits, *refs, stage):
-    pieces, out = refs[:-1], refs[-1]
+def order_kernel(digits, *refs, stage, count):
+    pieces, out = refs[:count], refs[-1]
     rows = pieces[0].shape[0]
     for c, piece in enumerate(pieces):
         out[pl.ds(pl.multiple_of((digits[9 + stage] ^ c) * rows, 16), rows)] = piece[...]
 
 
 def assemble_kernel(info, *refs):
-    own, other, out, wide, sems = refs[:4], *refs[4:]
+    own, other, out, token, wide, sems = refs[:4], *refs[4:]
+    token[...] = jnp.zeros_like(token)
     core = info[0]
     rows = out.shape[1]
 
@@ -819,7 +821,7 @@
 VMEM = pl.BlockSpec(memory_space=pltpu.VMEM)
 
 
-def call(kernel, info, operands, specs, outs, out_specs, scratch=(), grid=(), work=0, aliases={}):
+def call(kernel, info, operands, specs, outs, out_specs, scratch=(), grid=(), work=0, aliases={}, limit=VMEM_LIMIT):
     moved = sum(math.prod(a.shape) * a.dtype.itemsize for a in list(operands) + jax.tree.leaves(outs))
     single = not isinstance(outs, list)
     views = list(specs) + ([out_specs] if single else list(out_specs))
@@ -842,7 +844,7 @@
         ),
         out_shape=outs,
         input_output_aliases=aliases,
-        compiler_params=pltpu.CompilerParams(vmem_limit_bytes=VMEM_LIMIT),
+        compiler_params=pltpu.CompilerParams(vmem_limit_bytes=limit),
         cost_estimate=pl.CostEstimate(flops=int(work * 1.15e9), bytes_accessed=moved, transcendentals=0),
     )(info, *operands)
 
@@ -855,8 +857,8 @@
     return lambda ref: ref.at[pl.ds(pl.multiple_of(pl.program_id(0) * TB, TB), TB)]
 
 
-def tiled_after_window(ref):
-    return ref.at[pl.ds(pl.multiple_of(pl.program_id(0) * TB + WIN, WIN), TB)]
+def after_window(ref):
+    return ref.at[pl.ds(WIN, ref.shape[0] - WIN)]
 
 
 def last_rows(ref):
@@ -989,8 +991,8 @@
     outs = [rows_low, rows_q, rows_kv, rows_low, rows_stat, rows_hidden, rows_hidden, rows_wide, squares_shape]
     z, q1, kv1, o0, lse0, active0, slope0, mid0, squares0 = call(
         second_kernel, info, [x, q0, kv0, halo0, g0, b0, w_out[0], w_up[0], w_down[0], g1, b1, w_qkv[1]],
-        [tiled_after_window, tiled(q0)] + [whole(a) for a in (kv0, halo0, g0, b0, w_out[0], w_up[0], w_down[0], g1, b1, w_qkv[1])],
-        outs, [tiled(o) for o in outs[:-1]] + [whole(outs[-1])], [ext], steps, work=15,
+        [after_window] + [VMEM] * 11, outs, [VMEM] * len(outs), [ext], (1,), work=15,
+        limit=2 * VMEM_LIMIT,
     )
     kv_other = lax.ppermute(kv1, "section", first_to_second)
 
@@ -1055,9 +1057,12 @@
         return made[:sent], made[sent] if ways > 1 else None, made[-1] if riders else None
 
     def gather(piece, masks, number):
-        pieces = [piece] + [lax.ppermute(piece, ("dp", "section"), way) for _, way in partners(masks)[1]]
-        out = shape((len(pieces) * piece.shape[0], width), BF16)
-        return call(functools.partial(order_kernel, stage=number), info, pieces, [VMEM] * len(pieces), out, VMEM)
+        return in_order([piece] + [lax.ppermute(piece, ("dp", "section"), way) for _, way in partners(masks)[1]], number)
+
+    def in_order(pieces, number, awaited=()):
+        out = shape((len(pieces) * pieces[0].shape[0], width), BF16)
+        kernel = functools.partial(order_kernel, stage=number, count=len(pieces))
+        return call(kernel, info, pieces + list(awaited), [VMEM] * len(pieces) + [ANY] * len(awaited), out, VMEM)
 
     messages, kept_a, _ = stage([(keep_a, [pair(send_a)])], None, 4, 1)
     got_a = send_all(messages, plane)
@@ -1101,19 +1106,21 @@
     )
 
     def assemble(own, other):
-        out = call(
-            assemble_kernel, info, own + [other], [VMEM] * 5, shape((images, rows_piece, width), F32), ANY,
+        outs = [shape((images, rows_piece, width), F32), shape((8, 128), F32)]
+        out, token = call(
+            assemble_kernel, info, own + [other], [VMEM] * 5, outs, [ANY, VMEM],
             [pltpu.VMEM((images, rows_piece, width), F32), dma((images,))],
         )
         if rep > 1:
             out = lax.dynamic_slice_in_dim(out, twin * rows_dev, rows_dev, 1)
-        return out
+        return out, token
 
     backward_back = [send_back(local0, 0, 0), None, send_back(cross0, 1, 0), None]
-    groups = [(keep_early, [got_early]), (keep_late, [pair(send_late)])]
+    got_late = pair(send_late)
+    groups = [(keep_early, [got_early]), (keep_late, [got_late])]
     messages, kept, small = stage(groups, small, 4, 1)
     forward_trade = trade(forward_back, send_late)
-    forward_rows = assemble(forward_back, forward_trade)
+    forward_rows, forward_token = assemble(forward_back, forward_trade)
     groups = [(kept_a, got_a), (kept, send_all(messages, plane))]
     number = 2
     scattered = []
@@ -1123,8 +1130,8 @@
         scattered.append(number)
         number += 1
     scattered_rows = groups[-1][1]
-    backward_back[3] = send_back(after(cross1, backward_back[2], *scattered_rows, forward_rows), 1, 1)
-    backward_back[1] = send_back(after(local1, backward_back[2], *scattered_rows, forward_rows), 0, 1)
+    backward_back[3] = send_back(after(cross1, backward_back[2]), 1, 1)
+    backward_back[1] = send_back(after(local1, backward_back[2], *scattered_rows), 0, 1)
     (both,), _, small = stage(groups, small, 1, 0)
     both = after(both, backward_back[0], backward_back[2])
     rows_shape = shape((both.shape[0] - rider_rows, width), BF16)
@@ -1138,10 +1145,9 @@
     for number in scattered[::-1]:
         both = gather(both, [rest[number - 2]], number)
     backward_trade = trade(backward_back, rows)
-    both = gather(both, plane, 1)
-    both = after(both, backward_trade)
+    backward_rows, backward_token = assemble(backward_back, backward_trade)
+    both = in_order([both] + send_all([both] * 3, plane), 1, [backward_token, forward_token])
     theirs = pair(both)
-    backward_rows = assemble(backward_back, backward_trade)
     outs = [shape(w.shape, F32) for w in (w_qkv, w_out, w_up, w_down, norm_gain, norm_bias)] + [shape((6, images), F32)]
     sizes = (feed_rows, slab_rows, mix_rows, 1 << len(plane))
     grads = call(

time: 204 us -> 202 us (level)
  waiting for transfers between devices: 95.3 us -> 90.9 us
  starting transfers between devices: 36.9 us -> 39.7 us
    ppermute x4 -> x1, waiting for transfers between devices: 15.1 us -> 5.07 us  [gather(): lax.ppermute(piece, ('dp', 'section'), way)]
    ppermute x8, waiting for transfers between devices: 9.87 us -> 16.7 us  [send_back(): return lax.ppermute(message, 'section', route(pairs))]
    ppermute x8 -> x11, starting transfers between devices: 9.4 us -> 13.9 us  [send_all(): lax.ppermute(m, ('dp', 'section'), way)]
    ppermute x4 -> x1, starting transfers between devices: 3.62 us -> 0.06 us  [gather(): lax.ppermute(piece, ('dp', 'section'), way)]
    ppermute x8 -> x11, waiting for transfers between devices: 29.4 us -> 26.4 us  [send_all(): lax.ppermute(m, ('dp', 'section'), way)]
    ppermute x2, starting transfers between devices: 0.28 us -> 2.88 us  [trade(): return lax.ppermute(send, 'section', swap)]
  transfers between devices with their start and end apart: 35 -> 35, of which waited for: 20 -> 20; matrix products, arithmetic and copies ran while one was open for 1% -> 1% of each run, Pallas kernels for 16% -> 17%
where the time goes in v7:
time: 202 us
  waiting for transfers between devices  90.9 us (45%)
  Pallas kernels  66.4 us (33%)
  starting transfers between devices  39.7 us (20%)
  local copies, waits for them, and re-layouts  3.08 us (2%)
    pallas_call x20, Pallas kernels, call(): pl.pallas_call(body_of, grid_spec=pltpu.PrefetchScalarGridSpec(num_scalar...  66.4 us
    ppermute x4, waiting for transfers between devices, body(): received[t] = lax.ppermute(message, 'section', route(pairs))  33.2 us
    ppermute x11, waiting for transfers between devices, send_all(): lax.ppermute(m, ('dp', 'section'), way)  26.4 us
    ppermute x8, waiting for transfers between devices, send_back(): return lax.ppermute(message, 'section', route(pairs))  16.7 us
    ppermute x11, starting transfers between devices, send_all(): lax.ppermute(m, ('dp', 'section'), way)  13.9 us
    ppermute x8, starting transfers between devices, send_back(): return lax.ppermute(message, 'section', route(pairs))  8.2 us
    ppermute x4, starting transfers between devices, body(): received[t] = lax.ppermute(message, 'section', route(pairs))  6.37 us
    ppermute x1, waiting for transfers between devices, gather(): lax.ppermute(piece, ('dp', 'section'), way)  5.07 us
  transfers between devices with their start and end apart: 35, of which 20 were waited for; matrix products, arithmetic and copies ran while one was open for 1% of the time, Pallas kernels for 17%

profile of v7, /device:TPU:0, one launch (start us, length us, event | category | flops | bytes accessed | tf_op | source)
XLA Modules:
  0.0 201.9 jit_solution(9650456447448458661)
XLA Ops:
  4.9 5.0 %collective-permute-start.4 = (bf16[768,256]{1,0:T(8,128)(2,1)S(1)}, bf16[768,256]{1,0:T(8,128)(2,1)S(1)}, u32[]{:S(2)}, u32[]{:S(2)}) collective-permute-start(bf16[768,256]{1,0:T(8,128)(2,1)S(1)} %maximum_select_fusion.3), channel_id=1, source_target_pairs={{0,10},{1,14},{2,8},{3,12},{4,11},{5,15},{6,9},{7,13},{8,2},{9,6},... | collective-permute-start | bytes 1179656 | tf_op jit(solution)/shard_map/ppermute | solution.py:949
  11.8 24.9 %collective-permute-done.4.refs_3_ = bf16[768,256]{1,0:T(8,128)(2,1)S(1)} collective-permute-done((bf16[768,256]{1,0:T(8,128)(2,1)S(1)}, bf16[768,256]{1,0:T(8,128)(2,1)S(1)}, u32[]{:S(2)}, u32[]{:S(2)}) %collective-permute-start.4) | collective-permute-done | bytes 393248 | tf_op jit(solution)/shard_map/ppermute | solution.py:949
  36.7 8.3 %collective-permute-done.3.refs_2_ = bf16[768,256]{1,0:T(8,128)(2,1)S(1)} collective-permute-done((bf16[768,256]{1,0:T(8,128)(2,1)S(1)}, bf16[768,256]{1,0:T(8,128)(2,1)S(1)}, u32[]{:S(2)}, u32[]{:S(2)}) %collective-permute-start.3) | collective-permute-done | bytes 393248 | tf_op jit(solution)/shard_map/ppermute | solution.py:949
  49.3 6.6 %shard_map.152 = (bf16[1536,256]{1,0:T(8,128)(2,1)S(1)}, bf16[1536,128]{1,0:T(8,128)(2,1)S(1)}, bf16[1536,384]{1,0:T(8,128)(2,1)S(1)}, bf16[1536,256]{1,0:T(8,12...) custom-call(s32[13]{0:T(128)S(1)} %stack.42.info, ...), custom_call_target="tpu_custom_call" | custom-call | flops 17250000896 | bytes 12124160 | tf_op jit(solution)/shard_map/pallas_call | solution.py:836
  55.9 2.5 %collective-permute-start.6 = (bf16[1536,384]{1,0:T(8,128)(2,1)S(1)}, bf16[1536,384]{1,0:T(8,128)(2,1)S(1)}, u32[]{:S(2)}, u32[]{:S(2)}) collective-permute-start(bf16[1536,384]{1,0:T(8,128)(2,1)S(1)} %get-tuple-element.110.refs_1_.refs_5_), channel_id=1, source_target_pairs={{0,1},{2,3},{4,5},{6,7},{8,9},{10,11},{12,13},{14,15},{16,17},{18,... | collective-permute-start | bytes 3538952 | tf_op jit(solution)/shard_map/ppermute | solution.py:997
  60.6 4.1 %shard_map.153 = (bf16[1536,128]{1,0:T(8,128)(2,1)S(1)}, bf16[3072,128]{1,0:T(8,128)(2,1)S(1)}, bf16[3072,256]{1,0:T(8,128)(2,1)S(1)}, f32[1536,256]{1,0:T(8,128)S(1)}, f32[1536,128]{1,0:T(8,128)S(1)}) custom-call(s32[13]{0:T(128)S(1)} %stack.42.info, bf16[1536,128]{1,0:T(8,128)(2,1)S(1)} %get-tuple-element.109.refs_0_.refs_4_, ...), custom_call_target="tpu_custom_call" | custom-call | flops 16099999744 | bytes 7864320 | tf_op jit(solution)/shard_map/pallas_call | solution.py:836
  64.7 16.1 %shard_map.154 = (bf16[768,256]{1,0:T(8,128)(2,1)S(1)}, bf16[768,256]{1,0:T(8,128)(2,1)S(1)}, bf16[768,256]{1,0:T(8,128)(2,1)S(1)}, bf16[768,256]{1,0:T(8,128)(2...) custom-call(s32[13]{0:T(128)S(1)} %stack.42.info, ...), custom_call_target="tpu_custom_call" | custom-call | flops 27599998976 | bytes 17215488 | tf_op jit(solution)/shard_map/pallas_call | solution.py:836
  87.5 7.0 %shard_map.155 = (f32[1536,128]{1,0:T(8,128)S(1)}, f32[1536,384]{1,0:T(8,128)S(1)}, bf16[1536,384]{1,0:T(8,128)(2,1)S(1)}) custom-call(s32[13]{0:T(128)S(1)} %stack.42.info, bf16[1536,128]{1,0:T(8,128)(2,1)S(1)} %get-tuple-element.121.refs_0_, bf16[3072,128]{1,0:T(8,128)(2,1)S(1)} %get-tuple-element.122.refs_1_, ...), custom_call_target="tpu_custom_call" | custom-call | flops 20700000256 | bytes 11993088 | tf_op jit(solution)/shard_map/pallas_call | solution.py:836
  94.5 6.7 %collective-permute-done.7.refs_4_.refs_2_ = bf16[768,256]{1,0:T(8,128)(2,1)S(1)} collective-permute-done((bf16[768,256]{1,0:T(8,128)(2,1)S(1)}, bf16[768,256]{1,0:T(8,128)(2,1)S(1)}, u32[]{:S(2)}, u32[]{:S(2)}) %collective-permute-start.7) | collective-permute-done | bytes 393248 | tf_op jit(solution)/shard_map/ppermute | solution.py:956
  106.0 15.3 %shard_map.157 = (bf16[768,256]{1,0:T(8,128)(2,1)S(1)}, bf16[768,256]{1,0:T(8,128)(2,1)S(1)}, bf16[768,256]{1,0:T(8,128)(2,1)S(1)}, bf16[768,256]{1,0:T(8,128)(2...) custom-call(s32[13]{0:T(128)S(1)} %stack.42.info, ...), custom_call_target="tpu_custom_call" | custom-call | flops 23000000512 | bytes 20701184 | tf_op jit(solution)/shard_map/pallas_call | solution.py:836
  129.0 2.4 %collective-permute-start.19 = (bf16[768,256]{1,0:T(8,128)(2,1)S(1)}, bf16[768,256]{1,0:T(8,128)(2,1)S(1)}, u32[]{:S(2)}, u32[]{:S(2)}) collective-permute-start(bf16[768,256]{1,0:T(8,128)(2,1)S(1)} %get-tuple-element.169), channel_id=1, source_target_pairs={{0,8},{1,12},{2,10},{3,14},{4,9},{5,13},{6,11},{7,15},{8,0},{9,4},... | collective-permute-start | bytes 1179656 | tf_op jit(solution)/shard_map/ppermute | solution.py:956
  136.4 2.7 %collective-permute-done.22.refs_5_ = bf16[320,256]{1,0:T(8,128)(2,1)S(1)} collective-permute-done((bf16[320,256]{1,0:T(8,128)(2,1)S(1)}, bf16[320,256]{1,0:T(8,128)(2,1)S(1)}, u32[]{:S(2)}, u32[]{:S(2)}) %collective-permute-start.22) | collective-permute-done | bytes 163872 | tf_op jit(solution)/shard_map/ppermute | solution.py:1039
  139.1 5.2 %collective-permute-done.23.refs_6_ = bf16[320,256]{1,0:T(8,128)(2,1)S(1)} collective-permute-done((bf16[320,256]{1,0:T(8,128)(2,1)S(1)}, bf16[320,256]{1,0:T(8,128)(2,1)S(1)}, u32[]{:S(2)}, u32[]{:S(2)}) %collective-permute-start.23) | collective-permute-done | bytes 163872 | tf_op jit(solution)/shard_map/ppermute | solution.py:1039
  145.6 4.0 %collective-permute-done.19.refs_2_ = bf16[768,256]{1,0:T(8,128)(2,1)S(1)} collective-permute-done((bf16[768,256]{1,0:T(8,128)(2,1)S(1)}, bf16[768,256]{1,0:T(8,128)(2,1)S(1)}, u32[]{:S(2)}, u32[]{:S(2)}) %collective-permute-start.19) | collective-permute-done | bytes 393248 | tf_op jit(solution)/shard_map/ppermute | solution.py:956
  150.0 7.3 %collective-permute-done.25.refs_1_ = bf16[256,256]{1,0:T(8,128)(2,1)S(1)} collective-permute-done((bf16[256,256]{1,0:T(8,128)(2,1)S(1)}, bf16[256,256]{1,0:T(8,128)(2,1)S(1)}, u32[]{:S(2)}, u32[]{:S(2)}) %collective-permute-start.25) | collective-permute-done | bytes 131104 | tf_op jit(solution)/shard_map/ppermute | solution.py:1039
  162.0 5.5 %collective-permute-done.28.refs_1_ = bf16[256,256]{1,0:T(8,128)(2,1)S(1)} collective-permute-done((bf16[256,256]{1,0:T(8,128)(2,1)S(1)}, bf16[256,256]{1,0:T(8,128)(2,1)S(1)}, u32[]{:S(2)}, u32[]{:S(2)}) %collective-permute-start.28) | collective-permute-done | bytes 131104 | tf_op jit(solution)/shard_map/ppermute | solution.py:1039
  168.1 4.2 %collective-permute-done.26.refs_1_ = bf16[768,256]{1,0:T(8,128)(2,1)S(1)} collective-permute-done((bf16[768,256]{1,0:T(8,128)(2,1)S(1)}, bf16[768,256]{1,0:T(8,128)(2,1)S(1)}, u32[]{:S(2)}, u32[]{:S(2)}) %collective-permute-start.26) | collective-permute-done | bytes 393248 | tf_op jit(solution)/shard_map/ppermute | solution.py:956
  173.9 5.1 %collective-permute-done.30.refs_1_ = bf16[224,256]{1,0:T(8,128)(2,1)S(1)} collective-permute-done((bf16[224,256]{1,0:T(8,128)(2,1)S(1)}, bf16[224,256]{1,0:T(8,128)(2,1)S(1)}, u32[]{:S(2)}, u32[]{:S(2)}) %collective-permute-start.30) | collective-permute-done | bytes 114720 | tf_op jit(solution)/shard_map/ppermute | solution.py:1060
  179.6 4.7 %collective-permute-start.31 = (bf16[448,256]{1,0:T(8,128)(2,1)S(1)}, bf16[448,256]{1,0:T(8,128)(2,1)S(1)}, u32[]{:S(2)}, u32[]{:S(2)}) collective-permute-start(bf16[448,256]{1,0:T(8,128)(2,1)S(1)} %shard_map.168.refs_0_), channel_id=1, source_target_pairs={{0,16},{1,17},{2,18},{3,19},{4,20},{5,21},{6,22},{7,23},{8,24},{9,... | collective-permute-start | bytes 688136 | tf_op jit(solution)/shard_map/ppermute | solution.py:1039
  185.8 2.3 %shard_map.161 = (f32[8,384,256]{2,1,0:T(8,128)}, f32[8,128]{1,0:T(8,128)S(1)}) custom-call(s32[13]{0:T(128)S(1)} %stack.42.info, bf16[768,256]{1,0:T(8,128)(2,1)S(1)} %collective-permute-done.8.refs_2_.refs_0_, bf16[768,256]{1,0:T(8,128)(2,1)S(1)} %collective-permute-done.9.refs_3_.refs_1_, bf16[768,256]{1,0:T(8,128)(2,1)S(1)} %collective-permute-done.7.refs_4_.refs_2_, ...), custom_call_target="tpu_custom_call" | custom-call | bytes 5509120 | tf_op jit(solution)/shard_map/pallas_call | solution.py:836
  188.1 2.3 %shard_map.167 = (f32[8,384,256]{2,1,0:T(8,128)}, f32[8,128]{1,0:T(8,128)S(1)}) custom-call(s32[13]{0:T(128)S(1)} %stack.42.info, bf16[768,256]{1,0:T(8,128)(2,1)S(1)} %collective-permute-done.18.refs_0_, bf16[768,256]{1,0:T(8,128)(2,1)S(1)} %collective-permute-done.26.refs_1_, bf16[768,256]{1,0:T(8,128)(2,1)S(1)} %collective-permute-done.19.refs_2_, ...), custom_call_target="tpu_custom_call" | custom-call | bytes 5509120 | tf_op jit(solution)/shard_map/pallas_call | solution.py:836
  190.7 5.3 %collective-permute-done.32.refs_2_ = bf16[448,256]{1,0:T(8,128)(2,1)S(1)} collective-permute-done((bf16[448,256]{1,0:T(8,128)(2,1)S(1)}, bf16[448,256]{1,0:T(8,128)(2,1)S(1)}, u32[]{:S(2)}, u32[]{:S(2)}) %collective-permute-start.32) | collective-permute-done | bytes 229408 | tf_op jit(solution)/shard_map/ppermute | solution.py:1039
  196.8 2.4 %collective-permute-done.34.refs_1_ = bf16[1792,256]{1,0:T(8,128)(2,1)S(1)} collective-permute-done((bf16[1792,256]{1,0:T(8,128)(2,1)S(1)}, bf16[1792,256]{1,0:T(8,128)(2,1)S(1)}, u32[]{:S(2)}, u32[]{:S(2)}) %collective-permute-start.34) | collective-permute-done | bytes 917536 | tf_op jit(solution)/shard_map/ppermute | solution.py:1036
  199.2 2.7 %shard_map.170 = (f32[2,256,512]{2,1,0:T(8,128)}, f32[2,256,256]{2,1,0:T(8,128)}, f32[2,256,512]{2,1,0:T(8,128)}, f32[2,512,256]{2,1,0:T(8,128)}, f32[2,2,256]{2...) custom-call(s32[13]{0:T(128)S(1)} %stack.42.info, bf16[1792,256]{1,0:T(8,128)(2,1)S(1)} %shard_map.169.refs_0_, ...), custom_call_target="tpu_custom_call" | custom-call | bytes 5529824 | tf_op jit(solution)/shard_map/pallas_call | solution.py:836
  (95 shorter events, 48.1 us)
Async XLA Ops:
  4.9 31.8 %collective-permute-start.4 = (bf16[768,256]{1,0:T(8,128)(2,1)S(1)}, bf16[768,256]{1,0:T(8,128)(2,1)S(1)}, u32[]{:S(2)}, u32[]{:S(2)}) collective-permute-start(bf16[768,256]{1,0:T(8,128)(2,1)S(1)} %maximum_select_fusion.3), channel_id=1, source_target_pairs={{0,10},{1,14},{2,8},{3,12},{4,11},{5,15},{6,9},{7,13},{8,2},{9,6},... | collective-permute-start | bytes 1179656 | tf_op jit(solution)/shard_map/ppermute | solution.py:949
  10.0 35.0 %collective-permute-start.3 = (bf16[768,256]{1,0:T(8,128)(2,1)S(1)}, bf16[768,256]{1,0:T(8,128)(2,1)S(1)}, u32[]{:S(2)}, u32[]{:S(2)}) collective-permute-start(bf16[768,256]{1,0:T(8,128)(2,1)S(1)} %maximum_select_fusion.2), channel_id=1, source_target_pairs={{0,8},{1,12},{2,10},{3,14},{4,9},{5,13},{6,11},{7,15},{8,0},{9,4},... | collective-permute-start | bytes 1179656 | tf_op jit(solution)/shard_map/ppermute | solution.py:949
  10.6 34.4 %collective-permute-start.2 = (bf16[768,256]{1,0:T(8,128)(2,1)S(1)}, bf16[768,256]{1,0:T(8,128)(2,1)S(1)}, u32[]{:S(2)}, u32[]{:S(2)}) collective-permute-start(bf16[768,256]{1,0:T(8,128)(2,1)S(1)} %maximum_select_fusion.1), channel_id=1, source_target_pairs={{0,2},{1,6},{2,0},{3,4},{4,3},{5,7},{6,1},{7,5},{8,10},{9,14},{10,... | collective-permute-start | bytes 1179656 | tf_op jit(solution)/shard_map/ppermute | solution.py:949
  11.0 33.9 %collective-permute-start.1 = (bf16[768,256]{1,0:T(8,128)(2,1)S(1)}, bf16[768,256]{1,0:T(8,128)(2,1)S(1)}, u32[]{:S(2)}, u32[]{:S(2)}) collective-permute-start(bf16[768,256]{1,0:T(8,128)(2,1)S(1)} %maximum_select_fusion), channel_id=1, source_target_pairs={{0,0},{1,4},{2,2},{3,6},{4,1},{5,5},{6,3},{7,7},{8,8},{9,12},{10,1... | collective-permute-start | bytes 1179656 | tf_op jit(solution)/shard_map/ppermute | solution.py:949
  81.3 20.0 %collective-permute-start.7 = (bf16[768,256]{1,0:T(8,128)(2,1)S(1)}, bf16[768,256]{1,0:T(8,128)(2,1)S(1)}, u32[]{:S(2)}, u32[]{:S(2)}) collective-permute-start(bf16[768,256]{1,0:T(8,128)(2,1)S(1)} %get-tuple-element.115), channel_id=1, source_target_pairs={{0,8},{1,12},{2,10},{3,14},{4,9},{5,13},{6,11},{7,15},{8,0},{9,4},... | collective-permute-start | bytes 1179656 | tf_op jit(solution)/shard_map/ppermute | solution.py:956
  83.9 17.3 %collective-permute-start.12 = (bf16[160,256]{1,0:T(8,128)(2,1)S(1)}, bf16[160,256]{1,0:T(8,128)(2,1)S(1)}, u32[]{:S(2)}, u32[]{:S(2)}) collective-permute-start(bf16[160,256]{1,0:T(8,128)(2,1)S(1)} %get-tuple-element.134), channel_id=1, source_target_pairs={{0,16},{1,17},{2,18},{3,19},{4,20},{5,21},{6,22},{7,23},{8,24},{9,... | collective-permute-start | bytes 245768 | tf_op jit(solution)/shard_map/ppermute | solution.py:1039
  85.5 15.8 %collective-permute-start.13 = (bf16[160,256]{1,0:T(8,128)(2,1)S(1)}, bf16[160,256]{1,0:T(8,128)(2,1)S(1)}, u32[]{:S(2)}, u32[]{:S(2)}) collective-permute-start(bf16[160,256]{1,0:T(8,128)(2,1)S(1)} %get-tuple-element.135), channel_id=1, source_target_pairs={{0,2},{1,3},{2,0},{3,1},{4,6},{5,7},{6,4},{7,5},{8,10},{9,11},{10,... | collective-permute-start | bytes 245768 | tf_op jit(solution)/shard_map/ppermute | solution.py:1039
  86.0 15.3 %collective-permute-start.14 = (bf16[160,256]{1,0:T(8,128)(2,1)S(1)}, bf16[160,256]{1,0:T(8,128)(2,1)S(1)}, u32[]{:S(2)}, u32[]{:S(2)}) collective-permute-start(bf16[160,256]{1,0:T(8,128)(2,1)S(1)} %get-tuple-element.136), channel_id=1, source_target_pairs={{0,18},{1,19},{2,16},{3,17},{4,22},{5,23},{6,20},{7,21},{8,26},{9,... | collective-permute-start | bytes 245768 | tf_op jit(solution)/shard_map/ppermute | solution.py:1039
  102.6 20.0 %collective-permute-start.10 = (bf16[768,256]{1,0:T(8,128)(2,1)S(1)}, bf16[768,256]{1,0:T(8,128)(2,1)S(1)}, u32[]{:S(2)}, u32[]{:S(2)}) collective-permute-start(bf16[768,256]{1,0:T(8,128)(2,1)S(1)} %get-tuple-element.120), channel_id=1, source_target_pairs={{0,10},{1,14},{2,8},{3,12},{4,11},{5,15},{6,9},{7,13},{8,2},{9,6},... | collective-permute-start | bytes 1179656 | tf_op jit(solution)/shard_map/ppermute | solution.py:956
  102.7 20.5 %collective-permute-start.9 = (bf16[768,256]{1,0:T(8,128)(2,1)S(1)}, bf16[768,256]{1,0:T(8,128)(2,1)S(1)}, u32[]{:S(2)}, u32[]{:S(2)}) collective-permute-start(bf16[768,256]{1,0:T(8,128)(2,1)S(1)} %get-tuple-element.118), channel_id=1, source_target_pairs={{0,2},{1,6},{2,0},{3,4},{4,3},{5,7},{6,1},{7,5},{8,10},{9,14},{10,... | collective-permute-start | bytes 1179656 | tf_op jit(solution)/shard_map/ppermute | solution.py:956
  103.7 19.5 %collective-permute-start.8 = (bf16[768,256]{1,0:T(8,128)(2,1)S(1)}, bf16[768,256]{1,0:T(8,128)(2,1)S(1)}, u32[]{:S(2)}, u32[]{:S(2)}) collective-permute-start(bf16[768,256]{1,0:T(8,128)(2,1)S(1)} %get-tuple-element.116), channel_id=1, source_target_pairs={{0,0},{1,4},{2,2},{3,6},{4,1},{5,5},{6,3},{7,7},{8,8},{9,12},{10,1... | collective-permute-start | bytes 1179656 | tf_op jit(solution)/shard_map/ppermute | solution.py:956
  129.0 20.5 %collective-permute-start.19 = (bf16[768,256]{1,0:T(8,128)(2,1)S(1)}, bf16[768,256]{1,0:T(8,128)(2,1)S(1)}, u32[]{:S(2)}, u32[]{:S(2)}) collective-permute-start(bf16[768,256]{1,0:T(8,128)(2,1)S(1)} %get-tuple-element.169), channel_id=1, source_target_pairs={{0,8},{1,12},{2,10},{3,14},{4,9},{5,13},{6,11},{7,15},{8,0},{9,4},... | collective-permute-start | bytes 1179656 | tf_op jit(solution)/shard_map/ppermute | solution.py:956
  133.7 10.5 %collective-permute-start.23 = (bf16[320,256]{1,0:T(8,128)(2,1)S(1)}, bf16[320,256]{1,0:T(8,128)(2,1)S(1)}, u32[]{:S(2)}, u32[]{:S(2)}) collective-permute-start(bf16[320,256]{1,0:T(8,128)(2,1)S(1)} %get-tuple-element.177), channel_id=1, source_target_pairs={{0,2},{1,3},{2,0},{3,1},{4,6},{5,7},{6,4},{7,5},{8,10},{9,11},{10,... | collective-permute-start | bytes 491528 | tf_op jit(solution)/shard_map/ppermute | solution.py:1039
  135.3 9.0 %collective-permute-start.24 = (bf16[320,256]{1,0:T(8,128)(2,1)S(1)}, bf16[320,256]{1,0:T(8,128)(2,1)S(1)}, u32[]{:S(2)}, u32[]{:S(2)}) collective-permute-start(bf16[320,256]{1,0:T(8,128)(2,1)S(1)} %get-tuple-element.178), channel_id=1, source_target_pairs={{0,18},{1,19},{2,16},{3,17},{4,22},{5,23},{6,20},{7,21},{8,26},{9,... | collective-permute-start | bytes 491528 | tf_op jit(solution)/shard_map/ppermute | solution.py:1039
  135.7 23.7 %collective-permute-start.18 = (bf16[768,256]{1,0:T(8,128)(2,1)S(1)}, bf16[768,256]{1,0:T(8,128)(2,1)S(1)}, u32[]{:S(2)}, u32[]{:S(2)}) collective-permute-start(bf16[768,256]{1,0:T(8,128)(2,1)S(1)} %get-tuple-element.167), channel_id=1, source_target_pairs={{0,0},{1,4},{2,2},{3,6},{4,1},{5,5},{6,3},{7,7},{8,8},{9,12},{10,1... | collective-permute-start | bytes 1179656 | tf_op jit(solution)/shard_map/ppermute | solution.py:956
  145.0 12.4 %collective-permute-start.25 = (bf16[256,256]{1,0:T(8,128)(2,1)S(1)}, bf16[256,256]{1,0:T(8,128)(2,1)S(1)}, u32[]{:S(2)}, u32[]{:S(2)}) collective-permute-start(bf16[256,256]{1,0:T(8,128)(2,1)S(1)} %get-tuple-element.180), channel_id=1, source_target_pairs={{0,4},{1,5},{2,6},{3,7},{4,0},{5,1},{6,2},{7,3},{8,12},{9,13},{10,... | collective-permute-start | bytes 393224 | tf_op jit(solution)/shard_map/ppermute | solution.py:1039
  149.6 18.6 %collective-permute-start.27 = (bf16[768,256]{1,0:T(8,128)(2,1)S(1)}, bf16[768,256]{1,0:T(8,128)(2,1)S(1)}, u32[]{:S(2)}, u32[]{:S(2)}) collective-permute-start(bf16[768,256]{1,0:T(8,128)(2,1)S(1)} %get-tuple-element.183), channel_id=1, source_target_pairs={{0,10},{1,14},{2,8},{3,12},{4,11},{5,15},{6,9},{7,13},{8,2},{9,6},... | collective-permute-start | bytes 1179656 | tf_op jit(solution)/shard_map/ppermute | solution.py:956
  157.4 15.0 %collective-permute-start.26 = (bf16[768,256]{1,0:T(8,128)(2,1)S(1)}, bf16[768,256]{1,0:T(8,128)(2,1)S(1)}, u32[]{:S(2)}, u32[]{:S(2)}) collective-permute-start(bf16[768,256]{1,0:T(8,128)(2,1)S(1)} %get-tuple-element.181), channel_id=1, source_target_pairs={{0,2},{1,6},{2,0},{3,4},{4,3},{5,7},{6,1},{7,5},{8,10},{9,14},{10,... | collective-permute-start | bytes 1179656 | tf_op jit(solution)/shard_map/ppermute | solution.py:956
  159.5 8.1 %collective-permute-start.28 = (bf16[256,256]{1,0:T(8,128)(2,1)S(1)}, bf16[256,256]{1,0:T(8,128)(2,1)S(1)}, u32[]{:S(2)}, u32[]{:S(2)}) collective-permute-start(bf16[256,256]{1,0:T(8,128)(2,1)S(1)} %get-tuple-element.187.refs_0_), channel_id=1, source_target_pairs={{0,8},{1,9},{2,10},{3,11},{4,12},{5,13},{6,14},{7,15},{8,0},{9,1},... | collective-permute-start | bytes 393224 | tf_op jit(solution)/shard_map/ppermute | solution.py:1039
  160.1 25.7 %collective-permute-start.17 = (bf16[4,384,256]{2,1,0:T(8,128)(2,1)S(1)}, bf16[4,384,256]{2,1,0:T(8,128)(2,1)S(1)}, u32[]{:S(2)}, u32[]{:S(2)}) collective-permute-start(bf16[4,384,256]{2,1,0:T(8,128)(2,1)S(1)} %shard_map.160), channel_id=1, source_target_pairs={{0,1},{1,0},{2,3},{3,2},{4,5},{5,4},{6,7},{7,6},{8,9},{9,8},{10,11... | collective-permute-start | bytes 2359304 | tf_op jit(solution)/shard_map/ppermute | solution.py:961
  172.9 15.2 %collective-permute-start.29 = (bf16[4,384,256]{2,1,0:T(8,128)(2,1)S(1)}, bf16[4,384,256]{2,1,0:T(8,128)(2,1)S(1)}, u32[]{:S(2)}, u32[]{:S(2)}) collective-permute-start(bf16[4,384,256]{2,1,0:T(8,128)(2,1)S(1)} %shard_map.166), channel_id=1, source_target_pairs={{0,1},{1,0},{2,3},{3,2},{4,5},{5,4},{6,7},{7,6},{8,9},{9,8},{10,11... | collective-permute-start | bytes 2359304 | tf_op jit(solution)/shard_map/ppermute | solution.py:961
  179.6 11.1 %collective-permute-start.31 = (bf16[448,256]{1,0:T(8,128)(2,1)S(1)}, bf16[448,256]{1,0:T(8,128)(2,1)S(1)}, u32[]{:S(2)}, u32[]{:S(2)}) collective-permute-start(bf16[448,256]{1,0:T(8,128)(2,1)S(1)} %shard_map.168.refs_0_), channel_id=1, source_target_pairs={{0,16},{1,17},{2,18},{3,19},{4,20},{5,21},{6,22},{7,23},{8,24},{9,... | collective-permute-start | bytes 688136 | tf_op jit(solution)/shard_map/ppermute | solution.py:1039
  184.2 11.8 %collective-permute-start.32 = (bf16[448,256]{1,0:T(8,128)(2,1)S(1)}, bf16[448,256]{1,0:T(8,128)(2,1)S(1)}, u32[]{:S(2)}, u32[]{:S(2)}) collective-permute-start(bf16[448,256]{1,0:T(8,128)(2,1)S(1)} %shard_map.168.refs_0_), channel_id=1, source_target_pairs={{0,2},{1,3},{2,0},{3,1},{4,6},{5,7},{6,4},{7,5},{8,10},{9,11},{10,... | collective-permute-start | bytes 688136 | tf_op jit(solution)/shard_map/ppermute | solution.py:1039
  185.2 10.9 %collective-permute-start.33 = (bf16[448,256]{1,0:T(8,128)(2,1)S(1)}, bf16[448,256]{1,0:T(8,128)(2,1)S(1)}, u32[]{:S(2)}, u32[]{:S(2)}) collective-permute-start(bf16[448,256]{1,0:T(8,128)(2,1)S(1)} %shard_map.168.refs_0_), channel_id=1, source_target_pairs={{0,18},{1,19},{2,16},{3,17},{4,22},{5,23},{6,20},{7,21},{8,26},{9,... | collective-permute-start | bytes 688136 | tf_op jit(solution)/shard_map/ppermute | solution.py:1039
  (18 other events, 75.1 us)

commit v8 on v7

--- a/solution.py
+++ b/solution.py
@@ -996,14 +996,15 @@
     )
     kv_other = lax.ppermute(kv1, "section", first_to_second)
 
+    pad = 2 * n // STRIDE
     rows_k_all = shape((2 * n, qw), BF16)
     rows_v_all = shape((2 * n, width), BF16)
     outs = [rows_q, rows_k_all, rows_v_all, rows_wide, rows_stat]
     qr, kr, vr, o_far, lse_far = call(
         far_forward_kernel, info, [q1, kv1, kv_other], [whole(a) for a in (q1, kv1, kv_other)],
         outs, [whole(o) for o in outs],
-        [pltpu.VMEM((n, qw), F32), pltpu.VMEM((2 * n, qw), F32), pltpu.VMEM((HEADS, 2 * n, 128), F32),
-         pltpu.VMEM((HEADS, n, 128), F32), pltpu.VMEM((n, 128), F32)], work=14,
+        [pltpu.VMEM((n + pad, qw), F32), pltpu.VMEM((2 * n + pad, qw), F32), pltpu.VMEM((HEADS, 2 * n + pad, 128), F32),
+         pltpu.VMEM((HEADS, n + pad, 128), F32), pltpu.VMEM((n + pad, 128), F32)], work=14,
     )
 
     message = shape((2 * rows_piece, width), BF16)
@@ -1029,8 +1030,8 @@
     operands = [qr, kr, vr, go1, stat1, gq_near, gk_near, gv_near]
     gq1, gkv1, gkv_send = call(
         far_backward_kernel, info, operands, [whole(a) for a in operands], outs, [whole(o) for o in outs],
-        [pltpu.VMEM((HEADS, n, 128), F32), pltpu.VMEM((n, 128), F32), pltpu.VMEM((n, qw), F32),
-         pltpu.VMEM((2 * n, qw), F32), pltpu.VMEM((HEADS, 2 * n, 128), F32)], work=18,
+        [pltpu.VMEM((HEADS, n + pad, 128), F32), pltpu.VMEM((n + pad, 128), F32), pltpu.VMEM((n + pad, qw), F32),
+         pltpu.VMEM((2 * n + pad, qw), F32), pltpu.VMEM((HEADS, 2 * n + pad, 128), F32)], work=18,
     )
     def pair(message):
         return lax.ppermute(message, ("dp", "section"), partners([1])[1][0][1])

time: 202 us -> 202 us (level)
  no operation moved by 1% of the time
where the time goes in v8:
time: 202 us
  waiting for transfers between devices  90.9 us (45%)
  Pallas kernels  66.4 us (33%)
  starting transfers between devices  39.7 us (20%)
  local copies, waits for them, and re-layouts  3.08 us (2%)
    pallas_call x20, Pallas kernels, call(): pl.pallas_call(body_of, grid_spec=pltpu.PrefetchScalarGridSpec(num_scalar...  66.4 us
    ppermute x4, waiting for transfers between devices, body(): received[t] = lax.ppermute(message, 'section', route(pairs))  33.2 us
    ppermute x11, waiting for transfers between devices, send_all(): lax.ppermute(m, ('dp', 'section'), way)  26.4 us
    ppermute x8, waiting for transfers between devices, send_back(): return lax.ppermute(message, 'section', route(pairs))  16.7 us
    ppermute x11, starting transfers between devices, send_all(): lax.ppermute(m, ('dp', 'section'), way)  13.9 us
    ppermute x8, starting transfers between devices, send_back(): return lax.ppermute(message, 'section', route(pairs))  8.2 us
    ppermute x4, starting transfers between devices, body(): received[t] = lax.ppermute(message, 'section', route(pairs))  6.37 us
    ppermute x1, waiting for transfers between devices, gather(): lax.ppermute(piece, ('dp', 'section'), way)  5.07 us
  transfers between devices with their start and end apart: 35, of which 20 were waited for; matrix products, arithmetic and copies ran while one was open for 1% of the time, Pallas kernels for 17%

profile of v8, /device:TPU:0, one launch (start us, length us, event | category | flops | bytes accessed | tf_op | source)
XLA Modules:
  0.0 201.9 jit_solution(2879929970538848287)
XLA Ops:
  4.9 5.0 %collective-permute-start.4 = (bf16[768,256]{1,0:T(8,128)(2,1)S(1)}, bf16[768,256]{1,0:T(8,128)(2,1)S(1)}, u32[]{:S(2)}, u32[]{:S(2)}) collective-permute-start(bf16[768,256]{1,0:T(8,128)(2,1)S(1)} %maximum_select_fusion.3), channel_id=1, source_target_pairs={{0,10},{1,14},{2,8},{3,12},{4,11},{5,15},{6,9},{7,13},{8,2},{9,6},... | collective-permute-start | bytes 1179656 | tf_op jit(solution)/shard_map/ppermute | solution.py:949
  11.8 24.9 %collective-permute-done.4.refs_3_ = bf16[768,256]{1,0:T(8,128)(2,1)S(1)} collective-permute-done((bf16[768,256]{1,0:T(8,128)(2,1)S(1)}, bf16[768,256]{1,0:T(8,128)(2,1)S(1)}, u32[]{:S(2)}, u32[]{:S(2)}) %collective-permute-start.4) | collective-permute-done | bytes 393248 | tf_op jit(solution)/shard_map/ppermute | solution.py:949
  36.7 8.3 %collective-permute-done.3.refs_2_ = bf16[768,256]{1,0:T(8,128)(2,1)S(1)} collective-permute-done((bf16[768,256]{1,0:T(8,128)(2,1)S(1)}, bf16[768,256]{1,0:T(8,128)(2,1)S(1)}, u32[]{:S(2)}, u32[]{:S(2)}) %collective-permute-start.3) | collective-permute-done | bytes 393248 | tf_op jit(solution)/shard_map/ppermute | solution.py:949
  49.3 6.6 %shard_map.152 = (bf16[1536,256]{1,0:T(8,128)(2,1)S(1)}, bf16[1536,128]{1,0:T(8,128)(2,1)S(1)}, bf16[1536,384]{1,0:T(8,128)(2,1)S(1)}, bf16[1536,256]{1,0:T(8,12...) custom-call(s32[13]{0:T(128)S(1)} %stack.42.info, ...), custom_call_target="tpu_custom_call" | custom-call | flops 17250000896 | bytes 12124160 | tf_op jit(solution)/shard_map/pallas_call | solution.py:836
  55.9 2.5 %collective-permute-start.6 = (bf16[1536,384]{1,0:T(8,128)(2,1)S(1)}, bf16[1536,384]{1,0:T(8,128)(2,1)S(1)}, u32[]{:S(2)}, u32[]{:S(2)}) collective-permute-start(bf16[1536,384]{1,0:T(8,128)(2,1)S(1)} %get-tuple-element.110.refs_1_.refs_5_), channel_id=1, source_target_pairs={{0,1},{2,3},{4,5},{6,7},{8,9},{10,11},{12,13},{14,15},{16,17},{18,... | collective-permute-start | bytes 3538952 | tf_op jit(solution)/shard_map/ppermute | solution.py:997
  60.6 4.1 %shard_map.153 = (bf16[1536,128]{1,0:T(8,128)(2,1)S(1)}, bf16[3072,128]{1,0:T(8,128)(2,1)S(1)}, bf16[3072,256]{1,0:T(8,128)(2,1)S(1)}, f32[1536,256]{1,0:T(8,128)S(1)}, f32[1536,128]{1,0:T(8,128)S(1)}) custom-call(s32[13]{0:T(128)S(1)} %stack.42.info, bf16[1536,128]{1,0:T(8,128)(2,1)S(1)} %get-tuple-element.109.refs_0_.refs_4_, ...), custom_call_target="tpu_custom_call" | custom-call | flops 16099999744 | bytes 7864320 | tf_op jit(solution)/shard_map/pallas_call | solution.py:836
  64.7 16.1 %shard_map.154 = (bf16[768,256]{1,0:T(8,128)(2,1)S(1)}, bf16[768,256]{1,0:T(8,128)(2,1)S(1)}, bf16[768,256]{1,0:T(8,128)(2,1)S(1)}, bf16[768,256]{1,0:T(8,128)(2...) custom-call(s32[13]{0:T(128)S(1)} %stack.42.info, ...), custom_call_target="tpu_custom_call" | custom-call | flops 27599998976 | bytes 17215488 | tf_op jit(solution)/shard_map/pallas_call | solution.py:836
  87.5 7.0 %shard_map.155 = (f32[1536,128]{1,0:T(8,128)S(1)}, f32[1536,384]{1,0:T(8,128)S(1)}, bf16[1536,384]{1,0:T(8,128)(2,1)S(1)}) custom-call(s32[13]{0:T(128)S(1)} %stack.42.info, bf16[1536,128]{1,0:T(8,128)(2,1)S(1)} %get-tuple-element.121.refs_0_, bf16[3072,128]{1,0:T(8,128)(2,1)S(1)} %get-tuple-element.122.refs_1_, ...), custom_call_target="tpu_custom_call" | custom-call | flops 20700000256 | bytes 11993088 | tf_op jit(solution)/shard_map/pallas_call | solution.py:836
  94.5 6.7 %collective-permute-done.7.refs_4_.refs_2_ = bf16[768,256]{1,0:T(8,128)(2,1)S(1)} collective-permute-done((bf16[768,256]{1,0:T(8,128)(2,1)S(1)}, bf16[768,256]{1,0:T(8,128)(2,1)S(1)}, u32[]{:S(2)}, u32[]{:S(2)}) %collective-permute-start.7) | collective-permute-done | bytes 393248 | tf_op jit(solution)/shard_map/ppermute | solution.py:956
  106.0 15.3 %shard_map.157 = (bf16[768,256]{1,0:T(8,128)(2,1)S(1)}, bf16[768,256]{1,0:T(8,128)(2,1)S(1)}, bf16[768,256]{1,0:T(8,128)(2,1)S(1)}, bf16[768,256]{1,0:T(8,128)(2...) custom-call(s32[13]{0:T(128)S(1)} %stack.42.info, ...), custom_call_target="tpu_custom_call" | custom-call | flops 23000000512 | bytes 20701184 | tf_op jit(solution)/shard_map/pallas_call | solution.py:836
  129.0 2.4 %collective-permute-start.19 = (bf16[768,256]{1,0:T(8,128)(2,1)S(1)}, bf16[768,256]{1,0:T(8,128)(2,1)S(1)}, u32[]{:S(2)}, u32[]{:S(2)}) collective-permute-start(bf16[768,256]{1,0:T(8,128)(2,1)S(1)} %get-tuple-element.169), channel_id=1, source_target_pairs={{0,8},{1,12},{2,10},{3,14},{4,9},{5,13},{6,11},{7,15},{8,0},{9,4},... | collective-permute-start | bytes 1179656 | tf_op jit(solution)/shard_map/ppermute | solution.py:956
  136.4 2.7 %collective-permute-done.22.refs_5_ = bf16[320,256]{1,0:T(8,128)(2,1)S(1)} collective-permute-done((bf16[320,256]{1,0:T(8,128)(2,1)S(1)}, bf16[320,256]{1,0:T(8,128)(2,1)S(1)}, u32[]{:S(2)}, u32[]{:S(2)}) %collective-permute-start.22) | collective-permute-done | bytes 163872 | tf_op jit(solution)/shard_map/ppermute | solution.py:1040
  139.1 5.2 %collective-permute-done.23.refs_6_ = bf16[320,256]{1,0:T(8,128)(2,1)S(1)} collective-permute-done((bf16[320,256]{1,0:T(8,128)(2,1)S(1)}, bf16[320,256]{1,0:T(8,128)(2,1)S(1)}, u32[]{:S(2)}, u32[]{:S(2)}) %collective-permute-start.23) | collective-permute-done | bytes 163872 | tf_op jit(solution)/shard_map/ppermute | solution.py:1040
  145.6 4.0 %collective-permute-done.19.refs_2_ = bf16[768,256]{1,0:T(8,128)(2,1)S(1)} collective-permute-done((bf16[768,256]{1,0:T(8,128)(2,1)S(1)}, bf16[768,256]{1,0:T(8,128)(2,1)S(1)}, u32[]{:S(2)}, u32[]{:S(2)}) %collective-permute-start.19) | collective-permute-done | bytes 393248 | tf_op jit(solution)/shard_map/ppermute | solution.py:956
  150.0 7.3 %collective-permute-done.25.refs_1_ = bf16[256,256]{1,0:T(8,128)(2,1)S(1)} collective-permute-done((bf16[256,256]{1,0:T(8,128)(2,1)S(1)}, bf16[256,256]{1,0:T(8,128)(2,1)S(1)}, u32[]{:S(2)}, u32[]{:S(2)}) %collective-permute-start.25) | collective-permute-done | bytes 131104 | tf_op jit(solution)/shard_map/ppermute | solution.py:1040
  162.0 5.5 %collective-permute-done.28.refs_1_ = bf16[256,256]{1,0:T(8,128)(2,1)S(1)} collective-permute-done((bf16[256,256]{1,0:T(8,128)(2,1)S(1)}, bf16[256,256]{1,0:T(8,128)(2,1)S(1)}, u32[]{:S(2)}, u32[]{:S(2)}) %collective-permute-start.28) | collective-permute-done | bytes 131104 | tf_op jit(solution)/shard_map/ppermute | solution.py:1040
  168.1 4.2 %collective-permute-done.26.refs_1_ = bf16[768,256]{1,0:T(8,128)(2,1)S(1)} collective-permute-done((bf16[768,256]{1,0:T(8,128)(2,1)S(1)}, bf16[768,256]{1,0:T(8,128)(2,1)S(1)}, u32[]{:S(2)}, u32[]{:S(2)}) %collective-permute-start.26) | collective-permute-done | bytes 393248 | tf_op jit(solution)/shard_map/ppermute | solution.py:956
  173.9 5.1 %collective-permute-done.30.refs_1_ = bf16[224,256]{1,0:T(8,128)(2,1)S(1)} collective-permute-done((bf16[224,256]{1,0:T(8,128)(2,1)S(1)}, bf16[224,256]{1,0:T(8,128)(2,1)S(1)}, u32[]{:S(2)}, u32[]{:S(2)}) %collective-permute-start.30) | collective-permute-done | bytes 114720 | tf_op jit(solution)/shard_map/ppermute | solution.py:1061
  179.6 4.7 %collective-permute-start.31 = (bf16[448,256]{1,0:T(8,128)(2,1)S(1)}, bf16[448,256]{1,0:T(8,128)(2,1)S(1)}, u32[]{:S(2)}, u32[]{:S(2)}) collective-permute-start(bf16[448,256]{1,0:T(8,128)(2,1)S(1)} %shard_map.168.refs_0_), channel_id=1, source_target_pairs={{0,16},{1,17},{2,18},{3,19},{4,20},{5,21},{6,22},{7,23},{8,24},{9,... | collective-permute-start | bytes 688136 | tf_op jit(solution)/shard_map/ppermute | solution.py:1040
  185.8 2.3 %shard_map.161 = (f32[8,384,256]{2,1,0:T(8,128)}, f32[8,128]{1,0:T(8,128)S(1)}) custom-call(s32[13]{0:T(128)S(1)} %stack.42.info, bf16[768,256]{1,0:T(8,128)(2,1)S(1)} %collective-permute-done.8.refs_2_.refs_0_, bf16[768,256]{1,0:T(8,128)(2,1)S(1)} %collective-permute-done.9.refs_3_.refs_1_, bf16[768,256]{1,0:T(8,128)(2,1)S(1)} %collective-permute-done.7.refs_4_.refs_2_, ...), custom_call_target="tpu_custom_call" | custom-call | bytes 5509120 | tf_op jit(solution)/shard_map/pallas_call | solution.py:836
  188.1 2.3 %shard_map.167 = (f32[8,384,256]{2,1,0:T(8,128)}, f32[8,128]{1,0:T(8,128)S(1)}) custom-call(s32[13]{0:T(128)S(1)} %stack.42.info, bf16[768,256]{1,0:T(8,128)(2,1)S(1)} %collective-permute-done.18.refs_0_, bf16[768,256]{1,0:T(8,128)(2,1)S(1)} %collective-permute-done.26.refs_1_, bf16[768,256]{1,0:T(8,128)(2,1)S(1)} %collective-permute-done.19.refs_2_, ...), custom_call_target="tpu_custom_call" | custom-call | bytes 5509120 | tf_op jit(solution)/shard_map/pallas_call | solution.py:836
  190.7 5.3 %collective-permute-done.32.refs_2_ = bf16[448,256]{1,0:T(8,128)(2,1)S(1)} collective-permute-done((bf16[448,256]{1,0:T(8,128)(2,1)S(1)}, bf16[448,256]{1,0:T(8,128)(2,1)S(1)}, u32[]{:S(2)}, u32[]{:S(2)}) %collective-permute-start.32) | collective-permute-done | bytes 229408 | tf_op jit(solution)/shard_map/ppermute | solution.py:1040
  196.8 2.4 %collective-permute-done.34.refs_1_ = bf16[1792,256]{1,0:T(8,128)(2,1)S(1)} collective-permute-done((bf16[1792,256]{1,0:T(8,128)(2,1)S(1)}, bf16[1792,256]{1,0:T(8,128)(2,1)S(1)}, u32[]{:S(2)}, u32[]{:S(2)}) %collective-permute-start.34) | collective-permute-done | bytes 917536 | tf_op jit(solution)/shard_map/ppermute | solution.py:1037
  199.2 2.7 %shard_map.170 = (f32[2,256,512]{2,1,0:T(8,128)}, f32[2,256,256]{2,1,0:T(8,128)}, f32[2,256,512]{2,1,0:T(8,128)}, f32[2,512,256]{2,1,0:T(8,128)}, f32[2,2,256]{2...) custom-call(s32[13]{0:T(128)S(1)} %stack.42.info, bf16[1792,256]{1,0:T(8,128)(2,1)S(1)} %shard_map.169.refs_0_, ...), custom_call_target="tpu_custom_call" | custom-call | bytes 5529824 | tf_op jit(solution)/shard_map/pallas_call | solution.py:836
  (95 shorter events, 48.1 us)
Async XLA Ops:
  4.9 31.8 %collective-permute-start.4 = (bf16[768,256]{1,0:T(8,128)(2,1)S(1)}, bf16[768,256]{1,0:T(8,128)(2,1)S(1)}, u32[]{:S(2)}, u32[]{:S(2)}) collective-permute-start(bf16[768,256]{1,0:T(8,128)(2,1)S(1)} %maximum_select_fusion.3), channel_id=1, source_target_pairs={{0,10},{1,14},{2,8},{3,12},{4,11},{5,15},{6,9},{7,13},{8,2},{9,6},... | collective-permute-start | bytes 1179656 | tf_op jit(solution)/shard_map/ppermute | solution.py:949
  10.0 35.0 %collective-permute-start.3 = (bf16[768,256]{1,0:T(8,128)(2,1)S(1)}, bf16[768,256]{1,0:T(8,128)(2,1)S(1)}, u32[]{:S(2)}, u32[]{:S(2)}) collective-permute-start(bf16[768,256]{1,0:T(8,128)(2,1)S(1)} %maximum_select_fusion.2), channel_id=1, source_target_pairs={{0,8},{1,12},{2,10},{3,14},{4,9},{5,13},{6,11},{7,15},{8,0},{9,4},... | collective-permute-start | bytes 1179656 | tf_op jit(solution)/shard_map/ppermute | solution.py:949
  10.6 34.4 %collective-permute-start.2 = (bf16[768,256]{1,0:T(8,128)(2,1)S(1)}, bf16[768,256]{1,0:T(8,128)(2,1)S(1)}, u32[]{:S(2)}, u32[]{:S(2)}) collective-permute-start(bf16[768,256]{1,0:T(8,128)(2,1)S(1)} %maximum_select_fusion.1), channel_id=1, source_target_pairs={{0,2},{1,6},{2,0},{3,4},{4,3},{5,7},{6,1},{7,5},{8,10},{9,14},{10,... | collective-permute-start | bytes 1179656 | tf_op jit(solution)/shard_map/ppermute | solution.py:949
  11.0 33.9 %collective-permute-start.1 = (bf16[768,256]{1,0:T(8,128)(2,1)S(1)}, bf16[768,256]{1,0:T(8,128)(2,1)S(1)}, u32[]{:S(2)}, u32[]{:S(2)}) collective-permute-start(bf16[768,256]{1,0:T(8,128)(2,1)S(1)} %maximum_select_fusion), channel_id=1, source_target_pairs={{0,0},{1,4},{2,2},{3,6},{4,1},{5,5},{6,3},{7,7},{8,8},{9,12},{10,1... | collective-permute-start | bytes 1179656 | tf_op jit(solution)/shard_map/ppermute | solution.py:949
  81.3 20.0 %collective-permute-start.7 = (bf16[768,256]{1,0:T(8,128)(2,1)S(1)}, bf16[768,256]{1,0:T(8,128)(2,1)S(1)}, u32[]{:S(2)}, u32[]{:S(2)}) collective-permute-start(bf16[768,256]{1,0:T(8,128)(2,1)S(1)} %get-tuple-element.115), channel_id=1, source_target_pairs={{0,8},{1,12},{2,10},{3,14},{4,9},{5,13},{6,11},{7,15},{8,0},{9,4},... | collective-permute-start | bytes 1179656 | tf_op jit(solution)/shard_map/ppermute | solution.py:956
  83.9 17.3 %collective-permute-start.12 = (bf16[160,256]{1,0:T(8,128)(2,1)S(1)}, bf16[160,256]{1,0:T(8,128)(2,1)S(1)}, u32[]{:S(2)}, u32[]{:S(2)}) collective-permute-start(bf16[160,256]{1,0:T(8,128)(2,1)S(1)} %get-tuple-element.134), channel_id=1, source_target_pairs={{0,16},{1,17},{2,18},{3,19},{4,20},{5,21},{6,22},{7,23},{8,24},{9,... | collective-permute-start | bytes 245768 | tf_op jit(solution)/shard_map/ppermute | solution.py:1040
  85.5 15.8 %collective-permute-start.13 = (bf16[160,256]{1,0:T(8,128)(2,1)S(1)}, bf16[160,256]{1,0:T(8,128)(2,1)S(1)}, u32[]{:S(2)}, u32[]{:S(2)}) collective-permute-start(bf16[160,256]{1,0:T(8,128)(2,1)S(1)} %get-tuple-element.135), channel_id=1, source_target_pairs={{0,2},{1,3},{2,0},{3,1},{4,6},{5,7},{6,4},{7,5},{8,10},{9,11},{10,... | collective-permute-start | bytes 245768 | tf_op jit(solution)/shard_map/ppermute | solution.py:1040
  86.0 15.3 %collective-permute-start.14 = (bf16[160,256]{1,0:T(8,128)(2,1)S(1)}, bf16[160,256]{1,0:T(8,128)(2,1)S(1)}, u32[]{:S(2)}, u32[]{:S(2)}) collective-permute-start(bf16[160,256]{1,0:T(8,128)(2,1)S(1)} %get-tuple-element.136), channel_id=1, source_target_pairs={{0,18},{1,19},{2,16},{3,17},{4,22},{5,23},{6,20},{7,21},{8,26},{9,... | collective-permute-start | bytes 245768 | tf_op jit(solution)/shard_map/ppermute | solution.py:1040
  102.6 20.0 %collective-permute-start.10 = (bf16[768,256]{1,0:T(8,128)(2,1)S(1)}, bf16[768,256]{1,0:T(8,128)(2,1)S(1)}, u32[]{:S(2)}, u32[]{:S(2)}) collective-permute-start(bf16[768,256]{1,0:T(8,128)(2,1)S(1)} %get-tuple-element.120), channel_id=1, source_target_pairs={{0,10},{1,14},{2,8},{3,12},{4,11},{5,15},{6,9},{7,13},{8,2},{9,6},... | collective-permute-start | bytes 1179656 | tf_op jit(solution)/shard_map/ppermute | solution.py:956
  102.7 20.5 %collective-permute-start.9 = (bf16[768,256]{1,0:T(8,128)(2,1)S(1)}, bf16[768,256]{1,0:T(8,128)(2,1)S(1)}, u32[]{:S(2)}, u32[]{:S(2)}) collective-permute-start(bf16[768,256]{1,0:T(8,128)(2,1)S(1)} %get-tuple-element.118), channel_id=1, source_target_pairs={{0,2},{1,6},{2,0},{3,4},{4,3},{5,7},{6,1},{7,5},{8,10},{9,14},{10,... | collective-permute-start | bytes 1179656 | tf_op jit(solution)/shard_map/ppermute | solution.py:956
  103.7 19.5 %collective-permute-start.8 = (bf16[768,256]{1,0:T(8,128)(2,1)S(1)}, bf16[768,256]{1,0:T(8,128)(2,1)S(1)}, u32[]{:S(2)}, u32[]{:S(2)}) collective-permute-start(bf16[768,256]{1,0:T(8,128)(2,1)S(1)} %get-tuple-element.116), channel_id=1, source_target_pairs={{0,0},{1,4},{2,2},{3,6},{4,1},{5,5},{6,3},{7,7},{8,8},{9,12},{10,1... | collective-permute-start | bytes 1179656 | tf_op jit(solution)/shard_map/ppermute | solution.py:956
  129.0 20.5 %collective-permute-start.19 = (bf16[768,256]{1,0:T(8,128)(2,1)S(1)}, bf16[768,256]{1,0:T(8,128)(2,1)S(1)}, u32[]{:S(2)}, u32[]{:S(2)}) collective-permute-start(bf16[768,256]{1,0:T(8,128)(2,1)S(1)} %get-tuple-element.169), channel_id=1, source_target_pairs={{0,8},{1,12},{2,10},{3,14},{4,9},{5,13},{6,11},{7,15},{8,0},{9,4},... | collective-permute-start | bytes 1179656 | tf_op jit(solution)/shard_map/ppermute | solution.py:956
  133.7 10.5 %collective-permute-start.23 = (bf16[320,256]{1,0:T(8,128)(2,1)S(1)}, bf16[320,256]{1,0:T(8,128)(2,1)S(1)}, u32[]{:S(2)}, u32[]{:S(2)}) collective-permute-start(bf16[320,256]{1,0:T(8,128)(2,1)S(1)} %get-tuple-element.177), channel_id=1, source_target_pairs={{0,2},{1,3},{2,0},{3,1},{4,6},{5,7},{6,4},{7,5},{8,10},{9,11},{10,... | collective-permute-start | bytes 491528 | tf_op jit(solution)/shard_map/ppermute | solution.py:1040
  135.3 9.0 %collective-permute-start.24 = (bf16[320,256]{1,0:T(8,128)(2,1)S(1)}, bf16[320,256]{1,0:T(8,128)(2,1)S(1)}, u32[]{:S(2)}, u32[]{:S(2)}) collective-permute-start(bf16[320,256]{1,0:T(8,128)(2,1)S(1)} %get-tuple-element.178), channel_id=1, source_target_pairs={{0,18},{1,19},{2,16},{3,17},{4,22},{5,23},{6,20},{7,21},{8,26},{9,... | collective-permute-start | bytes 491528 | tf_op jit(solution)/shard_map/ppermute | solution.py:1040
  135.7 23.7 %collective-permute-start.18 = (bf16[768,256]{1,0:T(8,128)(2,1)S(1)}, bf16[768,256]{1,0:T(8,128)(2,1)S(1)}, u32[]{:S(2)}, u32[]{:S(2)}) collective-permute-start(bf16[768,256]{1,0:T(8,128)(2,1)S(1)} %get-tuple-element.167), channel_id=1, source_target_pairs={{0,0},{1,4},{2,2},{3,6},{4,1},{5,5},{6,3},{7,7},{8,8},{9,12},{10,1... | collective-permute-start | bytes 1179656 | tf_op jit(solution)/shard_map/ppermute | solution.py:956
  145.0 12.4 %collective-permute-start.25 = (bf16[256,256]{1,0:T(8,128)(2,1)S(1)}, bf16[256,256]{1,0:T(8,128)(2,1)S(1)}, u32[]{:S(2)}, u32[]{:S(2)}) collective-permute-start(bf16[256,256]{1,0:T(8,128)(2,1)S(1)} %get-tuple-element.180), channel_id=1, source_target_pairs={{0,4},{1,5},{2,6},{3,7},{4,0},{5,1},{6,2},{7,3},{8,12},{9,13},{10,... | collective-permute-start | bytes 393224 | tf_op jit(solution)/shard_map/ppermute | solution.py:1040
  149.6 18.6 %collective-permute-start.27 = (bf16[768,256]{1,0:T(8,128)(2,1)S(1)}, bf16[768,256]{1,0:T(8,128)(2,1)S(1)}, u32[]{:S(2)}, u32[]{:S(2)}) collective-permute-start(bf16[768,256]{1,0:T(8,128)(2,1)S(1)} %get-tuple-element.183), channel_id=1, source_target_pairs={{0,10},{1,14},{2,8},{3,12},{4,11},{5,15},{6,9},{7,13},{8,2},{9,6},... | collective-permute-start | bytes 1179656 | tf_op jit(solution)/shard_map/ppermute | solution.py:956
  157.4 15.0 %collective-permute-start.26 = (bf16[768,256]{1,0:T(8,128)(2,1)S(1)}, bf16[768,256]{1,0:T(8,128)(2,1)S(1)}, u32[]{:S(2)}, u32[]{:S(2)}) collective-permute-start(bf16[768,256]{1,0:T(8,128)(2,1)S(1)} %get-tuple-element.181), channel_id=1, source_target_pairs={{0,2},{1,6},{2,0},{3,4},{4,3},{5,7},{6,1},{7,5},{8,10},{9,14},{10,... | collective-permute-start | bytes 1179656 | tf_op jit(solution)/shard_map/ppermute | solution.py:956
  159.5 8.1 %collective-permute-start.28 = (bf16[256,256]{1,0:T(8,128)(2,1)S(1)}, bf16[256,256]{1,0:T(8,128)(2,1)S(1)}, u32[]{:S(2)}, u32[]{:S(2)}) collective-permute-start(bf16[256,256]{1,0:T(8,128)(2,1)S(1)} %get-tuple-element.187.refs_0_), channel_id=1, source_target_pairs={{0,8},{1,9},{2,10},{3,11},{4,12},{5,13},{6,14},{7,15},{8,0},{9,1},... | collective-permute-start | bytes 393224 | tf_op jit(solution)/shard_map/ppermute | solution.py:1040
  160.1 25.7 %collective-permute-start.17 = (bf16[4,384,256]{2,1,0:T(8,128)(2,1)S(1)}, bf16[4,384,256]{2,1,0:T(8,128)(2,1)S(1)}, u32[]{:S(2)}, u32[]{:S(2)}) collective-permute-start(bf16[4,384,256]{2,1,0:T(8,128)(2,1)S(1)} %shard_map.160), channel_id=1, source_target_pairs={{0,1},{1,0},{2,3},{3,2},{4,5},{5,4},{6,7},{7,6},{8,9},{9,8},{10,11... | collective-permute-start | bytes 2359304 | tf_op jit(solution)/shard_map/ppermute | solution.py:961
  172.9 15.2 %collective-permute-start.29 = (bf16[4,384,256]{2,1,0:T(8,128)(2,1)S(1)}, bf16[4,384,256]{2,1,0:T(8,128)(2,1)S(1)}, u32[]{:S(2)}, u32[]{:S(2)}) collective-permute-start(bf16[4,384,256]{2,1,0:T(8,128)(2,1)S(1)} %shard_map.166), channel_id=1, source_target_pairs={{0,1},{1,0},{2,3},{3,2},{4,5},{5,4},{6,7},{7,6},{8,9},{9,8},{10,11... | collective-permute-start | bytes 2359304 | tf_op jit(solution)/shard_map/ppermute | solution.py:961
  179.6 11.1 %collective-permute-start.31 = (bf16[448,256]{1,0:T(8,128)(2,1)S(1)}, bf16[448,256]{1,0:T(8,128)(2,1)S(1)}, u32[]{:S(2)}, u32[]{:S(2)}) collective-permute-start(bf16[448,256]{1,0:T(8,128)(2,1)S(1)} %shard_map.168.refs_0_), channel_id=1, source_target_pairs={{0,16},{1,17},{2,18},{3,19},{4,20},{5,21},{6,22},{7,23},{8,24},{9,... | collective-permute-start | bytes 688136 | tf_op jit(solution)/shard_map/ppermute | solution.py:1040
  184.2 11.8 %collective-permute-start.32 = (bf16[448,256]{1,0:T(8,128)(2,1)S(1)}, bf16[448,256]{1,0:T(8,128)(2,1)S(1)}, u32[]{:S(2)}, u32[]{:S(2)}) collective-permute-start(bf16[448,256]{1,0:T(8,128)(2,1)S(1)} %shard_map.168.refs_0_), channel_id=1, source_target_pairs={{0,2},{1,3},{2,0},{3,1},{4,6},{5,7},{6,4},{7,5},{8,10},{9,11},{10,... | collective-permute-start | bytes 688136 | tf_op jit(solution)/shard_map/ppermute | solution.py:1040
  185.2 10.9 %collective-permute-start.33 = (bf16[448,256]{1,0:T(8,128)(2,1)S(1)}, bf16[448,256]{1,0:T(8,128)(2,1)S(1)}, u32[]{:S(2)}, u32[]{:S(2)}) collective-permute-start(bf16[448,256]{1,0:T(8,128)(2,1)S(1)} %shard_map.168.refs_0_), channel_id=1, source_target_pairs={{0,18},{1,19},{2,16},{3,17},{4,22},{5,23},{6,20},{7,21},{8,26},{9,... | collective-permute-start | bytes 688136 | tf_op jit(solution)/shard_map/ppermute | solution.py:1040
  (18 other events, 75.1 us)

commit v9 on v8

--- a/solution.py
+++ b/solution.py
@@ -1088,9 +1088,8 @@
         [ext, pltpu.VMEM((slab_rows, width), F32), pltpu.VMEM((n + WIN, qw), F32), pltpu.VMEM((n + WIN, qw), F32),
          pltpu.VMEM((n + WIN, width), F32), pltpu.VMEM((n + WIN, width), F32)], steps, work=20,
     )
-    outs = [halo_shape, shape(early_shape, BF16)]
-    halo_send, send_early = call(
-        hold_kernel, info, [halo_send, send_early] + forward_back, [VMEM] * 2 + [ANY] * 4, outs, [VMEM] * 2
+    halo_send, _ = call(
+        hold_kernel, info, [halo_send, halo_send] + forward_back, [VMEM] * 2 + [ANY] * 4, [halo_shape] * 2, [VMEM] * 2
     )
     halo_got = lax.ppermute(halo_send, "section", second_to_first)
 

time: 202 us -> 201 us (level)
  starting transfers between devices: 39.7 us -> 36.5 us
    ppermute x11, waiting for transfers between devices: 26.4 us -> 32.9 us  [send_all(): lax.ppermute(m, ('dp', 'section'), way)]
    ppermute x8, waiting for transfers between devices: 16.7 us -> 10.9 us  [send_back(): return lax.ppermute(message, 'section', route(pairs))]
    ppermute x11, starting transfers between devices: 13.9 us -> 11.3 us  [send_all(): lax.ppermute(m, ('dp', 'section'), way)]
  transfers between devices with their start and end apart: 35 -> 35, of which waited for: 20 -> 18; matrix products, arithmetic and copies ran while one was open for 1% -> 1% of each run, Pallas kernels for 17% -> 17%
where the time goes in v9:
time: 201 us; the launch traced here: 200 us
  waiting for transfers between devices  92 us (46%)
  Pallas kernels  67.1 us (33%)
  starting transfers between devices  36.5 us (18%)
  local copies, waits for them, and re-layouts  3.08 us (2%)
    pallas_call x20, Pallas kernels, call(): pl.pallas_call(body_of, grid_spec=pltpu.PrefetchScalarGridSpec(num_scalar...  67.1 us
    ppermute x4, waiting for transfers between devices, body(): received[t] = lax.ppermute(message, 'section', route(pairs))  33.2 us
    ppermute x11, waiting for transfers between devices, send_all(): lax.ppermute(m, ('dp', 'section'), way)  32.9 us
    ppermute x11, starting transfers between devices, send_all(): lax.ppermute(m, ('dp', 'section'), way)  11.3 us
    ppermute x8, waiting for transfers between devices, send_back(): return lax.ppermute(message, 'section', route(pairs))  10.9 us
    ppermute x8, starting transfers between devices, send_back(): return lax.ppermute(message, 'section', route(pairs))  8.52 us
    ppermute x4, starting transfers between devices, body(): received[t] = lax.ppermute(message, 'section', route(pairs))  6.37 us
    ppermute x1, waiting for transfers between devices, gather(): lax.ppermute(piece, ('dp', 'section'), way)  5.48 us
  transfers between devices with their start and end apart: 35, of which 18 were waited for; matrix products, arithmetic and copies ran while one was open for 1% of the time, Pallas kernels for 17%

profile of v9, /device:TPU:0, one launch (start us, length us, event | category | flops | bytes accessed | tf_op | source)
XLA Modules:
  0.0 200.3 jit_solution(157242994839949560)
XLA Ops:
  4.9 5.0 %collective-permute-start.4 = (bf16[768,256]{1,0:T(8,128)(2,1)S(1)}, bf16[768,256]{1,0:T(8,128)(2,1)S(1)}, u32[]{:S(2)}, u32[]{:S(2)}) collective-permute-start(bf16[768,256]{1,0:T(8,128)(2,1)S(1)} %maximum_select_fusion.3), channel_id=1, source_target_pairs={{0,10},{1,14},{2,8},{3,12},{4,11},{5,15},{6,9},{7,13},{8,2},{9,6},... | collective-permute-start | bytes 1179656 | tf_op jit(solution)/shard_map/ppermute | solution.py:949
  11.8 24.9 %collective-permute-done.4.refs_3_ = bf16[768,256]{1,0:T(8,128)(2,1)S(1)} collective-permute-done((bf16[768,256]{1,0:T(8,128)(2,1)S(1)}, bf16[768,256]{1,0:T(8,128)(2,1)S(1)}, u32[]{:S(2)}, u32[]{:S(2)}) %collective-permute-start.4) | collective-permute-done | bytes 393248 | tf_op jit(solution)/shard_map/ppermute | solution.py:949
  36.7 8.3 %collective-permute-done.3.refs_2_ = bf16[768,256]{1,0:T(8,128)(2,1)S(1)} collective-permute-done((bf16[768,256]{1,0:T(8,128)(2,1)S(1)}, bf16[768,256]{1,0:T(8,128)(2,1)S(1)}, u32[]{:S(2)}, u32[]{:S(2)}) %collective-permute-start.3) | collective-permute-done | bytes 393248 | tf_op jit(solution)/shard_map/ppermute | solution.py:949
  45.0 2.1 %shard_map.151 = (bf16[1664,256]{1,0:T(8,128)(2,1)S(1)}, bf16[1536,128]{1,0:T(8,128)(2,1)S(1)}, bf16[1536,384]{1,0:T(8,128)(2,1)S(1)}, bf16[128,384]{1,0:T(8,128)(2,1)S(1)}) custom-call(s32[13]{0:T(128)S(1)} %stack.42.info, bf16[768,256]{1,0:T(8,128)(2,1)S(1)} %collective-permute-done.1.refs_0_, bf16[768,256]{1,0:T(8,128)(2,1)S(1)} %collective-permute-done.2.refs_1_, ...), custom_call_target="tpu_custom_call" | custom-call | flops 6899999744 | bytes 4362240 | tf_op jit(solution)/shard_map/pallas_call | solution.py:836
  49.3 6.6 %shard_map.152 = (bf16[1536,256]{1,0:T(8,128)(2,1)S(1)}, bf16[1536,128]{1,0:T(8,128)(2,1)S(1)}, bf16[1536,384]{1,0:T(8,128)(2,1)S(1)}, bf16[1536,256]{1,0:T(8,12...) custom-call(s32[13]{0:T(128)S(1)} %stack.42.info, ...), custom_call_target="tpu_custom_call" | custom-call | flops 17250000896 | bytes 12124160 | tf_op jit(solution)/shard_map/pallas_call | solution.py:836
  55.9 2.5 %collective-permute-start.6 = (bf16[1536,384]{1,0:T(8,128)(2,1)S(1)}, bf16[1536,384]{1,0:T(8,128)(2,1)S(1)}, u32[]{:S(2)}, u32[]{:S(2)}) collective-permute-start(bf16[1536,384]{1,0:T(8,128)(2,1)S(1)} %get-tuple-element.109.refs_1_.refs_5_), channel_id=1, source_target_pairs={{0,1},{2,3},{4,5},{6,7},{8,9},{10,11},{12,13},{14,15},{16,17},{18,... | collective-permute-start | bytes 3538952 | tf_op jit(solution)/shard_map/ppermute | solution.py:997
  58.4 2.2 %collective-permute-done.6.refs_2_.refs_6_ = bf16[1536,384]{1,0:T(8,128)(2,1)S(1)} collective-permute-done((bf16[1536,384]{1,0:T(8,128)(2,1)S(1)}, bf16[1536,384]{1,0:T(8,128)(2,1)S(1)}, u32[]{:S(2)}, u32[]{:S(2)}) %collective-permute-start.6) | collective-permute-done | bytes 1179680 | tf_op jit(solution)/shard_map/ppermute | solution.py:997
  60.6 4.1 %shard_map.153 = (bf16[1536,128]{1,0:T(8,128)(2,1)S(1)}, bf16[3072,128]{1,0:T(8,128)(2,1)S(1)}, bf16[3072,256]{1,0:T(8,128)(2,1)S(1)}, f32[1536,256]{1,0:T(8,128)S(1)}, f32[1536,128]{1,0:T(8,128)S(1)}) custom-call(s32[13]{0:T(128)S(1)} %stack.42.info, bf16[1536,128]{1,0:T(8,128)(2,1)S(1)} %get-tuple-element.108.refs_0_.refs_4_, ...), custom_call_target="tpu_custom_call" | custom-call | flops 16099999744 | bytes 7864320 | tf_op jit(solution)/shard_map/pallas_call | solution.py:836
  64.7 16.1 %shard_map.154 = (bf16[768,256]{1,0:T(8,128)(2,1)S(1)}, bf16[768,256]{1,0:T(8,128)(2,1)S(1)}, bf16[768,256]{1,0:T(8,128)(2,1)S(1)}, bf16[768,256]{1,0:T(8,128)(2...) custom-call(s32[13]{0:T(128)S(1)} %stack.42.info, ...), custom_call_target="tpu_custom_call" | custom-call | flops 27599998976 | bytes 17215488 | tf_op jit(solution)/shard_map/pallas_call | solution.py:836
  87.5 7.0 %shard_map.155 = (f32[1536,128]{1,0:T(8,128)S(1)}, f32[1536,384]{1,0:T(8,128)S(1)}, bf16[1536,384]{1,0:T(8,128)(2,1)S(1)}) custom-call(s32[13]{0:T(128)S(1)} %stack.42.info, bf16[1536,128]{1,0:T(8,128)(2,1)S(1)} %get-tuple-element.120.refs_0_, bf16[3072,128]{1,0:T(8,128)(2,1)S(1)} %get-tuple-element.121.refs_1_, ...), custom_call_target="tpu_custom_call" | custom-call | flops 20700000256 | bytes 11993088 | tf_op jit(solution)/shard_map/pallas_call | solution.py:836
  94.5 6.7 %collective-permute-done.7.refs_4_.refs_2_ = bf16[768,256]{1,0:T(8,128)(2,1)S(1)} collective-permute-done((bf16[768,256]{1,0:T(8,128)(2,1)S(1)}, bf16[768,256]{1,0:T(8,128)(2,1)S(1)}, u32[]{:S(2)}, u32[]{:S(2)}) %collective-permute-start.7) | collective-permute-done | bytes 393248 | tf_op jit(solution)/shard_map/ppermute | solution.py:956
  106.0 15.3 %shard_map.157 = (bf16[768,256]{1,0:T(8,128)(2,1)S(1)}, bf16[768,256]{1,0:T(8,128)(2,1)S(1)}, bf16[768,256]{1,0:T(8,128)(2,1)S(1)}, bf16[768,256]{1,0:T(8,128)(2...) custom-call(s32[13]{0:T(128)S(1)} %stack.42.info, ...), custom_call_target="tpu_custom_call" | custom-call | flops 23000000512 | bytes 20701184 | tf_op jit(solution)/shard_map/pallas_call | solution.py:836
  129.0 3.1 %collective-permute-start.19 = (bf16[768,256]{1,0:T(8,128)(2,1)S(1)}, bf16[768,256]{1,0:T(8,128)(2,1)S(1)}, u32[]{:S(2)}, u32[]{:S(2)}) collective-permute-start(bf16[768,256]{1,0:T(8,128)(2,1)S(1)} %get-tuple-element.167), channel_id=1, source_target_pairs={{0,8},{1,12},{2,10},{3,14},{4,9},{5,13},{6,11},{7,15},{8,0},{9,4},... | collective-permute-start | bytes 1179656 | tf_op jit(solution)/shard_map/ppermute | solution.py:956
  137.0 2.7 %collective-permute-done.22.refs_5_ = bf16[320,256]{1,0:T(8,128)(2,1)S(1)} collective-permute-done((bf16[320,256]{1,0:T(8,128)(2,1)S(1)}, bf16[320,256]{1,0:T(8,128)(2,1)S(1)}, u32[]{:S(2)}, u32[]{:S(2)}) %collective-permute-start.22) | collective-permute-done | bytes 163872 | tf_op jit(solution)/shard_map/ppermute | solution.py:1040
  139.7 5.2 %collective-permute-done.23.refs_6_ = bf16[320,256]{1,0:T(8,128)(2,1)S(1)} collective-permute-done((bf16[320,256]{1,0:T(8,128)(2,1)S(1)}, bf16[320,256]{1,0:T(8,128)(2,1)S(1)}, u32[]{:S(2)}, u32[]{:S(2)}) %collective-permute-start.23) | collective-permute-done | bytes 163872 | tf_op jit(solution)/shard_map/ppermute | solution.py:1040
  146.2 3.9 %collective-permute-done.19.refs_2_ = bf16[768,256]{1,0:T(8,128)(2,1)S(1)} collective-permute-done((bf16[768,256]{1,0:T(8,128)(2,1)S(1)}, bf16[768,256]{1,0:T(8,128)(2,1)S(1)}, u32[]{:S(2)}, u32[]{:S(2)}) %collective-permute-start.19) | collective-permute-done | bytes 393248 | tf_op jit(solution)/shard_map/ppermute | solution.py:956
  150.1 7.4 %collective-permute-done.25.refs_1_ = bf16[256,256]{1,0:T(8,128)(2,1)S(1)} collective-permute-done((bf16[256,256]{1,0:T(8,128)(2,1)S(1)}, bf16[256,256]{1,0:T(8,128)(2,1)S(1)}, u32[]{:S(2)}, u32[]{:S(2)}) %collective-permute-start.25) | collective-permute-done | bytes 131104 | tf_op jit(solution)/shard_map/ppermute | solution.py:1040
  161.2 12.1 %collective-permute-done.28.refs_1_ = bf16[256,256]{1,0:T(8,128)(2,1)S(1)} collective-permute-done((bf16[256,256]{1,0:T(8,128)(2,1)S(1)}, bf16[256,256]{1,0:T(8,128)(2,1)S(1)}, u32[]{:S(2)}, u32[]{:S(2)}) %collective-permute-start.28) | collective-permute-done | bytes 131104 | tf_op jit(solution)/shard_map/ppermute | solution.py:1040
  174.7 5.5 %collective-permute-done.30.refs_1_ = bf16[224,256]{1,0:T(8,128)(2,1)S(1)} collective-permute-done((bf16[224,256]{1,0:T(8,128)(2,1)S(1)}, bf16[224,256]{1,0:T(8,128)(2,1)S(1)}, u32[]{:S(2)}, u32[]{:S(2)}) %collective-permute-start.30) | collective-permute-done | bytes 114720 | tf_op jit(solution)/shard_map/ppermute | solution.py:1061
  184.4 2.3 %shard_map.161 = (f32[8,384,256]{2,1,0:T(8,128)}, f32[8,128]{1,0:T(8,128)S(1)}) custom-call(s32[13]{0:T(128)S(1)} %stack.42.info, bf16[768,256]{1,0:T(8,128)(2,1)S(1)} %collective-permute-done.8.refs_2_.refs_0_, bf16[768,256]{1,0:T(8,128)(2,1)S(1)} %collective-permute-done.9.refs_3_.refs_1_, bf16[768,256]{1,0:T(8,128)(2,1)S(1)} %collective-permute-done.7.refs_4_.refs_2_, ...), custom_call_target="tpu_custom_call" | custom-call | bytes 5509120 | tf_op jit(solution)/shard_map/pallas_call | solution.py:836
  186.7 2.3 %shard_map.167 = (f32[8,384,256]{2,1,0:T(8,128)}, f32[8,128]{1,0:T(8,128)S(1)}) custom-call(s32[13]{0:T(128)S(1)} %stack.42.info, bf16[768,256]{1,0:T(8,128)(2,1)S(1)} %collective-permute-done.18.refs_0_, bf16[768,256]{1,0:T(8,128)(2,1)S(1)} %collective-permute-done.26.refs_1_, bf16[768,256]{1,0:T(8,128)(2,1)S(1)} %collective-permute-done.19.refs_2_, ...), custom_call_target="tpu_custom_call" | custom-call | bytes 5509120 | tf_op jit(solution)/shard_map/pallas_call | solution.py:836
  189.4 5.1 %collective-permute-done.32.refs_2_ = bf16[448,256]{1,0:T(8,128)(2,1)S(1)} collective-permute-done((bf16[448,256]{1,0:T(8,128)(2,1)S(1)}, bf16[448,256]{1,0:T(8,128)(2,1)S(1)}, u32[]{:S(2)}, u32[]{:S(2)}) %collective-permute-start.32) | collective-permute-done | bytes 229408 | tf_op jit(solution)/shard_map/ppermute | solution.py:1040
  195.2 2.4 %collective-permute-done.34.refs_1_ = bf16[1792,256]{1,0:T(8,128)(2,1)S(1)} collective-permute-done((bf16[1792,256]{1,0:T(8,128)(2,1)S(1)}, bf16[1792,256]{1,0:T(8,128)(2,1)S(1)}, u32[]{:S(2)}, u32[]{:S(2)}) %collective-permute-start.34) | collective-permute-done | bytes 917536 | tf_op jit(solution)/shard_map/ppermute | solution.py:1037
  197.6 2.7 %shard_map.170 = (f32[2,256,512]{2,1,0:T(8,128)}, f32[2,256,256]{2,1,0:T(8,128)}, f32[2,256,512]{2,1,0:T(8,128)}, f32[2,512,256]{2,1,0:T(8,128)}, f32[2,2,256]{2...) custom-call(s32[13]{0:T(128)S(1)} %stack.42.info, bf16[1792,256]{1,0:T(8,128)(2,1)S(1)} %shard_map.169.refs_0_, ...), custom_call_target="tpu_custom_call" | custom-call | bytes 5529824 | tf_op jit(solution)/shard_map/pallas_call | solution.py:836
  (95 shorter events, 43.7 us)
Async XLA Ops:
  4.9 31.8 %collective-permute-start.4 = (bf16[768,256]{1,0:T(8,128)(2,1)S(1)}, bf16[768,256]{1,0:T(8,128)(2,1)S(1)}, u32[]{:S(2)}, u32[]{:S(2)}) collective-permute-start(bf16[768,256]{1,0:T(8,128)(2,1)S(1)} %maximum_select_fusion.3), channel_id=1, source_target_pairs={{0,10},{1,14},{2,8},{3,12},{4,11},{5,15},{6,9},{7,13},{8,2},{9,6},... | collective-permute-start | bytes 1179656 | tf_op jit(solution)/shard_map/ppermute | solution.py:949
  10.0 35.0 %collective-permute-start.3 = (bf16[768,256]{1,0:T(8,128)(2,1)S(1)}, bf16[768,256]{1,0:T(8,128)(2,1)S(1)}, u32[]{:S(2)}, u32[]{:S(2)}) collective-permute-start(bf16[768,256]{1,0:T(8,128)(2,1)S(1)} %maximum_select_fusion.2), channel_id=1, source_target_pairs={{0,8},{1,12},{2,10},{3,14},{4,9},{5,13},{6,11},{7,15},{8,0},{9,4},... | collective-permute-start | bytes 1179656 | tf_op jit(solution)/shard_map/ppermute | solution.py:949
  10.6 34.4 %collective-permute-start.2 = (bf16[768,256]{1,0:T(8,128)(2,1)S(1)}, bf16[768,256]{1,0:T(8,128)(2,1)S(1)}, u32[]{:S(2)}, u32[]{:S(2)}) collective-permute-start(bf16[768,256]{1,0:T(8,128)(2,1)S(1)} %maximum_select_fusion.1), channel_id=1, source_target_pairs={{0,2},{1,6},{2,0},{3,4},{4,3},{5,7},{6,1},{7,5},{8,10},{9,14},{10,... | collective-permute-start | bytes 1179656 | tf_op jit(solution)/shard_map/ppermute | solution.py:949
  11.0 33.9 %collective-permute-start.1 = (bf16[768,256]{1,0:T(8,128)(2,1)S(1)}, bf16[768,256]{1,0:T(8,128)(2,1)S(1)}, u32[]{:S(2)}, u32[]{:S(2)}) collective-permute-start(bf16[768,256]{1,0:T(8,128)(2,1)S(1)} %maximum_select_fusion), channel_id=1, source_target_pairs={{0,0},{1,4},{2,2},{3,6},{4,1},{5,5},{6,3},{7,7},{8,8},{9,12},{10,1... | collective-permute-start | bytes 1179656 | tf_op jit(solution)/shard_map/ppermute | solution.py:949
  81.3 20.0 %collective-permute-start.7 = (bf16[768,256]{1,0:T(8,128)(2,1)S(1)}, bf16[768,256]{1,0:T(8,128)(2,1)S(1)}, u32[]{:S(2)}, u32[]{:S(2)}) collective-permute-start(bf16[768,256]{1,0:T(8,128)(2,1)S(1)} %get-tuple-element.114), channel_id=1, source_target_pairs={{0,8},{1,12},{2,10},{3,14},{4,9},{5,13},{6,11},{7,15},{8,0},{9,4},... | collective-permute-start | bytes 1179656 | tf_op jit(solution)/shard_map/ppermute | solution.py:956
  83.9 17.3 %collective-permute-start.12 = (bf16[160,256]{1,0:T(8,128)(2,1)S(1)}, bf16[160,256]{1,0:T(8,128)(2,1)S(1)}, u32[]{:S(2)}, u32[]{:S(2)}) collective-permute-start(bf16[160,256]{1,0:T(8,128)(2,1)S(1)} %get-tuple-element.133), channel_id=1, source_target_pairs={{0,16},{1,17},{2,18},{3,19},{4,20},{5,21},{6,22},{7,23},{8,24},{9,... | collective-permute-start | bytes 245768 | tf_op jit(solution)/shard_map/ppermute | solution.py:1040
  85.5 15.8 %collective-permute-start.13 = (bf16[160,256]{1,0:T(8,128)(2,1)S(1)}, bf16[160,256]{1,0:T(8,128)(2,1)S(1)}, u32[]{:S(2)}, u32[]{:S(2)}) collective-permute-start(bf16[160,256]{1,0:T(8,128)(2,1)S(1)} %get-tuple-element.134), channel_id=1, source_target_pairs={{0,2},{1,3},{2,0},{3,1},{4,6},{5,7},{6,4},{7,5},{8,10},{9,11},{10,... | collective-permute-start | bytes 245768 | tf_op jit(solution)/shard_map/ppermute | solution.py:1040
  86.0 15.3 %collective-permute-start.14 = (bf16[160,256]{1,0:T(8,128)(2,1)S(1)}, bf16[160,256]{1,0:T(8,128)(2,1)S(1)}, u32[]{:S(2)}, u32[]{:S(2)}) collective-permute-start(bf16[160,256]{1,0:T(8,128)(2,1)S(1)} %get-tuple-element.135), channel_id=1, source_target_pairs={{0,18},{1,19},{2,16},{3,17},{4,22},{5,23},{6,20},{7,21},{8,26},{9,... | collective-permute-start | bytes 245768 | tf_op jit(solution)/shard_map/ppermute | solution.py:1040
  102.6 20.4 %collective-permute-start.10 = (bf16[768,256]{1,0:T(8,128)(2,1)S(1)}, bf16[768,256]{1,0:T(8,128)(2,1)S(1)}, u32[]{:S(2)}, u32[]{:S(2)}) collective-permute-start(bf16[768,256]{1,0:T(8,128)(2,1)S(1)} %get-tuple-element.119), channel_id=1, source_target_pairs={{0,10},{1,14},{2,8},{3,12},{4,11},{5,15},{6,9},{7,13},{8,2},{9,6},... | collective-permute-start | bytes 1179656 | tf_op jit(solution)/shard_map/ppermute | solution.py:956
  102.7 20.5 %collective-permute-start.9 = (bf16[768,256]{1,0:T(8,128)(2,1)S(1)}, bf16[768,256]{1,0:T(8,128)(2,1)S(1)}, u32[]{:S(2)}, u32[]{:S(2)}) collective-permute-start(bf16[768,256]{1,0:T(8,128)(2,1)S(1)} %get-tuple-element.117), channel_id=1, source_target_pairs={{0,2},{1,6},{2,0},{3,4},{4,3},{5,7},{6,1},{7,5},{8,10},{9,14},{10,... | collective-permute-start | bytes 1179656 | tf_op jit(solution)/shard_map/ppermute | solution.py:956
  103.7 19.5 %collective-permute-start.8 = (bf16[768,256]{1,0:T(8,128)(2,1)S(1)}, bf16[768,256]{1,0:T(8,128)(2,1)S(1)}, u32[]{:S(2)}, u32[]{:S(2)}) collective-permute-start(bf16[768,256]{1,0:T(8,128)(2,1)S(1)} %get-tuple-element.115), channel_id=1, source_target_pairs={{0,0},{1,4},{2,2},{3,6},{4,1},{5,5},{6,3},{7,7},{8,8},{9,12},{10,1... | collective-permute-start | bytes 1179656 | tf_op jit(solution)/shard_map/ppermute | solution.py:956
  121.3 10.7 %collective-permute-start.20 = (bf16[896,256]{1,0:T(8,128)(2,1)S(1)}, bf16[896,256]{1,0:T(8,128)(2,1)S(1)}, u32[]{:S(2)}, u32[]{:S(2)}) collective-permute-start(bf16[896,256]{1,0:T(8,128)(2,1)S(1)} %get-tuple-element.170), channel_id=1, source_target_pairs={{0,1},{1,0},{2,3},{3,2},{4,5},{5,4},{6,7},{7,6},{8,9},{9,8},{10,11... | collective-permute-start | bytes 1376264 | tf_op jit(solution)/shard_map/ppermute | solution.py:1037
  129.0 21.2 %collective-permute-start.19 = (bf16[768,256]{1,0:T(8,128)(2,1)S(1)}, bf16[768,256]{1,0:T(8,128)(2,1)S(1)}, u32[]{:S(2)}, u32[]{:S(2)}) collective-permute-start(bf16[768,256]{1,0:T(8,128)(2,1)S(1)} %get-tuple-element.167), channel_id=1, source_target_pairs={{0,8},{1,12},{2,10},{3,14},{4,9},{5,13},{6,11},{7,15},{8,0},{9,4},... | collective-permute-start | bytes 1179656 | tf_op jit(solution)/shard_map/ppermute | solution.py:956
  134.3 10.5 %collective-permute-start.23 = (bf16[320,256]{1,0:T(8,128)(2,1)S(1)}, bf16[320,256]{1,0:T(8,128)(2,1)S(1)}, u32[]{:S(2)}, u32[]{:S(2)}) collective-permute-start(bf16[320,256]{1,0:T(8,128)(2,1)S(1)} %get-tuple-element.175), channel_id=1, source_target_pairs={{0,2},{1,3},{2,0},{3,1},{4,6},{5,7},{6,4},{7,5},{8,10},{9,11},{10,... | collective-permute-start | bytes 491528 | tf_op jit(solution)/shard_map/ppermute | solution.py:1040
  134.9 10.0 %collective-permute-start.24 = (bf16[320,256]{1,0:T(8,128)(2,1)S(1)}, bf16[320,256]{1,0:T(8,128)(2,1)S(1)}, u32[]{:S(2)}, u32[]{:S(2)}) collective-permute-start(bf16[320,256]{1,0:T(8,128)(2,1)S(1)} %get-tuple-element.176), channel_id=1, source_target_pairs={{0,18},{1,19},{2,16},{3,17},{4,22},{5,23},{6,20},{7,21},{8,26},{9,... | collective-permute-start | bytes 491528 | tf_op jit(solution)/shard_map/ppermute | solution.py:1040
  136.3 23.4 %collective-permute-start.18 = (bf16[768,256]{1,0:T(8,128)(2,1)S(1)}, bf16[768,256]{1,0:T(8,128)(2,1)S(1)}, u32[]{:S(2)}, u32[]{:S(2)}) collective-permute-start(bf16[768,256]{1,0:T(8,128)(2,1)S(1)} %get-tuple-element.165), channel_id=1, source_target_pairs={{0,0},{1,4},{2,2},{3,6},{4,1},{5,5},{6,3},{7,7},{8,8},{9,12},{10,1... | collective-permute-start | bytes 1179656 | tf_op jit(solution)/shard_map/ppermute | solution.py:956
  145.6 11.9 %collective-permute-start.25 = (bf16[256,256]{1,0:T(8,128)(2,1)S(1)}, bf16[256,256]{1,0:T(8,128)(2,1)S(1)}, u32[]{:S(2)}, u32[]{:S(2)}) collective-permute-start(bf16[256,256]{1,0:T(8,128)(2,1)S(1)} %get-tuple-element.178), channel_id=1, source_target_pairs={{0,4},{1,5},{2,6},{3,7},{4,0},{5,1},{6,2},{7,3},{8,12},{9,13},{10,... | collective-permute-start | bytes 393224 | tf_op jit(solution)/shard_map/ppermute | solution.py:1040
  150.1 23.8 %collective-permute-start.27 = (bf16[768,256]{1,0:T(8,128)(2,1)S(1)}, bf16[768,256]{1,0:T(8,128)(2,1)S(1)}, u32[]{:S(2)}, u32[]{:S(2)}) collective-permute-start(bf16[768,256]{1,0:T(8,128)(2,1)S(1)} %get-tuple-element.181), channel_id=1, source_target_pairs={{0,10},{1,14},{2,8},{3,12},{4,11},{5,15},{6,9},{7,13},{8,2},{9,6},... | collective-permute-start | bytes 1179656 | tf_op jit(solution)/shard_map/ppermute | solution.py:956
  157.5 16.5 %collective-permute-start.26 = (bf16[768,256]{1,0:T(8,128)(2,1)S(1)}, bf16[768,256]{1,0:T(8,128)(2,1)S(1)}, u32[]{:S(2)}, u32[]{:S(2)}) collective-permute-start(bf16[768,256]{1,0:T(8,128)(2,1)S(1)} %get-tuple-element.179), channel_id=1, source_target_pairs={{0,2},{1,6},{2,0},{3,4},{4,3},{5,7},{6,1},{7,5},{8,10},{9,14},{10,... | collective-permute-start | bytes 1179656 | tf_op jit(solution)/shard_map/ppermute | solution.py:956
  159.7 13.7 %collective-permute-start.28 = (bf16[256,256]{1,0:T(8,128)(2,1)S(1)}, bf16[256,256]{1,0:T(8,128)(2,1)S(1)}, u32[]{:S(2)}, u32[]{:S(2)}) collective-permute-start(bf16[256,256]{1,0:T(8,128)(2,1)S(1)} %get-tuple-element.185.refs_0_), channel_id=1, source_target_pairs={{0,8},{1,9},{2,10},{3,11},{4,12},{5,13},{6,14},{7,15},{8,0},{9,1},... | collective-permute-start | bytes 393224 | tf_op jit(solution)/shard_map/ppermute | solution.py:1040
  160.3 24.0 %collective-permute-start.17 = (bf16[4,384,256]{2,1,0:T(8,128)(2,1)S(1)}, bf16[4,384,256]{2,1,0:T(8,128)(2,1)S(1)}, u32[]{:S(2)}, u32[]{:S(2)}) collective-permute-start(bf16[4,384,256]{2,1,0:T(8,128)(2,1)S(1)} %shard_map.160), channel_id=1, source_target_pairs={{0,1},{1,0},{2,3},{3,2},{4,5},{5,4},{6,7},{7,6},{8,9},{9,8},{10,11... | collective-permute-start | bytes 2359304 | tf_op jit(solution)/shard_map/ppermute | solution.py:961
  174.6 12.1 %collective-permute-start.29 = (bf16[4,384,256]{2,1,0:T(8,128)(2,1)S(1)}, bf16[4,384,256]{2,1,0:T(8,128)(2,1)S(1)}, u32[]{:S(2)}, u32[]{:S(2)}) collective-permute-start(bf16[4,384,256]{2,1,0:T(8,128)(2,1)S(1)} %shard_map.166), channel_id=1, source_target_pairs={{0,1},{1,0},{2,3},{3,2},{4,5},{5,4},{6,7},{7,6},{8,9},{9,8},{10,11... | collective-permute-start | bytes 2359304 | tf_op jit(solution)/shard_map/ppermute | solution.py:961
  182.7 11.8 %collective-permute-start.32 = (bf16[448,256]{1,0:T(8,128)(2,1)S(1)}, bf16[448,256]{1,0:T(8,128)(2,1)S(1)}, u32[]{:S(2)}, u32[]{:S(2)}) collective-permute-start(bf16[448,256]{1,0:T(8,128)(2,1)S(1)} %shard_map.168.refs_0_), channel_id=1, source_target_pairs={{0,2},{1,3},{2,0},{3,1},{4,6},{5,7},{6,4},{7,5},{8,10},{9,11},{10,... | collective-permute-start | bytes 688136 | tf_op jit(solution)/shard_map/ppermute | solution.py:1040
  183.6 10.8 %collective-permute-start.33 = (bf16[448,256]{1,0:T(8,128)(2,1)S(1)}, bf16[448,256]{1,0:T(8,128)(2,1)S(1)}, u32[]{:S(2)}, u32[]{:S(2)}) collective-permute-start(bf16[448,256]{1,0:T(8,128)(2,1)S(1)} %shard_map.168.refs_0_), channel_id=1, source_target_pairs={{0,18},{1,19},{2,16},{3,17},{4,22},{5,23},{6,20},{7,21},{8,26},{9,... | collective-permute-start | bytes 688136 | tf_op jit(solution)/shard_map/ppermute | solution.py:1040
  (18 other events, 77.1 us)

commit v10 on v9

--- a/solution.py
+++ b/solution.py
@@ -1089,7 +1089,7 @@
          pltpu.VMEM((n + WIN, width), F32), pltpu.VMEM((n + WIN, width), F32)], steps, work=20,
     )
     halo_send, _ = call(
-        hold_kernel, info, [halo_send, halo_send] + forward_back, [VMEM] * 2 + [ANY] * 4, [halo_shape] * 2, [VMEM] * 2
+        hold_kernel, info, [halo_send, halo_send] + forward_back[2:], [VMEM] * 2 + [ANY] * 2, [halo_shape] * 2, [VMEM] * 2
     )
     halo_got = lax.ppermute(halo_send, "section", second_to_first)
 

time: 201 us -> 201 us (level)
  starting transfers between devices: 36.5 us -> 40.8 us
  waiting for transfers between devices: 92 us -> 88.3 us
    ppermute x2, starting transfers between devices: 1.01 us -> 9.03 us  [trade(): return lax.ppermute(send, 'section', swap)]
    ppermute x11, waiting for transfers between devices: 32.9 us -> 27.5 us  [send_all(): lax.ppermute(m, ('dp', 'section'), way)]
    ppermute x8, starting transfers between devices: 8.52 us -> 6 us  [send_back(): return lax.ppermute(message, 'section', route(pairs))]
  transfers between devices with their start and end apart: 35 -> 35, of which waited for: 18 -> 19; matrix products, arithmetic and copies ran while one was open for 1% -> 1% of each run, Pallas kernels for 17% -> 17%
where the time goes in v10:
time: 201 us
  waiting for transfers between devices  88.3 us (44%)
  Pallas kernels  67 us (33%)
  starting transfers between devices  40.8 us (20%)
  local copies, waits for them, and re-layouts  3.08 us (2%)
    pallas_call x20, Pallas kernels, call(): pl.pallas_call(body_of, grid_spec=pltpu.PrefetchScalarGridSpec(num_scalar...  67 us
    ppermute x4, waiting for transfers between devices, body(): received[t] = lax.ppermute(message, 'section', route(pairs))  33.2 us
    ppermute x11, waiting for transfers between devices, send_all(): lax.ppermute(m, ('dp', 'section'), way)  27.5 us
    ppermute x11, starting transfers between devices, send_all(): lax.ppermute(m, ('dp', 'section'), way)  11.3 us
    ppermute x8, waiting for transfers between devices, send_back(): return lax.ppermute(message, 'section', route(pairs))  10.2 us
    ppermute x2, starting transfers between devices, trade(): return lax.ppermute(send, 'section', swap)  9.03 us
    ppermute x4, starting transfers between devices, body(): received[t] = lax.ppermute(message, 'section', route(pairs))  6.37 us
    ppermute x8, starting transfers between devices, send_back(): return lax.ppermute(message, 'section', route(pairs))  6 us
  transfers between devices with their start and end apart: 35, of which 19 were waited for; matrix products, arithmetic and copies ran while one was open for 1% of the time, Pallas kernels for 17%

profile of v10, /device:TPU:0, one launch (start us, length us, event | category | flops | bytes accessed | tf_op | source)
XLA Modules:
  0.0 200.9 jit_solution(6521640999742645375)
XLA Ops:
  4.9 5.0 %collective-permute-start.4 = (bf16[768,256]{1,0:T(8,128)(2,1)S(1)}, bf16[768,256]{1,0:T(8,128)(2,1)S(1)}, u32[]{:S(2)}, u32[]{:S(2)}) collective-permute-start(bf16[768,256]{1,0:T(8,128)(2,1)S(1)} %maximum_select_fusion.3), channel_id=1, source_target_pairs={{0,10},{1,14},{2,8},{3,12},{4,11},{5,15},{6,9},{7,13},{8,2},{9,6},... | collective-permute-start | bytes 1179656 | tf_op jit(solution)/shard_map/ppermute | solution.py:949
  11.8 24.9 %collective-permute-done.4.refs_3_ = bf16[768,256]{1,0:T(8,128)(2,1)S(1)} collective-permute-done((bf16[768,256]{1,0:T(8,128)(2,1)S(1)}, bf16[768,256]{1,0:T(8,128)(2,1)S(1)}, u32[]{:S(2)}, u32[]{:S(2)}) %collective-permute-start.4) | collective-permute-done | bytes 393248 | tf_op jit(solution)/shard_map/ppermute | solution.py:949
  36.7 8.3 %collective-permute-done.3.refs_2_ = bf16[768,256]{1,0:T(8,128)(2,1)S(1)} collective-permute-done((bf16[768,256]{1,0:T(8,128)(2,1)S(1)}, bf16[768,256]{1,0:T(8,128)(2,1)S(1)}, u32[]{:S(2)}, u32[]{:S(2)}) %collective-permute-start.3) | collective-permute-done | bytes 393248 | tf_op jit(solution)/shard_map/ppermute | solution.py:949
  49.3 6.6 %shard_map.152 = (bf16[1536,256]{1,0:T(8,128)(2,1)S(1)}, bf16[1536,128]{1,0:T(8,128)(2,1)S(1)}, bf16[1536,384]{1,0:T(8,128)(2,1)S(1)}, bf16[1536,256]{1,0:T(8,12...) custom-call(s32[13]{0:T(128)S(1)} %stack.42.info, ...), custom_call_target="tpu_custom_call" | custom-call | flops 17250000896 | bytes 12124160 | tf_op jit(solution)/shard_map/pallas_call | solution.py:836
  55.9 2.5 %collective-permute-start.6 = (bf16[1536,384]{1,0:T(8,128)(2,1)S(1)}, bf16[1536,384]{1,0:T(8,128)(2,1)S(1)}, u32[]{:S(2)}, u32[]{:S(2)}) collective-permute-start(bf16[1536,384]{1,0:T(8,128)(2,1)S(1)} %get-tuple-element.109.refs_1_.refs_5_), channel_id=1, source_target_pairs={{0,1},{2,3},{4,5},{6,7},{8,9},{10,11},{12,13},{14,15},{16,17},{18,... | collective-permute-start | bytes 3538952 | tf_op jit(solution)/shard_map/ppermute | solution.py:997
  58.4 2.2 %collective-permute-done.6.refs_2_.refs_6_ = bf16[1536,384]{1,0:T(8,128)(2,1)S(1)} collective-permute-done((bf16[1536,384]{1,0:T(8,128)(2,1)S(1)}, bf16[1536,384]{1,0:T(8,128)(2,1)S(1)}, u32[]{:S(2)}, u32[]{:S(2)}) %collective-permute-start.6) | collective-permute-done | bytes 1179680 | tf_op jit(solution)/shard_map/ppermute | solution.py:997
  60.6 4.1 %shard_map.153 = (bf16[1536,128]{1,0:T(8,128)(2,1)S(1)}, bf16[3072,128]{1,0:T(8,128)(2,1)S(1)}, bf16[3072,256]{1,0:T(8,128)(2,1)S(1)}, f32[1536,256]{1,0:T(8,128)S(1)}, f32[1536,128]{1,0:T(8,128)S(1)}) custom-call(s32[13]{0:T(128)S(1)} %stack.42.info, bf16[1536,128]{1,0:T(8,128)(2,1)S(1)} %get-tuple-element.108.refs_0_.refs_4_, ...), custom_call_target="tpu_custom_call" | custom-call | flops 16099999744 | bytes 7864320 | tf_op jit(solution)/shard_map/pallas_call | solution.py:836
  64.7 16.1 %shard_map.154 = (bf16[768,256]{1,0:T(8,128)(2,1)S(1)}, bf16[768,256]{1,0:T(8,128)(2,1)S(1)}, bf16[768,256]{1,0:T(8,128)(2,1)S(1)}, bf16[768,256]{1,0:T(8,128)(2...) custom-call(s32[13]{0:T(128)S(1)} %stack.42.info, ...), custom_call_target="tpu_custom_call" | custom-call | flops 27599998976 | bytes 17215488 | tf_op jit(solution)/shard_map/pallas_call | solution.py:836
  87.5 7.2 %shard_map.155 = (f32[1536,128]{1,0:T(8,128)S(1)}, f32[1536,384]{1,0:T(8,128)S(1)}, bf16[1536,384]{1,0:T(8,128)(2,1)S(1)}) custom-call(s32[13]{0:T(128)S(1)} %stack.42.info, bf16[1536,128]{1,0:T(8,128)(2,1)S(1)} %get-tuple-element.120.refs_0_, bf16[3072,128]{1,0:T(8,128)(2,1)S(1)} %get-tuple-element.121.refs_1_, ...), custom_call_target="tpu_custom_call" | custom-call | flops 20700000256 | bytes 11993088 | tf_op jit(solution)/shard_map/pallas_call | solution.py:836
  94.7 6.6 %collective-permute-done.7.refs_2_ = bf16[768,256]{1,0:T(8,128)(2,1)S(1)} collective-permute-done((bf16[768,256]{1,0:T(8,128)(2,1)S(1)}, bf16[768,256]{1,0:T(8,128)(2,1)S(1)}, u32[]{:S(2)}, u32[]{:S(2)}) %collective-permute-start.7) | collective-permute-done | bytes 393248 | tf_op jit(solution)/shard_map/ppermute | solution.py:956
  102.7 3.4 %collective-permute-done.15.refs_2_ = bf16[1536,384]{1,0:T(8,128)(2,1)S(1)} collective-permute-done((bf16[1536,384]{1,0:T(8,128)(2,1)S(1)}, bf16[1536,384]{1,0:T(8,128)(2,1)S(1)}, u32[]{:S(2)}, u32[]{:S(2)}) %collective-permute-start.15) | collective-permute-done | bytes 1179680 | tf_op jit(solution)/shard_map/ppermute | solution.py:1070
  106.0 15.1 %shard_map.157 = (bf16[768,256]{1,0:T(8,128)(2,1)S(1)}, bf16[768,256]{1,0:T(8,128)(2,1)S(1)}, bf16[768,256]{1,0:T(8,128)(2,1)S(1)}, bf16[768,256]{1,0:T(8,128)(2...) custom-call(s32[13]{0:T(128)S(1)} %stack.42.info, ...), custom_call_target="tpu_custom_call" | custom-call | flops 23000000512 | bytes 20701184 | tf_op jit(solution)/shard_map/pallas_call | solution.py:836
  134.7 2.8 %collective-permute-done.22.refs_5_ = bf16[320,256]{1,0:T(8,128)(2,1)S(1)} collective-permute-done((bf16[320,256]{1,0:T(8,128)(2,1)S(1)}, bf16[320,256]{1,0:T(8,128)(2,1)S(1)}, u32[]{:S(2)}, u32[]{:S(2)}) %collective-permute-start.22) | collective-permute-done | bytes 163872 | tf_op jit(solution)/shard_map/ppermute | solution.py:1040
  137.6 4.3 %collective-permute-done.23.refs_6_ = bf16[320,256]{1,0:T(8,128)(2,1)S(1)} collective-permute-done((bf16[320,256]{1,0:T(8,128)(2,1)S(1)}, bf16[320,256]{1,0:T(8,128)(2,1)S(1)}, u32[]{:S(2)}, u32[]{:S(2)}) %collective-permute-start.23) | collective-permute-done | bytes 163872 | tf_op jit(solution)/shard_map/ppermute | solution.py:1040
  144.9 2.5 %collective-permute-done.19.refs_2_ = bf16[768,256]{1,0:T(8,128)(2,1)S(1)} collective-permute-done((bf16[768,256]{1,0:T(8,128)(2,1)S(1)}, bf16[768,256]{1,0:T(8,128)(2,1)S(1)}, u32[]{:S(2)}, u32[]{:S(2)}) %collective-permute-start.19) | collective-permute-done | bytes 393248 | tf_op jit(solution)/shard_map/ppermute | solution.py:956
  147.4 3.7 %collective-permute-done.25.refs_1_ = bf16[256,256]{1,0:T(8,128)(2,1)S(1)} collective-permute-done((bf16[256,256]{1,0:T(8,128)(2,1)S(1)}, bf16[256,256]{1,0:T(8,128)(2,1)S(1)}, u32[]{:S(2)}, u32[]{:S(2)}) %collective-permute-start.25) | collective-permute-done | bytes 131104 | tf_op jit(solution)/shard_map/ppermute | solution.py:1040
  153.9 8.9 %collective-permute-start.17 = (bf16[4,384,256]{2,1,0:T(8,128)(2,1)S(1)}, bf16[4,384,256]{2,1,0:T(8,128)(2,1)S(1)}, u32[]{:S(2)}, u32[]{:S(2)}) collective-permute-start(bf16[4,384,256]{2,1,0:T(8,128)(2,1)S(1)} %shard_map.160), channel_id=1, source_target_pairs={{0,1},{1,0},{2,3},{3,2},{4,5},{5,4},{6,7},{7,6},{8,9},{9,8},{10,11... | collective-permute-start | bytes 2359304 | tf_op jit(solution)/shard_map/ppermute | solution.py:961
  162.8 11.8 %collective-permute-done.28.refs_1_ = bf16[256,256]{1,0:T(8,128)(2,1)S(1)} collective-permute-done((bf16[256,256]{1,0:T(8,128)(2,1)S(1)}, bf16[256,256]{1,0:T(8,128)(2,1)S(1)}, u32[]{:S(2)}, u32[]{:S(2)}) %collective-permute-start.28) | collective-permute-done | bytes 131104 | tf_op jit(solution)/shard_map/ppermute | solution.py:1040
  176.0 5.5 %collective-permute-done.30.refs_1_ = bf16[224,256]{1,0:T(8,128)(2,1)S(1)} collective-permute-done((bf16[224,256]{1,0:T(8,128)(2,1)S(1)}, bf16[224,256]{1,0:T(8,128)(2,1)S(1)}, u32[]{:S(2)}, u32[]{:S(2)}) %collective-permute-start.30) | collective-permute-done | bytes 114720 | tf_op jit(solution)/shard_map/ppermute | solution.py:1061
  185.6 2.3 %shard_map.161 = (f32[8,384,256]{2,1,0:T(8,128)}, f32[8,128]{1,0:T(8,128)S(1)}) custom-call(s32[13]{0:T(128)S(1)} %stack.42.info, bf16[768,256]{1,0:T(8,128)(2,1)S(1)} %collective-permute-done.8.refs_0_, bf16[768,256]{1,0:T(8,128)(2,1)S(1)} %collective-permute-done.9.refs_1_, bf16[768,256]{1,0:T(8,128)(2,1)S(1)} %collective-permute-done.7.refs_2_, ...), custom_call_target="tpu_custom_call" | custom-call | bytes 5509120 | tf_op jit(solution)/shard_map/pallas_call | solution.py:836
  187.9 2.3 %shard_map.167 = (f32[8,384,256]{2,1,0:T(8,128)}, f32[8,128]{1,0:T(8,128)S(1)}) custom-call(s32[13]{0:T(128)S(1)} %stack.42.info, bf16[768,256]{1,0:T(8,128)(2,1)S(1)} %collective-permute-done.18.refs_0_, bf16[768,256]{1,0:T(8,128)(2,1)S(1)} %collective-permute-done.26.refs_1_, bf16[768,256]{1,0:T(8,128)(2,1)S(1)} %collective-permute-done.19.refs_2_, ...), custom_call_target="tpu_custom_call" | custom-call | bytes 5509120 | tf_op jit(solution)/shard_map/pallas_call | solution.py:836
  190.6 4.5 %collective-permute-done.32.refs_2_ = bf16[448,256]{1,0:T(8,128)(2,1)S(1)} collective-permute-done((bf16[448,256]{1,0:T(8,128)(2,1)S(1)}, bf16[448,256]{1,0:T(8,128)(2,1)S(1)}, u32[]{:S(2)}, u32[]{:S(2)}) %collective-permute-start.32) | collective-permute-done | bytes 229408 | tf_op jit(solution)/shard_map/ppermute | solution.py:1040
  195.8 2.4 %collective-permute-done.34.refs_1_ = bf16[1792,256]{1,0:T(8,128)(2,1)S(1)} collective-permute-done((bf16[1792,256]{1,0:T(8,128)(2,1)S(1)}, bf16[1792,256]{1,0:T(8,128)(2,1)S(1)}, u32[]{:S(2)}, u32[]{:S(2)}) %collective-permute-start.34) | collective-permute-done | bytes 917536 | tf_op jit(solution)/shard_map/ppermute | solution.py:1037
  198.2 2.7 %shard_map.170 = (f32[2,256,512]{2,1,0:T(8,128)}, f32[2,256,256]{2,1,0:T(8,128)}, f32[2,256,512]{2,1,0:T(8,128)}, f32[2,512,256]{2,1,0:T(8,128)}, f32[2,2,256]{2...) custom-call(s32[13]{0:T(128)S(1)} %stack.42.info, bf16[1792,256]{1,0:T(8,128)(2,1)S(1)} %shard_map.169.refs_0_, ...), custom_call_target="tpu_custom_call" | custom-call | bytes 5529824 | tf_op jit(solution)/shard_map/pallas_call | solution.py:836
  (95 shorter events, 44.1 us)
Async XLA Ops:
  4.9 31.8 %collective-permute-start.4 = (bf16[768,256]{1,0:T(8,128)(2,1)S(1)}, bf16[768,256]{1,0:T(8,128)(2,1)S(1)}, u32[]{:S(2)}, u32[]{:S(2)}) collective-permute-start(bf16[768,256]{1,0:T(8,128)(2,1)S(1)} %maximum_select_fusion.3), channel_id=1, source_target_pairs={{0,10},{1,14},{2,8},{3,12},{4,11},{5,15},{6,9},{7,13},{8,2},{9,6},... | collective-permute-start | bytes 1179656 | tf_op jit(solution)/shard_map/ppermute | solution.py:949
  10.0 35.0 %collective-permute-start.3 = (bf16[768,256]{1,0:T(8,128)(2,1)S(1)}, bf16[768,256]{1,0:T(8,128)(2,1)S(1)}, u32[]{:S(2)}, u32[]{:S(2)}) collective-permute-start(bf16[768,256]{1,0:T(8,128)(2,1)S(1)} %maximum_select_fusion.2), channel_id=1, source_target_pairs={{0,8},{1,12},{2,10},{3,14},{4,9},{5,13},{6,11},{7,15},{8,0},{9,4},... | collective-permute-start | bytes 1179656 | tf_op jit(solution)/shard_map/ppermute | solution.py:949
  10.6 34.4 %collective-permute-start.2 = (bf16[768,256]{1,0:T(8,128)(2,1)S(1)}, bf16[768,256]{1,0:T(8,128)(2,1)S(1)}, u32[]{:S(2)}, u32[]{:S(2)}) collective-permute-start(bf16[768,256]{1,0:T(8,128)(2,1)S(1)} %maximum_select_fusion.1), channel_id=1, source_target_pairs={{0,2},{1,6},{2,0},{3,4},{4,3},{5,7},{6,1},{7,5},{8,10},{9,14},{10,... | collective-permute-start | bytes 1179656 | tf_op jit(solution)/shard_map/ppermute | solution.py:949
  11.0 33.9 %collective-permute-start.1 = (bf16[768,256]{1,0:T(8,128)(2,1)S(1)}, bf16[768,256]{1,0:T(8,128)(2,1)S(1)}, u32[]{:S(2)}, u32[]{:S(2)}) collective-permute-start(bf16[768,256]{1,0:T(8,128)(2,1)S(1)} %maximum_select_fusion), channel_id=1, source_target_pairs={{0,0},{1,4},{2,2},{3,6},{4,1},{5,5},{6,3},{7,7},{8,8},{9,12},{10,1... | collective-permute-start | bytes 1179656 | tf_op jit(solution)/shard_map/ppermute | solution.py:949
  81.3 20.0 %collective-permute-start.7 = (bf16[768,256]{1,0:T(8,128)(2,1)S(1)}, bf16[768,256]{1,0:T(8,128)(2,1)S(1)}, u32[]{:S(2)}, u32[]{:S(2)}) collective-permute-start(bf16[768,256]{1,0:T(8,128)(2,1)S(1)} %get-tuple-element.114), channel_id=1, source_target_pairs={{0,8},{1,12},{2,10},{3,14},{4,9},{5,13},{6,11},{7,15},{8,0},{9,4},... | collective-permute-start | bytes 1179656 | tf_op jit(solution)/shard_map/ppermute | solution.py:956
  83.9 17.4 %collective-permute-start.12 = (bf16[160,256]{1,0:T(8,128)(2,1)S(1)}, bf16[160,256]{1,0:T(8,128)(2,1)S(1)}, u32[]{:S(2)}, u32[]{:S(2)}) collective-permute-start(bf16[160,256]{1,0:T(8,128)(2,1)S(1)} %get-tuple-element.133), channel_id=1, source_target_pairs={{0,16},{1,17},{2,18},{3,19},{4,20},{5,21},{6,22},{7,23},{8,24},{9,... | collective-permute-start | bytes 245768 | tf_op jit(solution)/shard_map/ppermute | solution.py:1040
  85.5 15.8 %collective-permute-start.13 = (bf16[160,256]{1,0:T(8,128)(2,1)S(1)}, bf16[160,256]{1,0:T(8,128)(2,1)S(1)}, u32[]{:S(2)}, u32[]{:S(2)}) collective-permute-start(bf16[160,256]{1,0:T(8,128)(2,1)S(1)} %get-tuple-element.134), channel_id=1, source_target_pairs={{0,2},{1,3},{2,0},{3,1},{4,6},{5,7},{6,4},{7,5},{8,10},{9,11},{10,... | collective-permute-start | bytes 245768 | tf_op jit(solution)/shard_map/ppermute | solution.py:1040
  86.0 15.3 %collective-permute-start.14 = (bf16[160,256]{1,0:T(8,128)(2,1)S(1)}, bf16[160,256]{1,0:T(8,128)(2,1)S(1)}, u32[]{:S(2)}, u32[]{:S(2)}) collective-permute-start(bf16[160,256]{1,0:T(8,128)(2,1)S(1)} %get-tuple-element.135), channel_id=1, source_target_pairs={{0,18},{1,19},{2,16},{3,17},{4,22},{5,23},{6,20},{7,21},{8,26},{9,... | collective-permute-start | bytes 245768 | tf_op jit(solution)/shard_map/ppermute | solution.py:1040
  102.6 19.9 %collective-permute-start.10 = (bf16[768,256]{1,0:T(8,128)(2,1)S(1)}, bf16[768,256]{1,0:T(8,128)(2,1)S(1)}, u32[]{:S(2)}, u32[]{:S(2)}) collective-permute-start(bf16[768,256]{1,0:T(8,128)(2,1)S(1)} %get-tuple-element.119), channel_id=1, source_target_pairs={{0,10},{1,14},{2,8},{3,12},{4,11},{5,15},{6,9},{7,13},{8,2},{9,6},... | collective-permute-start | bytes 1179656 | tf_op jit(solution)/shard_map/ppermute | solution.py:956
  121.1 8.6 %collective-permute-start.20 = (bf16[896,256]{1,0:T(8,128)(2,1)S(1)}, bf16[896,256]{1,0:T(8,128)(2,1)S(1)}, u32[]{:S(2)}, u32[]{:S(2)}) collective-permute-start(bf16[896,256]{1,0:T(8,128)(2,1)S(1)} %get-tuple-element.170), channel_id=1, source_target_pairs={{0,1},{1,0},{2,3},{3,2},{4,5},{5,4},{6,7},{7,6},{8,9},{9,8},{10,11... | collective-permute-start | bytes 1376264 | tf_op jit(solution)/shard_map/ppermute | solution.py:1037
  128.5 18.9 %collective-permute-start.19 = (bf16[768,256]{1,0:T(8,128)(2,1)S(1)}, bf16[768,256]{1,0:T(8,128)(2,1)S(1)}, u32[]{:S(2)}, u32[]{:S(2)}) collective-permute-start(bf16[768,256]{1,0:T(8,128)(2,1)S(1)} %get-tuple-element.167), channel_id=1, source_target_pairs={{0,8},{1,12},{2,10},{3,14},{4,9},{5,13},{6,11},{7,15},{8,0},{9,4},... | collective-permute-start | bytes 1179656 | tf_op jit(solution)/shard_map/ppermute | solution.py:956
  132.0 9.8 %collective-permute-start.23 = (bf16[320,256]{1,0:T(8,128)(2,1)S(1)}, bf16[320,256]{1,0:T(8,128)(2,1)S(1)}, u32[]{:S(2)}, u32[]{:S(2)}) collective-permute-start(bf16[320,256]{1,0:T(8,128)(2,1)S(1)} %get-tuple-element.175), channel_id=1, source_target_pairs={{0,2},{1,3},{2,0},{3,1},{4,6},{5,7},{6,4},{7,5},{8,10},{9,11},{10,... | collective-permute-start | bytes 491528 | tf_op jit(solution)/shard_map/ppermute | solution.py:1040
  132.8 9.0 %collective-permute-start.24 = (bf16[320,256]{1,0:T(8,128)(2,1)S(1)}, bf16[320,256]{1,0:T(8,128)(2,1)S(1)}, u32[]{:S(2)}, u32[]{:S(2)}) collective-permute-start(bf16[320,256]{1,0:T(8,128)(2,1)S(1)} %get-tuple-element.176), channel_id=1, source_target_pairs={{0,18},{1,19},{2,16},{3,17},{4,22},{5,23},{6,20},{7,21},{8,26},{9,... | collective-permute-start | bytes 491528 | tf_op jit(solution)/shard_map/ppermute | solution.py:1040
  134.0 19.2 %collective-permute-start.18 = (bf16[768,256]{1,0:T(8,128)(2,1)S(1)}, bf16[768,256]{1,0:T(8,128)(2,1)S(1)}, u32[]{:S(2)}, u32[]{:S(2)}) collective-permute-start(bf16[768,256]{1,0:T(8,128)(2,1)S(1)} %get-tuple-element.165), channel_id=1, source_target_pairs={{0,0},{1,4},{2,2},{3,6},{4,1},{5,5},{6,3},{7,7},{8,8},{9,12},{10,1... | collective-permute-start | bytes 1179656 | tf_op jit(solution)/shard_map/ppermute | solution.py:956
  143.1 10.1 %collective-permute-start.9 = (bf16[768,256]{1,0:T(8,128)(2,1)S(1)}, bf16[768,256]{1,0:T(8,128)(2,1)S(1)}, u32[]{:S(2)}, u32[]{:S(2)}) collective-permute-start(bf16[768,256]{1,0:T(8,128)(2,1)S(1)} %get-tuple-element.117), channel_id=1, source_target_pairs={{0,2},{1,6},{2,0},{3,4},{4,3},{5,7},{6,1},{7,5},{8,10},{9,14},{10,... | collective-permute-start | bytes 1179656 | tf_op jit(solution)/shard_map/ppermute | solution.py:956
  144.2 9.1 %collective-permute-start.8 = (bf16[768,256]{1,0:T(8,128)(2,1)S(1)}, bf16[768,256]{1,0:T(8,128)(2,1)S(1)}, u32[]{:S(2)}, u32[]{:S(2)}) collective-permute-start(bf16[768,256]{1,0:T(8,128)(2,1)S(1)} %get-tuple-element.115), channel_id=1, source_target_pairs={{0,0},{1,4},{2,2},{3,6},{4,1},{5,5},{6,3},{7,7},{8,8},{9,12},{10,1... | collective-permute-start | bytes 1179656 | tf_op jit(solution)/shard_map/ppermute | solution.py:956
  147.4 27.8 %collective-permute-start.27 = (bf16[768,256]{1,0:T(8,128)(2,1)S(1)}, bf16[768,256]{1,0:T(8,128)(2,1)S(1)}, u32[]{:S(2)}, u32[]{:S(2)}) collective-permute-start(bf16[768,256]{1,0:T(8,128)(2,1)S(1)} %get-tuple-element.181), channel_id=1, source_target_pairs={{0,10},{1,14},{2,8},{3,12},{4,11},{5,15},{6,9},{7,13},{8,2},{9,6},... | collective-permute-start | bytes 1179656 | tf_op jit(solution)/shard_map/ppermute | solution.py:956
  151.1 24.1 %collective-permute-start.26 = (bf16[768,256]{1,0:T(8,128)(2,1)S(1)}, bf16[768,256]{1,0:T(8,128)(2,1)S(1)}, u32[]{:S(2)}, u32[]{:S(2)}) collective-permute-start(bf16[768,256]{1,0:T(8,128)(2,1)S(1)} %get-tuple-element.179), channel_id=1, source_target_pairs={{0,2},{1,6},{2,0},{3,4},{4,3},{5,7},{6,1},{7,5},{8,10},{9,14},{10,... | collective-permute-start | bytes 1179656 | tf_op jit(solution)/shard_map/ppermute | solution.py:956
  153.3 21.3 %collective-permute-start.28 = (bf16[256,256]{1,0:T(8,128)(2,1)S(1)}, bf16[256,256]{1,0:T(8,128)(2,1)S(1)}, u32[]{:S(2)}, u32[]{:S(2)}) collective-permute-start(bf16[256,256]{1,0:T(8,128)(2,1)S(1)} %get-tuple-element.185.refs_0_), channel_id=1, source_target_pairs={{0,8},{1,9},{2,10},{3,11},{4,12},{5,13},{6,14},{7,15},{8,0},{9,1},... | collective-permute-start | bytes 393224 | tf_op jit(solution)/shard_map/ppermute | solution.py:1040
  153.9 31.7 %collective-permute-start.17 = (bf16[4,384,256]{2,1,0:T(8,128)(2,1)S(1)}, bf16[4,384,256]{2,1,0:T(8,128)(2,1)S(1)}, u32[]{:S(2)}, u32[]{:S(2)}) collective-permute-start(bf16[4,384,256]{2,1,0:T(8,128)(2,1)S(1)} %shard_map.160), channel_id=1, source_target_pairs={{0,1},{1,0},{2,3},{3,2},{4,5},{5,4},{6,7},{7,6},{8,9},{9,8},{10,11... | collective-permute-start | bytes 2359304 | tf_op jit(solution)/shard_map/ppermute | solution.py:961
  175.8 12.1 %collective-permute-start.29 = (bf16[4,384,256]{2,1,0:T(8,128)(2,1)S(1)}, bf16[4,384,256]{2,1,0:T(8,128)(2,1)S(1)}, u32[]{:S(2)}, u32[]{:S(2)}) collective-permute-start(bf16[4,384,256]{2,1,0:T(8,128)(2,1)S(1)} %shard_map.166), channel_id=1, source_target_pairs={{0,1},{1,0},{2,3},{3,2},{4,5},{5,4},{6,7},{7,6},{8,9},{9,8},{10,11... | collective-permute-start | bytes 2359304 | tf_op jit(solution)/shard_map/ppermute | solution.py:961
  182.0 8.6 %collective-permute-start.31 = (bf16[448,256]{1,0:T(8,128)(2,1)S(1)}, bf16[448,256]{1,0:T(8,128)(2,1)S(1)}, u32[]{:S(2)}, u32[]{:S(2)}) collective-permute-start(bf16[448,256]{1,0:T(8,128)(2,1)S(1)} %shard_map.168.refs_0_), channel_id=1, source_target_pairs={{0,16},{1,17},{2,18},{3,19},{4,20},{5,21},{6,22},{7,23},{8,24},{9,... | collective-permute-start | bytes 688136 | tf_op jit(solution)/shard_map/ppermute | solution.py:1040
  183.4 11.7 %collective-permute-start.32 = (bf16[448,256]{1,0:T(8,128)(2,1)S(1)}, bf16[448,256]{1,0:T(8,128)(2,1)S(1)}, u32[]{:S(2)}, u32[]{:S(2)}) collective-permute-start(bf16[448,256]{1,0:T(8,128)(2,1)S(1)} %shard_map.168.refs_0_), channel_id=1, source_target_pairs={{0,2},{1,3},{2,0},{3,1},{4,6},{5,7},{6,4},{7,5},{8,10},{9,11},{10,... | collective-permute-start | bytes 688136 | tf_op jit(solution)/shard_map/ppermute | solution.py:1040
  184.4 10.6 %collective-permute-start.33 = (bf16[448,256]{1,0:T(8,128)(2,1)S(1)}, bf16[448,256]{1,0:T(8,128)(2,1)S(1)}, u32[]{:S(2)}, u32[]{:S(2)}) collective-permute-start(bf16[448,256]{1,0:T(8,128)(2,1)S(1)} %shard_map.168.refs_0_), channel_id=1, source_target_pairs={{0,18},{1,19},{2,16},{3,17},{4,22},{5,23},{6,20},{7,21},{8,26},{9,... | collective-permute-start | bytes 688136 | tf_op jit(solution)/shard_map/ppermute | solution.py:1040
  (18 other events, 75.6 us)
